TPU v7x, 128 devices: a whole 4x4x4 slice. The times are simulated.
128 devices in a mesh: seq: 32 (over y, z, core), ch: 4 (over x).
Axes of the slice: x: 4, y: 4, z: 4, core: 2. Of those that a mesh axis runs over, the one named last changes fastest.
Arguments:
- block_input: bfloat16 [16384, 1024], P('seq', 'ch'), may hold values from -36 to 36
- segment_ids: int32 [16384], P('seq'), may hold values from 0 to 1, as said below
- norm1_gain: float32 [1024], replicated, may hold values from 0.25 to 1.75
- in_weight: bfloat16 [1024, 3, 1024], P(None, None, 'ch'), may hold values from -0.1875 to 0.1875
- conv_weight: float32 [3, 1024], P(None, 'ch'), may hold values from -3 to 3
- out_weight: bfloat16 [1024, 1024], P(None, 'ch'), may hold values from -0.1875 to 0.1875
- norm2_gain: float32 [1024], replicated, may hold values from 0.25 to 1.75
- ffn_in_weight: bfloat16 [1024, 2, 4608], P(None, None, 'ch'), may hold values from -0.1875 to 0.1875
- ffn_out_weight: bfloat16 [1024, 4608], P(None, 'ch'), may hold values from -0.125 to 0.125
- out_grad: bfloat16 [16384, 1024], P('seq', 'ch'), may hold values from -6 to 6
Outputs:
- block_output: bfloat16 [16384, 1024], P('seq', 'ch')
- input_grad: bfloat16 [16384, 1024], P('seq', 'ch')
- grad_norm1_gain: float32 [1024], P('ch')
- grad_in_weight: float32 [1024, 3, 1024], P('seq', None, 'ch')
- grad_conv_weight: float32 [3, 1024], P(None, 'ch')
- grad_out_weight: float32 [1024, 1024], P('seq', 'ch')
- grad_norm2_gain: float32 [1024], P('ch')
- grad_ffn_in_weight: float32 [1024, 2, 4608], P('seq', None, 'ch')
- grad_ffn_out_weight: float32 [1024, 4608], P('seq', 'ch')
Inputs may be any that keep to these rules, and one draw needn't show every extreme that they name: `segment_ids`: two sequences: ids are 0 before a position b and 1 from b on, with 1024 <= b <= 15360 and b % 512 >= 3.
All inputs are finite; a program needn't handle non-finite values.
Results may differ from a plain program's by a relative error of at most 0.0099.
Values may be sent and summed in bfloat16 or wider, within the bound.
No kernel may reach another device: no remote copies, remote signals or barrier semaphores. Data moves between devices by JAX's collectives and lax.ppermute only.
A program may use at most 128 MiB of HBM per device.

v0:
```python
import jax
import jax.numpy as jnp
from jax import lax
from jax.experimental import pallas as pl
from jax.experimental.pallas import tpu as pltpu
from jax.sharding import PartitionSpec as P

EPS = 1e-05
F32 = jnp.float32
BF16 = jnp.bfloat16
CH = 4


def seq_index(y, z, core):
    return ((y % 4) * 4 + z % 4) * 2 + core


def seq_pairs(dy, dz, dcore):
    return [
        (seq_index(y, z, core), seq_index(y + dy, z + dz, core ^ dcore))
        for y in range(4)
        for z in range(4)
        for core in range(2)
    ]


def ch_pairs(step):
    return [(i, (i + step) % CH) for i in range(CH)]


def gather_ch(block):
    return [block] + [lax.ppermute(block, "ch", ch_pairs(-j)) for j in range(1, CH)]


def scatter_ch(chunks):
    total = chunks[0]
    for j in range(1, CH):
        total = total + lax.ppermute(chunks[j], "ch", ch_pairs(j)).astype(F32)
    return total


def sum_ch(vector):
    total = vector
    for j in range(1, CH):
        total = total + lax.ppermute(vector, "ch", ch_pairs(j))
    return total


def pick(array, index, axis):
    return lax.dynamic_index_in_dim(array, index, axis, keepdims=False)


def from_behind(array, axis, by):
    size = lax.axis_size(axis)
    pairs = [(i, i + by) for i in range(size) if 0 <= i + by < size]
    return lax.ppermute(array, axis, pairs)


def tap_masks(segment_ids):
    padded = jnp.concatenate([segment_ids[:1], segment_ids[:1], segment_ids])
    same_one = (padded[2:] == padded[1:-1]).astype(F32)[:, None]
    same_two = (padded[2:] == padded[:-2]).astype(F32)[:, None]
    return (same_one, same_two)


def tie(*arrays):
    return lax.optimization_barrier(arrays)


def reduce_axis(array, axis, me, along_y):
    total = pick(array, me, axis).astype(F32)
    for step in (1, 3, 2):
        pairs = seq_pairs(step, 0, 0) if along_y else seq_pairs(0, step, 0)
        total = total + lax.ppermute(pick(array, (me + step) % 4, axis), "seq", pairs).astype(F32)
    return total


def dot_nt(a, b):
    return lax.dot_general(a, b, (((1,), (1,)), ((), ())), preferred_element_type=F32)


def dot_tn(a, b):
    return lax.dot_general(a, b, (((0,), (0,)), ((), ())), preferred_element_type=F32)


def dot_nn(a, b):
    return lax.dot_general(a, b, (((1,), (0,)), ((), ())), preferred_element_type=F32)


def rel_rows(x, j, width):
    return pl.ds(pl.multiple_of(lax.rem(x + j, CH) * width, width), width)


def vmem():
    return pl.BlockSpec(memory_space=pltpu.VMEM)


def smem():
    return pl.BlockSpec(memory_space=pltpu.SMEM)


def anywhere():
    return pl.BlockSpec(memory_space=pl.ANY)


def shape(dims, dtype):
    return jax.ShapeDtypeStruct(dims, dtype)


def params(megabytes):
    return pltpu.CompilerParams(vmem_limit_bytes=megabytes * 1024 * 1024)


def cost(macs, nbytes):
    return pl.CostEstimate(flops=2 * macs, bytes_accessed=nbytes, transcendentals=0)


def in_kernel(at, p0, p1, p2, p3, gain, weight, normed, rms, b_out, c_out, v_out, gated, held, sem):
    x = at[0]
    width = p0.shape[1]
    copies = [
        pltpu.make_async_copy(
            weight.at[:, rel_rows(x, j, width), :],
            held.at[:, pl.ds(j * width, width), :],
            sem.at[j],
        )
        for j in range(CH)
    ]
    for copy in copies:
        copy.start()
    pieces = [p0, p1, p2, p3]
    square = jnp.zeros((p0.shape[0], 1), F32)
    for piece in pieces:
        rows = piece[...].astype(F32)
        square = square + jnp.sum(rows * rows, axis=1, keepdims=True)
    r = lax.rsqrt(square / (CH * width) + EPS)
    rms[...] = r
    for j, piece in enumerate(pieces):
        scale = gain[:, rel_rows(x, j, width)]
        normed[:, j * width : (j + 1) * width] = (piece[...].astype(F32) * r * scale).astype(BF16)
    for copy in copies:
        copy.wait()
    b = dot_nn(normed[...], held[0])
    v = dot_nn(normed[...], held[2])
    b_out[...] = b
    v_out[...] = v
    gated[...] = (b * v).astype(BF16)
    c_out[...] = dot_nn(normed[...], held[1])


def in_project(at, pieces, gain, weight):
    rows, width = pieces[0].shape
    features = CH * width
    out = shape((rows, width), F32)
    return pl.pallas_call(
        in_kernel,
        out_shape=(
            shape((rows, features), BF16),
            shape((rows, 1), F32),
            out,
            out,
            out,
            shape((rows, width), BF16),
        ),
        in_specs=[smem()] + [vmem()] * 5 + [anywhere()],
        out_specs=(vmem(),) * 6,
        scratch_shapes=[
            pltpu.VMEM((3, features, width), BF16),
            pltpu.SemaphoreType.DMA((CH,)),
        ],
        compiler_params=params(24),
        cost_estimate=cost(rows * features * 3 * width, 6 * 2**20),
    )(at, *pieces, gain[None], weight)


def ffn_kernel(
    at,
    x0, x1, x2, x3,
    m0, m1, m2, m3,
    gain,
    half,
    other,
    planes,
    down,
    cotangent,
    h_own, rms, normed, act, d_gate_up, d_own, d1, d2, d3, inner,
    w_out, w_in, w_down, g_rows, mixed, h, acc, sem,
):
    x, core = at[0], at[1]
    width = x0.shape[1]
    units = down.shape[1]
    step = units // 3
    halves = [
        pltpu.make_async_copy(half, w_out.at[0], sem.at[0]),
        pltpu.make_async_copy(other, w_out.at[1], sem.at[1]),
    ]
    planes_in = [
        pltpu.make_async_copy(
            planes.at[:, rel_rows(x, j, width), :],
            w_in.at[:, pl.ds(j * width, width), :],
            sem.at[2 + j],
        )
        for j in range(CH)
    ]
    rest = [
        pltpu.make_async_copy(cotangent, g_rows, sem.at[6]),
        pltpu.make_async_copy(down, w_down, sem.at[7]),
    ]
    for copy in halves + planes_in + rest:
        copy.start()
    for j, piece in enumerate((m0, m1, m2, m3)):
        mixed[:, j * width : (j + 1) * width] = piece[...]
    for copy in halves:
        copy.wait()
    square = jnp.zeros((x0.shape[0], 1), F32)
    for j, piece in enumerate((x0, x1, x2, x3)):
        block = lax.rem(x + j, CH)
        which = lax.rem(block // 2 + core, 2)
        rows = pl.ds(pl.multiple_of(lax.rem(block, 2) * width, width), width)
        hj = piece[...].astype(F32) + dot_nt(mixed[...], w_out[which, rows, :])
        h[:, j * width : (j + 1) * width] = hj
        square = square + jnp.sum(hj * hj, axis=1, keepdims=True)
    r = lax.rsqrt(square / (CH * width) + EPS)
    rms[...] = r
    h_own[...] = h[:, :width]
    for j in range(CH):
        columns = slice(j * width, (j + 1) * width)
        scale = gain[:, rel_rows(x, j, width)]
        normed[:, columns] = (h[:, columns] * r * scale).astype(BF16)
    for copy in planes_in + rest:
        copy.wait()

    def part(i, carry):
        f = pl.ds(pl.multiple_of(i * step, 128), step)
        f_up = pl.ds(pl.multiple_of(units + i * step, 128), step)
        gate = dot_nn(normed[...], w_in[0, :, f])
        up = dot_nn(normed[...], w_in[1, :, f])
        d_act = dot_nn(g_rows[...], w_down[:, f])
        sigma = jax.nn.sigmoid(gate)
        swish = gate * sigma
        act[:, f] = (swish * up).astype(BF16)
        d_gate = (d_act * up * sigma * (1.0 + gate * (1.0 - sigma))).astype(BF16)
        d_up = (d_act * swish).astype(BF16)
        d_gate_up[:, f] = d_gate
        d_gate_up[:, f_up] = d_up
        for j in range(CH):
            rows = slice(j * width, (j + 1) * width)
            term = dot_nt(d_gate, w_in[0, rows, f]) + dot_nt(d_up, w_in[1, rows, f])
            acc[j] = jnp.where(i == 0, term, acc[j] + term)
        return carry

    lax.fori_loop(0, 3, part, 0)
    total = jnp.zeros((x0.shape[0], 1), F32)
    for j in range(CH):
        scale = gain[:, rel_rows(x, j, width)]
        total = total + jnp.sum(
            scale * acc[j] * h[:, j * width : (j + 1) * width], axis=1, keepdims=True
        )
    inner[...] = total
    d_own[...] = acc[0]
    d1[...] = acc[1].astype(BF16)
    d2[...] = acc[2].astype(BF16)
    d3[...] = acc[3].astype(BF16)


def ffn(at, pieces, mixed_pieces, gain, half, other, planes, down, cotangent):
    rows, width = pieces[0].shape
    features = CH * width
    units = down.shape[1]
    block, column = shape((rows, width), BF16), shape((rows, 1), F32)
    wide = shape((rows, width), F32)
    return pl.pallas_call(
        ffn_kernel,
        out_shape=(
            wide,
            column,
            shape((rows, features), BF16),
            shape((rows, units), BF16),
            shape((rows, 2 * units), BF16),
            wide,
            block,
            block,
            block,
            column,
        ),
        in_specs=[smem()] + [vmem()] * 9 + [anywhere()] * 5,
        out_specs=(vmem(),) * 10,
        scratch_shapes=[
            pltpu.VMEM((2, features // 2, features), BF16),
            pltpu.VMEM((2, features, units), BF16),
            pltpu.VMEM((features, units), BF16),
            pltpu.VMEM((rows, features), BF16),
            pltpu.VMEM((rows, features), BF16),
            pltpu.VMEM((rows, features), F32),
            pltpu.VMEM((CH, rows, width), F32),
            pltpu.SemaphoreType.DMA((8,)),
        ],
        compiler_params=params(48),
        cost_estimate=cost(rows * features * (features + 5 * units), 20 * 2**20),
    )(at, *pieces, *mixed_pieces, gain[None], half, other, planes, down, cotangent)


def pair_kernel(
    at, a_left, a_right, b_left, b_right, give, keep, held, *, a_rolled, b_rolled
):
    x, core = at[0], at[1]
    y = pl.program_id(0)
    wide = give.shape[2] * 8
    turned = lax.rem(y + CH - x, CH)
    cut = a_right.shape[1]
    for left, right, rolled, base in (
        (a_left, a_right, a_rolled, 0),
        (b_left, b_right, b_rolled, cut),
    ):
        where = turned if rolled else y
        block = left[:, pl.ds(pl.multiple_of(where * wide, wide), wide)]
        columns = right.shape[1]
        step = columns // 3 if columns % 384 == 0 else columns
        for first in range(0, columns, step):
            held[:, base + first : base + first + step] = dot_tn(
                block, right[:, first : first + step]
            )
    for z in range(4):
        mine = pl.multiple_of((2 * z + core) * 32, 32)
        theirs = pl.multiple_of((2 * z + 1 - core) * 32, 32)
        keep[z, 0] = held[pl.ds(mine, 32), :].astype(BF16)
        give[z, 0] = held[pl.ds(theirs, 32), :].astype(BF16)


def pair_products(at, a_left, a_right, b_left, b_right, a_rolled, b_rolled):
    columns = a_right.shape[1] + b_right.shape[1]
    tokens, features = a_left.shape
    out = shape((4, 4, features // 32, columns), BF16)
    spec = pl.BlockSpec((4, 1, features // 32, columns), lambda y: (0, y, 0, 0))

    def body(*refs):
        pair_kernel(*refs, a_rolled=a_rolled, b_rolled=b_rolled)

    return pl.pallas_call(
        body,
        grid=(4,),
        out_shape=(out, out),
        in_specs=[smem()] + [vmem()] * 4,
        out_specs=(spec, spec),
        scratch_shapes=[pltpu.VMEM((features // 4, columns), F32)],
        compiler_params=params(40),
        cost_estimate=cost(tokens * features * columns, 4 * features * columns),
    )(at, a_left, a_right, b_left, b_right)


def back_kernel(at, p0, p1, p2, p3, grads, gain, weight, d_own, d1, d2, d3, inner, held, sem):
    x = at[0]
    width = p0.shape[1]
    copies = [
        pltpu.make_async_copy(
            weight.at[:, rel_rows(x, j, width), :],
            held.at[:, pl.ds(j * width, width), :],
            sem.at[j],
        )
        for j in range(CH)
    ]
    for copy in copies:
        copy.start()
    total = jnp.zeros((p0.shape[0], 1), F32)
    for j, piece in enumerate((p0, p1, p2, p3)):
        copies[j].wait()
        rows = slice(j * width, (j + 1) * width)
        term = dot_nt(grads[:, :width], held[0, rows, :])
        for k in (1, 2):
            term = term + dot_nt(grads[:, k * width : (k + 1) * width], held[k, rows, :])
        scale = gain[:, rel_rows(x, j, width)]
        total = total + jnp.sum(scale * term * piece[...].astype(F32), axis=1, keepdims=True)
        if j == 0:
            d_own[...] = term
        else:
            (d1, d2, d3)[j - 1][...] = term.astype(BF16)
    inner[...] = total


def back_project(at, pieces, grads, gain, weight):
    rows, width = pieces[0].shape
    features = CH * width
    block = shape((rows, width), BF16)
    return pl.pallas_call(
        back_kernel,
        out_shape=(shape((rows, width), F32), block, block, block, shape((rows, 1), F32)),
        in_specs=[smem()] + [vmem()] * 6 + [anywhere()],
        out_specs=(vmem(),) * 5,
        scratch_shapes=[
            pltpu.VMEM((3, features, width), BF16),
            pltpu.SemaphoreType.DMA((CH,)),
        ],
        compiler_params=params(24),
        cost_estimate=cost(rows * features * 3 * width, 6 * 2**20),
    )(at, *pieces, grads, gain[None], weight)


def scatter_groups(array, groups):
    return lax.psum_scatter(array, "seq", scatter_dimension=0, axis_index_groups=groups)


def shards(
    block_input,
    segment_ids,
    norm1_gain,
    in_weight,
    conv_weight,
    out_weight,
    norm2_gain,
    ffn_in_weight,
    ffn_out_weight,
    out_grad,
):
    x = lax.axis_index("ch")
    seq = lax.axis_index("seq")
    core, z, y = seq % 2, (seq // 2) % 4, seq // 8
    features = norm1_gain.shape[0]
    width = block_input.shape[1]
    hidden_units = ffn_out_weight.shape[1]

    def rolled(array):
        blocks = array.reshape((CH, width) + array.shape[1:])
        return jnp.concatenate([pick(blocks, (x + j) % CH, 0) for j in range(CH)], axis=0)

    at = jnp.stack([x, core]).astype(jnp.int32)
    own_one = pick(norm1_gain.reshape(CH, width), x, 0)
    own_two = pick(norm2_gain.reshape(CH, width), x, 0)
    in_planes = jnp.transpose(in_weight, (1, 0, 2))

    pieces = gather_ch(block_input)
    half_rows = out_weight.shape[0] // 2
    half = lax.dynamic_slice_in_dim(out_weight, core * half_rows, half_rows, 0)
    half_pieces = gather_ch(half)
    grad_full = lax.all_gather(out_grad, "ch", axis=1, tiled=True)
    ffn_planes = jnp.transpose(ffn_in_weight, (1, 0, 2))
    ffn_planes, *pieces = tie(ffn_planes, *pieces)

    normed_one, r_one, b_gate, c_gate, value_rows, gated_rows = in_project(
        at, pieces, norm1_gain, in_planes
    )
    own_rows = block_input.astype(F32)
    carried = from_behind(gated_rows[-2:], "seq", 1)
    extended = jnp.concatenate([carried, gated_rows], axis=0).astype(F32)
    same_one, same_two = tap_masks(segment_ids)
    current = extended[2:]
    prior_one = extended[1:-1] * same_one
    prior_two = extended[:-2] * same_two
    conv_out = conv_weight[0] * current + conv_weight[1] * prior_one + conv_weight[2] * prior_two
    mixed_rows = (c_gate * conv_out).astype(BF16)

    mixed_pieces = gather_ch(mixed_rows)
    half_pieces = tie(*half_pieces, mixed_rows)[:CH]
    half_full = jnp.concatenate(half_pieces, axis=1)
    other_half = lax.ppermute(half_full, "seq", seq_pairs(0, 0, 1))
    out_rolled = rolled(tie(out_weight, mixed_rows)[0])
    (
        hidden_own,
        r_two,
        normed_two,
        act_rows,
        d_gate_up,
        d_own,
        d_one,
        d_two,
        d_three,
        inner,
    ) = ffn(
        at,
        pieces,
        mixed_pieces,
        norm2_gain,
        half_full,
        other_half,
        ffn_planes,
        ffn_out_weight,
        grad_full,
    )
    d_normed_own = scatter_ch([d_own, d_one, d_two, d_three])
    inner_two = sum_ch(inner[:, 0])[:, None]

    give, keep = pair_products(at, normed_two, d_gate_up, grad_full, act_rows, True, False)
    got = lax.ppermute(give, "seq", seq_pairs(0, 0, 1))
    down_terms = jnp.einsum(
        "tf,ef->te", act_rows, ffn_out_weight, preferred_element_type=F32
    ).astype(BF16)
    down = lax.psum_scatter(down_terms, "ch", scatter_dimension=1, tiled=True)
    block_output = (hidden_own + down.astype(F32)).astype(BF16)

    grad_gain_two = jnp.sum(d_normed_own * hidden_own * r_two, axis=0)
    d_hidden = (
        out_grad.astype(F32)
        + r_two * own_two * d_normed_own
        - hidden_own * (r_two * r_two * r_two) / features * inner_two
    )
    d_branch = jnp.concatenate(gather_ch(d_hidden.astype(BF16)), axis=1)
    ffn_kept = (keep.astype(F32) + got.astype(F32)).astype(BF16)
    d_branch, ffn_kept, out_rolled = tie(d_branch, ffn_kept, out_rolled)
    groups = [[seq_index(i, k, c) for k in range(4)] for i in range(4) for c in range(2)]
    ffn_sum = scatter_groups(ffn_kept, groups)
    groups = [[seq_index(k, i, c) for k in range(4)] for i in range(4) for c in range(2)]
    ffn_sum = scatter_groups(ffn_sum, groups).astype(F32)
    grad_ffn_in = ffn_sum[:, : 2 * hidden_units].reshape(-1, 2, hidden_units)
    grad_ffn_out = ffn_sum[:, 2 * hidden_units :]

    d_mixed = jnp.dot(d_branch, out_rolled, preferred_element_type=F32)
    d_cgate = d_mixed * conv_out
    d_conv = d_mixed * c_gate
    following = from_behind(d_conv[:2], "seq", -1)
    edge_one = d_conv * same_one
    edge_two = d_conv * same_two
    after_one = jnp.concatenate([edge_one[1:], following[:1]], axis=0)
    after_two = jnp.concatenate([edge_two[2:], following], axis=0)
    d_gated = conv_weight[0] * d_conv + conv_weight[1] * after_one + conv_weight[2] * after_two
    d_proj = jnp.concatenate(
        [d_gated * value_rows, d_cgate, d_gated * b_gate], axis=1
    ).astype(BF16)
    d_own, d_one, d_two, d_three, inner = back_project(
        at, pieces, d_proj, norm1_gain, in_planes
    )
    d_own_one = scatter_ch([d_own, d_one, d_two, d_three])
    inner_one = sum_ch(inner[:, 0])[:, None]

    give, keep = pair_products(at, normed_one, d_proj, d_branch, mixed_rows, True, True)
    got = lax.ppermute(give, "seq", seq_pairs(0, 0, 1))
    mix_sum = (keep.astype(F32) + got.astype(F32)).astype(BF16)
    mix_sum = reduce_axis(mix_sum, 0, z, False).astype(BF16)
    mix_sum = reduce_axis(mix_sum, 0, y, True)
    grad_in = mix_sum[:, : 3 * width].reshape(-1, 3, width)
    grad_out = mix_sum[:, 3 * width :]

    grad_conv = jnp.stack(
        [
            jnp.sum(d_conv * current, axis=0),
            jnp.sum(d_conv * prior_one, axis=0),
            jnp.sum(d_conv * prior_two, axis=0),
        ],
        axis=0,
    )
    grad_gain_one = jnp.sum(d_own_one * own_rows * r_one, axis=0)
    input_grad = (
        d_hidden
        + r_one * own_one * d_own_one
        - own_rows * (r_one * r_one * r_one) / features * inner_one
    ).astype(BF16)

    small = jnp.concatenate([grad_conv, grad_gain_one[None], grad_gain_two[None]], axis=0)
    small = small + lax.ppermute(small, "seq", seq_pairs(0, 0, 1))
    for along in (0, 1):
        steps = [(0, 1), (0, 2), (0, 3)] if along == 0 else [(1, 0), (2, 0), (3, 0)]
        small = small + sum(lax.ppermute(small, "seq", seq_pairs(dy, dz, 0)) for dy, dz in steps)
    return (
        block_output,
        input_grad,
        small[3],
        grad_in,
        small[:3],
        grad_out,
        small[4],
        grad_ffn_in,
        grad_ffn_out,
    )


def solution(mesh):
    return jax.shard_map(
        shards,
        mesh=mesh,
        in_specs=(
            P("seq", "ch"),
            P("seq"),
            P(),
            P(None, None, "ch"),
            P(None, "ch"),
            P(None, "ch"),
            P(),
            P(None, None, "ch"),
            P(None, "ch"),
            P("seq", "ch"),
        ),
        out_specs=(
            P("seq", "ch"),
            P("seq", "ch"),
            P("ch"),
            P("seq", None, "ch"),
            P(None, "ch"),
            P("seq", "ch"),
            P("ch"),
            P("seq", None, "ch"),
            P("seq", "ch"),
        ),
        check_vma=False,
    )
```

profile of v0, /device:TPU:0, one launch (start us, length us, event | category | flops | bytes accessed | tf_op | source)
XLA Modules:
  0.0 243.1 jit_solution(2403743459524802479)
XLA Ops:
  7.2 2.9 %collective-permute-start = (bf16[512,256]{1,0:T(8,128)(2,1)}, bf16[512,256]{1,0:T(8,128)(2,1)S(1)}, u32[]{:S(2)}, u32[]{:S(2)}) collective-permute-start(bf16[512,256]{1,0:T(8,128)(2,1)} %p0.1), channel_id=1, source_target_pairs={{0,3},{1,0},{2,1},{3,2},{4,7},{5,4},{6,5},{7,6},{8,11},{9,8},{10,9... | collective-permute-start | bytes 786440 | tf_op jit(solution)/shard_map/ppermute | solution.py:32
  12.8 2.4 collective-permute-start.7
  20.9 5.2 %copy.26 = bf16[1024,2,1152]{2,0,1:T(8,128)(2,1)} copy(bf16[1024,2,1152]{2,1,0:T(2,128)(2,1)} %param.17) | data formatting | bytes 9437184 | tf_op args[7]
  26.7 2.4 shard_map.169
  34.9 4.5 %collective-permute-done.9 = bf16[512,256]{1,0:T(8,128)(2,1)S(1)} collective-permute-done((bf16[512,256]{1,0:T(8,128)(2,1)S(1)}, bf16[512,256]{1,0:T(8,128)(2,1)S(1)}, u32[]{:S(2)}, u32[]{:S(2)}) %collective-permute-start.9) | collective-permute-done | bytes 262176 | tf_op jit(solution)/shard_map/ppermute | solution.py:32
  42.3 9.3 %collective-permute-done.4.m1 = bf16[512,256]{1,0:T(8,128)(2,1)S(1)} collective-permute-done((bf16[512,256]{1,0:T(8,128)(2,1)S(1)}, bf16[512,256]{1,0:T(8,128)(2,1)S(1)}, u32[]{:S(2)}, u32[]{:S(2)}) %collective-permute-start.4) | collective-permute-done | bytes 262176 | tf_op jit(solution)/shard_map/ppermute | solution.py:32
  52.8 5.3 %collective-permute-done.6.m3 = bf16[512,256]{1,0:T(8,128)(2,1)S(1)} collective-permute-done((bf16[512,256]{1,0:T(8,128)(2,1)S(1)}, bf16[512,256]{1,0:T(8,128)(2,1)S(1)}, u32[]{:S(2)}, u32[]{:S(2)}) %collective-permute-start.6) | collective-permute-done | bytes 262176 | tf_op jit(solution)/shard_map/ppermute | solution.py:32
  59.1 15.1 %shard_map.170 = (f32[512,256]{1,0:T(8,128)S(1)}, f32[512,1]{1,0:T(8,128)S(1)}, bf16[512,1024]{1,0:T(8,128)(2,1)S(1)}, bf16[512,1152]{1,0:T(8,128)(2,1)}, bf16[5...) custom-call(s32[2]{0:T(128)S(1)} %pad_add_fusion.2.at.refs_0_, ...), custom_call_target="tpu_custom_call" | custom-call | flops 7113539584 | bytes 20971520 | tf_op jit(solution)/shard_map/pallas_call | solution.py:272
  74.4 2.4 %copy-done.38 = bf16[512,2304]{1,0:T(8,128)(2,1)S(1)} copy-done((bf16[512,2304]{1,0:T(8,128)(2,1)S(1)}, bf16[512,2304]{1,0:T(8,128)(2,1)}, u32[]{:S(2)}) %copy-start.38) | copy-done | bytes 2359320
  78.1 7.4 %shard_map.171 = (bf16[4,4,32,3456]{3,2,1,0:T(8,128)(2,1)}, bf16[4,4,32,3456]{3,2,1,0:T(8,128)(2,1)S(1)}) custom-call(s32[2]{0:T(128)S(1)} %pad_add_fusion.2.at.refs_0_, bf16[512,1024]{1,0:T(8,128)(2,1)S(1)} %get-tuple-element.67.refs_1_, bf16[512,2304]{1,0:T(8,128)(2,1)S(1)} %copy-done.38, bf16[512,1024]{1,0:T(8,128)(2,1)S(1)} %copy-done.29, ...), custom_call_target="tpu_custom_call" | custom-call | flops 3623878656 | bytes 14155776 | tf_op jit(solution)/shard_map/pallas_call | solution.py:339
  85.8 2.6 %convolution_convert_fusion = bf16[512,1024]{1,0:T(8,128)(2,1)} fusion(bf16[512,1152]{1,0:T(8,128)(2,1)S(1)} %copy-done.39, bf16[1024,1152]{1,0:T(8,128)(2,1)S(1)} %copy-done.55), kind=kOutput, calls=%fused_computation.3 | convolution fusion | flops 1208483840 | bytes 4587520 | tf_op jit(solution)/shard_map/tf,ef->te/dot_general | solution.py:483
  94.4 2.7 %collective-permute-start.13 = (bf16[512,256]{1,0:T(8,128)(2,1)}, bf16[512,256]{1,0:T(8,128)(2,1)}, u32[]{:S(2)}, u32[]{:S(2)}) collective-permute-start(bf16[512,256]{1,0:T(8,128)(2,1)} %copy-done.32), channel_id=1, source_target_pairs={{0,3},{1,0},{2,1},{3,2},{4,7},{5,4},{6,5},{7,6},{8,11},{9,8},{10,9... | collective-permute-start | bytes 786440 | tf_op jit(solution)/shard_map/ppermute | solution.py:38
  101.4 8.0 %collective-permute-done.13 = bf16[512,256]{1,0:T(8,128)(2,1)} collective-permute-done((bf16[512,256]{1,0:T(8,128)(2,1)}, bf16[512,256]{1,0:T(8,128)(2,1)}, u32[]{:S(2)}, u32[]{:S(2)}) %collective-permute-start.13) | collective-permute-done | bytes 262176 | tf_op jit(solution)/shard_map/ppermute | solution.py:38
  109.4 2.7 %collective-permute-done.12 = bf16[512,256]{1,0:T(8,128)(2,1)} collective-permute-done((bf16[512,256]{1,0:T(8,128)(2,1)}, bf16[512,256]{1,0:T(8,128)(2,1)}, u32[]{:S(2)}, u32[]{:S(2)}) %collective-permute-start.12) | collective-permute-done | bytes 262176 | tf_op jit(solution)/shard_map/ppermute | solution.py:38
  112.1 5.6 %collective-permute-done.11 = bf16[512,256]{1,0:T(8,128)(2,1)} collective-permute-done((bf16[512,256]{1,0:T(8,128)(2,1)}, bf16[512,256]{1,0:T(8,128)(2,1)}, u32[]{:S(2)}, u32[]{:S(2)}) %collective-permute-start.11) | collective-permute-done | bytes 262176 | tf_op jit(solution)/shard_map/ppermute | solution.py:38
  117.7 3.7 %reduce-scatter.4.cloned.1.call-done = bf16[512,256]{1,0:T(8,128)(2,1)} async-done(((bf16[512,1024]{1,0:T(8,128)(2,1)}), bf16[512,256]{1,0:T(8,128)(2,1)}) %reduce-scatter.4.cloned.1.call-update) | async-done | bytes 262160 | tf_op jit(solution)/shard_map/reduce_scatter | solution.py:486
  121.4 3.5 %fusion.19 = (bf16[512,256]{1,0:T(8,128)(2,1)}, f32[512,256]{1,0:T(8,128)}, f32[256]{0:T(256)}, bf16[512,256]{1,0:T(8,128)(2,1)}) fusion(f32[512]{0:T(512)} %add_multiply_fusion.1, f32[512,256]{1,0:T(8,128)} %copy-done.12, f32[512]{0:T(512)} %get-tuple-element.109, bf16[512,256]{1,0:T(8,128)(2,1)} %collective-permute-done.13, ...), kind=kLoop, calls=%fused_computation.79 | loop fusion | flops 2621184 | bytes 3416064 | tf_op jit(solution)/shard_map/convert_element_type | solution.py:495
  126.1 2.7 %collective-permute-start.18 = (bf16[512,256]{1,0:T(8,128)(2,1)}, bf16[512,256]{1,0:T(8,128)(2,1)}, u32[]{:S(2)}, u32[]{:S(2)}) collective-permute-start(bf16[512,256]{1,0:T(8,128)(2,1)} %get-tuple-element.113), channel_id=1, source_target_pairs={{0,2},{1,3},{2,0},{3,1},{4,6},{5,7},{6,4},{7,5},{8,10},{9,11},{10,... | collective-permute-start | bytes 786440 | tf_op jit(solution)/shard_map/ppermute | solution.py:32
  130.9 9.5 %collective-permute-done.19 = bf16[512,256]{1,0:T(8,128)(2,1)} collective-permute-done((bf16[512,256]{1,0:T(8,128)(2,1)}, bf16[512,256]{1,0:T(8,128)(2,1)}, u32[]{:S(2)}, u32[]{:S(2)}) %collective-permute-start.19) | collective-permute-done | bytes 262176 | tf_op jit(solution)/shard_map/ppermute | solution.py:32
  140.9 2.4 pad_maximum_fusion.refs_3_
  143.3 4.6 %add_convert_fusion = bf16[4,4,32,3456]{3,2,1,0:T(8,128)(2,1)} fusion(bf16[4,4,32,3456]{3,2,1,0:T(8,128)(2,1)} %collective-permute-done.20, bf16[4,4,32,3456]{3,2,1,0:T(8,128)(2,1)S(1)} %get-tuple-element.69), kind=kLoop, calls=%fused_computation | loop fusion | flops 7077888 | bytes 10616832 | tf_op jit(solution)/shard_map/convert_element_type | solution.py:496
  156.2 3.6 %shard_map.173 = (bf16[4,4,32,1024]{3,2,1,0:T(8,128)(2,1)}, bf16[4,4,32,1024]{3,2,1,0:T(8,128)(2,1)S(1)}) custom-call(s32[2]{0:T(128)S(1)} %pad_add_fusion.2.at.refs_0_, bf16[512,1024]{1,0:T(8,128)(2,1)S(1)} %copy-done.37, bf16[512,768]{1,0:T(8,128)(2,1)S(1)} %pad_maximum_fusion.1.grads.refs_2_, bf16[512,1024]{1,0:T(8,128)(2,1)S(1)} %copy-done.5, ...), custom_call_target="tpu_custom_call" | custom-call | flops 1073741824 | bytes 4194304 | tf_op jit(solution)/shard_map/pallas_call | solution.py:339
  165.8 3.5 %shard_map.172 = (f32[512,256]{1,0:T(8,128)S(1)}, bf16[512,256]{1,0:T(8,128)(2,1)S(1)}, bf16[512,256]{1,0:T(8,128)(2,1)S(1)}, bf16[512,256]{1,0:T(8,128)(2,1)S(1)}, f32[512,1]{1,0:T(8,128)S(1)}) custom-call(s32[2]{0:T(128)S(1)} %pad_add_fusion.2.at.refs_0_, bf16[512,256]{1,0:T(8,128)(2,1)S(1)} %copy-done.3, bf16[512,256]{1,0:T(8,128)(2,1)S(1)} %copy-done.16, ...), custom_call_target="tpu_custom_call" | custom-call | flops 805306368 | bytes 6291456 | tf_op jit(solution)/shard_map/pallas_call | solution.py:384
  174.1 2.7 %collective-permute-start.27 = (f32[512]{0:T(512)S(1)}, f32[512]{0:T(512)S(1)}, u32[]{:S(2)}, u32[]{:S(2)}) collective-permute-start(f32[512]{0:T(512)S(1)} %reduce.5), channel_id=1, source_target_pairs={{0,3},{1,0},{2,1},{3,2},{4,7},{5,4},{6,5},{7,6},{8,11},{9,8},{10,9... | collective-permute-start | bytes 6152 | tf_op jit(solution)/shard_map/ppermute | solution.py:45
  177.7 2.6 %collective-permute-start.24 = (bf16[512,256]{1,0:T(8,128)(2,1)}, bf16[512,256]{1,0:T(8,128)(2,1)S(1)}, u32[]{:S(2)}, u32[]{:S(2)}) collective-permute-start(bf16[512,256]{1,0:T(8,128)(2,1)} %copy-done.35), channel_id=1, source_target_pairs={{0,3},{1,0},{2,1},{3,2},{4,7},{5,4},{6,5},{7,6},{8,11},{9,8},{10,9... | collective-permute-start | bytes 786440 | tf_op jit(solution)/shard_map/ppermute | solution.py:38
  183.6 8.6 %reduce-scatter.6.cloned.1.call-done = bf16[1,4,32,3456]{3,2,1,0:T(8,128)(2,1)} async-done(((bf16[4,4,32,3456]{3,2,1,0:T(8,128)(2,1)}), bf16[1,4,32,3456]{3,2,1,0:T(8,128)(2,1)}) %reduce-scatter.6.cloned.1.call-update) | async-done | bytes 884752 | tf_op jit(solution)/shard_map/reduce_scatter | solution.py:399
  192.3 2.6 %collective-permute-done.22 = bf16[512,256]{1,0:T(8,128)(2,1)S(1)} collective-permute-done((bf16[512,256]{1,0:T(8,128)(2,1)}, bf16[512,256]{1,0:T(8,128)(2,1)S(1)}, u32[]{:S(2)}, u32[]{:S(2)}) %collective-permute-start.22) | collective-permute-done | bytes 262176 | tf_op jit(solution)/shard_map/ppermute | solution.py:38
  198.4 6.2 %collective-permute-start.31 = (f32[5,256]{1,0:T(8,128)S(1)}, f32[5,256]{1,0:T(8,128)S(1)}, u32[]{:S(2)}, u32[]{:S(2)}) collective-permute-start(f32[5,256]{1,0:T(8,128)S(1)} %add.255), channel_id=1, source_target_pairs={{0,24},{4,28},{8,0},{12,4},{16,8},{20,12},{24,16},{28,20},{32,56},... | collective-permute-start | bytes 15368 | tf_op jit(solution)/shard_map/ppermute | solution.py:550
  210.0 3.2 %collective-permute-start.37 = (bf16[4,32,1024]{2,1,0:T(8,128)(2,1)S(1)}, bf16[4,32,1024]{2,1,0:T(8,128)(2,1)S(1)}, u32[]{:S(2)}, u32[]{:S(2)}) collective-permute-start(bf16[4,32,1024]{2,1,0:T(8,128)(2,1)S(1)} %get-tuple-element.122), channel_id=1, source_target_pairs={{0,24},{4,28},{8,0},{12,4},{16,8},{20,12},{24,16},{28,20},{32,56},... | collective-permute-start | bytes 786440 | tf_op jit(solution)/shard_map/ppermute | solution.py:74
  217.0 3.0 %collective-permute-start.33 = (f32[5,256]{1,0:T(8,128)S(1)}, f32[5,256]{1,0:T(8,128)S(1)}, u32[]{:S(2)}, u32[]{:S(2)}) collective-permute-start(f32[5,256]{1,0:T(8,128)S(1)} %add_add_fusion.1), channel_id=1, source_target_pairs={{0,64},{4,68},{8,72},{12,76},{16,80},{20,84},{24,88},{28,92},{32,9... | collective-permute-start | bytes 15368 | tf_op jit(solution)/shard_map/ppermute | solution.py:550
  223.1 3.1 %collective-permute-start.41 = (bf16[32,1024]{1,0:T(8,128)(2,1)S(1)}, bf16[32,1024]{1,0:T(8,128)(2,1)S(1)}, u32[]{:S(2)}, u32[]{:S(2)}) collective-permute-start(bf16[32,1024]{1,0:T(8,128)(2,1)S(1)} %get-tuple-element.130), channel_id=1, source_target_pairs={{0,64},{4,68},{8,72},{12,76},{16,80},{20,84},{24,88},{28,92},{32,9... | collective-permute-start | bytes 196616 | tf_op jit(solution)/shard_map/ppermute | solution.py:74
  230.4 2.4 collective-permute-done.39
  (243 shorter events, 82.3 us)
Async XLA Ops:
  7.2 50.9 %all-gather.2.cloned.1.call-start = ((), (), s32[]{:S(2)}) async-start(), calls=%async_computation.3 | async-start | bytes 1310720 | tf_op jit(solution)/shard_map/all_gather | solution.py:434
  7.2 18.9 %collective-permute-start = (bf16[512,256]{1,0:T(8,128)(2,1)}, bf16[512,256]{1,0:T(8,128)(2,1)S(1)}, u32[]{:S(2)}, u32[]{:S(2)}) collective-permute-start(bf16[512,256]{1,0:T(8,128)(2,1)} %p0.1), channel_id=1, source_target_pairs={{0,3},{1,0},{2,1},{3,2},{4,7},{5,4},{6,5},{7,6},{8,11},{9,8},{10,9... | collective-permute-start | bytes 786440 | tf_op jit(solution)/shard_map/ppermute | solution.py:32
  10.1 16.1 %collective-permute-start.1 = (bf16[512,256]{1,0:T(8,128)(2,1)}, bf16[512,256]{1,0:T(8,128)(2,1)S(1)}, u32[]{:S(2)}, u32[]{:S(2)}) collective-permute-start(bf16[512,256]{1,0:T(8,128)(2,1)} %p0.1), channel_id=1, source_target_pairs={{0,2},{1,3},{2,0},{3,1},{4,6},{5,7},{6,4},{7,5},{8,10},{9,11},{10,... | collective-permute-start | bytes 786440 | tf_op jit(solution)/shard_map/ppermute | solution.py:32
  10.9 15.7 %collective-permute-start.2 = (bf16[512,256]{1,0:T(8,128)(2,1)}, bf16[512,256]{1,0:T(8,128)(2,1)S(1)}, u32[]{:S(2)}, u32[]{:S(2)}) collective-permute-start(bf16[512,256]{1,0:T(8,128)(2,1)} %p0.1), channel_id=1, source_target_pairs={{0,1},{1,2},{2,3},{3,0},{4,5},{5,6},{6,7},{7,4},{8,9},{9,10},{10,1... | collective-permute-start | bytes 786440 | tf_op jit(solution)/shard_map/ppermute | solution.py:32
  12.8 22.1 %collective-permute-start.7 = (bf16[512,256]{1,0:T(8,128)(2,1)S(1)}, bf16[512,256]{1,0:T(8,128)(2,1)S(1)}, u32[]{:S(2)}, u32[]{:S(2)}) collective-permute-start(bf16[512,256]{1,0:T(8,128)(2,1)S(1)} %constant_dynamic-slice_fusion.2), channel_id=1, source_target_pairs={{0,3},{1,0},{2,1},{3,2},{4,7},{5,4},{6,5},{7,6},{8,11},{9,8},{10,9... | collective-permute-start | bytes 786440 | tf_op jit(solution)/shard_map/ppermute | solution.py:32
  15.2 19.6 %collective-permute-start.8 = (bf16[512,256]{1,0:T(8,128)(2,1)S(1)}, bf16[512,256]{1,0:T(8,128)(2,1)S(1)}, u32[]{:S(2)}, u32[]{:S(2)}) collective-permute-start(bf16[512,256]{1,0:T(8,128)(2,1)S(1)} %constant_dynamic-slice_fusion.2), channel_id=1, source_target_pairs={{0,2},{1,3},{2,0},{3,1},{4,6},{5,7},{6,4},{7,5},{8,10},{9,11},{10,... | collective-permute-start | bytes 786440 | tf_op jit(solution)/shard_map/ppermute | solution.py:32
  16.8 104.6 %reduce-scatter.4.cloned.1.call-start = ((), (), s32[]{:S(2)}) async-start(), calls=%async_computation.4 | async-start | bytes 1310720 | tf_op jit(solution)/shard_map/reduce_scatter | solution.py:486
  26.2 13.2 %collective-permute-start.9 = (bf16[512,256]{1,0:T(8,128)(2,1)S(1)}, bf16[512,256]{1,0:T(8,128)(2,1)S(1)}, u32[]{:S(2)}, u32[]{:S(2)}) collective-permute-start(bf16[512,256]{1,0:T(8,128)(2,1)S(1)} %constant_dynamic-slice_fusion.2), channel_id=1, source_target_pairs={{0,1},{1,2},{2,3},{3,0},{4,5},{5,6},{6,7},{7,4},{8,9},{9,10},{10,1... | collective-permute-start | bytes 786440 | tf_op jit(solution)/shard_map/ppermute | solution.py:32
  39.5 18.5 %collective-permute-start.10 = (bf16[512,1024]{1,0:T(8,128)(2,1)S(1)}, bf16[512,1024]{1,0:T(8,128)(2,1)S(1)}, u32[]{:S(2)}, u32[]{:S(2)}) collective-permute-start(bf16[512,1024]{1,0:T(8,128)(2,1)S(1)} %constant_dynamic-update-slice_fusion.half), channel_id=1, source_target_pairs={{0,4},{4,0},{8,12},{12,8},{16,20},{20,16},{24,28},{28,24},{32,36},... | collective-permute-start | bytes 3145736 | tf_op jit(solution)/shard_map/ppermute | solution.py:454
  39.6 12.0 %collective-permute-start.4 = (bf16[512,256]{1,0:T(8,128)(2,1)S(1)}, bf16[512,256]{1,0:T(8,128)(2,1)S(1)}, u32[]{:S(2)}, u32[]{:S(2)}) collective-permute-start(bf16[512,256]{1,0:T(8,128)(2,1)S(1)} %get-tuple-element.115.m0.refs_4_), channel_id=1, source_target_pairs={{0,3},{1,0},{2,1},{3,2},{4,7},{5,4},{6,5},{7,6},{8,11},{9,8},{10,9... | collective-permute-start | bytes 786440 | tf_op jit(solution)/shard_map/ppermute | solution.py:32
  40.3 12.5 %collective-permute-start.5 = (bf16[512,256]{1,0:T(8,128)(2,1)S(1)}, bf16[512,256]{1,0:T(8,128)(2,1)S(1)}, u32[]{:S(2)}, u32[]{:S(2)}) collective-permute-start(bf16[512,256]{1,0:T(8,128)(2,1)S(1)} %get-tuple-element.115.m0.refs_4_), channel_id=1, source_target_pairs={{0,2},{1,3},{2,0},{3,1},{4,6},{5,7},{6,4},{7,5},{8,10},{9,11},{10,... | collective-permute-start | bytes 786440 | tf_op jit(solution)/shard_map/ppermute | solution.py:32
  41.1 17.0 %collective-permute-start.6 = (bf16[512,256]{1,0:T(8,128)(2,1)S(1)}, bf16[512,256]{1,0:T(8,128)(2,1)S(1)}, u32[]{:S(2)}, u32[]{:S(2)}) collective-permute-start(bf16[512,256]{1,0:T(8,128)(2,1)S(1)} %get-tuple-element.115.m0.refs_4_), channel_id=1, source_target_pairs={{0,1},{1,2},{2,3},{3,0},{4,5},{5,6},{6,7},{7,4},{8,9},{9,10},{10,1... | collective-permute-start | bytes 786440 | tf_op jit(solution)/shard_map/ppermute | solution.py:32
  85.5 57.8 %collective-permute-start.20 = (bf16[4,4,32,3456]{3,2,1,0:T(8,128)(2,1)}, bf16[4,4,32,3456]{3,2,1,0:T(8,128)(2,1)}, u32[]{:S(2)}, u32[]{:S(2)}) collective-permute-start(bf16[4,4,32,3456]{3,2,1,0:T(8,128)(2,1)} %get-tuple-element.70), channel_id=1, source_target_pairs={{0,4},{4,0},{8,12},{12,8},{16,20},{20,16},{24,28},{28,24},{32,36},... | collective-permute-start | bytes 10616840 | tf_op jit(solution)/shard_map/ppermute | solution.py:482
  88.4 103.8 %reduce-scatter.6.cloned.1.call-start = ((), (), s32[]{:S(2)}) async-start(), calls=%async_computation.5 | async-start | bytes 4423680 | tf_op jit(solution)/shard_map/reduce_scatter | solution.py:399
  93.8 7.0 %collective-permute-start.14 = (f32[512]{0:T(512)S(1)}, f32[512]{0:T(512)S(1)}, u32[]{:S(2)}, u32[]{:S(2)}) collective-permute-start(f32[512]{0:T(512)S(1)} %reduce.2), channel_id=1, source_target_pairs={{0,1},{1,2},{2,3},{3,0},{4,5},{5,6},{6,7},{7,4},{8,9},{9,10},{10,1... | collective-permute-start | bytes 6152 | tf_op jit(solution)/shard_map/ppermute | solution.py:45
  94.4 15.0 %collective-permute-start.13 = (bf16[512,256]{1,0:T(8,128)(2,1)}, bf16[512,256]{1,0:T(8,128)(2,1)}, u32[]{:S(2)}, u32[]{:S(2)}) collective-permute-start(bf16[512,256]{1,0:T(8,128)(2,1)} %copy-done.32), channel_id=1, source_target_pairs={{0,3},{1,0},{2,1},{3,2},{4,7},{5,4},{6,5},{7,6},{8,11},{9,8},{10,9... | collective-permute-start | bytes 786440 | tf_op jit(solution)/shard_map/ppermute | solution.py:38
  97.1 15.0 %collective-permute-start.12 = (bf16[512,256]{1,0:T(8,128)(2,1)}, bf16[512,256]{1,0:T(8,128)(2,1)}, u32[]{:S(2)}, u32[]{:S(2)}) collective-permute-start(bf16[512,256]{1,0:T(8,128)(2,1)} %copy-done.31), channel_id=1, source_target_pairs={{0,2},{1,3},{2,0},{3,1},{4,6},{5,7},{6,4},{7,5},{8,10},{9,11},{10,... | collective-permute-start | bytes 786440 | tf_op jit(solution)/shard_map/ppermute | solution.py:38
  98.5 19.2 %collective-permute-start.11 = (bf16[512,256]{1,0:T(8,128)(2,1)}, bf16[512,256]{1,0:T(8,128)(2,1)}, u32[]{:S(2)}, u32[]{:S(2)}) collective-permute-start(bf16[512,256]{1,0:T(8,128)(2,1)} %copy-done.30), channel_id=1, source_target_pairs={{0,1},{1,2},{2,3},{3,0},{4,5},{5,6},{6,7},{7,4},{8,9},{9,10},{10,1... | collective-permute-start | bytes 786440 | tf_op jit(solution)/shard_map/ppermute | solution.py:38
  124.9 15.4 %collective-permute-start.19 = (bf16[512,256]{1,0:T(8,128)(2,1)}, bf16[512,256]{1,0:T(8,128)(2,1)}, u32[]{:S(2)}, u32[]{:S(2)}) collective-permute-start(bf16[512,256]{1,0:T(8,128)(2,1)} %get-tuple-element.113), channel_id=1, source_target_pairs={{0,1},{1,2},{2,3},{3,0},{4,5},{5,6},{6,7},{7,4},{8,9},{9,10},{10,1... | collective-permute-start | bytes 786440 | tf_op jit(solution)/shard_map/ppermute | solution.py:32
  126.1 14.2 %collective-permute-start.18 = (bf16[512,256]{1,0:T(8,128)(2,1)}, bf16[512,256]{1,0:T(8,128)(2,1)}, u32[]{:S(2)}, u32[]{:S(2)}) collective-permute-start(bf16[512,256]{1,0:T(8,128)(2,1)} %get-tuple-element.113), channel_id=1, source_target_pairs={{0,2},{1,3},{2,0},{3,1},{4,6},{5,7},{6,4},{7,5},{8,10},{9,11},{10,... | collective-permute-start | bytes 786440 | tf_op jit(solution)/shard_map/ppermute | solution.py:32
  128.8 12.1 %collective-permute-start.17 = (bf16[512,256]{1,0:T(8,128)(2,1)}, bf16[512,256]{1,0:T(8,128)(2,1)}, u32[]{:S(2)}, u32[]{:S(2)}) collective-permute-start(bf16[512,256]{1,0:T(8,128)(2,1)} %get-tuple-element.113), channel_id=1, source_target_pairs={{0,3},{1,0},{2,1},{3,2},{4,7},{5,4},{6,5},{7,6},{8,11},{9,8},{10,9... | collective-permute-start | bytes 786440 | tf_op jit(solution)/shard_map/ppermute | solution.py:32
  148.0 86.1 %reduce-scatter.8.cloned.1.call-start = ((), (), s32[]{:S(2)}) async-start(), calls=%async_computation.6 | async-start | bytes 1105920 | tf_op jit(solution)/shard_map/reduce_scatter | solution.py:399
  159.9 46.3 %collective-permute-start.35 = (bf16[4,4,32,1024]{3,2,1,0:T(8,128)(2,1)}, bf16[4,4,32,1024]{3,2,1,0:T(8,128)(2,1)}, u32[]{:S(2)}, u32[]{:S(2)}) collective-permute-start(bf16[4,4,32,1024]{3,2,1,0:T(8,128)(2,1)} %get-tuple-element.83), channel_id=1, source_target_pairs={{0,4},{4,0},{8,12},{12,8},{16,20},{20,16},{24,28},{28,24},{32,36},... | collective-permute-start | bytes 3145736 | tf_op jit(solution)/shard_map/ppermute | solution.py:524
  177.7 14.5 %collective-permute-start.24 = (bf16[512,256]{1,0:T(8,128)(2,1)}, bf16[512,256]{1,0:T(8,128)(2,1)S(1)}, u32[]{:S(2)}, u32[]{:S(2)}) collective-permute-start(bf16[512,256]{1,0:T(8,128)(2,1)} %copy-done.35), channel_id=1, source_target_pairs={{0,3},{1,0},{2,1},{3,2},{4,7},{5,4},{6,5},{7,6},{8,11},{9,8},{10,9... | collective-permute-start | bytes 786440 | tf_op jit(solution)/shard_map/ppermute | solution.py:38
  180.4 11.9 %collective-permute-start.23 = (bf16[512,256]{1,0:T(8,128)(2,1)}, bf16[512,256]{1,0:T(8,128)(2,1)S(1)}, u32[]{:S(2)}, u32[]{:S(2)}) collective-permute-start(bf16[512,256]{1,0:T(8,128)(2,1)} %copy-done.34), channel_id=1, source_target_pairs={{0,2},{1,3},{2,0},{3,1},{4,6},{5,7},{6,4},{7,5},{8,10},{9,11},{10,... | collective-permute-start | bytes 786440 | tf_op jit(solution)/shard_map/ppermute | solution.py:38
  182.4 12.5 %collective-permute-start.22 = (bf16[512,256]{1,0:T(8,128)(2,1)}, bf16[512,256]{1,0:T(8,128)(2,1)S(1)}, u32[]{:S(2)}, u32[]{:S(2)}) collective-permute-start(bf16[512,256]{1,0:T(8,128)(2,1)} %copy-done.33), channel_id=1, source_target_pairs={{0,1},{1,2},{2,3},{3,0},{4,5},{5,6},{6,7},{7,4},{8,9},{9,10},{10,1... | collective-permute-start | bytes 786440 | tf_op jit(solution)/shard_map/ppermute | solution.py:38
  198.4 14.8 %collective-permute-start.31 = (f32[5,256]{1,0:T(8,128)S(1)}, f32[5,256]{1,0:T(8,128)S(1)}, u32[]{:S(2)}, u32[]{:S(2)}) collective-permute-start(f32[5,256]{1,0:T(8,128)S(1)} %add.255), channel_id=1, source_target_pairs={{0,24},{4,28},{8,0},{12,4},{16,8},{20,12},{24,16},{28,20},{32,56},... | collective-permute-start | bytes 15368 | tf_op jit(solution)/shard_map/ppermute | solution.py:550
  204.7 8.6 %collective-permute-start.29 = (f32[5,256]{1,0:T(8,128)S(1)}, f32[5,256]{1,0:T(8,128)S(1)}, u32[]{:S(2)}, u32[]{:S(2)}) collective-permute-start(f32[5,256]{1,0:T(8,128)S(1)} %add.255), channel_id=1, source_target_pairs={{0,8},{4,12},{8,16},{12,20},{16,24},{20,28},{24,0},{28,4},{32,40},... | collective-permute-start | bytes 15368 | tf_op jit(solution)/shard_map/ppermute | solution.py:550
  204.7 8.6 %collective-permute-start.30 = (f32[5,256]{1,0:T(8,128)S(1)}, f32[5,256]{1,0:T(8,128)S(1)}, u32[]{:S(2)}, u32[]{:S(2)}) collective-permute-start(f32[5,256]{1,0:T(8,128)S(1)} %add.255), channel_id=1, source_target_pairs={{0,16},{4,20},{8,24},{12,28},{16,0},{20,4},{24,8},{28,12},{32,48},... | collective-permute-start | bytes 15368 | tf_op jit(solution)/shard_map/ppermute | solution.py:550
  207.8 14.3 %collective-permute-start.38 = (bf16[4,32,1024]{2,1,0:T(8,128)(2,1)S(1)}, bf16[4,32,1024]{2,1,0:T(8,128)(2,1)S(1)}, u32[]{:S(2)}, u32[]{:S(2)}) collective-permute-start(bf16[4,32,1024]{2,1,0:T(8,128)(2,1)S(1)} %get-tuple-element.121), channel_id=1, source_target_pairs={{0,16},{4,20},{8,24},{12,28},{16,0},{20,4},{24,8},{28,12},{32,48},... | collective-permute-start | bytes 786440 | tf_op jit(solution)/shard_map/ppermute | solution.py:74
  210.0 12.2 %collective-permute-start.37 = (bf16[4,32,1024]{2,1,0:T(8,128)(2,1)S(1)}, bf16[4,32,1024]{2,1,0:T(8,128)(2,1)S(1)}, u32[]{:S(2)}, u32[]{:S(2)}) collective-permute-start(bf16[4,32,1024]{2,1,0:T(8,128)(2,1)S(1)} %get-tuple-element.122), channel_id=1, source_target_pairs={{0,24},{4,28},{8,0},{12,4},{16,8},{20,12},{24,16},{28,20},{32,56},... | collective-permute-start | bytes 786440 | tf_op jit(solution)/shard_map/ppermute | solution.py:74
  213.2 9.6 %collective-permute-start.36 = (bf16[4,32,1024]{2,1,0:T(8,128)(2,1)S(1)}, bf16[4,32,1024]{2,1,0:T(8,128)(2,1)S(1)}, u32[]{:S(2)}, u32[]{:S(2)}) collective-permute-start(bf16[4,32,1024]{2,1,0:T(8,128)(2,1)S(1)} %get-tuple-element.120), channel_id=1, source_target_pairs={{0,8},{4,12},{8,16},{12,20},{16,24},{20,28},{24,0},{28,4},{32,40},... | collective-permute-start | bytes 786440 | tf_op jit(solution)/shard_map/ppermute | solution.py:74
  (71 other events, 547.9 us)
Sparse Core Ops, SparseCore 0:
  16.9 38.4 all-gather.1
  88.6 32.7 reduce-scatter.3
  148.1 44.0 reduce-scatter.5
  194.6 22.3 reduce-scatter.7
where the time goes:
time: 244 us; the launch traced here: 243 us
  waiting for transfers between devices  75 us (31%)
  starting transfers between devices  60.4 us (25%)
  Pallas kernels  32.1 us (13%)
  local copies, waits for them, and re-layouts  29.9 us (12%)
  other arithmetic  26.8 us (11%)
  between operations  14.7 us (6%)
  matrix products  4.27 us (2%)
    ppermute x12, waiting for transfers between devices, gather_ch(): lax.ppermute(block, 'ch', ch_pairs(-j))  32.6 us
    unnamed x118, local copies, waits for them, and re-layouts  20.5 us
    ppermute x6, waiting for transfers between devices, scatter_ch(): total = total + lax.ppermute(chunks[j], 'ch', ch_pairs(j)).astype(F32)  18.8 us
    ppermute x12, starting transfers between devices, gather_ch(): lax.ppermute(block, 'ch', ch_pairs(-j))  15.3 us
    pallas_call x1, Pallas kernels, ffn(): pl.pallas_call(ffn_kernel, out_shape=(wide, column, shape((rows, features...  15.1 us
    ppermute x6, starting transfers between devices, shards(): lax.ppermute(small, 'seq', seq_pairs(dy, dz, 0))  12.7 us
    pallas_call x2, Pallas kernels, pair_products(): pl.pallas_call(body, grid=(4,), out_shape=(out, out), in_specs=[smem()] +...  11.1 us
    ppermute x6, starting transfers between devices, reduce_axis(): lax.ppermute(pick(array, (me + step) % 4, axis), 'seq', pairs).astype(F32)  10.5 us
  transfers between devices with their start and end apart: 46, of which 23 were waited for; matrix products, arithmetic and copies ran while one was open for 16% of the time, Pallas kernels for 4%

commit v1 on v0

--- a/solution.py
+++ b/solution.py
@@ -56,10 +56,14 @@
     return lax.ppermute(array, axis, pairs)
 
 
-def tap_masks(segment_ids):
-    padded = jnp.concatenate([segment_ids[:1], segment_ids[:1], segment_ids])
-    same_one = (padded[2:] == padded[1:-1]).astype(F32)[:, None]
-    same_two = (padded[2:] == padded[:-2]).astype(F32)[:, None]
+def first_count(segment_ids):
+    return jnp.sum((segment_ids == segment_ids[0]).astype(jnp.int32))
+
+
+def tap_masks(count, rows):
+    token = lax.broadcasted_iota(jnp.int32, (rows, 1), 0)
+    same_one = (token != count).astype(F32)
+    same_two = ((token != count) & (token != count + 1)).astype(F32)
     return (same_one, same_two)
 
 
@@ -183,8 +187,8 @@
     planes,
     down,
     cotangent,
-    h_own, rms, normed, act, d_gate_up, d_own, d1, d2, d3, inner,
-    w_out, w_in, w_down, g_rows, mixed, h, acc, sem,
+    h, rms, normed, act, d_gate_up, d_own, d1, d2, d3,
+    w_out, w_in, w_down, g_rows, mixed, acc, sem,
 ):
     x, core = at[0], at[1]
     width = x0.shape[1]
@@ -222,7 +226,6 @@
         square = square + jnp.sum(hj * hj, axis=1, keepdims=True)
     r = lax.rsqrt(square / (CH * width) + EPS)
     rms[...] = r
-    h_own[...] = h[:, :width]
     for j in range(CH):
         columns = slice(j * width, (j + 1) * width)
         scale = gain[:, rel_rows(x, j, width)]
@@ -250,13 +253,6 @@
         return carry
 
     lax.fori_loop(0, 3, part, 0)
-    total = jnp.zeros((x0.shape[0], 1), F32)
-    for j in range(CH):
-        scale = gain[:, rel_rows(x, j, width)]
-        total = total + jnp.sum(
-            scale * acc[j] * h[:, j * width : (j + 1) * width], axis=1, keepdims=True
-        )
-    inner[...] = total
     d_own[...] = acc[0]
     d1[...] = acc[1].astype(BF16)
     d2[...] = acc[2].astype(BF16)
@@ -267,31 +263,28 @@
     rows, width = pieces[0].shape
     features = CH * width
     units = down.shape[1]
-    block, column = shape((rows, width), BF16), shape((rows, 1), F32)
-    wide = shape((rows, width), F32)
+    block = shape((rows, width), BF16)
     return pl.pallas_call(
         ffn_kernel,
         out_shape=(
-            wide,
-            column,
+            shape((rows, features), F32),
+            shape((rows, 1), F32),
             shape((rows, features), BF16),
             shape((rows, units), BF16),
             shape((rows, 2 * units), BF16),
-            wide,
+            shape((rows, width), F32),
             block,
             block,
             block,
-            column,
         ),
         in_specs=[smem()] + [vmem()] * 9 + [anywhere()] * 5,
-        out_specs=(vmem(),) * 10,
+        out_specs=(vmem(),) * 9,
         scratch_shapes=[
             pltpu.VMEM((2, features // 2, features), BF16),
             pltpu.VMEM((2, features, units), BF16),
             pltpu.VMEM((features, units), BF16),
             pltpu.VMEM((rows, features), BF16),
             pltpu.VMEM((rows, features), BF16),
-            pltpu.VMEM((rows, features), F32),
             pltpu.VMEM((CH, rows, width), F32),
             pltpu.SemaphoreType.DMA((8,)),
         ],
@@ -301,11 +294,11 @@
 
 
 def pair_kernel(
-    at, a_left, a_right, b_left, b_right, give, keep, held, *, a_rolled, b_rolled
+    at, a_left, a_right, b_left, b_right, give_a, give_b, keep, held, *, a_rolled, b_rolled
 ):
     x, core = at[0], at[1]
     y = pl.program_id(0)
-    wide = give.shape[2] * 8
+    wide = keep.shape[2] * 8
     turned = lax.rem(y + CH - x, CH)
     cut = a_right.shape[1]
     for left, right, rolled, base in (
@@ -324,7 +317,7 @@
         mine = pl.multiple_of((2 * z + core) * 32, 32)
         theirs = pl.multiple_of((2 * z + 1 - core) * 32, 32)
         keep[z, 0] = held[pl.ds(mine, 32), :].astype(BF16)
-        give[z, 0] = held[pl.ds(theirs, 32), :].astype(BF16)
+        (give_a, give_b)[z // 2][z % 2, 0] = held[pl.ds(theirs, 32), :].astype(BF16)
 
 
 def pair_products(at, a_left, a_right, b_left, b_right, a_rolled, b_rolled):
@@ -332,6 +325,8 @@
     tokens, features = a_left.shape
     out = shape((4, 4, features // 32, columns), BF16)
     spec = pl.BlockSpec((4, 1, features // 32, columns), lambda y: (0, y, 0, 0))
+    half = shape((2, 4, features // 32, columns), BF16)
+    half_spec = pl.BlockSpec((2, 1, features // 32, columns), lambda y: (0, y, 0, 0))
 
     def body(*refs):
         pair_kernel(*refs, a_rolled=a_rolled, b_rolled=b_rolled)
@@ -339,18 +334,228 @@
     return pl.pallas_call(
         body,
         grid=(4,),
-        out_shape=(out, out),
+        out_shape=(half, half, out),
         in_specs=[smem()] + [vmem()] * 4,
-        out_specs=(spec, spec),
+        out_specs=(half_spec, half_spec, spec),
         scratch_shapes=[pltpu.VMEM((features // 4, columns), F32)],
         compiler_params=params(40),
         cost_estimate=cost(tokens * features * columns, 4 * features * columns),
     )(at, a_left, a_right, b_left, b_right)
 
 
-def back_kernel(at, p0, p1, p2, p3, grads, gain, weight, d_own, d1, d2, d3, inner, held, sem):
+def swap_cores(halves):
+    return [lax.ppermute(half, "seq", seq_pairs(0, 0, 1)) for half in halves]
+
+
+def add_kernel(keep, got_a, got_b, out):
+    out[:2] = (keep[:2].astype(F32) + got_a[...].astype(F32)).astype(BF16)
+    out[2:] = (keep[2:].astype(F32) + got_b[...].astype(F32)).astype(BF16)
+
+
+def add_cores(keep, got):
+    spec = pl.BlockSpec((4, 1) + keep.shape[2:], lambda y: (0, y, 0, 0))
+    half = pl.BlockSpec((2, 1) + keep.shape[2:], lambda y: (0, y, 0, 0))
+    return pl.pallas_call(
+        add_kernel,
+        grid=(4,),
+        out_shape=shape(keep.shape, BF16),
+        in_specs=[spec, half, half],
+        out_specs=spec,
+        compiler_params=params(24),
+        cost_estimate=cost(2**20, 6 * keep.size),
+    )(keep, *got)
+
+
+def spread(small):
+    high = small.astype(BF16)
+    low = (small - high.astype(F32)).astype(BF16)
+    return high, low
+
+
+def join(message, width):
+    return message[:8, :width].astype(F32) + message[:8, width : 2 * width].astype(F32)
+
+
+def send_kernel(at, keep, got_a, got_b, small, own, m1, m2, m3):
+    z = at[3]
+    rows = own.shape[0]
+    width = small.shape[1]
+    for j, out in enumerate((own, m1, m2, m3)):
+        block = lax.rem(z + j, 4)
+        inside = lax.rem(block, 2)
+        got = jnp.where(block < 2, got_a[inside].astype(F32), got_b[inside].astype(F32))
+        total = keep[block].astype(F32) + got
+        out[:rows] = total.reshape(own.shape).astype(out.dtype)
+    high, low = spread(jnp.concatenate([small[...], jnp.zeros_like(small[...])], axis=0))
+    for out in (m1, m2, m3):
+        out[rows:, :width] = high
+        out[rows:, width : 2 * width] = low
+
+
+def send_z(at, keep, got, small):
+    rows, columns = keep.shape[1] * keep.shape[2], keep.shape[3]
+    message = shape((rows + 16, columns), BF16)
+    return pl.pallas_call(
+        send_kernel,
+        out_shape=(shape((rows, columns), F32), message, message, message),
+        in_specs=[smem()] + [vmem()] * 4,
+        out_specs=(vmem(),) * 4,
+        compiler_params=params(24),
+        cost_estimate=cost(2**20, 2**22),
+    )(at, keep, *got, small)
+
+
+def turn_kernel(at, own, m1, m2, m3, small, left, n1, n2, n3, small_out, total):
+    y = at[4]
+    rows = own.shape[0]
+    width = small.shape[1]
+    total[...] = own[...]
+    small_sum = small[...]
+    for m in (m1, m2, m3):
+        total[...] += m[:rows].astype(F32)
+        small_sum = small_sum + join(m[rows:], width)
+    small_out[...] = small_sum
+    part = rows // 4
+    for j, out in enumerate((left, n1, n2, n3)):
+        block = pl.multiple_of(lax.rem(y + j, 4) * part, part)
+        out[:part] = total[pl.ds(block, part)].astype(out.dtype)
+    high, low = spread(jnp.concatenate([small_sum, jnp.zeros_like(small_sum)], axis=0))
+    for out in (n1, n2, n3):
+        out[part:, :width] = high
+        out[part:, width : 2 * width] = low
+
+
+def turn(at, own, messages, small):
+    rows, columns = own.shape
+    message = shape((rows // 4 + 16, columns), BF16)
+    return pl.pallas_call(
+        turn_kernel,
+        out_shape=(
+            shape((rows // 4, columns), F32),
+            message,
+            message,
+            message,
+            shape(small.shape, F32),
+        ),
+        in_specs=[smem()] + [vmem()] * 5,
+        out_specs=(vmem(),) * 5,
+        scratch_shapes=[pltpu.VMEM((rows, columns), F32)],
+        compiler_params=params(24),
+        cost_estimate=cost(2**20, 2**21),
+    )(at, own, *messages, small)
+
+
+def last_kernel(own, m1, m2, m3, small, in_out, out_out, small_out):
+    rows = own.shape[0]
+    width = small.shape[1]
+    total = own[...]
+    small_sum = small[...]
+    for m in (m1, m2, m3):
+        total = total + m[:rows].astype(F32)
+        small_sum = small_sum + join(m[rows:], width)
+    for k in range(3):
+        in_out[k] = total[:, k * width : (k + 1) * width]
+    out_out[...] = total[:, 3 * width :]
+    small_out[...] = small_sum
+
+
+def last(own, messages, small):
+    rows, columns = own.shape
+    width = small.shape[1]
+    return pl.pallas_call(
+        last_kernel,
+        out_shape=(
+            shape((3, rows, width), F32),
+            shape((rows, columns - 3 * width), F32),
+            shape(small.shape, F32),
+        ),
+        in_specs=[vmem()] * 5,
+        out_specs=(vmem(),) * 3,
+        compiler_params=params(24),
+        cost_estimate=cost(2**20, 2**20),
+    )(own, *messages, small)
+
+
+def end_kernel(d_own, d1, d2, d3, inner, d_hidden, rows_in, rms, gain, grad, gain_grad):
+    rows, width = d_own.shape
+    total = d_own[...]
+    line = inner[...]
+    for d in (d1, d2, d3):
+        total = total + d[:rows].astype(F32)
+        high = [d[rows + 16 * i : rows + 16 * (i + 1)].astype(F32) for i in range(4)]
+        line = line + jnp.concatenate(
+            [high[0] + high[2], high[1] + high[3]], axis=1
+        )
+    column = lax.dot_general(
+        line, jnp.full((16, width), 1.0 / 16, F32), (((0,), (0,)), ((), ())),
+        precision=lax.Precision.HIGHEST, preferred_element_type=F32,
+    )
+    r = rms[...]
+    xs = rows_in[...].astype(F32)
+    gain_grad[...] = jnp.sum(total * xs * r, axis=0, keepdims=True)
+    grad[...] = (
+        d_hidden[...] + r * gain[...] * total - xs * (r * r * r / (CH * width)) * column
+    ).astype(BF16)
+
+
+def end(d_own, received, inner, d_hidden, rows_in, rms, gain):
+    rows, width = d_own.shape
+    return pl.pallas_call(
+        end_kernel,
+        out_shape=(shape((rows, width), BF16), shape((1, width), F32)),
+        in_specs=[vmem()] * 9,
+        out_specs=(vmem(),) * 2,
+        compiler_params=params(24),
+        cost_estimate=cost(2**20, 2**21),
+    )(d_own, *received, inner, d_hidden, rows_in, rms, gain[None])
+
+
+def mid_kernel(
+    at, u_own, u1, u2, u3, h, rms, cotangent, weight, c_gate, conv_out,
+    d_branch, d_hidden, d_conv, d_cgate,
+):
     x = at[0]
-    width = p0.shape[1]
+    width = u_own.shape[1]
+    dot = jnp.zeros((u_own.shape[0], 1), F32)
+    us = (u_own, u1, u2, u3)
+    for j, u in enumerate(us):
+        g = cotangent[:, rel_rows(x, j, width)].astype(F32)
+        hj = h[:, j * width : (j + 1) * width]
+        dot = dot + jnp.sum((u[...].astype(F32) - g) * hj, axis=1, keepdims=True)
+    r = rms[...]
+    scale = dot * (r * r / (CH * width))
+    d_mixed = jnp.zeros(u_own.shape, F32)
+    for j, u in enumerate(us):
+        columns = slice(j * width, (j + 1) * width)
+        full = u[...].astype(F32) - h[:, columns] * scale
+        if j == 0:
+            d_hidden[...] = full
+        rounded = full.astype(BF16)
+        d_branch[:, columns] = rounded
+        d_mixed = d_mixed + dot_nn(rounded, weight[rel_rows(x, j, width), :])
+    d_conv[...] = d_mixed * c_gate[...]
+    d_cgate[...] = (d_mixed * conv_out[...]).astype(BF16)
+
+
+def mid(at, pieces, h, rms, cotangent, weight, c_gate, conv_out):
+    rows, width = c_gate.shape
+    wide = shape((rows, width), F32)
+    return pl.pallas_call(
+        mid_kernel,
+        out_shape=(shape((rows, CH * width), BF16), wide, wide, shape((rows, width), BF16)),
+        in_specs=[smem()] + [vmem()] * 10,
+        out_specs=(vmem(),) * 4,
+        compiler_params=params(24),
+        cost_estimate=cost(rows * CH * width * width, 6 * 2**20),
+    )(at, *pieces, h, rms, cotangent, weight, c_gate, conv_out)
+
+
+def back_kernel(
+    at, p0, p1, p2, p3, d_conv, following, taps, value, b_gate, d_cgate, gain, weight,
+    grads, d_own, d1, d2, d3, inner, held, sem,
+):
+    x, count = at[0], at[2]
+    rows, width = p0.shape
     copies = [
         pltpu.make_async_copy(
             weight.at[:, rel_rows(x, j, width), :],
@@ -361,38 +566,70 @@
     ]
     for copy in copies:
         copy.start()
-    total = jnp.zeros((p0.shape[0], 1), F32)
+    token = lax.broadcasted_iota(jnp.int32, (rows, width), 0)
+    d = d_conv[...]
+    next_one, next_two = following[0:1, :], following[1:2, :]
+    after_one = jnp.where(token + 1 == count, 0.0, pltpu.roll(d, rows - 1, 0))
+    after_one = jnp.where(token == rows - 1, next_one, after_one)
+    after_two = pltpu.roll(d, rows - 2, 0)
+    after_two = jnp.where((token + 2 == count) | (token + 1 == count), 0.0, after_two)
+    after_two = jnp.where(token == rows - 2, next_one, after_two)
+    after_two = jnp.where(token == rows - 1, next_two, after_two)
+    d_gated = taps[0:1, :] * d + taps[1:2, :] * after_one + taps[2:3, :] * after_two
+    grads[:, :width] = (d_gated * value[...]).astype(BF16)
+    grads[:, width : 2 * width] = d_cgate[...]
+    grads[:, 2 * width :] = (d_gated * b_gate[...]).astype(BF16)
+    total = jnp.zeros((rows, width), F32)
     for j, piece in enumerate((p0, p1, p2, p3)):
         copies[j].wait()
-        rows = slice(j * width, (j + 1) * width)
-        term = dot_nt(grads[:, :width], held[0, rows, :])
+        block = slice(j * width, (j + 1) * width)
+        term = dot_nt(grads[:, :width], held[0, block, :])
         for k in (1, 2):
-            term = term + dot_nt(grads[:, k * width : (k + 1) * width], held[k, rows, :])
+            term = term + dot_nt(grads[:, k * width : (k + 1) * width], held[k, block, :])
         scale = gain[:, rel_rows(x, j, width)]
-        total = total + jnp.sum(scale * term * piece[...].astype(F32), axis=1, keepdims=True)
+        total = total + scale * term * piece[...].astype(F32)
         if j == 0:
             d_own[...] = term
         else:
-            (d1, d2, d3)[j - 1][...] = term.astype(BF16)
-    inner[...] = total
-
-
-def back_project(at, pieces, grads, gain, weight):
+            (d1, d2, d3)[j - 1][:rows, :] = term.astype(BF16)
+    ones = jnp.ones((16, width), F32)
+    row = lax.dot_general(
+        ones, total, (((1,), (1,)), ((), ())),
+        precision=lax.Precision.HIGHEST, preferred_element_type=F32,
+    )
+    inner[...] = row
+    high = row.astype(BF16)
+    low = (row - high.astype(F32)).astype(BF16)
+    for out in (d1, d2, d3):
+        out[rows : rows + 16, :] = high[:, :width]
+        out[rows + 16 : rows + 32, :] = high[:, width:]
+        out[rows + 32 : rows + 48, :] = low[:, :width]
+        out[rows + 48 : rows + 64, :] = low[:, width:]
+
+
+def back_project(at, pieces, d_conv, following, taps, value, b_gate, d_cgate, gain, weight):
     rows, width = pieces[0].shape
     features = CH * width
-    block = shape((rows, width), BF16)
+    block = shape((rows + 64, width), BF16)
     return pl.pallas_call(
         back_kernel,
-        out_shape=(shape((rows, width), F32), block, block, block, shape((rows, 1), F32)),
-        in_specs=[smem()] + [vmem()] * 6 + [anywhere()],
-        out_specs=(vmem(),) * 5,
+        out_shape=(
+            shape((rows, 3 * width), BF16),
+            shape((rows, width), F32),
+            block,
+            block,
+            block,
+            shape((16, rows), F32),
+        ),
+        in_specs=[smem()] + [vmem()] * 11 + [anywhere()],
+        out_specs=(vmem(),) * 6,
         scratch_shapes=[
             pltpu.VMEM((3, features, width), BF16),
             pltpu.SemaphoreType.DMA((CH,)),
         ],
-        compiler_params=params(24),
+        compiler_params=params(32),
         cost_estimate=cost(rows * features * 3 * width, 6 * 2**20),
-    )(at, *pieces, grads, gain[None], weight)
+    )(at, *pieces, d_conv, following, taps, value, b_gate, d_cgate, gain[None], weight)
 
 
 def scatter_groups(array, groups):
@@ -422,7 +659,8 @@
         blocks = array.reshape((CH, width) + array.shape[1:])
         return jnp.concatenate([pick(blocks, (x + j) % CH, 0) for j in range(CH)], axis=0)
 
-    at = jnp.stack([x, core]).astype(jnp.int32)
+    count = first_count(segment_ids)
+    at = jnp.stack([x, core, count, z, y]).astype(jnp.int32)
     own_one = pick(norm1_gain.reshape(CH, width), x, 0)
     own_two = pick(norm2_gain.reshape(CH, width), x, 0)
     in_planes = jnp.transpose(in_weight, (1, 0, 2))
@@ -441,7 +679,7 @@
     own_rows = block_input.astype(F32)
     carried = from_behind(gated_rows[-2:], "seq", 1)
     extended = jnp.concatenate([carried, gated_rows], axis=0).astype(F32)
-    same_one, same_two = tap_masks(segment_ids)
+    same_one, same_two = tap_masks(count, block_input.shape[0])
     current = extended[2:]
     prior_one = extended[1:-1] * same_one
     prior_two = extended[:-2] * same_two
@@ -452,9 +690,8 @@
     half_pieces = tie(*half_pieces, mixed_rows)[:CH]
     half_full = jnp.concatenate(half_pieces, axis=1)
     other_half = lax.ppermute(half_full, "seq", seq_pairs(0, 0, 1))
-    out_rolled = rolled(tie(out_weight, mixed_rows)[0])
     (
-        hidden_own,
+        hidden,
         r_two,
         normed_two,
         act_rows,
@@ -463,7 +700,6 @@
         d_one,
         d_two,
         d_three,
-        inner,
     ) = ffn(
         at,
         pieces,
@@ -475,59 +711,35 @@
         ffn_out_weight,
         grad_full,
     )
+    hidden_own = hidden[:, :width]
     d_normed_own = scatter_ch([d_own, d_one, d_two, d_three])
-    inner_two = sum_ch(inner[:, 0])[:, None]
-
-    give, keep = pair_products(at, normed_two, d_gate_up, grad_full, act_rows, True, False)
-    got = lax.ppermute(give, "seq", seq_pairs(0, 0, 1))
     down_terms = jnp.einsum(
         "tf,ef->te", act_rows, ffn_out_weight, preferred_element_type=F32
     ).astype(BF16)
     down = lax.psum_scatter(down_terms, "ch", scatter_dimension=1, tiled=True)
-    block_output = (hidden_own + down.astype(F32)).astype(BF16)
+    *gives, keep = pair_products(at, normed_two, d_gate_up, grad_full, act_rows, True, False)
+    got = swap_cores(gives)
 
     grad_gain_two = jnp.sum(d_normed_own * hidden_own * r_two, axis=0)
-    d_hidden = (
-        out_grad.astype(F32)
-        + r_two * own_two * d_normed_own
-        - hidden_own * (r_two * r_two * r_two) / features * inner_two
-    )
-    d_branch = jnp.concatenate(gather_ch(d_hidden.astype(BF16)), axis=1)
-    ffn_kept = (keep.astype(F32) + got.astype(F32)).astype(BF16)
-    d_branch, ffn_kept, out_rolled = tie(d_branch, ffn_kept, out_rolled)
+    u_own = out_grad.astype(F32) + r_two * own_two * d_normed_own
+    u_pieces = [u_own] + gather_ch(u_own.astype(BF16))[1:]
+    ffn_kept = add_cores(keep, got)
+    ffn_kept, *u_pieces = tie(ffn_kept, *u_pieces)
     groups = [[seq_index(i, k, c) for k in range(4)] for i in range(4) for c in range(2)]
     ffn_sum = scatter_groups(ffn_kept, groups)
-    groups = [[seq_index(k, i, c) for k in range(4)] for i in range(4) for c in range(2)]
-    ffn_sum = scatter_groups(ffn_sum, groups).astype(F32)
-    grad_ffn_in = ffn_sum[:, : 2 * hidden_units].reshape(-1, 2, hidden_units)
-    grad_ffn_out = ffn_sum[:, 2 * hidden_units :]
-
-    d_mixed = jnp.dot(d_branch, out_rolled, preferred_element_type=F32)
-    d_cgate = d_mixed * conv_out
-    d_conv = d_mixed * c_gate
+
+    d_branch, d_hidden, d_conv, d_cgate = mid(
+        at, u_pieces, hidden, r_two, grad_full, out_weight, c_gate, conv_out
+    )
     following = from_behind(d_conv[:2], "seq", -1)
-    edge_one = d_conv * same_one
-    edge_two = d_conv * same_two
-    after_one = jnp.concatenate([edge_one[1:], following[:1]], axis=0)
-    after_two = jnp.concatenate([edge_two[2:], following], axis=0)
-    d_gated = conv_weight[0] * d_conv + conv_weight[1] * after_one + conv_weight[2] * after_two
-    d_proj = jnp.concatenate(
-        [d_gated * value_rows, d_cgate, d_gated * b_gate], axis=1
-    ).astype(BF16)
-    d_own, d_one, d_two, d_three, inner = back_project(
-        at, pieces, d_proj, norm1_gain, in_planes
-    )
-    d_own_one = scatter_ch([d_own, d_one, d_two, d_three])
-    inner_one = sum_ch(inner[:, 0])[:, None]
-
-    give, keep = pair_products(at, normed_one, d_proj, d_branch, mixed_rows, True, True)
-    got = lax.ppermute(give, "seq", seq_pairs(0, 0, 1))
-    mix_sum = (keep.astype(F32) + got.astype(F32)).astype(BF16)
-    mix_sum = reduce_axis(mix_sum, 0, z, False).astype(BF16)
-    mix_sum = reduce_axis(mix_sum, 0, y, True)
-    grad_in = mix_sum[:, : 3 * width].reshape(-1, 3, width)
-    grad_out = mix_sum[:, 3 * width :]
-
+    d_proj, d_own, d_one, d_two, d_three, inner = back_project(
+        at, pieces, d_conv, following, conv_weight, value_rows, b_gate, d_cgate, norm1_gain,
+        in_planes,
+    )
+    received = [lax.ppermute(d, "ch", ch_pairs(j)) for j, d in ((1, d_one), (2, d_two), (3, d_three))]
+
+    *gives, keep = pair_products(at, normed_one, d_proj, d_branch, mixed_rows, True, True)
+    got = swap_cores(gives)
     grad_conv = jnp.stack(
         [
             jnp.sum(d_conv * current, axis=0),
@@ -536,23 +748,34 @@
         ],
         axis=0,
     )
-    grad_gain_one = jnp.sum(d_own_one * own_rows * r_one, axis=0)
-    input_grad = (
-        d_hidden
-        + r_one * own_one * d_own_one
-        - own_rows * (r_one * r_one * r_one) / features * inner_one
-    ).astype(BF16)
-
-    small = jnp.concatenate([grad_conv, grad_gain_one[None], grad_gain_two[None]], axis=0)
+    input_grad, grad_gain_one = end(
+        d_own, received, inner, d_hidden, block_input, r_one, own_one
+    )
+    small = jnp.concatenate(
+        [grad_conv, grad_gain_one, grad_gain_two[None], jnp.zeros((3, width), F32)], axis=0
+    )
     small = small + lax.ppermute(small, "seq", seq_pairs(0, 0, 1))
-    for along in (0, 1):
-        steps = [(0, 1), (0, 2), (0, 3)] if along == 0 else [(1, 0), (2, 0), (3, 0)]
-        small = small + sum(lax.ppermute(small, "seq", seq_pairs(dy, dz, 0)) for dy, dz in steps)
+    own, *messages = send_z(at, keep, got, small)
+    messages = [
+        lax.ppermute(m, "seq", seq_pairs(0, j, 0)) for j, m in ((1, messages[0]), (2, messages[1]), (3, messages[2]))
+    ]
+    down, ffn_sum, *messages = tie(down, ffn_sum, *messages)
+    block_output = (hidden_own + down.astype(F32)).astype(BF16)
+    own, *messages, small = turn(at, own, messages, small)
+    messages = [
+        lax.ppermute(m, "seq", seq_pairs(j, 0, 0)) for j, m in ((1, messages[0]), (2, messages[1]), (3, messages[2]))
+    ]
+    grad_in, grad_out, small = last(own, messages, small)
+
+    groups = [[seq_index(k, i, c) for k in range(4)] for i in range(4) for c in range(2)]
+    ffn_sum = scatter_groups(ffn_sum, groups).astype(F32)
+    grad_ffn_in = ffn_sum[:, : 2 * hidden_units].reshape(-1, 2, hidden_units)
+    grad_ffn_out = ffn_sum[:, 2 * hidden_units :]
     return (
         block_output,
         input_grad,
         small[3],
-        grad_in,
+        jnp.transpose(grad_in, (1, 0, 2)),
         small[:3],
         grad_out,
         small[4],

time: 244 us -> 243 us (level)
  starting transfers between devices: 60.4 us -> 40.7 us
  local copies, waits for them, and re-layouts: 29.9 us -> 46.1 us
  other arithmetic: 26.8 us -> 10.8 us
  Pallas kernels: 32.1 us -> 44.9 us
  waiting for transfers between devices: 75 us -> 80.1 us
    ppermute x20 -> x13, waiting for transfers between devices: 7.98 us -> 28.9 us  [the longest x3 13.6 us: shards(): lax.ppermute(m, 'seq', seq_pairs(0, j, 0))]
    unnamed x118 -> x128, local copies, waits for them, and re-layouts: 20.5 us -> 39.7 us
    ppermute x20 -> x13, starting transfers between devices: 32.3 us -> 18 us  [the longest x3 6.26 us: shards(): lax.ppermute(m, 'seq', seq_pairs(0, j, 0))]
    pallas_call x4 -> x10, Pallas kernels: 29.7 us -> 42.5 us  [the longest x1 15.4 us: ffn(): pl.pallas_call(ffn_kernel, out_shape=(shape((rows, features), F32), shape...]
    ppermute x12, waiting for transfers between devices: 32.6 us -> 25.4 us  [gather_ch(): lax.ppermute(block, 'ch', ch_pairs(-j))]
    concatenate x5 -> x0, other arithmetic: 6.07 us -> none  [the longest x2 2.8 us: tap_masks(): padded = jnp.concatenate([segment_ids[:1], segment_ids[:1], segment_ids])]
    convert_element_type x5 -> x3, other arithmetic: 9.93 us -> 4.86 us  [the longest x1 2.46 us: shards(): u_pieces = [u_own] + gather_ch(u_own.astype(BF16))[1:]]
    pallas_call x4 -> x1, other arithmetic: 5.11 us -> 0.14 us  [ffn(): pl.pallas_call(ffn_kernel, out_shape=(shape((rows, features), F32), shape...]
  transfers between devices with their start and end apart: 46 -> 36, of which waited for: 23 -> 18; matrix products, arithmetic and copies ran while one was open for 16% -> 9% of each run, Pallas kernels for 4% -> 12%
where the time goes in v1:
time: 243 us; the launch traced here: 242 us
  waiting for transfers between devices  80.1 us (33%)
  local copies, waits for them, and re-layouts  46.1 us (19%)
  Pallas kernels  44.9 us (18%)
  starting transfers between devices  40.7 us (17%)
  between operations  15 us (6%)
  other arithmetic  10.8 us (4%)
  matrix products  4 us (2%)
    unnamed x128, local copies, waits for them, and re-layouts  39.7 us
    ppermute x12, waiting for transfers between devices, gather_ch(): lax.ppermute(block, 'ch', ch_pairs(-j))  25.4 us
    pallas_call x1, Pallas kernels, ffn(): pl.pallas_call(ffn_kernel, out_shape=(shape((rows, features), F32), shape...  15.4 us
    ppermute x12, starting transfers between devices, gather_ch(): lax.ppermute(block, 'ch', ch_pairs(-j))  14.3 us
    ppermute x3, waiting for transfers between devices, scatter_ch(): total = total + lax.ppermute(chunks[j], 'ch', ch_pairs(j)).astype(F32)  14.1 us
    ppermute x3, waiting for transfers between devices, shards(): lax.ppermute(m, 'seq', seq_pairs(0, j, 0))  13.6 us
    ppermute x3, waiting for transfers between devices, shards(): lax.ppermute(d, 'ch', ch_pairs(j))  12.8 us
    pallas_call x2, Pallas kernels, pair_products(): pl.pallas_call(body, grid=(4,), out_shape=(half, half, out), in_specs=[sm...  11 us
  transfers between devices with their start and end apart: 36, of which 18 were waited for; matrix products, arithmetic and copies ran while one was open for 9% of the time, Pallas kernels for 12%

profile of v1, /device:TPU:0, one launch (start us, length us, event | category | flops | bytes accessed | tf_op | source)
XLA Modules:
  0.0 241.6 jit_solution(6052871253771706226)
XLA Ops:
  7.2 2.9 %collective-permute-start = (bf16[512,256]{1,0:T(8,128)(2,1)}, bf16[512,256]{1,0:T(8,128)(2,1)S(1)}, u32[]{:S(2)}, u32[]{:S(2)}) collective-permute-start(bf16[512,256]{1,0:T(8,128)(2,1)} %rows_in.1), channel_id=1, source_target_pairs={{0,3},{1,0},{2,1},{3,2},{4,7},{5,4},{6,5},{7,6},{8,11},{9,8},{10,9... | collective-permute-start | bytes 786440 | tf_op jit(solution)/shard_map/ppermute | solution.py:32
  13.5 2.4 collective-permute-start.7
  20.6 5.2 %copy.22 = bf16[1024,2,1152]{2,0,1:T(8,128)(2,1)} copy(bf16[1024,2,1152]{2,1,0:T(2,128)(2,1)} %param.17) | data formatting | bytes 9437184 | tf_op args[7]
  27.4 2.4 shard_map.169
  33.1 2.2 collective-permute-done.7
  35.3 4.2 %collective-permute-done.9 = bf16[512,256]{1,0:T(8,128)(2,1)S(1)} collective-permute-done((bf16[512,256]{1,0:T(8,128)(2,1)}, bf16[512,256]{1,0:T(8,128)(2,1)S(1)}, u32[]{:S(2)}, u32[]{:S(2)}) %collective-permute-start.9) | collective-permute-done | bytes 262176 | tf_op jit(solution)/shard_map/ppermute | solution.py:32
  44.8 8.7 %collective-permute-done.4.m1 = bf16[512,256]{1,0:T(8,128)(2,1)S(1)} collective-permute-done((bf16[512,256]{1,0:T(8,128)(2,1)S(1)}, bf16[512,256]{1,0:T(8,128)(2,1)S(1)}, u32[]{:S(2)}, u32[]{:S(2)}) %collective-permute-start.4) | collective-permute-done | bytes 262176 | tf_op jit(solution)/shard_map/ppermute | solution.py:32
  54.9 3.6 %collective-permute-done.6.m3 = bf16[512,256]{1,0:T(8,128)(2,1)S(1)} collective-permute-done((bf16[512,256]{1,0:T(8,128)(2,1)S(1)}, bf16[512,256]{1,0:T(8,128)(2,1)S(1)}, u32[]{:S(2)}, u32[]{:S(2)}) %collective-permute-start.6) | collective-permute-done | bytes 262176 | tf_op jit(solution)/shard_map/ppermute | solution.py:32
  62.2 15.4 %shard_map.170 = (f32[512,1024]{1,0:T(8,128)}, f32[512,1]{1,0:T(8,128)S(1)}, bf16[512,1024]{1,0:T(8,128)(2,1)S(1)}, bf16[512,1152]{1,0:T(8,128)(2,1)}, bf16[512,...) custom-call(s32[5]{0:T(128)S(1)} %stack.32.at.refs_0_, ...), custom_call_target="tpu_custom_call" | custom-call | flops 7113539584 | bytes 20971520 | tf_op jit(solution)/shard_map/pallas_call | solution.py:267
  79.4 4.0 %convolution_convert_fusion = bf16[512,1024]{1,0:T(8,128)(2,1)} fusion(bf16[512,1152]{1,0:T(8,128)(2,1)} %get-tuple-element.85.refs_4_, bf16[1024,1152]{1,0:T(8,128)(2,1)S(1)} %copy-done.61), kind=kOutput, calls=%fused_computation.1 | convolution fusion | flops 1208483840 | bytes 4587520 | tf_op jit(solution)/shard_map/tf,ef->te/dot_general | solution.py:716
  89.0 7.4 %shard_map.171 = (bf16[2,4,32,3456]{3,2,1,0:T(8,128)(2,1)}, bf16[2,4,32,3456]{3,2,1,0:T(8,128)(2,1)}, bf16[4,4,32,3456]{3,2,1,0:T(8,128)(2,1)S(1)}) custom-call(s32[5]{0:T(128)S(1)} %stack.32.at.refs_0_, bf16[512,1024]{1,0:T(8,128)(2,1)S(1)} %copy-done.59, bf16[512,2304]{1,0:T(8,128)(2,1)S(1)} %copy-done.56, bf16[512,1024]{1,0:T(8,128)(2,1)S(1)} %copy-done.8, ...), custom_call_target="tpu_custom_call" | custom-call | flops 3623878656 | bytes 14155776 | tf_op jit(solution)/shard_map/pallas_call | solution.py:334
  100.7 3.4 %collective-permute-start.14 = (bf16[512,256]{1,0:T(8,128)(2,1)}, bf16[512,256]{1,0:T(8,128)(2,1)}, u32[]{:S(2)}, u32[]{:S(2)}) collective-permute-start(bf16[512,256]{1,0:T(8,128)(2,1)} %get-tuple-element.94), channel_id=1, source_target_pairs={{0,2},{1,3},{2,0},{3,1},{4,6},{5,7},{6,4},{7,5},{8,10},{9,11},{10,... | collective-permute-start | bytes 786440 | tf_op jit(solution)/shard_map/ppermute | solution.py:38
  104.3 8.1 %collective-permute-done.13 = bf16[512,256]{1,0:T(8,128)(2,1)} collective-permute-done((bf16[512,256]{1,0:T(8,128)(2,1)}, bf16[512,256]{1,0:T(8,128)(2,1)}, u32[]{:S(2)}, u32[]{:S(2)}) %collective-permute-start.13) | collective-permute-done | bytes 262176 | tf_op jit(solution)/shard_map/ppermute | solution.py:38
  112.4 6.0 %collective-permute-done.14 = bf16[512,256]{1,0:T(8,128)(2,1)} collective-permute-done((bf16[512,256]{1,0:T(8,128)(2,1)}, bf16[512,256]{1,0:T(8,128)(2,1)}, u32[]{:S(2)}, u32[]{:S(2)}) %collective-permute-start.14) | collective-permute-done | bytes 262176 | tf_op jit(solution)/shard_map/ppermute | solution.py:38
  118.3 2.5 %fusion.3 = (bf16[512,256]{1,0:T(8,128)(2,1)}, f32[512,256]{1,0:T(8,128)}, f32[256]{0:T(256)S(1)}) fusion(bf16[512,256]{1,0:T(8,128)(2,1)} %collective-permute-done.15, bf16[512,256]{1,0:T(8,128)(2,1)} %collective-permute-done.14, f32[512,256]{1,0:T(8,128)} %copy-done.23, bf16[512,256]{1,0:T(8,128)(2,1)} %collective-permute-done.13, f32[256]{0:T(256)S(1)} %bitcast.40, ...), kind=kLoop, calls=%fused_computation.28 | loop fusion | flops 1834752 | bytes 2887680 | tf_op jit(solution)/shard_map/convert_element_type | solution.py:725
  124.4 2.0 copy-done.2
  126.4 4.8 %shard_map.172 = bf16[4,4,32,3456]{3,2,1,0:T(8,128)(2,1)} custom-call(bf16[4,4,32,3456]{3,2,1,0:T(8,128)(2,1)S(1)} %copy-done.2, bf16[2,4,32,3456]{3,2,1,0:T(8,128)(2,1)} %collective-permute-done.11.got_a, bf16[2,4,32,3456]{3,2,1,0:T(8,128)(2,1)} %collective-permute-done.12.got_b), custom_call_target="tpu_custom_call" | custom-call | flops 2097152 | bytes 10616832 | tf_op jit(solution)/shard_map/pallas_call | solution.py:358
  131.1 3.1 %collective-permute-done.16.u1 = bf16[512,256]{1,0:T(8,128)(2,1)S(1)} collective-permute-done((bf16[512,256]{1,0:T(8,128)(2,1)}, bf16[512,256]{1,0:T(8,128)(2,1)S(1)}, u32[]{:S(2)}, u32[]{:S(2)}) %collective-permute-start.16) | collective-permute-done | bytes 262176 | tf_op jit(solution)/shard_map/ppermute | solution.py:32
  134.2 3.5 %collective-permute-done.18.u3 = bf16[512,256]{1,0:T(8,128)(2,1)} collective-permute-done((bf16[512,256]{1,0:T(8,128)(2,1)}, bf16[512,256]{1,0:T(8,128)(2,1)}, u32[]{:S(2)}, u32[]{:S(2)}) %collective-permute-start.18) | collective-permute-done | bytes 262176 | tf_op jit(solution)/shard_map/ppermute | solution.py:32
  145.1 2.2 shard_map.173
  151.2 4.0 %shard_map.174 = (bf16[512,768]{1,0:T(8,128)(2,1)S(1)}, f32[512,256]{1,0:T(8,128)S(1)}, bf16[576,256]{1,0:T(8,128)(2,1)S(1)}, bf16[576,256]{1,0:T(8,128)(2,1)S(1...) custom-call(s32[5]{0:T(128)S(1)} %stack.32.at.refs_0_, bf16[512,256]{1,0:T(8,128)(2,1)S(1)} %copy-done.10, ...), custom_call_target="tpu_custom_call" | custom-call | flops 805306368 | bytes 6291456 | tf_op jit(solution)/shard_map/pallas_call | solution.py:614
  156.9 3.6 %shard_map.175 = (bf16[2,4,32,1024]{3,2,1,0:T(8,128)(2,1)}, bf16[2,4,32,1024]{3,2,1,0:T(8,128)(2,1)}, bf16[4,4,32,1024]{3,2,1,0:T(8,128)(2,1)S(1)}) custom-call(s32[5]{0:T(128)S(1)} %stack.32.at.refs_0_, bf16[512,1024]{1,0:T(8,128)(2,1)S(1)} %copy-done.55, bf16[512,768]{1,0:T(8,128)(2,1)S(1)} %get-tuple-element.106.refs_2_, ...), custom_call_target="tpu_custom_call" | custom-call | flops 1073741824 | bytes 4194304 | tf_op jit(solution)/shard_map/pallas_call | solution.py:334
  161.6 2.2 collective-permute-start.20
  163.8 2.2 collective-permute-start.23
  168.8 12.2 %collective-permute-done.22.d1 = bf16[576,256]{1,0:T(8,128)(2,1)S(1)} collective-permute-done((bf16[576,256]{1,0:T(8,128)(2,1)}, bf16[576,256]{1,0:T(8,128)(2,1)S(1)}, u32[]{:S(2)}, u32[]{:S(2)}) %collective-permute-start.22) | collective-permute-done | bytes 294944 | tf_op jit(solution)/shard_map/ppermute | solution.py:739
  187.2 2.3 shard_map.177
  191.8 4.7 %collective-permute-start.27 = (bf16[144,1024]{1,0:T(8,128)(2,1)}, bf16[144,1024]{1,0:T(8,128)(2,1)S(1)}, u32[]{:S(2)}, u32[]{:S(2)}) collective-permute-start(bf16[144,1024]{1,0:T(8,128)(2,1)} %get-tuple-element.120), channel_id=1, source_target_pairs={{0,16},{4,20},{8,24},{12,28},{16,0},{20,4},{24,8},{28,12},{32,48},... | collective-permute-start | bytes 884744 | tf_op jit(solution)/shard_map/ppermute | solution.py:760
  196.6 6.1 %collective-permute-done.26.m1 = bf16[144,1024]{1,0:T(8,128)(2,1)S(1)} collective-permute-done((bf16[144,1024]{1,0:T(8,128)(2,1)}, bf16[144,1024]{1,0:T(8,128)(2,1)S(1)}, u32[]{:S(2)}, u32[]{:S(2)}) %collective-permute-start.26) | collective-permute-done | bytes 294944 | tf_op jit(solution)/shard_map/ppermute | solution.py:760
  202.7 7.5 %collective-permute-done.27.m2 = bf16[144,1024]{1,0:T(8,128)(2,1)S(1)} collective-permute-done((bf16[144,1024]{1,0:T(8,128)(2,1)}, bf16[144,1024]{1,0:T(8,128)(2,1)S(1)}, u32[]{:S(2)}, u32[]{:S(2)}) %collective-permute-start.27) | collective-permute-done | bytes 294944 | tf_op jit(solution)/shard_map/ppermute | solution.py:760
  215.2 2.5 %collective-permute-start.31 = (bf16[48,1024]{1,0:T(8,128)(2,1)S(1)}, bf16[48,1024]{1,0:T(8,128)(2,1)S(1)}, u32[]{:S(2)}, u32[]{:S(2)}) collective-permute-start(bf16[48,1024]{1,0:T(8,128)(2,1)S(1)} %get-tuple-element.131), channel_id=1, source_target_pairs={{0,96},{4,100},{8,104},{12,108},{16,112},{20,116},{24,120},{28,124... | collective-permute-start | bytes 294920 | tf_op jit(solution)/shard_map/ppermute | solution.py:766
  220.0 2.0 collective-permute-done.31.m3
  223.8 8.7 %reduce-scatter.8.cloned.1.call-done = bf16[1,32,3456]{2,1,0:T(8,128)(2,1)} async-done(((bf16[4,32,3456]{2,1,0:T(8,128)(2,1)}), bf16[1,32,3456]{2,1,0:T(8,128)(2,1)}) %reduce-scatter.8.cloned.1.call-update) | async-done | bytes 221200 | tf_op jit(solution)/shard_map/reduce_scatter | solution.py:636
  (212 shorter events, 74.6 us)
Async XLA Ops:
  7.2 52.1 %all-gather.2.cloned.1.call-start = ((), (), s32[]{:S(2)}) async-start(), calls=%async_computation.3 | async-start | bytes 1310720 | tf_op jit(solution)/shard_map/all_gather | solution.py:672
  7.2 20.0 %collective-permute-start = (bf16[512,256]{1,0:T(8,128)(2,1)}, bf16[512,256]{1,0:T(8,128)(2,1)S(1)}, u32[]{:S(2)}, u32[]{:S(2)}) collective-permute-start(bf16[512,256]{1,0:T(8,128)(2,1)} %rows_in.1), channel_id=1, source_target_pairs={{0,3},{1,0},{2,1},{3,2},{4,7},{5,4},{6,5},{7,6},{8,11},{9,8},{10,9... | collective-permute-start | bytes 786440 | tf_op jit(solution)/shard_map/ppermute | solution.py:32
  10.1 17.2 %collective-permute-start.1 = (bf16[512,256]{1,0:T(8,128)(2,1)}, bf16[512,256]{1,0:T(8,128)(2,1)S(1)}, u32[]{:S(2)}, u32[]{:S(2)}) collective-permute-start(bf16[512,256]{1,0:T(8,128)(2,1)} %rows_in.1), channel_id=1, source_target_pairs={{0,2},{1,3},{2,0},{3,1},{4,6},{5,7},{6,4},{7,5},{8,10},{9,11},{10,... | collective-permute-start | bytes 786440 | tf_op jit(solution)/shard_map/ppermute | solution.py:32
  10.9 16.4 %collective-permute-start.2 = (bf16[512,256]{1,0:T(8,128)(2,1)}, bf16[512,256]{1,0:T(8,128)(2,1)S(1)}, u32[]{:S(2)}, u32[]{:S(2)}) collective-permute-start(bf16[512,256]{1,0:T(8,128)(2,1)} %rows_in.1), channel_id=1, source_target_pairs={{0,1},{1,2},{2,3},{3,0},{4,5},{5,6},{6,7},{7,4},{8,9},{9,10},{10,1... | collective-permute-start | bytes 786440 | tf_op jit(solution)/shard_map/ppermute | solution.py:32
  13.5 21.8 %collective-permute-start.7 = (bf16[512,256]{1,0:T(8,128)(2,1)}, bf16[512,256]{1,0:T(8,128)(2,1)}, u32[]{:S(2)}, u32[]{:S(2)}) collective-permute-start(bf16[512,256]{1,0:T(8,128)(2,1)} %constant_dynamic-slice_fusion.2), channel_id=1, source_target_pairs={{0,3},{1,0},{2,1},{3,2},{4,7},{5,4},{6,5},{7,6},{8,11},{9,8},{10,9... | collective-permute-start | bytes 786440 | tf_op jit(solution)/shard_map/ppermute | solution.py:32
  15.8 19.4 %collective-permute-start.8 = (bf16[512,256]{1,0:T(8,128)(2,1)}, bf16[512,256]{1,0:T(8,128)(2,1)}, u32[]{:S(2)}, u32[]{:S(2)}) collective-permute-start(bf16[512,256]{1,0:T(8,128)(2,1)} %constant_dynamic-slice_fusion.2), channel_id=1, source_target_pairs={{0,2},{1,3},{2,0},{3,1},{4,6},{5,7},{6,4},{7,5},{8,10},{9,11},{10,... | collective-permute-start | bytes 786440 | tf_op jit(solution)/shard_map/ppermute | solution.py:32
  17.4 179.2 %reduce-scatter.4.cloned.1.call-start = ((), (), s32[]{:S(2)}) async-start(), calls=%async_computation.4 | async-start | bytes 1310720 | tf_op jit(solution)/shard_map/reduce_scatter | solution.py:719
  27.3 12.2 %collective-permute-start.9 = (bf16[512,256]{1,0:T(8,128)(2,1)}, bf16[512,256]{1,0:T(8,128)(2,1)S(1)}, u32[]{:S(2)}, u32[]{:S(2)}) collective-permute-start(bf16[512,256]{1,0:T(8,128)(2,1)} %constant_dynamic-slice_fusion.2), channel_id=1, source_target_pairs={{0,1},{1,2},{2,3},{3,0},{4,5},{5,6},{6,7},{7,4},{8,9},{9,10},{10,1... | collective-permute-start | bytes 786440 | tf_op jit(solution)/shard_map/ppermute | solution.py:32
  42.5 16.8 %collective-permute-start.10 = (bf16[512,1024]{1,0:T(8,128)(2,1)S(1)}, bf16[512,1024]{1,0:T(8,128)(2,1)}, u32[]{:S(2)}, u32[]{:S(2)}) collective-permute-start(bf16[512,1024]{1,0:T(8,128)(2,1)S(1)} %constant_dynamic-update-slice_fusion.half), channel_id=1, source_target_pairs={{0,4},{4,0},{8,12},{12,8},{16,20},{20,16},{24,28},{28,24},{32,36},... | collective-permute-start | bytes 3145736 | tf_op jit(solution)/shard_map/ppermute | solution.py:692
  42.6 10.9 %collective-permute-start.4 = (bf16[512,256]{1,0:T(8,128)(2,1)S(1)}, bf16[512,256]{1,0:T(8,128)(2,1)S(1)}, u32[]{:S(2)}, u32[]{:S(2)}) collective-permute-start(bf16[512,256]{1,0:T(8,128)(2,1)S(1)} %get-tuple-element.142.m0.refs_4_), channel_id=1, source_target_pairs={{0,3},{1,0},{2,1},{3,2},{4,7},{5,4},{6,5},{7,6},{8,11},{9,8},{10,9... | collective-permute-start | bytes 786440 | tf_op jit(solution)/shard_map/ppermute | solution.py:32
  43.1 11.2 %collective-permute-start.5 = (bf16[512,256]{1,0:T(8,128)(2,1)S(1)}, bf16[512,256]{1,0:T(8,128)(2,1)S(1)}, u32[]{:S(2)}, u32[]{:S(2)}) collective-permute-start(bf16[512,256]{1,0:T(8,128)(2,1)S(1)} %get-tuple-element.142.m0.refs_4_), channel_id=1, source_target_pairs={{0,2},{1,3},{2,0},{3,1},{4,6},{5,7},{6,4},{7,5},{8,10},{9,11},{10,... | collective-permute-start | bytes 786440 | tf_op jit(solution)/shard_map/ppermute | solution.py:32
  43.9 14.7 %collective-permute-start.6 = (bf16[512,256]{1,0:T(8,128)(2,1)S(1)}, bf16[512,256]{1,0:T(8,128)(2,1)S(1)}, u32[]{:S(2)}, u32[]{:S(2)}) collective-permute-start(bf16[512,256]{1,0:T(8,128)(2,1)S(1)} %get-tuple-element.142.m0.refs_4_), channel_id=1, source_target_pairs={{0,1},{1,2},{2,3},{3,0},{4,5},{5,6},{6,7},{7,4},{8,9},{9,10},{10,1... | collective-permute-start | bytes 786440 | tf_op jit(solution)/shard_map/ppermute | solution.py:32
  83.4 126.8 %reduce-scatter.6.cloned.1.call-start = ((), (), s32[]{:S(2)}) async-start(), calls=%async_computation.5 | async-start | bytes 4423680 | tf_op jit(solution)/shard_map/reduce_scatter | solution.py:636
  98.2 26.1 %collective-permute-start.11 = (bf16[2,4,32,3456]{3,2,1,0:T(8,128)(2,1)}, bf16[2,4,32,3456]{3,2,1,0:T(8,128)(2,1)}, u32[]{:S(2)}, u32[]{:S(2)}) collective-permute-start(bf16[2,4,32,3456]{3,2,1,0:T(8,128)(2,1)} %get-tuple-element.89), channel_id=1, source_target_pairs={{0,4},{4,0},{8,12},{12,8},{16,20},{20,16},{24,28},{28,24},{32,36},... | collective-permute-start | bytes 5308424 | tf_op jit(solution)/shard_map/ppermute | solution.py:347
  98.2 26.1 %collective-permute-start.12 = (bf16[2,4,32,3456]{3,2,1,0:T(8,128)(2,1)}, bf16[2,4,32,3456]{3,2,1,0:T(8,128)(2,1)}, u32[]{:S(2)}, u32[]{:S(2)}) collective-permute-start(bf16[2,4,32,3456]{3,2,1,0:T(8,128)(2,1)} %get-tuple-element.90), channel_id=1, source_target_pairs={{0,4},{4,0},{8,12},{12,8},{16,20},{20,16},{24,28},{28,24},{32,36},... | collective-permute-start | bytes 5308424 | tf_op jit(solution)/shard_map/ppermute | solution.py:347
  98.7 13.7 %collective-permute-start.13 = (bf16[512,256]{1,0:T(8,128)(2,1)}, bf16[512,256]{1,0:T(8,128)(2,1)}, u32[]{:S(2)}, u32[]{:S(2)}) collective-permute-start(bf16[512,256]{1,0:T(8,128)(2,1)} %get-tuple-element.93), channel_id=1, source_target_pairs={{0,1},{1,2},{2,3},{3,0},{4,5},{5,6},{6,7},{7,4},{8,9},{9,10},{10,1... | collective-permute-start | bytes 786440 | tf_op jit(solution)/shard_map/ppermute | solution.py:38
  100.7 17.6 %collective-permute-start.14 = (bf16[512,256]{1,0:T(8,128)(2,1)}, bf16[512,256]{1,0:T(8,128)(2,1)}, u32[]{:S(2)}, u32[]{:S(2)}) collective-permute-start(bf16[512,256]{1,0:T(8,128)(2,1)} %get-tuple-element.94), channel_id=1, source_target_pairs={{0,2},{1,3},{2,0},{3,1},{4,6},{5,7},{6,4},{7,5},{8,10},{9,11},{10,... | collective-permute-start | bytes 786440 | tf_op jit(solution)/shard_map/ppermute | solution.py:38
  104.1 14.3 %collective-permute-start.15 = (bf16[512,256]{1,0:T(8,128)(2,1)S(1)}, bf16[512,256]{1,0:T(8,128)(2,1)}, u32[]{:S(2)}, u32[]{:S(2)}) collective-permute-start(bf16[512,256]{1,0:T(8,128)(2,1)S(1)} %copy-done.47), channel_id=1, source_target_pairs={{0,3},{1,0},{2,1},{3,2},{4,7},{5,4},{6,5},{7,6},{8,11},{9,8},{10,9... | collective-permute-start | bytes 786440 | tf_op jit(solution)/shard_map/ppermute | solution.py:38
  120.8 13.4 %collective-permute-start.16 = (bf16[512,256]{1,0:T(8,128)(2,1)}, bf16[512,256]{1,0:T(8,128)(2,1)S(1)}, u32[]{:S(2)}, u32[]{:S(2)}) collective-permute-start(bf16[512,256]{1,0:T(8,128)(2,1)} %get-tuple-element.140), channel_id=1, source_target_pairs={{0,3},{1,0},{2,1},{3,2},{4,7},{5,4},{6,5},{7,6},{8,11},{9,8},{10,9... | collective-permute-start | bytes 786440 | tf_op jit(solution)/shard_map/ppermute | solution.py:32
  122.6 11.6 %collective-permute-start.17 = (bf16[512,256]{1,0:T(8,128)(2,1)}, bf16[512,256]{1,0:T(8,128)(2,1)S(1)}, u32[]{:S(2)}, u32[]{:S(2)}) collective-permute-start(bf16[512,256]{1,0:T(8,128)(2,1)} %get-tuple-element.140), channel_id=1, source_target_pairs={{0,2},{1,3},{2,0},{3,1},{4,6},{5,7},{6,4},{7,5},{8,10},{9,11},{10,... | collective-permute-start | bytes 786440 | tf_op jit(solution)/shard_map/ppermute | solution.py:32
  122.9 14.8 %collective-permute-start.18 = (bf16[512,256]{1,0:T(8,128)(2,1)}, bf16[512,256]{1,0:T(8,128)(2,1)}, u32[]{:S(2)}, u32[]{:S(2)}) collective-permute-start(bf16[512,256]{1,0:T(8,128)(2,1)} %get-tuple-element.140), channel_id=1, source_target_pairs={{0,1},{1,2},{2,3},{3,0},{4,5},{5,6},{6,7},{7,4},{8,9},{9,10},{10,1... | collective-permute-start | bytes 786440 | tf_op jit(solution)/shard_map/ppermute | solution.py:32
  137.8 94.7 %reduce-scatter.8.cloned.1.call-start = ((), (), s32[]{:S(2)}) async-start(), calls=%async_computation.6 | async-start | bytes 1105920 | tf_op jit(solution)/shard_map/reduce_scatter | solution.py:636
  161.6 25.7 %collective-permute-start.20 = (bf16[2,4,32,1024]{3,2,1,0:T(8,128)(2,1)}, bf16[2,4,32,1024]{3,2,1,0:T(8,128)(2,1)}, u32[]{:S(2)}, u32[]{:S(2)}) collective-permute-start(bf16[2,4,32,1024]{3,2,1,0:T(8,128)(2,1)} %get-tuple-element.109), channel_id=1, source_target_pairs={{0,4},{4,0},{8,12},{12,8},{16,20},{20,16},{24,28},{28,24},{32,36},... | collective-permute-start | bytes 1572872 | tf_op jit(solution)/shard_map/ppermute | solution.py:347
  163.8 23.5 %collective-permute-start.21 = (bf16[2,4,32,1024]{3,2,1,0:T(8,128)(2,1)}, bf16[2,4,32,1024]{3,2,1,0:T(8,128)(2,1)}, u32[]{:S(2)}, u32[]{:S(2)}) collective-permute-start(bf16[2,4,32,1024]{3,2,1,0:T(8,128)(2,1)} %get-tuple-element.110), channel_id=1, source_target_pairs={{0,4},{4,0},{8,12},{12,8},{16,20},{20,16},{24,28},{28,24},{32,36},... | collective-permute-start | bytes 1572872 | tf_op jit(solution)/shard_map/ppermute | solution.py:347
  163.8 17.2 %collective-permute-start.22 = (bf16[576,256]{1,0:T(8,128)(2,1)}, bf16[576,256]{1,0:T(8,128)(2,1)S(1)}, u32[]{:S(2)}, u32[]{:S(2)}) collective-permute-start(bf16[576,256]{1,0:T(8,128)(2,1)} %copy-done.45), channel_id=1, source_target_pairs={{0,1},{1,2},{2,3},{3,0},{4,5},{5,6},{6,7},{7,4},{8,9},{9,10},{10,1... | collective-permute-start | bytes 884744 | tf_op jit(solution)/shard_map/ppermute | solution.py:739
  163.8 17.2 %collective-permute-start.23 = (bf16[576,256]{1,0:T(8,128)(2,1)}, bf16[576,256]{1,0:T(8,128)(2,1)S(1)}, u32[]{:S(2)}, u32[]{:S(2)}) collective-permute-start(bf16[576,256]{1,0:T(8,128)(2,1)} %copy-done.44), channel_id=1, source_target_pairs={{0,2},{1,3},{2,0},{3,1},{4,6},{5,7},{6,4},{7,5},{8,10},{9,11},{10,... | collective-permute-start | bytes 884744 | tf_op jit(solution)/shard_map/ppermute | solution.py:739
  166.0 15.6 %collective-permute-start.24 = (bf16[576,256]{1,0:T(8,128)(2,1)}, bf16[576,256]{1,0:T(8,128)(2,1)S(1)}, u32[]{:S(2)}, u32[]{:S(2)}) collective-permute-start(bf16[576,256]{1,0:T(8,128)(2,1)} %copy-done.43), channel_id=1, source_target_pairs={{0,3},{1,0},{2,1},{3,2},{4,7},{5,4},{6,5},{7,6},{8,11},{9,8},{10,9... | collective-permute-start | bytes 884744 | tf_op jit(solution)/shard_map/ppermute | solution.py:739
  190.3 12.3 %collective-permute-start.26 = (bf16[144,1024]{1,0:T(8,128)(2,1)}, bf16[144,1024]{1,0:T(8,128)(2,1)S(1)}, u32[]{:S(2)}, u32[]{:S(2)}) collective-permute-start(bf16[144,1024]{1,0:T(8,128)(2,1)} %get-tuple-element.119), channel_id=1, source_target_pairs={{0,8},{4,12},{8,16},{12,20},{16,24},{20,28},{24,0},{28,4},{32,40},... | collective-permute-start | bytes 884744 | tf_op jit(solution)/shard_map/ppermute | solution.py:760
  191.8 18.3 %collective-permute-start.27 = (bf16[144,1024]{1,0:T(8,128)(2,1)}, bf16[144,1024]{1,0:T(8,128)(2,1)S(1)}, u32[]{:S(2)}, u32[]{:S(2)}) collective-permute-start(bf16[144,1024]{1,0:T(8,128)(2,1)} %get-tuple-element.120), channel_id=1, source_target_pairs={{0,16},{4,20},{8,24},{12,28},{16,0},{20,4},{24,8},{28,12},{32,48},... | collective-permute-start | bytes 884744 | tf_op jit(solution)/shard_map/ppermute | solution.py:760
  196.6 13.6 %collective-permute-start.28 = (bf16[144,1024]{1,0:T(8,128)(2,1)}, bf16[144,1024]{1,0:T(8,128)(2,1)S(1)}, u32[]{:S(2)}, u32[]{:S(2)}) collective-permute-start(bf16[144,1024]{1,0:T(8,128)(2,1)} %get-tuple-element.121), channel_id=1, source_target_pairs={{0,24},{4,28},{8,0},{12,4},{16,8},{20,12},{24,16},{28,20},{32,56},... | collective-permute-start | bytes 884744 | tf_op jit(solution)/shard_map/ppermute | solution.py:760
  212.0 8.0 %collective-permute-start.29 = (bf16[48,1024]{1,0:T(8,128)(2,1)S(1)}, bf16[48,1024]{1,0:T(8,128)(2,1)S(1)}, u32[]{:S(2)}, u32[]{:S(2)}) collective-permute-start(bf16[48,1024]{1,0:T(8,128)(2,1)S(1)} %get-tuple-element.129), channel_id=1, source_target_pairs={{0,32},{4,36},{8,40},{12,44},{16,48},{20,52},{24,56},{28,60},{32,6... | collective-permute-start | bytes 294920 | tf_op jit(solution)/shard_map/ppermute | solution.py:766
  215.2 6.8 %collective-permute-start.31 = (bf16[48,1024]{1,0:T(8,128)(2,1)S(1)}, bf16[48,1024]{1,0:T(8,128)(2,1)S(1)}, u32[]{:S(2)}, u32[]{:S(2)}) collective-permute-start(bf16[48,1024]{1,0:T(8,128)(2,1)S(1)} %get-tuple-element.131), channel_id=1, source_target_pairs={{0,96},{4,100},{8,104},{12,108},{16,112},{20,116},{24,120},{28,124... | collective-permute-start | bytes 294920 | tf_op jit(solution)/shard_map/ppermute | solution.py:766
  (66 other events, 454.7 us)
Sparse Core Ops, SparseCore 0:
  17.5 33.4 all-gather.1
  83.5 30.4 reduce-scatter.3
  137.9 40.6 reduce-scatter.5
  210.3 22.1 reduce-scatter.7

commit v2 on v1

--- a/solution.py
+++ b/solution.py
@@ -9,6 +9,7 @@
 F32 = jnp.float32
 BF16 = jnp.bfloat16
 CH = 4
+LONG = 2**36
 
 
 def seq_index(y, z, core):
@@ -172,23 +173,41 @@
             pltpu.VMEM((3, features, width), BF16),
             pltpu.SemaphoreType.DMA((CH,)),
         ],
-        compiler_params=params(24),
+        compiler_params=params(16),
         cost_estimate=cost(rows * features * 3 * width, 6 * 2**20),
     )(at, *pieces, gain[None], weight)
+
+
+def columns_kernel(p0, p1, p2, p3, out):
+    width = p0.shape[1]
+    for j, piece in enumerate((p0, p1, p2, p3)):
+        out[:, j * width : (j + 1) * width] = piece[...]
+
+
+def join_columns(pieces, weight):
+    rows, width = pieces[0].shape
+    return pl.pallas_call(
+        columns_kernel,
+        out_shape=shape((rows, CH * width), BF16),
+        in_specs=[vmem()] * CH,
+        out_specs=vmem(),
+        compiler_params=params(8),
+        cost_estimate=cost(weight, 2**21),
+    )(*pieces)
 
 
 def ffn_kernel(
     at,
     x0, x1, x2, x3,
-    m0, m1, m2, m3,
+    mixed,
     gain,
     half,
     other,
     planes,
     down,
     cotangent,
-    h, rms, normed, act, d_gate_up, d_own, d1, d2, d3,
-    w_out, w_in, w_down, g_rows, mixed, acc, sem,
+    h, rms, normed, act, d_gate_up, d_own, d1, d2, d3, down_out,
+    w_out, w_in, w_down, g_rows, acc, down_acc, sem,
 ):
     x, core = at[0], at[1]
     width = x0.shape[1]
@@ -212,8 +231,6 @@
     ]
     for copy in halves + planes_in + rest:
         copy.start()
-    for j, piece in enumerate((m0, m1, m2, m3)):
-        mixed[:, j * width : (j + 1) * width] = piece[...]
     for copy in halves:
         copy.wait()
     square = jnp.zeros((x0.shape[0], 1), F32)
@@ -241,7 +258,12 @@
         d_act = dot_nn(g_rows[...], w_down[:, f])
         sigma = jax.nn.sigmoid(gate)
         swish = gate * sigma
-        act[:, f] = (swish * up).astype(BF16)
+        active = (swish * up).astype(BF16)
+        act[:, f] = active
+        for j in range(CH):
+            rows = slice(j * width, (j + 1) * width)
+            term = dot_nt(active, w_down[rows, f])
+            down_acc[j] = jnp.where(i == 0, term, down_acc[j] + term)
         d_gate = (d_act * up * sigma * (1.0 + gate * (1.0 - sigma))).astype(BF16)
         d_up = (d_act * swish).astype(BF16)
         d_gate_up[:, f] = d_gate
@@ -257,9 +279,11 @@
     d1[...] = acc[1].astype(BF16)
     d2[...] = acc[2].astype(BF16)
     d3[...] = acc[3].astype(BF16)
-
-
-def ffn(at, pieces, mixed_pieces, gain, half, other, planes, down, cotangent):
+    for j in range(CH):
+        down_out[:, j * width : (j + 1) * width] = down_acc[j].astype(BF16)
+
+
+def ffn(at, pieces, mixed, gain, half, other, planes, down, cotangent):
     rows, width = pieces[0].shape
     features = CH * width
     units = down.shape[1]
@@ -276,21 +300,22 @@
             block,
             block,
             block,
+            shape((rows, features), BF16),
         ),
-        in_specs=[smem()] + [vmem()] * 9 + [anywhere()] * 5,
-        out_specs=(vmem(),) * 9,
+        in_specs=[smem()] + [vmem()] * 6 + [anywhere()] * 5,
+        out_specs=(vmem(),) * 10,
         scratch_shapes=[
             pltpu.VMEM((2, features // 2, features), BF16),
             pltpu.VMEM((2, features, units), BF16),
             pltpu.VMEM((features, units), BF16),
             pltpu.VMEM((rows, features), BF16),
-            pltpu.VMEM((rows, features), BF16),
+            pltpu.VMEM((CH, rows, width), F32),
             pltpu.VMEM((CH, rows, width), F32),
             pltpu.SemaphoreType.DMA((8,)),
         ],
-        compiler_params=params(48),
-        cost_estimate=cost(rows * features * (features + 5 * units), 20 * 2**20),
-    )(at, *pieces, *mixed_pieces, gain[None], half, other, planes, down, cotangent)
+        compiler_params=params(34),
+        cost_estimate=cost(rows * features * (features + 6 * units), 20 * 2**20),
+    )(at, *pieces, mixed, gain[None], half, other, planes, down, cotangent)
 
 
 def pair_kernel(
@@ -338,7 +363,7 @@
         in_specs=[smem()] + [vmem()] * 4,
         out_specs=(half_spec, half_spec, spec),
         scratch_shapes=[pltpu.VMEM((features // 4, columns), F32)],
-        compiler_params=params(40),
+        compiler_params=params(22),
         cost_estimate=cost(tokens * features * columns, 4 * features * columns),
     )(at, a_left, a_right, b_left, b_right)
 
@@ -361,7 +386,7 @@
         out_shape=shape(keep.shape, BF16),
         in_specs=[spec, half, half],
         out_specs=spec,
-        compiler_params=params(24),
+        compiler_params=params(16),
         cost_estimate=cost(2**20, 6 * keep.size),
     )(keep, *got)
 
@@ -400,7 +425,7 @@
         out_shape=(shape((rows, columns), F32), message, message, message),
         in_specs=[smem()] + [vmem()] * 4,
         out_specs=(vmem(),) * 4,
-        compiler_params=params(24),
+        compiler_params=params(16),
         cost_estimate=cost(2**20, 2**22),
     )(at, keep, *got, small)
 
@@ -440,7 +465,7 @@
         in_specs=[smem()] + [vmem()] * 5,
         out_specs=(vmem(),) * 5,
         scratch_shapes=[pltpu.VMEM((rows, columns), F32)],
-        compiler_params=params(24),
+        compiler_params=params(16),
         cost_estimate=cost(2**20, 2**21),
     )(at, own, *messages, small)
 
@@ -471,7 +496,7 @@
         ),
         in_specs=[vmem()] * 5,
         out_specs=(vmem(),) * 3,
-        compiler_params=params(24),
+        compiler_params=params(16),
         cost_estimate=cost(2**20, 2**20),
     )(own, *messages, small)
 
@@ -505,9 +530,36 @@
         out_shape=(shape((rows, width), BF16), shape((1, width), F32)),
         in_specs=[vmem()] * 9,
         out_specs=(vmem(),) * 2,
-        compiler_params=params(24),
-        cost_estimate=cost(2**20, 2**21),
+        compiler_params=params(16),
+        cost_estimate=cost(2**32, 2**21),
     )(d_own, *received, inner, d_hidden, rows_in, rms, gain[None])
+
+
+def norm_kernel(d_own, d1, d2, d3, h, rms, gain, cotangent, u, u_low, gain_grad):
+    total = d_own[...]
+    for d in (d1, d2, d3):
+        total = total + d[...].astype(F32)
+    r = rms[...]
+    gain_grad[...] = jnp.sum(total * h[...] * r, axis=0, keepdims=True)
+    full = cotangent[...].astype(F32) + r * gain[...] * total
+    u[...] = full
+    u_low[...] = full.astype(BF16)
+
+
+def norm_back(d_own, received, h, rms, gain, cotangent):
+    rows, width = d_own.shape
+    return pl.pallas_call(
+        norm_kernel,
+        out_shape=(
+            shape((rows, width), F32),
+            shape((rows, width), BF16),
+            shape((1, width), F32),
+        ),
+        in_specs=[vmem()] * 8,
+        out_specs=(vmem(),) * 3,
+        compiler_params=params(10),
+        cost_estimate=cost(LONG, 2**21),
+    )(d_own, *received, h, rms, gain[None], cotangent)
 
 
 def mid_kernel(
@@ -545,7 +597,7 @@
         out_shape=(shape((rows, CH * width), BF16), wide, wide, shape((rows, width), BF16)),
         in_specs=[smem()] + [vmem()] * 10,
         out_specs=(vmem(),) * 4,
-        compiler_params=params(24),
+        compiler_params=params(16),
         cost_estimate=cost(rows * CH * width * width, 6 * 2**20),
     )(at, *pieces, h, rms, cotangent, weight, c_gate, conv_out)
 
@@ -627,7 +679,7 @@
             pltpu.VMEM((3, features, width), BF16),
             pltpu.SemaphoreType.DMA((CH,)),
         ],
-        compiler_params=params(32),
+        compiler_params=params(18),
         cost_estimate=cost(rows * features * 3 * width, 6 * 2**20),
     )(at, *pieces, d_conv, following, taps, value, b_gate, d_cgate, gain[None], weight)
 
@@ -670,8 +722,6 @@
     half = lax.dynamic_slice_in_dim(out_weight, core * half_rows, half_rows, 0)
     half_pieces = gather_ch(half)
     grad_full = lax.all_gather(out_grad, "ch", axis=1, tiled=True)
-    ffn_planes = jnp.transpose(ffn_in_weight, (1, 0, 2))
-    ffn_planes, *pieces = tie(ffn_planes, *pieces)
 
     normed_one, r_one, b_gate, c_gate, value_rows, gated_rows = in_project(
         at, pieces, norm1_gain, in_planes
@@ -687,8 +737,11 @@
     mixed_rows = (c_gate * conv_out).astype(BF16)
 
     mixed_pieces = gather_ch(mixed_rows)
-    half_pieces = tie(*half_pieces, mixed_rows)[:CH]
-    half_full = jnp.concatenate(half_pieces, axis=1)
+    *half_pieces, ffn_weight, _ = tie(*half_pieces, ffn_in_weight, mixed_rows)
+    ffn_planes = jnp.transpose(ffn_weight, (1, 0, 2))
+    half_full = join_columns(half_pieces, 2**20)
+    mixed_full = join_columns(mixed_pieces, 2**32)
+    ffn_planes, mixed_full = tie(ffn_planes, mixed_full)
     other_half = lax.ppermute(half_full, "seq", seq_pairs(0, 0, 1))
     (
         hidden,
@@ -700,10 +753,11 @@
         d_one,
         d_two,
         d_three,
+        down_terms,
     ) = ffn(
         at,
         pieces,
-        mixed_pieces,
+        mixed_full,
         norm2_gain,
         half_full,
         other_half,
@@ -712,17 +766,17 @@
         grad_full,
     )
     hidden_own = hidden[:, :width]
-    d_normed_own = scatter_ch([d_own, d_one, d_two, d_three])
-    down_terms = jnp.einsum(
-        "tf,ef->te", act_rows, ffn_out_weight, preferred_element_type=F32
-    ).astype(BF16)
+    received = [
+        lax.ppermute(d, "ch", ch_pairs(j)) for j, d in ((1, d_one), (2, d_two), (3, d_three))
+    ]
     down = lax.psum_scatter(down_terms, "ch", scatter_dimension=1, tiled=True)
     *gives, keep = pair_products(at, normed_two, d_gate_up, grad_full, act_rows, True, False)
     got = swap_cores(gives)
 
-    grad_gain_two = jnp.sum(d_normed_own * hidden_own * r_two, axis=0)
-    u_own = out_grad.astype(F32) + r_two * own_two * d_normed_own
-    u_pieces = [u_own] + gather_ch(u_own.astype(BF16))[1:]
+    u_own, u_low, grad_gain_two = norm_back(
+        d_own, received, hidden_own, r_two, own_two, out_grad
+    )
+    u_pieces = [u_own] + gather_ch(u_low)[1:]
     ffn_kept = add_cores(keep, got)
     ffn_kept, *u_pieces = tie(ffn_kept, *u_pieces)
     groups = [[seq_index(i, k, c) for k in range(4)] for i in range(4) for c in range(2)]
@@ -752,7 +806,7 @@
         d_own, received, inner, d_hidden, block_input, r_one, own_one
     )
     small = jnp.concatenate(
-        [grad_conv, grad_gain_one, grad_gain_two[None], jnp.zeros((3, width), F32)], axis=0
+        [grad_conv, grad_gain_one, grad_gain_two, jnp.zeros((3, width), F32)], axis=0
     )
     small = small + lax.ppermute(small, "seq", seq_pairs(0, 0, 1))
     own, *messages = send_z(at, keep, got, small)

time: 243 us -> 227 us (0.934)
  waiting for transfers between devices: 80.1 us -> 69.5 us
  other arithmetic: 10.8 us -> 6.7 us
  matrix products: 4 us -> 0 us
  Pallas kernels: 44.9 us -> 48.2 us
    ppermute x3 -> x0, waiting for transfers between devices: 14.1 us -> none  [scatter_ch(): total = total + lax.ppermute(chunks[j], 'ch', ch_pairs(j)).astype(F32)]
    unnamed x128 -> x120, local copies, waits for them, and re-layouts: 39.7 us -> 32.4 us
    ppermute x3 -> x0, starting transfers between devices: 5.35 us -> none  [scatter_ch(): total = total + lax.ppermute(chunks[j], 'ch', ch_pairs(j)).astype(F32)]
    optimization_barrier x0 -> x1, local copies, waits for them, and re-layouts: none -> 5.12 us  [tie(): return lax.optimization_barrier(arrays)]
    ppermute x3 -> x6, starting transfers between devices: 3.24 us -> 7.42 us  [shards(): lax.ppermute(d, 'ch', ch_pairs(j))]
    ppermute x12, waiting for transfers between devices: 25.4 us -> 29.4 us  [gather_ch(): lax.ppermute(block, 'ch', ch_pairs(-j))]
    dot_general x1 -> x0, matrix products: 4 us -> none  [shards(): jnp.einsum('tf,ef->te', act_rows, ffn_out_weight, preferred_element_type=...]
    pallas_call x0 -> x3, Pallas kernels: none -> 3.26 us  [the longest x1 2.06 us: norm_back(): pl.pallas_call(norm_kernel, out_shape=(shape((rows, width), F32), shape((...]
  transfers between devices with their start and end apart: 36 -> 36, of which waited for: 18 -> 20; matrix products, arithmetic and copies ran while one was open for 9% -> 7% of each run, Pallas kernels for 12% -> 15%
where the time goes in v2:
time: 227 us; the launch traced here: 226 us
  waiting for transfers between devices  69.5 us (31%)
  Pallas kernels  48.2 us (21%)
  local copies, waits for them, and re-layouts  45 us (20%)
  starting transfers between devices  41.6 us (18%)
  between operations  14.9 us (7%)
  other arithmetic  6.7 us (3%)
    unnamed x120, local copies, waits for them, and re-layouts  32.4 us
    ppermute x12, waiting for transfers between devices, gather_ch(): lax.ppermute(block, 'ch', ch_pairs(-j))  29.4 us
    pallas_call x1, Pallas kernels, ffn(): pl.pallas_call(ffn_kernel, out_shape=(shape((rows, features), F32), shape...  15.4 us
    ppermute x12, starting transfers between devices, gather_ch(): lax.ppermute(block, 'ch', ch_pairs(-j))  14.2 us
    ppermute x6, waiting for transfers between devices, shards(): lax.ppermute(d, 'ch', ch_pairs(j))  12.6 us
    ppermute x3, waiting for transfers between devices, shards(): lax.ppermute(m, 'seq', seq_pairs(0, j, 0))  12.4 us
    pallas_call x2, Pallas kernels, pair_products(): pl.pallas_call(body, grid=(4,), out_shape=(half, half, out), in_specs=[sm...  11.1 us
    reduce_scatter x2, waiting for transfers between devices, scatter_groups(): lax.psum_scatter(array, 'seq', scatter_dimension=0, axis_index_groups=gro...  10.5 us
  transfers between devices with their start and end apart: 36, of which 20 were waited for; matrix products, arithmetic and copies ran while one was open for 7% of the time, Pallas kernels for 15%

profile of v2, /device:TPU:0, one launch (start us, length us, event | category | flops | bytes accessed | tf_op | source)
XLA Modules:
  0.0 225.9 jit_solution(4182215201282690710)
XLA Ops:
  7.2 2.9 %collective-permute-start = (bf16[512,256]{1,0:T(8,128)(2,1)}, bf16[512,256]{1,0:T(8,128)(2,1)S(1)}, u32[]{:S(2)}, u32[]{:S(2)}) collective-permute-start(bf16[512,256]{1,0:T(8,128)(2,1)} %rows_in.1), channel_id=1, source_target_pairs={{0,3},{1,0},{2,1},{3,2},{4,7},{5,4},{6,5},{7,6},{8,11},{9,8},{10,9... | collective-permute-start | bytes 786440 | tf_op jit(solution)/shard_map/ppermute | solution.py:33
  12.8 2.4 %collective-permute-start.3 = (bf16[512,256]{1,0:T(8,128)(2,1)S(1)}, bf16[512,256]{1,0:T(8,128)(2,1)S(1)}, u32[]{:S(2)}, u32[]{:S(2)}) collective-permute-start(bf16[512,256]{1,0:T(8,128)(2,1)S(1)} %constant_dynamic-slice_fusion.2.p0), channel_id=1, source_target_pairs={{0,3},{1,0},{2,1},{3,2},{4,7},{5,4},{6,5},{7,6},{8,11},{9,8},{10,9... | collective-permute-start | bytes 786440 | tf_op jit(solution)/shard_map/ppermute | solution.py:33
  18.0 2.0 convert_reduce_fusion
  22.6 4.2 %collective-permute-done.2.p3.x3 = bf16[512,256]{1,0:T(8,128)(2,1)S(1)} collective-permute-done((bf16[512,256]{1,0:T(8,128)(2,1)}, bf16[512,256]{1,0:T(8,128)(2,1)S(1)}, u32[]{:S(2)}, u32[]{:S(2)}) %collective-permute-start.2) | collective-permute-done | bytes 262176 | tf_op jit(solution)/shard_map/ppermute | solution.py:33
  30.0 2.4 %shard_map.169 = (bf16[512,1024]{1,0:T(8,128)(2,1)S(1)}, f32[512,1]{1,0:T(8,128)S(1)}, f32[512,256]{1,0:T(8,128)S(1)}, f32[512,256]{1,0:T(8,128)S(1)}, f32[512,2...) custom-call(s32[5]{0:T(128)S(1)} %stack.32.at.refs_0_, bf16[512,256]{1,0:T(8,128)(2,1)S(1)} %copy-done.20, ...), custom_call_target="tpu_custom_call" | custom-call | flops 805306368 | bytes 6291456 | tf_op jit(solution)/shard_map/pallas_call | solution.py:160
  39.9 1.8 collective-permute-start.10
  41.7 5.1 %copy.21 = bf16[1024,2,1152]{2,0,1:T(8,128)(2,1)} copy(bf16[1024,2,1152]{2,1,0:T(2,128)(2,1)} %param.17) | data formatting | bytes 9437184 | tf_op jit(solution)/shard_map/optimization_barrier | solution.py:72
  46.8 3.7 %collective-permute-done.7.p1 = bf16[512,256]{1,0:T(8,128)(2,1)S(1)} collective-permute-done((bf16[512,256]{1,0:T(8,128)(2,1)S(1)}, bf16[512,256]{1,0:T(8,128)(2,1)S(1)}, u32[]{:S(2)}, u32[]{:S(2)}) %collective-permute-start.7) | collective-permute-done | bytes 262176 | tf_op jit(solution)/shard_map/ppermute | solution.py:33
  50.5 6.3 %collective-permute-done.9.p3 = bf16[512,256]{1,0:T(8,128)(2,1)} collective-permute-done((bf16[512,256]{1,0:T(8,128)(2,1)S(1)}, bf16[512,256]{1,0:T(8,128)(2,1)}, u32[]{:S(2)}, u32[]{:S(2)}) %collective-permute-start.9) | collective-permute-done | bytes 262176 | tf_op jit(solution)/shard_map/ppermute | solution.py:33
  63.1 15.4 %shard_map.172 = (f32[512,1024]{1,0:T(8,128)S(1)}, f32[512,1]{1,0:T(8,128)S(1)}, bf16[512,1024]{1,0:T(8,128)(2,1)S(1)}, bf16[512,1152]{1,0:T(8,128)(2,1)S(1)}, b...) custom-call(s32[5]{0:T(128)S(1)} %stack.32.at.refs_0_, ...), custom_call_target="tpu_custom_call" | custom-call | flops 8321499136 | bytes 20971520 | tf_op jit(solution)/shard_map/pallas_call | solution.py:291
  81.0 2.4 %collective-permute-start.14 = (bf16[512,256]{1,0:T(8,128)(2,1)}, bf16[512,256]{1,0:T(8,128)(2,1)}, u32[]{:S(2)}, u32[]{:S(2)}) collective-permute-start(bf16[512,256]{1,0:T(8,128)(2,1)} %get-tuple-element.94), channel_id=1, source_target_pairs={{0,2},{1,3},{2,0},{3,1},{4,6},{5,7},{6,4},{7,5},{8,10},{9,11},{10,... | collective-permute-start | bytes 786440 | tf_op jit(solution)/shard_map/ppermute | solution.py:770
  83.9 7.4 %shard_map.173 = (bf16[2,4,32,3456]{3,2,1,0:T(8,128)(2,1)}, bf16[2,4,32,3456]{3,2,1,0:T(8,128)(2,1)}, bf16[4,4,32,3456]{3,2,1,0:T(8,128)(2,1)S(1)}) custom-call(s32[5]{0:T(128)S(1)} %stack.32.at.refs_0_, bf16[512,1024]{1,0:T(8,128)(2,1)S(1)} %get-tuple-element.86.refs_1_, bf16[512,2304]{1,0:T(8,128)(2,1)S(1)} %get-tuple-element.87.refs_2_, ...), custom_call_target="tpu_custom_call" | custom-call | flops 3623878656 | bytes 14155776 | tf_op jit(solution)/shard_map/pallas_call | solution.py:359
  91.9 4.1 %collective-permute-done.14.d2 = bf16[512,256]{1,0:T(8,128)(2,1)} collective-permute-done((bf16[512,256]{1,0:T(8,128)(2,1)}, bf16[512,256]{1,0:T(8,128)(2,1)}, u32[]{:S(2)}, u32[]{:S(2)}) %collective-permute-start.14) | collective-permute-done | bytes 262176 | tf_op jit(solution)/shard_map/ppermute | solution.py:770
  100.3 2.1 shard_map.175
  103.2 2.6 %collective-permute-start.16 = (bf16[512,256]{1,0:T(8,128)(2,1)}, bf16[512,256]{1,0:T(8,128)(2,1)}, u32[]{:S(2)}, u32[]{:S(2)}) collective-permute-start(bf16[512,256]{1,0:T(8,128)(2,1)} %get-tuple-element.98), channel_id=1, source_target_pairs={{0,3},{1,0},{2,1},{3,2},{4,7},{5,4},{6,5},{7,6},{8,11},{9,8},{10,9... | collective-permute-start | bytes 786440 | tf_op jit(solution)/shard_map/ppermute | solution.py:33
  106.7 4.8 %shard_map.174 = bf16[4,4,32,3456]{3,2,1,0:T(8,128)(2,1)} custom-call(bf16[4,4,32,3456]{3,2,1,0:T(8,128)(2,1)S(1)} %get-tuple-element.89.keep, bf16[2,4,32,3456]{3,2,1,0:T(8,128)(2,1)} %collective-permute-done.11.got_a, bf16[2,4,32,3456]{3,2,1,0:T(8,128)(2,1)} %collective-permute-done.12.got_b), custom_call_target="tpu_custom_call" | custom-call | flops 2097152 | bytes 10616832 | tf_op jit(solution)/shard_map/pallas_call | solution.py:383
  111.5 6.6 %collective-permute-done.16.u1 = bf16[512,256]{1,0:T(8,128)(2,1)} collective-permute-done((bf16[512,256]{1,0:T(8,128)(2,1)}, bf16[512,256]{1,0:T(8,128)(2,1)}, u32[]{:S(2)}, u32[]{:S(2)}) %collective-permute-start.16) | collective-permute-done | bytes 262176 | tf_op jit(solution)/shard_map/ppermute | solution.py:33
  118.1 2.9 %collective-permute-done.17.u2 = bf16[512,256]{1,0:T(8,128)(2,1)} collective-permute-done((bf16[512,256]{1,0:T(8,128)(2,1)}, bf16[512,256]{1,0:T(8,128)(2,1)}, u32[]{:S(2)}, u32[]{:S(2)}) %collective-permute-start.17) | collective-permute-done | bytes 262176 | tf_op jit(solution)/shard_map/ppermute | solution.py:33
  121.0 5.3 %collective-permute-done.18.u3 = bf16[512,256]{1,0:T(8,128)(2,1)} collective-permute-done((bf16[512,256]{1,0:T(8,128)(2,1)}, bf16[512,256]{1,0:T(8,128)(2,1)}, u32[]{:S(2)}, u32[]{:S(2)}) %collective-permute-start.18) | collective-permute-done | bytes 262176 | tf_op jit(solution)/shard_map/ppermute | solution.py:33
  131.7 2.2 shard_map.176
  146.7 4.0 %shard_map.177 = (bf16[512,768]{1,0:T(8,128)(2,1)S(1)}, f32[512,256]{1,0:T(8,128)S(1)}, bf16[576,256]{1,0:T(8,128)(2,1)S(1)}, bf16[576,256]{1,0:T(8,128)(2,1)S(1...) custom-call(s32[5]{0:T(128)S(1)} %stack.32.at.refs_0_, bf16[512,256]{1,0:T(8,128)(2,1)S(1)} %copy-done.22, ...), custom_call_target="tpu_custom_call" | custom-call | flops 805306368 | bytes 6291456 | tf_op jit(solution)/shard_map/pallas_call | solution.py:666
  151.7 2.4 %collective-permute-start.23 = (bf16[576,256]{1,0:T(8,128)(2,1)S(1)}, bf16[576,256]{1,0:T(8,128)(2,1)S(1)}, u32[]{:S(2)}, u32[]{:S(2)}) collective-permute-start(bf16[576,256]{1,0:T(8,128)(2,1)S(1)} %get-tuple-element.116), channel_id=1, source_target_pairs={{0,2},{1,3},{2,0},{3,1},{4,6},{5,7},{6,4},{7,5},{8,10},{9,11},{10,... | collective-permute-start | bytes 884744 | tf_op jit(solution)/shard_map/ppermute | solution.py:793
  154.8 3.7 %shard_map.178 = (bf16[2,4,32,1024]{3,2,1,0:T(8,128)(2,1)}, bf16[2,4,32,1024]{3,2,1,0:T(8,128)(2,1)}, bf16[4,4,32,1024]{3,2,1,0:T(8,128)(2,1)S(1)}) custom-call(s32[5]{0:T(128)S(1)} %stack.32.at.refs_0_, bf16[512,1024]{1,0:T(8,128)(2,1)S(1)} %copy-done.47, bf16[512,768]{1,0:T(8,128)(2,1)S(1)} %get-tuple-element.109.refs_2_, ...), custom_call_target="tpu_custom_call" | custom-call | flops 1073741824 | bytes 4194304 | tf_op jit(solution)/shard_map/pallas_call | solution.py:359
  160.6 7.3 %collective-permute-done.23.d2 = bf16[576,256]{1,0:T(8,128)(2,1)S(1)} collective-permute-done((bf16[576,256]{1,0:T(8,128)(2,1)S(1)}, bf16[576,256]{1,0:T(8,128)(2,1)S(1)}, u32[]{:S(2)}, u32[]{:S(2)}) %collective-permute-start.23) | collective-permute-done | bytes 294944 | tf_op jit(solution)/shard_map/ppermute | solution.py:793
  171.6 2.3 %shard_map.180 = (f32[128,1024]{1,0:T(8,128)S(1)}, bf16[144,1024]{1,0:T(8,128)(2,1)}, bf16[144,1024]{1,0:T(8,128)(2,1)}, bf16[144,1024]{1,0:T(8,128)(2,1)S(1)}) custom-call(s32[5]{0:T(128)S(1)} %stack.32.at.refs_0_, bf16[4,4,32,1024]{3,2,1,0:T(8,128)(2,1)S(1)} %get-tuple-element.111.keep, bf16[2,4,32,1024]{3,2,1,0:T(8,128)(2,1)} %collective-permute-done.20.got_a, ...), custom_call_target="tpu_custom_call" | custom-call | flops 2097152 | bytes 4194304 | tf_op jit(solution)/shard_map/pallas_call | solution.py:423
  176.1 2.9 %collective-permute-start.27 = (bf16[144,1024]{1,0:T(8,128)(2,1)}, bf16[144,1024]{1,0:T(8,128)(2,1)S(1)}, u32[]{:S(2)}, u32[]{:S(2)}) collective-permute-start(bf16[144,1024]{1,0:T(8,128)(2,1)} %get-tuple-element.124), channel_id=1, source_target_pairs={{0,16},{4,20},{8,24},{12,28},{16,0},{20,4},{24,8},{28,12},{32,48},... | collective-permute-start | bytes 884744 | tf_op jit(solution)/shard_map/ppermute | solution.py:814
  180.4 5.0 %collective-permute-done.26.m1 = bf16[144,1024]{1,0:T(8,128)(2,1)S(1)} collective-permute-done((bf16[144,1024]{1,0:T(8,128)(2,1)}, bf16[144,1024]{1,0:T(8,128)(2,1)S(1)}, u32[]{:S(2)}, u32[]{:S(2)}) %collective-permute-start.26) | collective-permute-done | bytes 294944 | tf_op jit(solution)/shard_map/ppermute | solution.py:814
  185.4 7.4 %collective-permute-done.27.m2 = bf16[144,1024]{1,0:T(8,128)(2,1)S(1)} collective-permute-done((bf16[144,1024]{1,0:T(8,128)(2,1)}, bf16[144,1024]{1,0:T(8,128)(2,1)S(1)}, u32[]{:S(2)}, u32[]{:S(2)}) %collective-permute-start.27) | collective-permute-done | bytes 294944 | tf_op jit(solution)/shard_map/ppermute | solution.py:814
  194.6 2.1 collective-permute-start.29
  196.7 2.7 %collective-permute-start.30 = (bf16[48,1024]{1,0:T(8,128)(2,1)S(1)}, bf16[48,1024]{1,0:T(8,128)(2,1)S(1)}, u32[]{:S(2)}, u32[]{:S(2)}) collective-permute-start(bf16[48,1024]{1,0:T(8,128)(2,1)S(1)} %get-tuple-element.134), channel_id=1, source_target_pairs={{0,64},{4,68},{8,72},{12,76},{16,80},{20,84},{24,88},{28,92},{32,9... | collective-permute-start | bytes 294920 | tf_op jit(solution)/shard_map/ppermute | solution.py:820
  200.9 1.7 add_convert_fusion
  206.3 10.5 %reduce-scatter.8.cloned.1.call-done = bf16[1,32,3456]{2,1,0:T(8,128)(2,1)} async-done(((bf16[4,32,3456]{2,1,0:T(8,128)(2,1)}), bf16[1,32,3456]{2,1,0:T(8,128)(2,1)}) %reduce-scatter.8.cloned.1.call-update) | async-done | bytes 221200 | tf_op jit(solution)/shard_map/reduce_scatter | solution.py:688
  (205 shorter events, 72.6 us)
Async XLA Ops:
  7.2 51.8 %all-gather.2.cloned.1.call-start = ((), (), s32[]{:S(2)}) async-start(), calls=%async_computation.3 | async-start | bytes 1310720 | tf_op jit(solution)/shard_map/all_gather | solution.py:724
  7.2 15.4 %collective-permute-start = (bf16[512,256]{1,0:T(8,128)(2,1)}, bf16[512,256]{1,0:T(8,128)(2,1)S(1)}, u32[]{:S(2)}, u32[]{:S(2)}) collective-permute-start(bf16[512,256]{1,0:T(8,128)(2,1)} %rows_in.1), channel_id=1, source_target_pairs={{0,3},{1,0},{2,1},{3,2},{4,7},{5,4},{6,5},{7,6},{8,11},{9,8},{10,9... | collective-permute-start | bytes 786440 | tf_op jit(solution)/shard_map/ppermute | solution.py:33
  10.1 12.5 %collective-permute-start.1 = (bf16[512,256]{1,0:T(8,128)(2,1)}, bf16[512,256]{1,0:T(8,128)(2,1)S(1)}, u32[]{:S(2)}, u32[]{:S(2)}) collective-permute-start(bf16[512,256]{1,0:T(8,128)(2,1)} %rows_in.1), channel_id=1, source_target_pairs={{0,2},{1,3},{2,0},{3,1},{4,6},{5,7},{6,4},{7,5},{8,10},{9,11},{10,... | collective-permute-start | bytes 786440 | tf_op jit(solution)/shard_map/ppermute | solution.py:33
  10.9 15.9 %collective-permute-start.2 = (bf16[512,256]{1,0:T(8,128)(2,1)}, bf16[512,256]{1,0:T(8,128)(2,1)S(1)}, u32[]{:S(2)}, u32[]{:S(2)}) collective-permute-start(bf16[512,256]{1,0:T(8,128)(2,1)} %rows_in.1), channel_id=1, source_target_pairs={{0,1},{1,2},{2,3},{3,0},{4,5},{5,6},{6,7},{7,4},{8,9},{9,10},{10,1... | collective-permute-start | bytes 786440 | tf_op jit(solution)/shard_map/ppermute | solution.py:33
  12.8 25.7 %collective-permute-start.3 = (bf16[512,256]{1,0:T(8,128)(2,1)S(1)}, bf16[512,256]{1,0:T(8,128)(2,1)S(1)}, u32[]{:S(2)}, u32[]{:S(2)}) collective-permute-start(bf16[512,256]{1,0:T(8,128)(2,1)S(1)} %constant_dynamic-slice_fusion.2.p0), channel_id=1, source_target_pairs={{0,3},{1,0},{2,1},{3,2},{4,7},{5,4},{6,5},{7,6},{8,11},{9,8},{10,9... | collective-permute-start | bytes 786440 | tf_op jit(solution)/shard_map/ppermute | solution.py:33
  15.2 24.5 %collective-permute-start.4 = (bf16[512,256]{1,0:T(8,128)(2,1)S(1)}, bf16[512,256]{1,0:T(8,128)(2,1)S(1)}, u32[]{:S(2)}, u32[]{:S(2)}) collective-permute-start(bf16[512,256]{1,0:T(8,128)(2,1)S(1)} %constant_dynamic-slice_fusion.2.p0), channel_id=1, source_target_pairs={{0,2},{1,3},{2,0},{3,1},{4,6},{5,7},{6,4},{7,5},{8,10},{9,11},{10,... | collective-permute-start | bytes 786440 | tf_op jit(solution)/shard_map/ppermute | solution.py:33
  16.8 163.6 %reduce-scatter.4.cloned.1.call-start = ((), (), s32[]{:S(2)}) async-start(), calls=%async_computation.4 | async-start | bytes 1310720 | tf_op jit(solution)/shard_map/reduce_scatter | solution.py:772
  22.6 17.1 %collective-permute-start.5 = (bf16[512,256]{1,0:T(8,128)(2,1)S(1)}, bf16[512,256]{1,0:T(8,128)(2,1)S(1)}, u32[]{:S(2)}, u32[]{:S(2)}) collective-permute-start(bf16[512,256]{1,0:T(8,128)(2,1)S(1)} %constant_dynamic-slice_fusion.2.p0), channel_id=1, source_target_pairs={{0,1},{1,2},{2,3},{3,0},{4,5},{5,6},{6,7},{7,4},{8,9},{9,10},{10,1... | collective-permute-start | bytes 786440 | tf_op jit(solution)/shard_map/ppermute | solution.py:33
  37.6 12.9 %collective-permute-start.7 = (bf16[512,256]{1,0:T(8,128)(2,1)S(1)}, bf16[512,256]{1,0:T(8,128)(2,1)S(1)}, u32[]{:S(2)}, u32[]{:S(2)}) collective-permute-start(bf16[512,256]{1,0:T(8,128)(2,1)S(1)} %get-tuple-element.144.p0.refs_4_), channel_id=1, source_target_pairs={{0,3},{1,0},{2,1},{3,2},{4,7},{5,4},{6,5},{7,6},{8,11},{9,8},{10,9... | collective-permute-start | bytes 786440 | tf_op jit(solution)/shard_map/ppermute | solution.py:33
  37.7 12.9 %collective-permute-start.8 = (bf16[512,256]{1,0:T(8,128)(2,1)S(1)}, bf16[512,256]{1,0:T(8,128)(2,1)S(1)}, u32[]{:S(2)}, u32[]{:S(2)}) collective-permute-start(bf16[512,256]{1,0:T(8,128)(2,1)S(1)} %get-tuple-element.144.p0.refs_4_), channel_id=1, source_target_pairs={{0,2},{1,3},{2,0},{3,1},{4,6},{5,7},{6,4},{7,5},{8,10},{9,11},{10,... | collective-permute-start | bytes 786440 | tf_op jit(solution)/shard_map/ppermute | solution.py:33
  38.5 18.4 %collective-permute-start.9 = (bf16[512,256]{1,0:T(8,128)(2,1)S(1)}, bf16[512,256]{1,0:T(8,128)(2,1)}, u32[]{:S(2)}, u32[]{:S(2)}) collective-permute-start(bf16[512,256]{1,0:T(8,128)(2,1)S(1)} %get-tuple-element.144.p0.refs_4_), channel_id=1, source_target_pairs={{0,1},{1,2},{2,3},{3,0},{4,5},{5,6},{6,7},{7,4},{8,9},{9,10},{10,1... | collective-permute-start | bytes 786440 | tf_op jit(solution)/shard_map/ppermute | solution.py:33
  39.9 19.0 %collective-permute-start.10 = (bf16[512,1024]{1,0:T(8,128)(2,1)S(1)}, bf16[512,1024]{1,0:T(8,128)(2,1)}, u32[]{:S(2)}, u32[]{:S(2)}) collective-permute-start(bf16[512,1024]{1,0:T(8,128)(2,1)S(1)} %shard_map.171.half), channel_id=1, source_target_pairs={{0,4},{4,0},{8,12},{12,8},{16,20},{20,16},{24,28},{28,24},{32,36},... | collective-permute-start | bytes 3145736 | tf_op jit(solution)/shard_map/ppermute | solution.py:745
  80.2 11.7 %collective-permute-start.13 = (bf16[512,256]{1,0:T(8,128)(2,1)}, bf16[512,256]{1,0:T(8,128)(2,1)}, u32[]{:S(2)}, u32[]{:S(2)}) collective-permute-start(bf16[512,256]{1,0:T(8,128)(2,1)} %get-tuple-element.93), channel_id=1, source_target_pairs={{0,1},{1,2},{2,3},{3,0},{4,5},{5,6},{6,7},{7,4},{8,9},{9,10},{10,1... | collective-permute-start | bytes 786440 | tf_op jit(solution)/shard_map/ppermute | solution.py:770
  81.0 15.0 %collective-permute-start.14 = (bf16[512,256]{1,0:T(8,128)(2,1)}, bf16[512,256]{1,0:T(8,128)(2,1)}, u32[]{:S(2)}, u32[]{:S(2)}) collective-permute-start(bf16[512,256]{1,0:T(8,128)(2,1)} %get-tuple-element.94), channel_id=1, source_target_pairs={{0,2},{1,3},{2,0},{3,1},{4,6},{5,7},{6,4},{7,5},{8,10},{9,11},{10,... | collective-permute-start | bytes 786440 | tf_op jit(solution)/shard_map/ppermute | solution.py:770
  83.4 13.0 %collective-permute-start.15 = (bf16[512,256]{1,0:T(8,128)(2,1)}, bf16[512,256]{1,0:T(8,128)(2,1)}, u32[]{:S(2)}, u32[]{:S(2)}) collective-permute-start(bf16[512,256]{1,0:T(8,128)(2,1)} %get-tuple-element.95), channel_id=1, source_target_pairs={{0,3},{1,0},{2,1},{3,2},{4,7},{5,4},{6,5},{7,6},{8,11},{9,8},{10,9... | collective-permute-start | bytes 786440 | tf_op jit(solution)/shard_map/ppermute | solution.py:770
  91.3 15.4 %collective-permute-start.11 = (bf16[2,4,32,3456]{3,2,1,0:T(8,128)(2,1)}, bf16[2,4,32,3456]{3,2,1,0:T(8,128)(2,1)}, u32[]{:S(2)}, u32[]{:S(2)}) collective-permute-start(bf16[2,4,32,3456]{3,2,1,0:T(8,128)(2,1)} %get-tuple-element.90), channel_id=1, source_target_pairs={{0,4},{4,0},{8,12},{12,8},{16,20},{20,16},{24,28},{28,24},{32,36},... | collective-permute-start | bytes 5308424 | tf_op jit(solution)/shard_map/ppermute | solution.py:372
  91.4 15.3 %collective-permute-start.12 = (bf16[2,4,32,3456]{3,2,1,0:T(8,128)(2,1)}, bf16[2,4,32,3456]{3,2,1,0:T(8,128)(2,1)}, u32[]{:S(2)}, u32[]{:S(2)}) collective-permute-start(bf16[2,4,32,3456]{3,2,1,0:T(8,128)(2,1)} %get-tuple-element.91), channel_id=1, source_target_pairs={{0,4},{4,0},{8,12},{12,8},{16,20},{20,16},{24,28},{28,24},{32,36},... | collective-permute-start | bytes 5308424 | tf_op jit(solution)/shard_map/ppermute | solution.py:372
  91.9 100.9 %reduce-scatter.6.cloned.1.call-start = ((), (), s32[]{:S(2)}) async-start(), calls=%async_computation.5 | async-start | bytes 4423680 | tf_op jit(solution)/shard_map/reduce_scatter | solution.py:688
  103.2 14.9 %collective-permute-start.16 = (bf16[512,256]{1,0:T(8,128)(2,1)}, bf16[512,256]{1,0:T(8,128)(2,1)}, u32[]{:S(2)}, u32[]{:S(2)}) collective-permute-start(bf16[512,256]{1,0:T(8,128)(2,1)} %get-tuple-element.98), channel_id=1, source_target_pairs={{0,3},{1,0},{2,1},{3,2},{4,7},{5,4},{6,5},{7,6},{8,11},{9,8},{10,9... | collective-permute-start | bytes 786440 | tf_op jit(solution)/shard_map/ppermute | solution.py:33
  105.8 15.2 %collective-permute-start.17 = (bf16[512,256]{1,0:T(8,128)(2,1)}, bf16[512,256]{1,0:T(8,128)(2,1)}, u32[]{:S(2)}, u32[]{:S(2)}) collective-permute-start(bf16[512,256]{1,0:T(8,128)(2,1)} %get-tuple-element.98), channel_id=1, source_target_pairs={{0,2},{1,3},{2,0},{3,1},{4,6},{5,7},{6,4},{7,5},{8,10},{9,11},{10,... | collective-permute-start | bytes 786440 | tf_op jit(solution)/shard_map/ppermute | solution.py:33
  105.9 20.3 %collective-permute-start.18 = (bf16[512,256]{1,0:T(8,128)(2,1)}, bf16[512,256]{1,0:T(8,128)(2,1)}, u32[]{:S(2)}, u32[]{:S(2)}) collective-permute-start(bf16[512,256]{1,0:T(8,128)(2,1)} %get-tuple-element.98), channel_id=1, source_target_pairs={{0,1},{1,2},{2,3},{3,0},{4,5},{5,6},{6,7},{7,4},{8,9},{9,10},{10,1... | collective-permute-start | bytes 786440 | tf_op jit(solution)/shard_map/ppermute | solution.py:33
  126.3 90.5 %reduce-scatter.8.cloned.1.call-start = ((), (), s32[]{:S(2)}) async-start(), calls=%async_computation.6 | async-start | bytes 1105920 | tf_op jit(solution)/shard_map/reduce_scatter | solution.py:688
  150.7 9.8 %collective-permute-start.22 = (bf16[576,256]{1,0:T(8,128)(2,1)S(1)}, bf16[576,256]{1,0:T(8,128)(2,1)S(1)}, u32[]{:S(2)}, u32[]{:S(2)}) collective-permute-start(bf16[576,256]{1,0:T(8,128)(2,1)S(1)} %get-tuple-element.115), channel_id=1, source_target_pairs={{0,1},{1,2},{2,3},{3,0},{4,5},{5,6},{6,7},{7,4},{8,9},{9,10},{10,1... | collective-permute-start | bytes 884744 | tf_op jit(solution)/shard_map/ppermute | solution.py:793
  151.7 16.1 %collective-permute-start.23 = (bf16[576,256]{1,0:T(8,128)(2,1)S(1)}, bf16[576,256]{1,0:T(8,128)(2,1)S(1)}, u32[]{:S(2)}, u32[]{:S(2)}) collective-permute-start(bf16[576,256]{1,0:T(8,128)(2,1)S(1)} %get-tuple-element.116), channel_id=1, source_target_pairs={{0,2},{1,3},{2,0},{3,1},{4,6},{5,7},{6,4},{7,5},{8,10},{9,11},{10,... | collective-permute-start | bytes 884744 | tf_op jit(solution)/shard_map/ppermute | solution.py:793
  154.1 14.0 %collective-permute-start.24 = (bf16[576,256]{1,0:T(8,128)(2,1)S(1)}, bf16[576,256]{1,0:T(8,128)(2,1)S(1)}, u32[]{:S(2)}, u32[]{:S(2)}) collective-permute-start(bf16[576,256]{1,0:T(8,128)(2,1)S(1)} %get-tuple-element.117), channel_id=1, source_target_pairs={{0,3},{1,0},{2,1},{3,2},{4,7},{5,4},{6,5},{7,6},{8,11},{9,8},{10,9... | collective-permute-start | bytes 884744 | tf_op jit(solution)/shard_map/ppermute | solution.py:793
  158.5 13.1 %collective-permute-start.20 = (bf16[2,4,32,1024]{3,2,1,0:T(8,128)(2,1)}, bf16[2,4,32,1024]{3,2,1,0:T(8,128)(2,1)}, u32[]{:S(2)}, u32[]{:S(2)}) collective-permute-start(bf16[2,4,32,1024]{3,2,1,0:T(8,128)(2,1)} %get-tuple-element.112), channel_id=1, source_target_pairs={{0,4},{4,0},{8,12},{12,8},{16,20},{20,16},{24,28},{28,24},{32,36},... | collective-permute-start | bytes 1572872 | tf_op jit(solution)/shard_map/ppermute | solution.py:372
  159.9 11.7 %collective-permute-start.21 = (bf16[2,4,32,1024]{3,2,1,0:T(8,128)(2,1)}, bf16[2,4,32,1024]{3,2,1,0:T(8,128)(2,1)}, u32[]{:S(2)}, u32[]{:S(2)}) collective-permute-start(bf16[2,4,32,1024]{3,2,1,0:T(8,128)(2,1)} %get-tuple-element.113), channel_id=1, source_target_pairs={{0,4},{4,0},{8,12},{12,8},{16,20},{20,16},{24,28},{28,24},{32,36},... | collective-permute-start | bytes 1572872 | tf_op jit(solution)/shard_map/ppermute | solution.py:372
  174.7 10.7 %collective-permute-start.26 = (bf16[144,1024]{1,0:T(8,128)(2,1)}, bf16[144,1024]{1,0:T(8,128)(2,1)S(1)}, u32[]{:S(2)}, u32[]{:S(2)}) collective-permute-start(bf16[144,1024]{1,0:T(8,128)(2,1)} %get-tuple-element.123), channel_id=1, source_target_pairs={{0,8},{4,12},{8,16},{12,20},{16,24},{20,28},{24,0},{28,4},{32,40},... | collective-permute-start | bytes 884744 | tf_op jit(solution)/shard_map/ppermute | solution.py:814
  176.1 16.7 %collective-permute-start.27 = (bf16[144,1024]{1,0:T(8,128)(2,1)}, bf16[144,1024]{1,0:T(8,128)(2,1)S(1)}, u32[]{:S(2)}, u32[]{:S(2)}) collective-permute-start(bf16[144,1024]{1,0:T(8,128)(2,1)} %get-tuple-element.124), channel_id=1, source_target_pairs={{0,16},{4,20},{8,24},{12,28},{16,0},{20,4},{24,8},{28,12},{32,48},... | collective-permute-start | bytes 884744 | tf_op jit(solution)/shard_map/ppermute | solution.py:814
  179.0 13.8 %collective-permute-start.28 = (bf16[144,1024]{1,0:T(8,128)(2,1)S(1)}, bf16[144,1024]{1,0:T(8,128)(2,1)S(1)}, u32[]{:S(2)}, u32[]{:S(2)}) collective-permute-start(bf16[144,1024]{1,0:T(8,128)(2,1)S(1)} %get-tuple-element.125), channel_id=1, source_target_pairs={{0,24},{4,28},{8,0},{12,4},{16,8},{20,12},{24,16},{28,20},{32,56},... | collective-permute-start | bytes 884744 | tf_op jit(solution)/shard_map/ppermute | solution.py:814
  194.6 8.0 %collective-permute-start.29 = (bf16[48,1024]{1,0:T(8,128)(2,1)S(1)}, bf16[48,1024]{1,0:T(8,128)(2,1)S(1)}, u32[]{:S(2)}, u32[]{:S(2)}) collective-permute-start(bf16[48,1024]{1,0:T(8,128)(2,1)S(1)} %get-tuple-element.133), channel_id=1, source_target_pairs={{0,32},{4,36},{8,40},{12,44},{16,48},{20,52},{24,56},{28,60},{32,6... | collective-permute-start | bytes 294920 | tf_op jit(solution)/shard_map/ppermute | solution.py:820
  196.7 6.5 %collective-permute-start.30 = (bf16[48,1024]{1,0:T(8,128)(2,1)S(1)}, bf16[48,1024]{1,0:T(8,128)(2,1)S(1)}, u32[]{:S(2)}, u32[]{:S(2)}) collective-permute-start(bf16[48,1024]{1,0:T(8,128)(2,1)S(1)} %get-tuple-element.134), channel_id=1, source_target_pairs={{0,64},{4,68},{8,72},{12,76},{16,80},{20,84},{24,88},{28,92},{32,9... | collective-permute-start | bytes 294920 | tf_op jit(solution)/shard_map/ppermute | solution.py:820
  (64 other events, 366.1 us)
Sparse Core Ops, SparseCore 0:
  16.9 38.1 all-gather.1
  92.0 35.0 reduce-scatter.3
  129.7 41.7 reduce-scatter.5
  192.9 23.7 reduce-scatter.7

commit v3 on v2

--- a/solution.py
+++ b/solution.py
@@ -173,7 +173,7 @@
             pltpu.VMEM((3, features, width), BF16),
             pltpu.SemaphoreType.DMA((CH,)),
         ],
-        compiler_params=params(16),
+        compiler_params=params(56),
         cost_estimate=cost(rows * features * 3 * width, 6 * 2**20),
     )(at, *pieces, gain[None], weight)
 
@@ -191,7 +191,7 @@
         out_shape=shape((rows, CH * width), BF16),
         in_specs=[vmem()] * CH,
         out_specs=vmem(),
-        compiler_params=params(8),
+        compiler_params=params(56),
         cost_estimate=cost(weight, 2**21),
     )(*pieces)
 
@@ -206,7 +206,7 @@
     planes,
     down,
     cotangent,
-    h, rms, normed, act, d_gate_up, d_own, d1, d2, d3, down_out,
+    h, rms, normed, act, d_gate_up, d_own, d1, d2, d3, f0, f1, f2, f3,
     w_out, w_in, w_down, g_rows, acc, down_acc, sem,
 ):
     x, core = at[0], at[1]
@@ -279,8 +279,8 @@
     d1[...] = acc[1].astype(BF16)
     d2[...] = acc[2].astype(BF16)
     d3[...] = acc[3].astype(BF16)
-    for j in range(CH):
-        down_out[:, j * width : (j + 1) * width] = down_acc[j].astype(BF16)
+    for j, out in enumerate((f0, f1, f2, f3)):
+        out[...] = down_acc[lax.rem(x + j, CH)].astype(BF16)
 
 
 def ffn(at, pieces, mixed, gain, half, other, planes, down, cotangent):
@@ -297,13 +297,10 @@
             shape((rows, units), BF16),
             shape((rows, 2 * units), BF16),
             shape((rows, width), F32),
-            block,
-            block,
-            block,
-            shape((rows, features), BF16),
-        ),
+        )
+        + (block,) * 7,
         in_specs=[smem()] + [vmem()] * 6 + [anywhere()] * 5,
-        out_specs=(vmem(),) * 10,
+        out_specs=(vmem(),) * 13,
         scratch_shapes=[
             pltpu.VMEM((2, features // 2, features), BF16),
             pltpu.VMEM((2, features, units), BF16),
@@ -313,7 +310,7 @@
             pltpu.VMEM((CH, rows, width), F32),
             pltpu.SemaphoreType.DMA((8,)),
         ],
-        compiler_params=params(34),
+        compiler_params=params(56),
         cost_estimate=cost(rows * features * (features + 6 * units), 20 * 2**20),
     )(at, *pieces, mixed, gain[None], half, other, planes, down, cotangent)
 
@@ -363,7 +360,7 @@
         in_specs=[smem()] + [vmem()] * 4,
         out_specs=(half_spec, half_spec, spec),
         scratch_shapes=[pltpu.VMEM((features // 4, columns), F32)],
-        compiler_params=params(22),
+        compiler_params=params(56),
         cost_estimate=cost(tokens * features * columns, 4 * features * columns),
     )(at, a_left, a_right, b_left, b_right)
 
@@ -386,7 +383,7 @@
         out_shape=shape(keep.shape, BF16),
         in_specs=[spec, half, half],
         out_specs=spec,
-        compiler_params=params(16),
+        compiler_params=params(56),
         cost_estimate=cost(2**20, 6 * keep.size),
     )(keep, *got)
 
@@ -425,7 +422,7 @@
         out_shape=(shape((rows, columns), F32), message, message, message),
         in_specs=[smem()] + [vmem()] * 4,
         out_specs=(vmem(),) * 4,
-        compiler_params=params(16),
+        compiler_params=params(56),
         cost_estimate=cost(2**20, 2**22),
     )(at, keep, *got, small)
 
@@ -465,7 +462,7 @@
         in_specs=[smem()] + [vmem()] * 5,
         out_specs=(vmem(),) * 5,
         scratch_shapes=[pltpu.VMEM((rows, columns), F32)],
-        compiler_params=params(16),
+        compiler_params=params(56),
         cost_estimate=cost(2**20, 2**21),
     )(at, own, *messages, small)
 
@@ -496,7 +493,7 @@
         ),
         in_specs=[vmem()] * 5,
         out_specs=(vmem(),) * 3,
-        compiler_params=params(16),
+        compiler_params=params(56),
         cost_estimate=cost(2**20, 2**20),
     )(own, *messages, small)
 
@@ -530,7 +527,7 @@
         out_shape=(shape((rows, width), BF16), shape((1, width), F32)),
         in_specs=[vmem()] * 9,
         out_specs=(vmem(),) * 2,
-        compiler_params=params(16),
+        compiler_params=params(56),
         cost_estimate=cost(2**32, 2**21),
     )(d_own, *received, inner, d_hidden, rows_in, rms, gain[None])
 
@@ -557,7 +554,7 @@
         ),
         in_specs=[vmem()] * 8,
         out_specs=(vmem(),) * 3,
-        compiler_params=params(10),
+        compiler_params=params(56),
         cost_estimate=cost(LONG, 2**21),
     )(d_own, *received, h, rms, gain[None], cotangent)
 
@@ -597,7 +594,7 @@
         out_shape=(shape((rows, CH * width), BF16), wide, wide, shape((rows, width), BF16)),
         in_specs=[smem()] + [vmem()] * 10,
         out_specs=(vmem(),) * 4,
-        compiler_params=params(16),
+        compiler_params=params(56),
         cost_estimate=cost(rows * CH * width * width, 6 * 2**20),
     )(at, *pieces, h, rms, cotangent, weight, c_gate, conv_out)
 
@@ -679,7 +676,7 @@
             pltpu.VMEM((3, features, width), BF16),
             pltpu.SemaphoreType.DMA((CH,)),
         ],
-        compiler_params=params(18),
+        compiler_params=params(56),
         cost_estimate=cost(rows * features * 3 * width, 6 * 2**20),
     )(at, *pieces, d_conv, following, taps, value, b_gate, d_cgate, gain[None], weight)
 
@@ -753,7 +750,7 @@
         d_one,
         d_two,
         d_three,
-        down_terms,
+        *down_parts,
     ) = ffn(
         at,
         pieces,
@@ -769,7 +766,6 @@
     received = [
         lax.ppermute(d, "ch", ch_pairs(j)) for j, d in ((1, d_one), (2, d_two), (3, d_three))
     ]
-    down = lax.psum_scatter(down_terms, "ch", scatter_dimension=1, tiled=True)
     *gives, keep = pair_products(at, normed_two, d_gate_up, grad_full, act_rows, True, False)
     got = swap_cores(gives)
 
@@ -809,12 +805,18 @@
         [grad_conv, grad_gain_one, grad_gain_two, jnp.zeros((3, width), F32)], axis=0
     )
     small = small + lax.ppermute(small, "seq", seq_pairs(0, 0, 1))
+    small, ffn_sum, *got = tie(small, ffn_sum, *got)
     own, *messages = send_z(at, keep, got, small)
+    down_parts, messages = lax.optimization_barrier((down_parts, messages))
+    downs = [lax.ppermute(down_parts[j], "ch", ch_pairs(j)) for j in (1, 2, 3)]
     messages = [
         lax.ppermute(m, "seq", seq_pairs(0, j, 0)) for j, m in ((1, messages[0]), (2, messages[1]), (3, messages[2]))
     ]
-    down, ffn_sum, *messages = tie(down, ffn_sum, *messages)
-    block_output = (hidden_own + down.astype(F32)).astype(BF16)
+    downs, messages = lax.optimization_barrier((downs, messages))
+    block_output = hidden_own + down_parts[0].astype(F32)
+    for down in downs:
+        block_output = block_output + down.astype(F32)
+    block_output = block_output.astype(BF16)
     own, *messages, small = turn(at, own, messages, small)
     messages = [
         lax.ppermute(m, "seq", seq_pairs(j, 0, 0)) for j, m in ((1, messages[0]), (2, messages[1]), (3, messages[2]))

time: 227 us -> 215 us (0.947)
  waiting for transfers between devices: 69.5 us -> 39.1 us
  Pallas kernels: 48.2 us -> 73.2 us
  local copies, waits for them, and re-layouts: 45 us -> 29.8 us
  starting transfers between devices: 41.6 us -> 47.7 us
  other arithmetic: 6.7 us -> 9.44 us
    unnamed x120 -> x92, local copies, waits for them, and re-layouts: 32.4 us -> 11 us
    ppermute x12, waiting for transfers between devices: 29.4 us -> 16.2 us  [gather_ch(): lax.ppermute(block, 'ch', ch_pairs(-j))]
    ppermute x3, waiting for transfers between devices: 12.4 us -> 0.01 us  [shards(): lax.ppermute(m, 'seq', seq_pairs(0, j, 0))]
    ppermute x0 -> x3, waiting for transfers between devices: none -> 10.7 us  [shards(): downs = [lax.ppermute(down_parts[j], 'ch', ch_pairs(j)) for j in (1, 2, 3)]]
    reduce_scatter x2, waiting for transfers between devices: 10.5 us -> 0.4 us  [scatter_groups(): lax.psum_scatter(array, 'seq', scatter_dimension=0, axis_index_groups=gro...]
    ppermute x6, waiting for transfers between devices: 12.6 us -> 7.52 us  [shards(): lax.ppermute(d, 'ch', ch_pairs(j))]
    ppermute x0 -> x3, starting transfers between devices: none -> 4.8 us  [shards(): downs = [lax.ppermute(down_parts[j], 'ch', ch_pairs(j)) for j in (1, 2, 3)]]
    pallas_call x2, Pallas kernels: 11.1 us -> 14.9 us  [pair_products(): pl.pallas_call(body, grid=(4,), out_shape=(half, half, out), in_specs=[sm...]
  transfers between devices with their start and end apart: 36 -> 38, of which waited for: 20 -> 16; matrix products, arithmetic and copies ran while one was open for 7% -> 11% of each run, Pallas kernels for 15% -> 25%
where the time goes in v3:
time: 215 us; the launch traced here: 214 us
  Pallas kernels  73.2 us (34%)
  starting transfers between devices  47.7 us (22%)
  waiting for transfers between devices  39.1 us (18%)
  local copies, waits for them, and re-layouts  29.8 us (14%)
  between operations  14.8 us (7%)
  other arithmetic  9.44 us (4%)
    pallas_call x1, Pallas kernels, ffn(): pl.pallas_call(ffn_kernel, out_shape=(shape((rows, features), F32), shape...  19.2 us
    ppermute x12, waiting for transfers between devices, gather_ch(): lax.ppermute(block, 'ch', ch_pairs(-j))  16.2 us
    pallas_call x2, Pallas kernels, pair_products(): pl.pallas_call(body, grid=(4,), out_shape=(half, half, out), in_specs=[sm...  14.9 us
    ppermute x12, starting transfers between devices, gather_ch(): lax.ppermute(block, 'ch', ch_pairs(-j))  14.3 us
    unnamed x92, local copies, waits for them, and re-layouts  11 us
    ppermute x3, waiting for transfers between devices, shards(): downs = [lax.ppermute(down_parts[j], 'ch', ch_pairs(j)) for j in (1, 2, 3)]  10.7 us
    ppermute x6, starting transfers between devices, shards(): lax.ppermute(d, 'ch', ch_pairs(j))  7.77 us
    ppermute x6, waiting for transfers between devices, shards(): lax.ppermute(d, 'ch', ch_pairs(j))  7.52 us
  transfers between devices with their start and end apart: 38, of which 16 were waited for; matrix products, arithmetic and copies ran while one was open for 11% of the time, Pallas kernels for 25%

profile of v3, /device:TPU:0, one launch (start us, length us, event | category | flops | bytes accessed | tf_op | source)
XLA Modules:
  0.0 214.0 jit_solution(12122191421928032985)
XLA Ops:
  7.2 2.9 %collective-permute-start = (bf16[512,256]{1,0:T(8,128)(2,1)}, bf16[512,256]{1,0:T(8,128)(2,1)S(1)}, u32[]{:S(2)}, u32[]{:S(2)}) collective-permute-start(bf16[512,256]{1,0:T(8,128)(2,1)} %rows_in.1), channel_id=1, source_target_pairs={{0,3},{1,0},{2,1},{3,2},{4,7},{5,4},{6,5},{7,6},{8,11},{9,8},{10,9... | collective-permute-start | bytes 786440 | tf_op jit(solution)/shard_map/ppermute | solution.py:33
  12.8 2.4 %collective-permute-start.3 = (bf16[512,256]{1,0:T(8,128)(2,1)S(1)}, bf16[512,256]{1,0:T(8,128)(2,1)S(1)}, u32[]{:S(2)}, u32[]{:S(2)}) collective-permute-start(bf16[512,256]{1,0:T(8,128)(2,1)S(1)} %constant_dynamic-slice_fusion.2.p0), channel_id=1, source_target_pairs={{0,3},{1,0},{2,1},{3,2},{4,7},{5,4},{6,5},{7,6},{8,11},{9,8},{10,9... | collective-permute-start | bytes 786440 | tf_op jit(solution)/shard_map/ppermute | solution.py:33
  18.0 2.0 convert_reduce_fusion
  22.8 4.0 %collective-permute-done.2.p3.x3 = bf16[512,256]{1,0:T(8,128)(2,1)S(1)} collective-permute-done((bf16[512,256]{1,0:T(8,128)(2,1)}, bf16[512,256]{1,0:T(8,128)(2,1)S(1)}, u32[]{:S(2)}, u32[]{:S(2)}) %collective-permute-start.2) | collective-permute-done | bytes 262176 | tf_op jit(solution)/shard_map/ppermute | solution.py:33
  27.5 4.8 %shard_map.169 = (bf16[512,1024]{1,0:T(8,128)(2,1)}, f32[512,1]{1,0:T(8,128)}, f32[512,256]{1,0:T(8,128)}, f32[512,256]{1,0:T(8,128)}, f32[512,256]{1,0:T(8,128)}, /*index=5*/bf16[512,256]{1,0:T(8,128)(2,1)}) custom-call(s32[5]{0:T(128)} %stack.32.at.refs_0_, bf16[512,256]{1,0:T(8,128)(2,1)} %rows_in.1, bf16[512,256]{1,0:T(8,128)(2,1)} %copy-done.11, ...), custom_call_target="tpu_custom_call" | custom-call | flops 805306368 | bytes 6291456 | tf_op jit(solution)/shard_map/pallas_call | solution.py:160
  37.3 2.1 multiply_convert_fusion
  43.0 2.3 %shard_map.171.half = bf16[512,1024]{1,0:T(8,128)(2,1)} custom-call(bf16[512,256]{1,0:T(8,128)(2,1)} %copy-done.5, bf16[512,256]{1,0:T(8,128)(2,1)} %copy-done.19, bf16[512,256]{1,0:T(8,128)(2,1)} %copy-done.20, bf16[512,256]{1,0:T(8,128)(2,1)} %copy-done.21), custom_call_target="tpu_custom_call" | custom-call | flops 2097152 | bytes 2097152 | tf_op jit(solution)/shard_map/pallas_call | solution.py:189
  47.6 5.1 %copy.21 = bf16[1024,2,1152]{2,0,1:T(8,128)(2,1)} copy(bf16[1024,2,1152]{2,1,0:T(2,128)(2,1)} %param.17) | data formatting | bytes 9437184 | tf_op jit(solution)/shard_map/optimization_barrier | solution.py:72
  52.7 5.3 %collective-permute-done.9.p3 = bf16[512,256]{1,0:T(8,128)(2,1)S(1)} collective-permute-done((bf16[512,256]{1,0:T(8,128)(2,1)S(1)}, bf16[512,256]{1,0:T(8,128)(2,1)S(1)}, u32[]{:S(2)}, u32[]{:S(2)}) %collective-permute-start.9) | collective-permute-done | bytes 262176 | tf_op jit(solution)/shard_map/ppermute | solution.py:33
  58.7 2.3 %shard_map.170.mixed = bf16[512,1024]{1,0:T(8,128)(2,1)} custom-call(bf16[512,256]{1,0:T(8,128)(2,1)} %copy-done.15, bf16[512,256]{1,0:T(8,128)(2,1)} %copy-done.40, bf16[512,256]{1,0:T(8,128)(2,1)} %copy-done.41, bf16[512,256]{1,0:T(8,128)(2,1)} %copy-done.43), custom_call_target="tpu_custom_call" | custom-call | flops 8589934592 | bytes 2097152 | tf_op jit(solution)/shard_map/pallas_call | solution.py:189
  62.0 19.2 %shard_map.172 = (f32[512,1024]{1,0:T(8,128)}, f32[512,1]{1,0:T(8,128)}, bf16[512,1024]{1,0:T(8,128)(2,1)}, bf16[512,1152]{1,0:T(8,128)(2,1)}, bf16[512,2304]{1,...) custom-call(s32[5]{0:T(128)} %stack.32.at.refs_0_, ...), custom_call_target="tpu_custom_call" | custom-call | flops 8321499136 | bytes 20971520 | tf_op jit(solution)/shard_map/pallas_call | solution.py:291
  83.5 2.3 %collective-permute-start.14 = (bf16[512,256]{1,0:T(8,128)(2,1)}, bf16[512,256]{1,0:T(8,128)(2,1)S(1)}, u32[]{:S(2)}, u32[]{:S(2)}) collective-permute-start(bf16[512,256]{1,0:T(8,128)(2,1)} %get-tuple-element.113), channel_id=1, source_target_pairs={{0,2},{1,3},{2,0},{3,1},{4,6},{5,7},{6,4},{7,5},{8,10},{9,11},{10,... | collective-permute-start | bytes 786440 | tf_op jit(solution)/shard_map/ppermute | solution.py:767
  87.2 9.7 %shard_map.173 = (bf16[2,4,32,3456]{3,2,1,0:T(8,128)(2,1)}, bf16[2,4,32,3456]{3,2,1,0:T(8,128)(2,1)}, bf16[4,4,32,3456]{3,2,1,0:T(8,128)(2,1)}) custom-call(s32[5]{0:T(128)} %stack.32.at.refs_0_, bf16[512,1024]{1,0:T(8,128)(2,1)} %get-tuple-element.105.refs_1_, bf16[512,2304]{1,0:T(8,128)(2,1)} %get-tuple-element.106.refs_2_, ...), custom_call_target="tpu_custom_call" | custom-call | flops 3623878656 | bytes 14155776 | tf_op jit(solution)/shard_map/pallas_call | solution.py:356
  99.8 2.7 %shard_map.175 = (f32[512,256]{1,0:T(8,128)}, bf16[512,256]{1,0:T(8,128)(2,1)}, f32[1,256]{1,0:T(1,128)}) custom-call(f32[512,256]{1,0:T(8,128)} %get-tuple-element.111.d_own, bf16[512,256]{1,0:T(8,128)(2,1)} %copy-done.42, bf16[512,256]{1,0:T(8,128)(2,1)} %copy-done.44, bf16[512,256]{1,0:T(8,128)(2,1)} %copy-done.45, f32[512,256]{1,0:T(8,128)} %slice.53.h, ...), custom_call_target="tpu_custom_call" | custom-call | flops 137438953472 | bytes 2097152 | tf_op jit(solution)/shard_map/pallas_call | solution.py:548
  102.5 2.6 %collective-permute-start.16 = (bf16[512,256]{1,0:T(8,128)(2,1)}, bf16[512,256]{1,0:T(8,128)(2,1)S(1)}, u32[]{:S(2)}, u32[]{:S(2)}) collective-permute-start(bf16[512,256]{1,0:T(8,128)(2,1)} %get-tuple-element.117), channel_id=1, source_target_pairs={{0,3},{1,0},{2,1},{3,2},{4,7},{5,4},{6,5},{7,6},{8,11},{9,8},{10,9... | collective-permute-start | bytes 786440 | tf_op jit(solution)/shard_map/ppermute | solution.py:33
  107.8 5.5 %shard_map.174 = bf16[4,4,32,3456]{3,2,1,0:T(8,128)(2,1)} custom-call(bf16[4,4,32,3456]{3,2,1,0:T(8,128)(2,1)} %get-tuple-element.108.keep, bf16[2,4,32,3456]{3,2,1,0:T(8,128)(2,1)} %copy-done.3, bf16[2,4,32,3456]{3,2,1,0:T(8,128)(2,1)} %copy-done.4), custom_call_target="tpu_custom_call" | custom-call | flops 2097152 | bytes 10616832 | tf_op jit(solution)/shard_map/pallas_call | solution.py:380
  113.3 3.6 %collective-permute-done.16.u1 = bf16[512,256]{1,0:T(8,128)(2,1)S(1)} collective-permute-done((bf16[512,256]{1,0:T(8,128)(2,1)}, bf16[512,256]{1,0:T(8,128)(2,1)S(1)}, u32[]{:S(2)}, u32[]{:S(2)}) %collective-permute-start.16) | collective-permute-done | bytes 262176 | tf_op jit(solution)/shard_map/ppermute | solution.py:33
  116.9 3.3 %collective-permute-done.18.u3 = bf16[512,256]{1,0:T(8,128)(2,1)S(1)} collective-permute-done((bf16[512,256]{1,0:T(8,128)(2,1)}, bf16[512,256]{1,0:T(8,128)(2,1)S(1)}, u32[]{:S(2)}, u32[]{:S(2)}) %collective-permute-start.18) | collective-permute-done | bytes 262176 | tf_op jit(solution)/shard_map/ppermute | solution.py:33
  120.9 5.0 %shard_map.176 = (bf16[512,1024]{1,0:T(8,128)(2,1)}, f32[512,256]{1,0:T(8,128)}, f32[512,256]{1,0:T(8,128)}, bf16[512,256]{1,0:T(8,128)(2,1)}) custom-call(s32[5]{0:T(128)} %stack.32.at.refs_0_, f32[512,256]{1,0:T(8,128)} %get-tuple-element.118.u_own, bf16[512,256]{1,0:T(8,128)(2,1)} %copy-done.16, bf16[512,256]{1,0:T(8,128)(2,1)} %copy-done.17, ...), custom_call_target="tpu_custom_call" | custom-call | flops 268435456 | bytes 6291456 | tf_op jit(solution)/shard_map/pallas_call | solution.py:592
  130.2 6.7 %shard_map.177 = (bf16[512,768]{1,0:T(8,128)(2,1)}, f32[512,256]{1,0:T(8,128)}, bf16[576,256]{1,0:T(8,128)(2,1)}, bf16[576,256]{1,0:T(8,128)(2,1)}, bf16[576,256]{1,0:T(8,128)(2,1)}, /*index=5*/f32[16,512]{1,0:T(8,128)}) custom-call(s32[5]{0:T(128)} %stack.32.at.refs_0_, bf16[512,256]{1,0:T(8,128)(2,1)} %rows_in.1, bf16[512,256]{1,0:T(8,128)(2,1)} %copy-done.11, ...), custom_call_target="tpu_custom_call" | custom-call | flops 805306368 | bytes 6291456 | tf_op jit(solution)/shard_map/pallas_call | solution.py:663
  136.9 2.9 %collective-permute-start.21 = (bf16[576,256]{1,0:T(8,128)(2,1)}, bf16[576,256]{1,0:T(8,128)(2,1)S(1)}, u32[]{:S(2)}, u32[]{:S(2)}) collective-permute-start(bf16[576,256]{1,0:T(8,128)(2,1)} %get-tuple-element.131), channel_id=1, source_target_pairs={{0,2},{1,3},{2,0},{3,1},{4,6},{5,7},{6,4},{7,5},{8,10},{9,11},{10,... | collective-permute-start | bytes 884744 | tf_op jit(solution)/shard_map/ppermute | solution.py:789
  141.4 5.2 %shard_map.178 = (bf16[2,4,32,1024]{3,2,1,0:T(8,128)(2,1)}, bf16[2,4,32,1024]{3,2,1,0:T(8,128)(2,1)}, bf16[4,4,32,1024]{3,2,1,0:T(8,128)(2,1)}) custom-call(s32[5]{0:T(128)} %stack.32.at.refs_0_, bf16[512,1024]{1,0:T(8,128)(2,1)} %get-tuple-element.104.refs_1_, bf16[512,768]{1,0:T(8,128)(2,1)} %get-tuple-element.126.refs_2_, ...), custom_call_target="tpu_custom_call" | custom-call | flops 1073741824 | bytes 4194304 | tf_op jit(solution)/shard_map/pallas_call | solution.py:356
  148.5 5.3 %collective-permute-done.21.d2 = bf16[576,256]{1,0:T(8,128)(2,1)S(1)} collective-permute-done((bf16[576,256]{1,0:T(8,128)(2,1)}, bf16[576,256]{1,0:T(8,128)(2,1)S(1)}, u32[]{:S(2)}, u32[]{:S(2)}) %collective-permute-start.21) | collective-permute-done | bytes 294944 | tf_op jit(solution)/shard_map/ppermute | solution.py:789
  155.1 3.0 %shard_map.179 = (bf16[512,256]{1,0:T(8,128)(2,1)}, f32[1,256]{1,0:T(1,128)}) custom-call(f32[512,256]{1,0:T(8,128)} %get-tuple-element.129.d_own, bf16[576,256]{1,0:T(8,128)(2,1)} %copy-done.34, bf16[576,256]{1,0:T(8,128)(2,1)} %copy-done.35, bf16[576,256]{1,0:T(8,128)(2,1)} %copy-done.36, f32[16,512]{1,0:T(8,128)} %get-tuple-element.133.inner, ...), custom_call_target="tpu_custom_call" | custom-call | flops 8589934592 | bytes 2097152 | tf_op jit(solution)/shard_map/pallas_call | solution.py:525
  162.7 2.8 %shard_map.180 = (f32[128,1024]{1,0:T(8,128)}, bf16[144,1024]{1,0:T(8,128)(2,1)}, bf16[144,1024]{1,0:T(8,128)(2,1)}, bf16[144,1024]{1,0:T(8,128)(2,1)}) custom-call(s32[5]{0:T(128)} %stack.32.at.refs_0_, bf16[4,4,32,1024]{3,2,1,0:T(8,128)(2,1)} %get-tuple-element.128.keep, bf16[2,4,32,1024]{3,2,1,0:T(8,128)(2,1)} %copy-done.6, ...), custom_call_target="tpu_custom_call" | custom-call | flops 2097152 | bytes 4194304 | tf_op jit(solution)/shard_map/pallas_call | solution.py:420
  166.6 2.1 collective-permute-start.29
  168.7 3.1 %collective-permute-start.30 = (bf16[144,1024]{1,0:T(8,128)(2,1)}, bf16[144,1024]{1,0:T(8,128)(2,1)S(1)}, u32[]{:S(2)}, u32[]{:S(2)}) collective-permute-start(bf16[144,1024]{1,0:T(8,128)(2,1)} %get-tuple-element.152), channel_id=1, source_target_pairs={{0,16},{4,20},{8,24},{12,28},{16,0},{20,4},{24,8},{28,12},{32,48},... | collective-permute-start | bytes 884744 | tf_op jit(solution)/shard_map/ppermute | solution.py:813
  172.9 3.5 %collective-permute-start.27 = (bf16[512,256]{1,0:T(8,128)(2,1)S(1)}, bf16[512,256]{1,0:T(8,128)(2,1)S(1)}, u32[]{:S(2)}, u32[]{:S(2)}) collective-permute-start(bf16[512,256]{1,0:T(8,128)(2,1)S(1)} %copy-done.38), channel_id=1, source_target_pairs={{0,2},{1,3},{2,0},{3,1},{4,6},{5,7},{6,4},{7,5},{8,10},{9,11},{10,... | collective-permute-start | bytes 786440 | tf_op jit(solution)/shard_map/ppermute | solution.py:811
  176.7 5.2 %collective-permute-done.27 = bf16[512,256]{1,0:T(8,128)(2,1)S(1)} collective-permute-done((bf16[512,256]{1,0:T(8,128)(2,1)S(1)}, bf16[512,256]{1,0:T(8,128)(2,1)S(1)}, u32[]{:S(2)}, u32[]{:S(2)}) %collective-permute-start.27) | collective-permute-done | bytes 262176 | tf_op jit(solution)/shard_map/ppermute | solution.py:811
  181.9 5.5 %collective-permute-done.28 = bf16[512,256]{1,0:T(8,128)(2,1)S(1)} collective-permute-done((bf16[512,256]{1,0:T(8,128)(2,1)S(1)}, bf16[512,256]{1,0:T(8,128)(2,1)S(1)}, u32[]{:S(2)}, u32[]{:S(2)}) %collective-permute-start.28) | collective-permute-done | bytes 262176 | tf_op jit(solution)/shard_map/ppermute | solution.py:811
  188.3 2.2 %shard_map.181 = (f32[32,1024]{1,0:T(8,128)}, bf16[48,1024]{1,0:T(8,128)(2,1)}, bf16[48,1024]{1,0:T(8,128)(2,1)}, bf16[48,1024]{1,0:T(8,128)(2,1)}, f32[8,256]{1,0:T(8,128)}) custom-call(s32[5]{0:T(128)} %stack.32.at.refs_0_, f32[128,1024]{1,0:T(8,128)} %get-tuple-element.158.own, bf16[144,1024]{1,0:T(8,128)(2,1)} %copy-done.8, bf16[144,1024]{1,0:T(8,128)(2,1)} %copy-done.9, ...), custom_call_target="tpu_custom_call" | custom-call | flops 2097152 | bytes 2097152 | tf_op jit(solution)/shard_map/pallas_call | solution.py:453
  192.1 3.0 %collective-permute-start.33 = (bf16[48,1024]{1,0:T(8,128)(2,1)}, bf16[48,1024]{1,0:T(8,128)(2,1)S(1)}, u32[]{:S(2)}, u32[]{:S(2)}) collective-permute-start(bf16[48,1024]{1,0:T(8,128)(2,1)} %get-tuple-element.164), channel_id=1, source_target_pairs={{0,64},{4,68},{8,72},{12,76},{16,80},{20,84},{24,88},{28,92},{32,9... | collective-permute-start | bytes 294920 | tf_op jit(solution)/shard_map/ppermute | solution.py:822
  (180 shorter events, 61.7 us)
Async XLA Ops:
  7.2 53.9 %all-gather.2.cloned.1.call-start = ((), (), s32[]{:S(2)}) async-start(), calls=%async_computation.2 | async-start | bytes 1310720 | tf_op jit(solution)/shard_map/all_gather | solution.py:721
  7.2 15.5 %collective-permute-start = (bf16[512,256]{1,0:T(8,128)(2,1)}, bf16[512,256]{1,0:T(8,128)(2,1)S(1)}, u32[]{:S(2)}, u32[]{:S(2)}) collective-permute-start(bf16[512,256]{1,0:T(8,128)(2,1)} %rows_in.1), channel_id=1, source_target_pairs={{0,3},{1,0},{2,1},{3,2},{4,7},{5,4},{6,5},{7,6},{8,11},{9,8},{10,9... | collective-permute-start | bytes 786440 | tf_op jit(solution)/shard_map/ppermute | solution.py:33
  10.1 12.7 %collective-permute-start.1 = (bf16[512,256]{1,0:T(8,128)(2,1)}, bf16[512,256]{1,0:T(8,128)(2,1)S(1)}, u32[]{:S(2)}, u32[]{:S(2)}) collective-permute-start(bf16[512,256]{1,0:T(8,128)(2,1)} %rows_in.1), channel_id=1, source_target_pairs={{0,2},{1,3},{2,0},{3,1},{4,6},{5,7},{6,4},{7,5},{8,10},{9,11},{10,... | collective-permute-start | bytes 786440 | tf_op jit(solution)/shard_map/ppermute | solution.py:33
  10.9 15.9 %collective-permute-start.2 = (bf16[512,256]{1,0:T(8,128)(2,1)}, bf16[512,256]{1,0:T(8,128)(2,1)S(1)}, u32[]{:S(2)}, u32[]{:S(2)}) collective-permute-start(bf16[512,256]{1,0:T(8,128)(2,1)} %rows_in.1), channel_id=1, source_target_pairs={{0,1},{1,2},{2,3},{3,0},{4,5},{5,6},{6,7},{7,4},{8,9},{9,10},{10,1... | collective-permute-start | bytes 786440 | tf_op jit(solution)/shard_map/ppermute | solution.py:33
  12.8 27.5 %collective-permute-start.3 = (bf16[512,256]{1,0:T(8,128)(2,1)S(1)}, bf16[512,256]{1,0:T(8,128)(2,1)S(1)}, u32[]{:S(2)}, u32[]{:S(2)}) collective-permute-start(bf16[512,256]{1,0:T(8,128)(2,1)S(1)} %constant_dynamic-slice_fusion.2.p0), channel_id=1, source_target_pairs={{0,3},{1,0},{2,1},{3,2},{4,7},{5,4},{6,5},{7,6},{8,11},{9,8},{10,9... | collective-permute-start | bytes 786440 | tf_op jit(solution)/shard_map/ppermute | solution.py:33
  15.2 26.4 %collective-permute-start.4 = (bf16[512,256]{1,0:T(8,128)(2,1)S(1)}, bf16[512,256]{1,0:T(8,128)(2,1)S(1)}, u32[]{:S(2)}, u32[]{:S(2)}) collective-permute-start(bf16[512,256]{1,0:T(8,128)(2,1)S(1)} %constant_dynamic-slice_fusion.2.p0), channel_id=1, source_target_pairs={{0,2},{1,3},{2,0},{3,1},{4,6},{5,7},{6,4},{7,5},{8,10},{9,11},{10,... | collective-permute-start | bytes 786440 | tf_op jit(solution)/shard_map/ppermute | solution.py:33
  16.8 145.4 %reduce-scatter.3.cloned.1.call-start = ((), (), s32[]{:S(2)}) async-start(), calls=%async_computation.3 | async-start | bytes 4423680 | tf_op jit(solution)/shard_map/reduce_scatter | solution.py:685
  22.7 18.9 %collective-permute-start.5 = (bf16[512,256]{1,0:T(8,128)(2,1)S(1)}, bf16[512,256]{1,0:T(8,128)(2,1)S(1)}, u32[]{:S(2)}, u32[]{:S(2)}) collective-permute-start(bf16[512,256]{1,0:T(8,128)(2,1)S(1)} %constant_dynamic-slice_fusion.2.p0), channel_id=1, source_target_pairs={{0,1},{1,2},{2,3},{3,0},{4,5},{5,6},{6,7},{7,4},{8,9},{9,10},{10,1... | collective-permute-start | bytes 786440 | tf_op jit(solution)/shard_map/ppermute | solution.py:33
  39.5 13.2 %collective-permute-start.7 = (bf16[512,256]{1,0:T(8,128)(2,1)S(1)}, bf16[512,256]{1,0:T(8,128)(2,1)S(1)}, u32[]{:S(2)}, u32[]{:S(2)}) collective-permute-start(bf16[512,256]{1,0:T(8,128)(2,1)S(1)} %get-tuple-element.174.p0.refs_4_), channel_id=1, source_target_pairs={{0,3},{1,0},{2,1},{3,2},{4,7},{5,4},{6,5},{7,6},{8,11},{9,8},{10,9... | collective-permute-start | bytes 786440 | tf_op jit(solution)/shard_map/ppermute | solution.py:33
  39.5 13.2 %collective-permute-start.8 = (bf16[512,256]{1,0:T(8,128)(2,1)S(1)}, bf16[512,256]{1,0:T(8,128)(2,1)S(1)}, u32[]{:S(2)}, u32[]{:S(2)}) collective-permute-start(bf16[512,256]{1,0:T(8,128)(2,1)S(1)} %get-tuple-element.174.p0.refs_4_), channel_id=1, source_target_pairs={{0,2},{1,3},{2,0},{3,1},{4,6},{5,7},{6,4},{7,5},{8,10},{9,11},{10,... | collective-permute-start | bytes 786440 | tf_op jit(solution)/shard_map/ppermute | solution.py:33
  40.3 17.7 %collective-permute-start.9 = (bf16[512,256]{1,0:T(8,128)(2,1)S(1)}, bf16[512,256]{1,0:T(8,128)(2,1)S(1)}, u32[]{:S(2)}, u32[]{:S(2)}) collective-permute-start(bf16[512,256]{1,0:T(8,128)(2,1)S(1)} %get-tuple-element.174.p0.refs_4_), channel_id=1, source_target_pairs={{0,1},{1,2},{2,3},{3,0},{4,5},{5,6},{6,7},{7,4},{8,9},{9,10},{10,1... | collective-permute-start | bytes 786440 | tf_op jit(solution)/shard_map/ppermute | solution.py:33
  45.4 15.6 %collective-permute-start.10 = (bf16[512,1024]{1,0:T(8,128)(2,1)}, bf16[512,1024]{1,0:T(8,128)(2,1)S(1)}, u32[]{:S(2)}, u32[]{:S(2)}) collective-permute-start(bf16[512,1024]{1,0:T(8,128)(2,1)} %shard_map.171.half), channel_id=1, source_target_pairs={{0,4},{4,0},{8,12},{12,8},{16,20},{20,16},{24,28},{28,24},{32,36},... | collective-permute-start | bytes 3145736 | tf_op jit(solution)/shard_map/ppermute | solution.py:742
  83.1 14.3 %collective-permute-start.13 = (bf16[512,256]{1,0:T(8,128)(2,1)}, bf16[512,256]{1,0:T(8,128)(2,1)S(1)}, u32[]{:S(2)}, u32[]{:S(2)}) collective-permute-start(bf16[512,256]{1,0:T(8,128)(2,1)} %get-tuple-element.112), channel_id=1, source_target_pairs={{0,1},{1,2},{2,3},{3,0},{4,5},{5,6},{6,7},{7,4},{8,9},{9,10},{10,1... | collective-permute-start | bytes 786440 | tf_op jit(solution)/shard_map/ppermute | solution.py:767
  83.5 15.3 %collective-permute-start.14 = (bf16[512,256]{1,0:T(8,128)(2,1)}, bf16[512,256]{1,0:T(8,128)(2,1)S(1)}, u32[]{:S(2)}, u32[]{:S(2)}) collective-permute-start(bf16[512,256]{1,0:T(8,128)(2,1)} %get-tuple-element.113), channel_id=1, source_target_pairs={{0,2},{1,3},{2,0},{3,1},{4,6},{5,7},{6,4},{7,5},{8,10},{9,11},{10,... | collective-permute-start | bytes 786440 | tf_op jit(solution)/shard_map/ppermute | solution.py:767
  85.8 13.3 %collective-permute-start.15 = (bf16[512,256]{1,0:T(8,128)(2,1)}, bf16[512,256]{1,0:T(8,128)(2,1)S(1)}, u32[]{:S(2)}, u32[]{:S(2)}) collective-permute-start(bf16[512,256]{1,0:T(8,128)(2,1)} %get-tuple-element.114), channel_id=1, source_target_pairs={{0,3},{1,0},{2,1},{3,2},{4,7},{5,4},{6,5},{7,6},{8,11},{9,8},{10,9... | collective-permute-start | bytes 786440 | tf_op jit(solution)/shard_map/ppermute | solution.py:767
  96.9 9.1 %collective-permute-start.11 = (bf16[2,4,32,3456]{3,2,1,0:T(8,128)(2,1)}, bf16[2,4,32,3456]{3,2,1,0:T(8,128)(2,1)S(1)}, u32[]{:S(2)}, u32[]{:S(2)}) collective-permute-start(bf16[2,4,32,3456]{3,2,1,0:T(8,128)(2,1)} %get-tuple-element.109), channel_id=1, source_target_pairs={{0,4},{4,0},{8,12},{12,8},{16,20},{20,16},{24,28},{28,24},{32,36},... | collective-permute-start | bytes 5308424 | tf_op jit(solution)/shard_map/ppermute | solution.py:369
  96.9 9.1 %collective-permute-start.12 = (bf16[2,4,32,3456]{3,2,1,0:T(8,128)(2,1)}, bf16[2,4,32,3456]{3,2,1,0:T(8,128)(2,1)S(1)}, u32[]{:S(2)}, u32[]{:S(2)}) collective-permute-start(bf16[2,4,32,3456]{3,2,1,0:T(8,128)(2,1)} %get-tuple-element.110), channel_id=1, source_target_pairs={{0,4},{4,0},{8,12},{12,8},{16,20},{20,16},{24,28},{28,24},{32,36},... | collective-permute-start | bytes 5308424 | tf_op jit(solution)/shard_map/ppermute | solution.py:369
  102.5 14.3 %collective-permute-start.16 = (bf16[512,256]{1,0:T(8,128)(2,1)}, bf16[512,256]{1,0:T(8,128)(2,1)S(1)}, u32[]{:S(2)}, u32[]{:S(2)}) collective-permute-start(bf16[512,256]{1,0:T(8,128)(2,1)} %get-tuple-element.117), channel_id=1, source_target_pairs={{0,3},{1,0},{2,1},{3,2},{4,7},{5,4},{6,5},{7,6},{8,11},{9,8},{10,9... | collective-permute-start | bytes 786440 | tf_op jit(solution)/shard_map/ppermute | solution.py:33
  105.2 11.7 %collective-permute-start.17 = (bf16[512,256]{1,0:T(8,128)(2,1)}, bf16[512,256]{1,0:T(8,128)(2,1)S(1)}, u32[]{:S(2)}, u32[]{:S(2)}) collective-permute-start(bf16[512,256]{1,0:T(8,128)(2,1)} %get-tuple-element.117), channel_id=1, source_target_pairs={{0,2},{1,3},{2,0},{3,1},{4,6},{5,7},{6,4},{7,5},{8,10},{9,11},{10,... | collective-permute-start | bytes 786440 | tf_op jit(solution)/shard_map/ppermute | solution.py:33
  105.4 14.8 %collective-permute-start.18 = (bf16[512,256]{1,0:T(8,128)(2,1)}, bf16[512,256]{1,0:T(8,128)(2,1)S(1)}, u32[]{:S(2)}, u32[]{:S(2)}) collective-permute-start(bf16[512,256]{1,0:T(8,128)(2,1)} %get-tuple-element.117), channel_id=1, source_target_pairs={{0,1},{1,2},{2,3},{3,0},{4,5},{5,6},{6,7},{7,4},{8,9},{9,10},{10,1... | collective-permute-start | bytes 786440 | tf_op jit(solution)/shard_map/ppermute | solution.py:33
  120.2 84.7 %reduce-scatter.5.cloned.1.call-start = ((), (), s32[]{:S(2)}) async-start(), calls=%async_computation.4 | async-start | bytes 1105920 | tf_op jit(solution)/shard_map/reduce_scatter | solution.py:685
  136.9 11.7 %collective-permute-start.20 = (bf16[576,256]{1,0:T(8,128)(2,1)}, bf16[576,256]{1,0:T(8,128)(2,1)S(1)}, u32[]{:S(2)}, u32[]{:S(2)}) collective-permute-start(bf16[576,256]{1,0:T(8,128)(2,1)} %get-tuple-element.130), channel_id=1, source_target_pairs={{0,1},{1,2},{2,3},{3,0},{4,5},{5,6},{6,7},{7,4},{8,9},{9,10},{10,1... | collective-permute-start | bytes 884744 | tf_op jit(solution)/shard_map/ppermute | solution.py:789
  136.9 16.9 %collective-permute-start.21 = (bf16[576,256]{1,0:T(8,128)(2,1)}, bf16[576,256]{1,0:T(8,128)(2,1)S(1)}, u32[]{:S(2)}, u32[]{:S(2)}) collective-permute-start(bf16[576,256]{1,0:T(8,128)(2,1)} %get-tuple-element.131), channel_id=1, source_target_pairs={{0,2},{1,3},{2,0},{3,1},{4,6},{5,7},{6,4},{7,5},{8,10},{9,11},{10,... | collective-permute-start | bytes 884744 | tf_op jit(solution)/shard_map/ppermute | solution.py:789
  139.9 14.5 %collective-permute-start.22 = (bf16[576,256]{1,0:T(8,128)(2,1)}, bf16[576,256]{1,0:T(8,128)(2,1)S(1)}, u32[]{:S(2)}, u32[]{:S(2)}) collective-permute-start(bf16[576,256]{1,0:T(8,128)(2,1)} %get-tuple-element.132), channel_id=1, source_target_pairs={{0,3},{1,0},{2,1},{3,2},{4,7},{5,4},{6,5},{7,6},{8,11},{9,8},{10,9... | collective-permute-start | bytes 884744 | tf_op jit(solution)/shard_map/ppermute | solution.py:789
  146.6 15.1 %collective-permute-start.24 = (bf16[2,4,32,1024]{3,2,1,0:T(8,128)(2,1)}, bf16[2,4,32,1024]{3,2,1,0:T(8,128)(2,1)S(1)}, u32[]{:S(2)}, u32[]{:S(2)}) collective-permute-start(bf16[2,4,32,1024]{3,2,1,0:T(8,128)(2,1)} %get-tuple-element.139), channel_id=1, source_target_pairs={{0,4},{4,0},{8,12},{12,8},{16,20},{20,16},{24,28},{28,24},{32,36},... | collective-permute-start | bytes 1572872 | tf_op jit(solution)/shard_map/ppermute | solution.py:369
  148.5 13.3 %collective-permute-start.25 = (bf16[2,4,32,1024]{3,2,1,0:T(8,128)(2,1)}, bf16[2,4,32,1024]{3,2,1,0:T(8,128)(2,1)S(1)}, u32[]{:S(2)}, u32[]{:S(2)}) collective-permute-start(bf16[2,4,32,1024]{3,2,1,0:T(8,128)(2,1)} %get-tuple-element.140), channel_id=1, source_target_pairs={{0,4},{4,0},{8,12},{12,8},{16,20},{20,16},{24,28},{28,24},{32,36},... | collective-permute-start | bytes 1572872 | tf_op jit(solution)/shard_map/ppermute | solution.py:369
  165.6 10.9 %collective-permute-start.26 = (bf16[512,256]{1,0:T(8,128)(2,1)S(1)}, bf16[512,256]{1,0:T(8,128)(2,1)S(1)}, u32[]{:S(2)}, u32[]{:S(2)}) collective-permute-start(bf16[512,256]{1,0:T(8,128)(2,1)S(1)} %copy-done.39), channel_id=1, source_target_pairs={{0,1},{1,2},{2,3},{3,0},{4,5},{5,6},{6,7},{7,4},{8,9},{9,10},{10,1... | collective-permute-start | bytes 786440 | tf_op jit(solution)/shard_map/ppermute | solution.py:811
  166.6 20.8 %collective-permute-start.29 = (bf16[144,1024]{1,0:T(8,128)(2,1)}, bf16[144,1024]{1,0:T(8,128)(2,1)S(1)}, u32[]{:S(2)}, u32[]{:S(2)}) collective-permute-start(bf16[144,1024]{1,0:T(8,128)(2,1)} %get-tuple-element.151), channel_id=1, source_target_pairs={{0,8},{4,12},{8,16},{12,20},{16,24},{20,28},{24,0},{28,4},{32,40},... | collective-permute-start | bytes 884744 | tf_op jit(solution)/shard_map/ppermute | solution.py:813
  168.7 18.7 %collective-permute-start.30 = (bf16[144,1024]{1,0:T(8,128)(2,1)}, bf16[144,1024]{1,0:T(8,128)(2,1)S(1)}, u32[]{:S(2)}, u32[]{:S(2)}) collective-permute-start(bf16[144,1024]{1,0:T(8,128)(2,1)} %get-tuple-element.152), channel_id=1, source_target_pairs={{0,16},{4,20},{8,24},{12,28},{16,0},{20,4},{24,8},{28,12},{32,48},... | collective-permute-start | bytes 884744 | tf_op jit(solution)/shard_map/ppermute | solution.py:813
  171.7 15.7 %collective-permute-start.31 = (bf16[144,1024]{1,0:T(8,128)(2,1)}, bf16[144,1024]{1,0:T(8,128)(2,1)S(1)}, u32[]{:S(2)}, u32[]{:S(2)}) collective-permute-start(bf16[144,1024]{1,0:T(8,128)(2,1)} %get-tuple-element.153), channel_id=1, source_target_pairs={{0,24},{4,28},{8,0},{12,4},{16,8},{20,12},{24,16},{28,20},{32,56},... | collective-permute-start | bytes 884744 | tf_op jit(solution)/shard_map/ppermute | solution.py:813
  172.9 9.0 %collective-permute-start.27 = (bf16[512,256]{1,0:T(8,128)(2,1)S(1)}, bf16[512,256]{1,0:T(8,128)(2,1)S(1)}, u32[]{:S(2)}, u32[]{:S(2)}) collective-permute-start(bf16[512,256]{1,0:T(8,128)(2,1)S(1)} %copy-done.38), channel_id=1, source_target_pairs={{0,2},{1,3},{2,0},{3,1},{4,6},{5,7},{6,4},{7,5},{8,10},{9,11},{10,... | collective-permute-start | bytes 786440 | tf_op jit(solution)/shard_map/ppermute | solution.py:811
  176.4 11.0 %collective-permute-start.28 = (bf16[512,256]{1,0:T(8,128)(2,1)S(1)}, bf16[512,256]{1,0:T(8,128)(2,1)S(1)}, u32[]{:S(2)}, u32[]{:S(2)}) collective-permute-start(bf16[512,256]{1,0:T(8,128)(2,1)S(1)} %copy-done.37), channel_id=1, source_target_pairs={{0,3},{1,0},{2,1},{3,2},{4,7},{5,4},{6,5},{7,6},{8,11},{9,8},{10,9... | collective-permute-start | bytes 786440 | tf_op jit(solution)/shard_map/ppermute | solution.py:811
  (52 other events, 278.9 us)
Sparse Core Ops, SparseCore 0:
  16.9 38.3 all-gather.1
  120.3 41.8 reduce-scatter.2
  164.6 22.3 reduce-scatter.4

commit v4 on v3

--- a/solution.py
+++ b/solution.py
@@ -30,7 +30,9 @@
 
 
 def gather_ch(block):
-    return [block] + [lax.ppermute(block, "ch", ch_pairs(-j)) for j in range(1, CH)]
+    far = lax.ppermute(block, "ch", ch_pairs(2))
+    near = [lax.ppermute(block, "ch", ch_pairs(-j)) for j in (1, 3)]
+    return [block, near[0], far, near[1]]
 
 
 def scatter_ch(chunks):
@@ -59,13 +61,6 @@
 
 def first_count(segment_ids):
     return jnp.sum((segment_ids == segment_ids[0]).astype(jnp.int32))
-
-
-def tap_masks(count, rows):
-    token = lax.broadcasted_iota(jnp.int32, (rows, 1), 0)
-    same_one = (token != count).astype(F32)
-    same_two = ((token != count) & (token != count + 1)).astype(F32)
-    return (same_one, same_two)
 
 
 def tie(*arrays):
@@ -120,7 +115,7 @@
     return pl.CostEstimate(flops=2 * macs, bytes_accessed=nbytes, transcendentals=0)
 
 
-def in_kernel(at, p0, p1, p2, p3, gain, weight, normed, rms, b_out, c_out, v_out, gated, held, sem):
+def in_kernel(at, p0, p1, p2, p3, gain, weight, normed, rms, b_out, c_out, v_out, gated, edge, held, sem):
     x = at[0]
     width = p0.shape[1]
     copies = [
@@ -149,7 +144,9 @@
     v = dot_nn(normed[...], held[2])
     b_out[...] = b
     v_out[...] = v
-    gated[...] = (b * v).astype(BF16)
+    product = (b * v).astype(BF16)
+    gated[...] = product
+    edge[...] = product[-16:]
     c_out[...] = dot_nn(normed[...], held[1])
 
 
@@ -166,9 +163,10 @@
             out,
             out,
             shape((rows, width), BF16),
+            shape((16, width), BF16),
         ),
         in_specs=[smem()] + [vmem()] * 5 + [anywhere()],
-        out_specs=(vmem(),) * 6,
+        out_specs=(vmem(),) * 7,
         scratch_shapes=[
             pltpu.VMEM((3, features, width), BF16),
             pltpu.SemaphoreType.DMA((CH,)),
@@ -196,18 +194,66 @@
     )(*pieces)
 
 
+def conv_kernel(at, gated, carried, c_gate, taps, mixed, conv_out, one_out, two_out):
+    count = at[2]
+    rows, width = gated.shape
+    token = lax.broadcasted_iota(jnp.int32, (rows, width), 0)
+    current = gated[...].astype(F32)
+    before = carried[...].astype(F32)
+    last, second = before[15:16], before[14:15]
+    one = jnp.where(token == 0, last, pltpu.roll(current, 1, 0))
+    one = jnp.where(token == count, 0.0, one)
+    two = jnp.where(token == 0, second, pltpu.roll(current, 2, 0))
+    two = jnp.where(token == 1, last, two)
+    two = jnp.where((token == count) | (token == count + 1), 0.0, two)
+    out = taps[0:1] * current + taps[1:2] * one + taps[2:3] * two
+    mixed[...] = (c_gate[...] * out).astype(BF16)
+    conv_out[...] = out
+    one_out[...] = one.astype(BF16)
+    two_out[...] = two.astype(BF16)
+
+
+def convolve(at, gated, carried, c_gate, taps):
+    rows, width = gated.shape
+    low = shape((rows, width), BF16)
+    mixed, out, one, two = pl.pallas_call(
+        conv_kernel,
+        out_shape=(low, shape((rows, width), F32), low, low),
+        in_specs=[smem()] + [vmem()] * 4,
+        out_specs=(vmem(),) * 4,
+        compiler_params=params(56),
+        cost_estimate=cost(2**22, 2**21),
+    )(at, gated, carried, c_gate, taps)
+    return mixed, out, gated, one, two
+
+
+def copy_kernel(row, out):
+    out[...] = row[...]
+
+
+def copy_row(row):
+    return pl.pallas_call(
+        copy_kernel,
+        out_shape=shape(row.shape, F32),
+        in_specs=[vmem()],
+        out_specs=vmem(),
+        compiler_params=params(56),
+        cost_estimate=cost(LONG, 2**13),
+    )(row)
+
+
 def ffn_kernel(
     at,
     x0, x1, x2, x3,
-    mixed,
+    m0, m1, m2, m3,
     gain,
     half,
     other,
     planes,
     down,
     cotangent,
-    h, rms, normed, act, d_gate_up, d_own, d1, d2, d3, f0, f1, f2, f3,
-    w_out, w_in, w_down, g_rows, acc, down_acc, sem,
+    h, h_own, rms, normed, act, d_gate_up, d_own, d1, d2, d3, f0, f1, f2, f3,
+    w_out, w_in, w_down, g_rows, mixed, acc, down_acc, sem,
 ):
     x, core = at[0], at[1]
     width = x0.shape[1]
@@ -231,6 +277,8 @@
     ]
     for copy in halves + planes_in + rest:
         copy.start()
+    for j, piece in enumerate((m0, m1, m2, m3)):
+        mixed[:, j * width : (j + 1) * width] = piece[...]
     for copy in halves:
         copy.wait()
     square = jnp.zeros((x0.shape[0], 1), F32)
@@ -243,6 +291,7 @@
         square = square + jnp.sum(hj * hj, axis=1, keepdims=True)
     r = lax.rsqrt(square / (CH * width) + EPS)
     rms[...] = r
+    h_own[...] = h[:, :width]
     for j in range(CH):
         columns = slice(j * width, (j + 1) * width)
         scale = gain[:, rel_rows(x, j, width)]
@@ -283,7 +332,7 @@
         out[...] = down_acc[lax.rem(x + j, CH)].astype(BF16)
 
 
-def ffn(at, pieces, mixed, gain, half, other, planes, down, cotangent):
+def ffn(at, pieces, mixed_pieces, gain, half, other, planes, down, cotangent):
     rows, width = pieces[0].shape
     features = CH * width
     units = down.shape[1]
@@ -292,6 +341,7 @@
         ffn_kernel,
         out_shape=(
             shape((rows, features), F32),
+            shape((rows, width), F32),
             shape((rows, 1), F32),
             shape((rows, features), BF16),
             shape((rows, units), BF16),
@@ -299,20 +349,21 @@
             shape((rows, width), F32),
         )
         + (block,) * 7,
-        in_specs=[smem()] + [vmem()] * 6 + [anywhere()] * 5,
-        out_specs=(vmem(),) * 13,
+        in_specs=[smem()] + [vmem()] * 9 + [anywhere()] * 5,
+        out_specs=(vmem(),) * 14,
         scratch_shapes=[
             pltpu.VMEM((2, features // 2, features), BF16),
             pltpu.VMEM((2, features, units), BF16),
             pltpu.VMEM((features, units), BF16),
             pltpu.VMEM((rows, features), BF16),
+            pltpu.VMEM((rows, features), BF16),
             pltpu.VMEM((CH, rows, width), F32),
             pltpu.VMEM((CH, rows, width), F32),
             pltpu.SemaphoreType.DMA((8,)),
         ],
         compiler_params=params(56),
         cost_estimate=cost(rows * features * (features + 6 * units), 20 * 2**20),
-    )(at, *pieces, mixed, gain[None], half, other, planes, down, cotangent)
+    )(at, *pieces, *mixed_pieces, gain, half, other, planes, down, cotangent)
 
 
 def pair_kernel(
@@ -561,7 +612,7 @@
 
 def mid_kernel(
     at, u_own, u1, u2, u3, h, rms, cotangent, weight, c_gate, conv_out,
-    d_branch, d_hidden, d_conv, d_cgate,
+    d_branch, d_hidden, d_conv, d_cgate, edge,
 ):
     x = at[0]
     width = u_own.shape[1]
@@ -582,7 +633,9 @@
         rounded = full.astype(BF16)
         d_branch[:, columns] = rounded
         d_mixed = d_mixed + dot_nn(rounded, weight[rel_rows(x, j, width), :])
-    d_conv[...] = d_mixed * c_gate[...]
+    product = d_mixed * c_gate[...]
+    d_conv[...] = product
+    edge[...] = product[:8]
     d_cgate[...] = (d_mixed * conv_out[...]).astype(BF16)
 
 
@@ -591,9 +644,15 @@
     wide = shape((rows, width), F32)
     return pl.pallas_call(
         mid_kernel,
-        out_shape=(shape((rows, CH * width), BF16), wide, wide, shape((rows, width), BF16)),
+        out_shape=(
+            shape((rows, CH * width), BF16),
+            wide,
+            wide,
+            shape((rows, width), BF16),
+            shape((8, width), F32),
+        ),
         in_specs=[smem()] + [vmem()] * 10,
-        out_specs=(vmem(),) * 4,
+        out_specs=(vmem(),) * 5,
         compiler_params=params(56),
         cost_estimate=cost(rows * CH * width * width, 6 * 2**20),
     )(at, *pieces, h, rms, cotangent, weight, c_gate, conv_out)
@@ -720,28 +779,24 @@
     half_pieces = gather_ch(half)
     grad_full = lax.all_gather(out_grad, "ch", axis=1, tiled=True)
 
-    normed_one, r_one, b_gate, c_gate, value_rows, gated_rows = in_project(
+    normed_one, r_one, b_gate, c_gate, value_rows, gated_rows, edge = in_project(
         at, pieces, norm1_gain, in_planes
     )
-    own_rows = block_input.astype(F32)
-    carried = from_behind(gated_rows[-2:], "seq", 1)
-    extended = jnp.concatenate([carried, gated_rows], axis=0).astype(F32)
-    same_one, same_two = tap_masks(count, block_input.shape[0])
-    current = extended[2:]
-    prior_one = extended[1:-1] * same_one
-    prior_two = extended[:-2] * same_two
-    conv_out = conv_weight[0] * current + conv_weight[1] * prior_one + conv_weight[2] * prior_two
-    mixed_rows = (c_gate * conv_out).astype(BF16)
+    carried = from_behind(edge, "seq", 1)
+    mixed_rows, conv_out, current, prior_one, prior_two = convolve(
+        at, gated_rows, carried, c_gate, conv_weight
+    )
 
     mixed_pieces = gather_ch(mixed_rows)
     *half_pieces, ffn_weight, _ = tie(*half_pieces, ffn_in_weight, mixed_rows)
     ffn_planes = jnp.transpose(ffn_weight, (1, 0, 2))
     half_full = join_columns(half_pieces, 2**20)
-    mixed_full = join_columns(mixed_pieces, 2**32)
-    ffn_planes, mixed_full = tie(ffn_planes, mixed_full)
+    gain_row = copy_row(tie(norm2_gain, mixed_rows)[0][None])
+    ffn_planes, gain_row = tie(ffn_planes, gain_row)
     other_half = lax.ppermute(half_full, "seq", seq_pairs(0, 0, 1))
     (
         hidden,
+        hidden_own,
         r_two,
         normed_two,
         act_rows,
@@ -754,17 +809,16 @@
     ) = ffn(
         at,
         pieces,
-        mixed_full,
-        norm2_gain,
+        mixed_pieces,
+        gain_row,
         half_full,
         other_half,
         ffn_planes,
         ffn_out_weight,
         grad_full,
     )
-    hidden_own = hidden[:, :width]
     received = [
-        lax.ppermute(d, "ch", ch_pairs(j)) for j, d in ((1, d_one), (2, d_two), (3, d_three))
+        lax.ppermute(d, "ch", ch_pairs(j)) for j, d in ((2, d_two), (1, d_one), (3, d_three))
     ]
     *gives, keep = pair_products(at, normed_two, d_gate_up, grad_full, act_rows, True, False)
     got = swap_cores(gives)
@@ -778,23 +832,23 @@
     groups = [[seq_index(i, k, c) for k in range(4)] for i in range(4) for c in range(2)]
     ffn_sum = scatter_groups(ffn_kept, groups)
 
-    d_branch, d_hidden, d_conv, d_cgate = mid(
+    d_branch, d_hidden, d_conv, d_cgate, edge = mid(
         at, u_pieces, hidden, r_two, grad_full, out_weight, c_gate, conv_out
     )
-    following = from_behind(d_conv[:2], "seq", -1)
+    following = from_behind(edge, "seq", -1)
     d_proj, d_own, d_one, d_two, d_three, inner = back_project(
         at, pieces, d_conv, following, conv_weight, value_rows, b_gate, d_cgate, norm1_gain,
         in_planes,
     )
-    received = [lax.ppermute(d, "ch", ch_pairs(j)) for j, d in ((1, d_one), (2, d_two), (3, d_three))]
+    received = [lax.ppermute(d, "ch", ch_pairs(j)) for j, d in ((2, d_two), (1, d_one), (3, d_three))]
 
     *gives, keep = pair_products(at, normed_one, d_proj, d_branch, mixed_rows, True, True)
     got = swap_cores(gives)
     grad_conv = jnp.stack(
         [
-            jnp.sum(d_conv * current, axis=0),
-            jnp.sum(d_conv * prior_one, axis=0),
-            jnp.sum(d_conv * prior_two, axis=0),
+            jnp.sum(d_conv * current.astype(F32), axis=0),
+            jnp.sum(d_conv * prior_one.astype(F32), axis=0),
+            jnp.sum(d_conv * prior_two.astype(F32), axis=0),
         ],
         axis=0,
     )
@@ -808,9 +862,9 @@
     small, ffn_sum, *got = tie(small, ffn_sum, *got)
     own, *messages = send_z(at, keep, got, small)
     down_parts, messages = lax.optimization_barrier((down_parts, messages))
-    downs = [lax.ppermute(down_parts[j], "ch", ch_pairs(j)) for j in (1, 2, 3)]
+    downs = [lax.ppermute(down_parts[j], "ch", ch_pairs(j)) for j in (2, 1, 3)]
     messages = [
-        lax.ppermute(m, "seq", seq_pairs(0, j, 0)) for j, m in ((1, messages[0]), (2, messages[1]), (3, messages[2]))
+        lax.ppermute(m, "seq", seq_pairs(0, j, 0)) for j, m in ((2, messages[1]), (1, messages[0]), (3, messages[2]))
     ]
     downs, messages = lax.optimization_barrier((downs, messages))
     block_output = hidden_own + down_parts[0].astype(F32)
@@ -819,7 +873,7 @@
     block_output = block_output.astype(BF16)
     own, *messages, small = turn(at, own, messages, small)
     messages = [
-        lax.ppermute(m, "seq", seq_pairs(j, 0, 0)) for j, m in ((1, messages[0]), (2, messages[1]), (3, messages[2]))
+        lax.ppermute(m, "seq", seq_pairs(j, 0, 0)) for j, m in ((2, messages[1]), (1, messages[0]), (3, messages[2]))
     ]
     grad_in, grad_out, small = last(own, messages, small)
 

time: 215 us -> 208 us (0.967)
  local copies, waits for them, and re-layouts: 29.8 us -> 22.8 us
  other arithmetic: 9.44 us -> 4.55 us
  starting transfers between devices: 47.7 us -> 51.8 us
  Pallas kernels: 73.2 us -> 75.9 us
    ppermute x15, waiting for transfers between devices: 26.8 us -> 22.2 us  [the longest x8 13.9 us: gather_ch(): near = [lax.ppermute(block, 'ch', ch_pairs(-j)) for j in (1, 3)]]
    slice x4 -> x0, local copies, waits for them, and re-layouts: 4.08 us -> none  [the longest x1 1.89 us: shards(): hidden_own = hidden[:, :width]]
    pallas_call x0 -> x2, Pallas kernels: none -> 3.77 us  [the longest x1 2.43 us: convolve(): pl.pallas_call(conv_kernel, out_shape=(low, shape((rows, width), F32), lo...]
    convert_element_type x3 -> x0, other arithmetic: 3.76 us -> none  [the longest x1 2.1 us: shards(): mixed_rows = (c_gate * conv_out).astype(BF16)]
    ppermute x15, starting transfers between devices: 19.1 us -> 22.5 us  [the longest x8 11.3 us: gather_ch(): near = [lax.ppermute(block, 'ch', ch_pairs(-j)) for j in (1, 3)]]
    ppermute x6, starting transfers between devices: 7.77 us -> 10.3 us  [shards(): lax.ppermute(d, 'ch', ch_pairs(j))]
    ppermute x3, waiting for transfers between devices: 0.01 us -> 2.5 us  [shards(): lax.ppermute(m, 'seq', seq_pairs(0, j, 0))]
    optimization_barrier x1, local copies, waits for them, and re-layouts: 5.09 us -> 2.76 us  [tie(): return lax.optimization_barrier(arrays)]
  transfers between devices with their start and end apart: 38 -> 38, of which waited for: 16 -> 15; matrix products, arithmetic and copies ran while one was open for 11% -> 7% of each run, Pallas kernels for 25% -> 27%
where the time goes in v4:
time: 208 us; the launch traced here: 207 us
  Pallas kernels  75.9 us (36%)
  starting transfers between devices  51.8 us (25%)
  waiting for transfers between devices  37.6 us (18%)
  local copies, waits for them, and re-layouts  22.8 us (11%)
  between operations  14.1 us (7%)
  other arithmetic  4.55 us (2%)
    pallas_call x1, Pallas kernels, ffn(): pl.pallas_call(ffn_kernel, out_shape=(shape((rows, features), F32), shape...  19.6 us
    pallas_call x2, Pallas kernels, pair_products(): pl.pallas_call(body, grid=(4,), out_shape=(half, half, out), in_specs=[sm...  14.9 us
    ppermute x8, waiting for transfers between devices, gather_ch(): near = [lax.ppermute(block, 'ch', ch_pairs(-j)) for j in (1, 3)]  13.9 us
    ppermute x8, starting transfers between devices, gather_ch(): near = [lax.ppermute(block, 'ch', ch_pairs(-j)) for j in (1, 3)]  11.3 us
    ppermute x6, starting transfers between devices, shards(): lax.ppermute(d, 'ch', ch_pairs(j))  10.3 us
    unnamed x90, local copies, waits for them, and re-layouts  9.8 us
    pallas_call x1, Pallas kernels, back_project(): pl.pallas_call(back_kernel, out_shape=(shape((rows, 3 * width), BF16), sh...  7.16 us
    ppermute x3, starting transfers between devices, shards(): lax.ppermute(m, 'seq', seq_pairs(j, 0, 0))  6.23 us
  transfers between devices with their start and end apart: 38, of which 15 were waited for; matrix products, arithmetic and copies ran while one was open for 7% of the time, Pallas kernels for 27%

profile of v4, /device:TPU:0, one launch (start us, length us, event | category | flops | bytes accessed | tf_op | source)
XLA Modules:
  0.0 206.8 jit_solution(7116988302549957526)
XLA Ops:
  7.2 2.9 %collective-permute-start = (bf16[512,256]{1,0:T(8,128)(2,1)}, bf16[512,256]{1,0:T(8,128)(2,1)S(1)}, u32[]{:S(2)}, u32[]{:S(2)}) collective-permute-start(bf16[512,256]{1,0:T(8,128)(2,1)} %rows_in.1), channel_id=1, source_target_pairs={{0,3},{1,0},{2,1},{3,2},{4,7},{5,4},{6,5},{7,6},{8,11},{9,8},{10,9... | collective-permute-start | bytes 786440 | tf_op jit(solution)/shard_map/ppermute | solution.py:34
  12.8 2.4 %collective-permute-start.7 = (bf16[512,256]{1,0:T(8,128)(2,1)S(1)}, bf16[512,256]{1,0:T(8,128)(2,1)S(1)}, u32[]{:S(2)}, u32[]{:S(2)}) collective-permute-start(bf16[512,256]{1,0:T(8,128)(2,1)S(1)} %constant_dynamic-slice_fusion.2.p0), channel_id=1, source_target_pairs={{0,3},{1,0},{2,1},{3,2},{4,7},{5,4},{6,5},{7,6},{8,11},{9,8},{10,9... | collective-permute-start | bytes 786440 | tf_op jit(solution)/shard_map/ppermute | solution.py:34
  18.7 3.9 %collective-permute-done.p1.x1 = bf16[512,256]{1,0:T(8,128)(2,1)S(1)} collective-permute-done((bf16[512,256]{1,0:T(8,128)(2,1)}, bf16[512,256]{1,0:T(8,128)(2,1)S(1)}, u32[]{:S(2)}, u32[]{:S(2)}) %collective-permute-start) | collective-permute-done | bytes 262176 | tf_op jit(solution)/shard_map/ppermute | solution.py:34
  27.5 5.2 %shard_map.169 = (bf16[512,1024]{1,0:T(8,128)(2,1)}, f32[512,1]{1,0:T(8,128)}, f32[512,256]{1,0:T(8,128)}, f32[512,256]{1,0:T(8,128)}, f32[512,256]{1,0:T(8,128)...) custom-call(s32[5]{0:T(128)} %stack.32.at.refs_0_, bf16[512,256]{1,0:T(8,128)(2,1)} %rows_in.1, ...), custom_call_target="tpu_custom_call" | custom-call | flops 805306368 | bytes 6291456 | tf_op jit(solution)/shard_map/pallas_call | solution.py:157
  36.0 2.4 %shard_map.170 = (bf16[512,256]{1,0:T(8,128)(2,1)}, f32[512,256]{1,0:T(8,128)}, bf16[512,256]{1,0:T(8,128)(2,1)}, bf16[512,256]{1,0:T(8,128)(2,1)}) custom-call(s32[5]{0:T(128)} %stack.32.at.refs_0_, bf16[512,256]{1,0:T(8,128)(2,1)} %get-tuple-element.98.gated, bf16[16,256]{1,0:T(8,128)(2,1)} %copy-done.28, f32[512,256]{1,0:T(8,128)} %get-tuple-element.100.c_gate, ...), custom_call_target="tpu_custom_call" | custom-call | flops 8388608 | bytes 2097152 | tf_op jit(solution)/shard_map/pallas_call | solution.py:219
  38.4 2.5 %collective-permute-start.4 = (bf16[512,256]{1,0:T(8,128)(2,1)}, bf16[512,256]{1,0:T(8,128)(2,1)S(1)}, u32[]{:S(2)}, u32[]{:S(2)}) collective-permute-start(bf16[512,256]{1,0:T(8,128)(2,1)} %get-tuple-element.101.m0.refs_4_), channel_id=1, source_target_pairs={{0,3},{1,0},{2,1},{3,2},{4,7},{5,4},{6,5},{7,6},{8,11},{9,8},{10,9... | collective-permute-start | bytes 786440 | tf_op jit(solution)/shard_map/ppermute | solution.py:34
  45.2 2.3 %shard_map.172.half = bf16[512,1024]{1,0:T(8,128)(2,1)} custom-call(bf16[512,256]{1,0:T(8,128)(2,1)} %copy-done.4, bf16[512,256]{1,0:T(8,128)(2,1)} %copy-done.20, bf16[512,256]{1,0:T(8,128)(2,1)} %copy-done.21, bf16[512,256]{1,0:T(8,128)(2,1)} %copy-done.22), custom_call_target="tpu_custom_call" | custom-call | flops 2097152 | bytes 2097152 | tf_op jit(solution)/shard_map/pallas_call | solution.py:187
  50.6 2.8 %copy.21 = bf16[1024,2,1152]{2,0,1:T(8,128)(2,1)} copy(bf16[1024,2,1152]{2,1,0:T(2,128)(2,1)S(1)} %bitcast.23) | data formatting | bytes 9437184 | tf_op jit(solution)/shard_map/optimization_barrier | solution.py:67
  53.3 4.8 %collective-permute-done.6.m3 = bf16[512,256]{1,0:T(8,128)(2,1)S(1)} collective-permute-done((bf16[512,256]{1,0:T(8,128)(2,1)}, bf16[512,256]{1,0:T(8,128)(2,1)S(1)}, u32[]{:S(2)}, u32[]{:S(2)}) %collective-permute-start.6) | collective-permute-done | bytes 262176 | tf_op jit(solution)/shard_map/ppermute | solution.py:34
  59.2 19.6 %shard_map.173 = (f32[512,1024]{1,0:T(8,128)}, f32[512,256]{1,0:T(8,128)}, f32[512,1]{1,0:T(8,128)}, bf16[512,1024]{1,0:T(8,128)(2,1)}, bf16[512,1152]{1,0:T(8,1...) custom-call(s32[5]{0:T(128)} %stack.32.at.refs_0_, ...), custom_call_target="tpu_custom_call" | custom-call | flops 8321499136 | bytes 20971520 | tf_op jit(solution)/shard_map/pallas_call | solution.py:340
  78.8 2.5 %collective-permute-start.13 = (bf16[512,256]{1,0:T(8,128)(2,1)}, bf16[512,256]{1,0:T(8,128)(2,1)S(1)}, u32[]{:S(2)}, u32[]{:S(2)}) collective-permute-start(bf16[512,256]{1,0:T(8,128)(2,1)} %get-tuple-element.123), channel_id=1, source_target_pairs={{0,2},{1,3},{2,0},{3,1},{4,6},{5,7},{6,4},{7,5},{8,10},{9,11},{10,... | collective-permute-start | bytes 786440 | tf_op jit(solution)/shard_map/ppermute | solution.py:821
  81.3 3.2 %collective-permute-start.15 = (bf16[512,256]{1,0:T(8,128)(2,1)}, bf16[512,256]{1,0:T(8,128)(2,1)S(1)}, u32[]{:S(2)}, u32[]{:S(2)}) collective-permute-start(bf16[512,256]{1,0:T(8,128)(2,1)} %get-tuple-element.125), channel_id=1, source_target_pairs={{0,3},{1,0},{2,1},{3,2},{4,7},{5,4},{6,5},{7,6},{8,11},{9,8},{10,9... | collective-permute-start | bytes 786440 | tf_op jit(solution)/shard_map/ppermute | solution.py:821
  84.5 9.8 %shard_map.174 = (bf16[2,4,32,3456]{3,2,1,0:T(8,128)(2,1)}, bf16[2,4,32,3456]{3,2,1,0:T(8,128)(2,1)}, bf16[4,4,32,3456]{3,2,1,0:T(8,128)(2,1)}) custom-call(s32[5]{0:T(128)} %stack.32.at.refs_0_, bf16[512,1024]{1,0:T(8,128)(2,1)} %get-tuple-element.116.refs_1_, bf16[512,2304]{1,0:T(8,128)(2,1)} %get-tuple-element.117.refs_2_, ...), custom_call_target="tpu_custom_call" | custom-call | flops 3623878656 | bytes 14155776 | tf_op jit(solution)/shard_map/pallas_call | solution.py:407
  95.7 2.7 %shard_map.176 = (f32[512,256]{1,0:T(8,128)}, bf16[512,256]{1,0:T(8,128)(2,1)}, f32[1,256]{1,0:T(1,128)}) custom-call(f32[512,256]{1,0:T(8,128)} %get-tuple-element.122.d_own, bf16[512,256]{1,0:T(8,128)(2,1)} %copy-done.40, bf16[512,256]{1,0:T(8,128)(2,1)} %copy-done.41, bf16[512,256]{1,0:T(8,128)(2,1)} %copy-done.42, f32[512,256]{1,0:T(8,128)} %get-tuple-element.110.h, ...), custom_call_target="tpu_custom_call" | custom-call | flops 137438953472 | bytes 2097152 | tf_op jit(solution)/shard_map/pallas_call | solution.py:599
  103.0 5.4 %shard_map.175 = bf16[4,4,32,3456]{3,2,1,0:T(8,128)(2,1)} custom-call(bf16[4,4,32,3456]{3,2,1,0:T(8,128)(2,1)} %get-tuple-element.119.keep, bf16[2,4,32,3456]{3,2,1,0:T(8,128)(2,1)} %copy-done.1, bf16[2,4,32,3456]{3,2,1,0:T(8,128)(2,1)} %copy-done.2), custom_call_target="tpu_custom_call" | custom-call | flops 2097152 | bytes 10616832 | tf_op jit(solution)/shard_map/pallas_call | solution.py:431
  108.4 2.2 %collective-permute-done.17.u2 = bf16[512,256]{1,0:T(8,128)(2,1)S(1)} collective-permute-done((bf16[512,256]{1,0:T(8,128)(2,1)}, bf16[512,256]{1,0:T(8,128)(2,1)S(1)}, u32[]{:S(2)}, u32[]{:S(2)}) %collective-permute-start.17) | collective-permute-done | bytes 262176 | tf_op jit(solution)/shard_map/ppermute | solution.py:33
  110.6 4.3 %collective-permute-done.18.u3 = bf16[512,256]{1,0:T(8,128)(2,1)S(1)} collective-permute-done((bf16[512,256]{1,0:T(8,128)(2,1)}, bf16[512,256]{1,0:T(8,128)(2,1)S(1)}, u32[]{:S(2)}, u32[]{:S(2)}) %collective-permute-start.18) | collective-permute-done | bytes 262176 | tf_op jit(solution)/shard_map/ppermute | solution.py:34
  115.6 5.0 %shard_map.177 = (bf16[512,1024]{1,0:T(8,128)(2,1)}, f32[512,256]{1,0:T(8,128)}, f32[512,256]{1,0:T(8,128)}, bf16[512,256]{1,0:T(8,128)(2,1)}, f32[8,256]{1,0:T(8,128)}) custom-call(s32[5]{0:T(128)} %stack.32.at.refs_0_, f32[512,256]{1,0:T(8,128)} %get-tuple-element.129.u_own, bf16[512,256]{1,0:T(8,128)(2,1)} %copy-done.15, bf16[512,256]{1,0:T(8,128)(2,1)} %copy-done.16, ...), custom_call_target="tpu_custom_call" | custom-call | flops 268435456 | bytes 6291456 | tf_op jit(solution)/shard_map/pallas_call | solution.py:645
  124.5 7.2 %shard_map.178 = (bf16[512,768]{1,0:T(8,128)(2,1)}, f32[512,256]{1,0:T(8,128)}, bf16[576,256]{1,0:T(8,128)(2,1)}, bf16[576,256]{1,0:T(8,128)(2,1)}, bf16[576,256]{1,0:T(8,128)(2,1)}, /*index=5*/f32[16,512]{1,0:T(8,128)}) custom-call(s32[5]{0:T(128)} %stack.32.at.refs_0_, bf16[512,256]{1,0:T(8,128)(2,1)} %rows_in.1, bf16[512,256]{1,0:T(8,128)(2,1)} %copy-done.11, ...), custom_call_target="tpu_custom_call" | custom-call | flops 805306368 | bytes 6291456 | tf_op jit(solution)/shard_map/pallas_call | solution.py:722
  133.0 3.2 %collective-permute-start.22 = (bf16[576,256]{1,0:T(8,128)(2,1)}, bf16[576,256]{1,0:T(8,128)(2,1)S(1)}, u32[]{:S(2)}, u32[]{:S(2)}) collective-permute-start(bf16[576,256]{1,0:T(8,128)(2,1)} %get-tuple-element.148), channel_id=1, source_target_pairs={{0,3},{1,0},{2,1},{3,2},{4,7},{5,4},{6,5},{7,6},{8,11},{9,8},{10,9... | collective-permute-start | bytes 884744 | tf_op jit(solution)/shard_map/ppermute | solution.py:843
  136.9 5.2 %shard_map.179 = (bf16[2,4,32,1024]{3,2,1,0:T(8,128)(2,1)}, bf16[2,4,32,1024]{3,2,1,0:T(8,128)(2,1)}, bf16[4,4,32,1024]{3,2,1,0:T(8,128)(2,1)}) custom-call(s32[5]{0:T(128)} %stack.32.at.refs_0_, bf16[512,1024]{1,0:T(8,128)(2,1)} %get-tuple-element.115.refs_1_, bf16[512,768]{1,0:T(8,128)(2,1)} %get-tuple-element.140.refs_2_, ...), custom_call_target="tpu_custom_call" | custom-call | flops 1073741824 | bytes 4194304 | tf_op jit(solution)/shard_map/pallas_call | solution.py:407
  144.1 5.4 %collective-permute-done.21.d2 = bf16[576,256]{1,0:T(8,128)(2,1)S(1)} collective-permute-done((bf16[576,256]{1,0:T(8,128)(2,1)}, bf16[576,256]{1,0:T(8,128)(2,1)S(1)}, u32[]{:S(2)}, u32[]{:S(2)}) %collective-permute-start.21) | collective-permute-done | bytes 294944 | tf_op jit(solution)/shard_map/ppermute | solution.py:843
  150.4 3.1 %shard_map.180 = (bf16[512,256]{1,0:T(8,128)(2,1)}, f32[1,256]{1,0:T(1,128)}) custom-call(f32[512,256]{1,0:T(8,128)} %get-tuple-element.145.d_own, bf16[576,256]{1,0:T(8,128)(2,1)} %copy-done.31, bf16[576,256]{1,0:T(8,128)(2,1)} %copy-done.32, bf16[576,256]{1,0:T(8,128)(2,1)} %copy-done.33, f32[16,512]{1,0:T(8,128)} %get-tuple-element.149.inner, ...), custom_call_target="tpu_custom_call" | custom-call | flops 8589934592 | bytes 2097152 | tf_op jit(solution)/shard_map/pallas_call | solution.py:576
  158.2 2.9 %shard_map.181 = (f32[128,1024]{1,0:T(8,128)}, bf16[144,1024]{1,0:T(8,128)(2,1)}, bf16[144,1024]{1,0:T(8,128)(2,1)}, bf16[144,1024]{1,0:T(8,128)(2,1)}) custom-call(s32[5]{0:T(128)} %stack.32.at.refs_0_, bf16[4,4,32,1024]{3,2,1,0:T(8,128)(2,1)} %get-tuple-element.142.keep, bf16[2,4,32,1024]{3,2,1,0:T(8,128)(2,1)} %copy-done.6, ...), custom_call_target="tpu_custom_call" | custom-call | flops 2097152 | bytes 4194304 | tf_op jit(solution)/shard_map/pallas_call | solution.py:471
  161.0 3.0 %collective-permute-start.26 = (bf16[512,256]{1,0:T(8,128)(2,1)S(1)}, bf16[512,256]{1,0:T(8,128)(2,1)S(1)}, u32[]{:S(2)}, u32[]{:S(2)}) collective-permute-start(bf16[512,256]{1,0:T(8,128)(2,1)S(1)} %copy-done.36), channel_id=1, source_target_pairs={{0,2},{1,3},{2,0},{3,1},{4,6},{5,7},{6,4},{7,5},{8,10},{9,11},{10,... | collective-permute-start | bytes 786440 | tf_op jit(solution)/shard_map/ppermute | solution.py:865
  166.9 2.2 %collective-permute-start.31 = (bf16[144,1024]{1,0:T(8,128)(2,1)}, bf16[144,1024]{1,0:T(8,128)(2,1)S(1)}, u32[]{:S(2)}, u32[]{:S(2)}) collective-permute-start(bf16[144,1024]{1,0:T(8,128)(2,1)} %get-tuple-element.169), channel_id=1, source_target_pairs={{0,24},{4,28},{8,0},{12,4},{16,8},{20,12},{24,16},{28,20},{32,56},... | collective-permute-start | bytes 884744 | tf_op jit(solution)/shard_map/ppermute | solution.py:867
  170.7 2.7 %collective-permute-start.28 = (bf16[512,256]{1,0:T(8,128)(2,1)S(1)}, bf16[512,256]{1,0:T(8,128)(2,1)S(1)}, u32[]{:S(2)}, u32[]{:S(2)}) collective-permute-start(bf16[512,256]{1,0:T(8,128)(2,1)S(1)} %copy-done.34), channel_id=1, source_target_pairs={{0,3},{1,0},{2,1},{3,2},{4,7},{5,4},{6,5},{7,6},{8,11},{9,8},{10,9... | collective-permute-start | bytes 786440 | tf_op jit(solution)/shard_map/ppermute | solution.py:865
  173.3 4.5 %collective-permute-done.27 = bf16[512,256]{1,0:T(8,128)(2,1)S(1)} collective-permute-done((bf16[512,256]{1,0:T(8,128)(2,1)S(1)}, bf16[512,256]{1,0:T(8,128)(2,1)S(1)}, u32[]{:S(2)}, u32[]{:S(2)}) %collective-permute-start.27) | collective-permute-done | bytes 262176 | tf_op jit(solution)/shard_map/ppermute | solution.py:865
  178.1 2.5 %collective-permute-done.30.m2 = bf16[144,1024]{1,0:T(8,128)(2,1)S(1)} collective-permute-done((bf16[144,1024]{1,0:T(8,128)(2,1)}, bf16[144,1024]{1,0:T(8,128)(2,1)S(1)}, u32[]{:S(2)}, u32[]{:S(2)}) %collective-permute-start.30) | collective-permute-done | bytes 294944 | tf_op jit(solution)/shard_map/ppermute | solution.py:867
  181.4 2.2 %shard_map.182 = (f32[32,1024]{1,0:T(8,128)}, bf16[48,1024]{1,0:T(8,128)(2,1)}, bf16[48,1024]{1,0:T(8,128)(2,1)}, bf16[48,1024]{1,0:T(8,128)(2,1)}, f32[8,256]{1,0:T(8,128)}) custom-call(s32[5]{0:T(128)} %stack.32.at.refs_0_, f32[128,1024]{1,0:T(8,128)} %get-tuple-element.174.own, bf16[144,1024]{1,0:T(8,128)(2,1)} %copy-done.8, bf16[144,1024]{1,0:T(8,128)(2,1)} %copy-done.9, ...), custom_call_target="tpu_custom_call" | custom-call | flops 2097152 | bytes 2097152 | tf_op jit(solution)/shard_map/pallas_call | solution.py:504
  183.6 3.0 %collective-permute-start.32 = (bf16[48,1024]{1,0:T(8,128)(2,1)}, bf16[48,1024]{1,0:T(8,128)(2,1)S(1)}, u32[]{:S(2)}, u32[]{:S(2)}) collective-permute-start(bf16[48,1024]{1,0:T(8,128)(2,1)} %get-tuple-element.179), channel_id=1, source_target_pairs={{0,64},{4,68},{8,72},{12,76},{16,80},{20,84},{24,88},{28,92},{32,9... | collective-permute-start | bytes 294920 | tf_op jit(solution)/shard_map/ppermute | solution.py:876
  187.2 2.6 %collective-permute-start.34 = (bf16[48,1024]{1,0:T(8,128)(2,1)}, bf16[48,1024]{1,0:T(8,128)(2,1)S(1)}, u32[]{:S(2)}, u32[]{:S(2)}) collective-permute-start(bf16[48,1024]{1,0:T(8,128)(2,1)} %get-tuple-element.181), channel_id=1, source_target_pairs={{0,96},{4,100},{8,104},{12,108},{16,112},{20,116},{24,120},{28,124... | collective-permute-start | bytes 294920 | tf_op jit(solution)/shard_map/ppermute | solution.py:876
  (173 shorter events, 59.1 us)
Async XLA Ops:
  7.2 51.0 %all-gather.2.cloned.1.call-start = ((), (), s32[]{:S(2)}) async-start(), calls=%async_computation.2 | async-start | bytes 1310720 | tf_op jit(solution)/shard_map/all_gather | solution.py:780
  7.2 15.4 %collective-permute-start = (bf16[512,256]{1,0:T(8,128)(2,1)}, bf16[512,256]{1,0:T(8,128)(2,1)S(1)}, u32[]{:S(2)}, u32[]{:S(2)}) collective-permute-start(bf16[512,256]{1,0:T(8,128)(2,1)} %rows_in.1), channel_id=1, source_target_pairs={{0,3},{1,0},{2,1},{3,2},{4,7},{5,4},{6,5},{7,6},{8,11},{9,8},{10,9... | collective-permute-start | bytes 786440 | tf_op jit(solution)/shard_map/ppermute | solution.py:34
  10.1 15.7 %collective-permute-start.1 = (bf16[512,256]{1,0:T(8,128)(2,1)}, bf16[512,256]{1,0:T(8,128)(2,1)S(1)}, u32[]{:S(2)}, u32[]{:S(2)}) collective-permute-start(bf16[512,256]{1,0:T(8,128)(2,1)} %rows_in.1), channel_id=1, source_target_pairs={{0,2},{1,3},{2,0},{3,1},{4,6},{5,7},{6,4},{7,5},{8,10},{9,11},{10,... | collective-permute-start | bytes 786440 | tf_op jit(solution)/shard_map/ppermute | solution.py:33
  10.9 15.9 %collective-permute-start.2 = (bf16[512,256]{1,0:T(8,128)(2,1)}, bf16[512,256]{1,0:T(8,128)(2,1)S(1)}, u32[]{:S(2)}, u32[]{:S(2)}) collective-permute-start(bf16[512,256]{1,0:T(8,128)(2,1)} %rows_in.1), channel_id=1, source_target_pairs={{0,1},{1,2},{2,3},{3,0},{4,5},{5,6},{6,7},{7,4},{8,9},{9,10},{10,1... | collective-permute-start | bytes 786440 | tf_op jit(solution)/shard_map/ppermute | solution.py:34
  12.8 29.6 %collective-permute-start.7 = (bf16[512,256]{1,0:T(8,128)(2,1)S(1)}, bf16[512,256]{1,0:T(8,128)(2,1)S(1)}, u32[]{:S(2)}, u32[]{:S(2)}) collective-permute-start(bf16[512,256]{1,0:T(8,128)(2,1)S(1)} %constant_dynamic-slice_fusion.2.p0), channel_id=1, source_target_pairs={{0,3},{1,0},{2,1},{3,2},{4,7},{5,4},{6,5},{7,6},{8,11},{9,8},{10,9... | collective-permute-start | bytes 786440 | tf_op jit(solution)/shard_map/ppermute | solution.py:34
  15.2 28.6 %collective-permute-start.8 = (bf16[512,256]{1,0:T(8,128)(2,1)S(1)}, bf16[512,256]{1,0:T(8,128)(2,1)S(1)}, u32[]{:S(2)}, u32[]{:S(2)}) collective-permute-start(bf16[512,256]{1,0:T(8,128)(2,1)S(1)} %constant_dynamic-slice_fusion.2.p0), channel_id=1, source_target_pairs={{0,2},{1,3},{2,0},{3,1},{4,6},{5,7},{6,4},{7,5},{8,10},{9,11},{10,... | collective-permute-start | bytes 786440 | tf_op jit(solution)/shard_map/ppermute | solution.py:33
  16.8 141.4 %reduce-scatter.3.cloned.1.call-start = ((), (), s32[]{:S(2)}) async-start(), calls=%async_computation.3 | async-start | bytes 4423680 | tf_op jit(solution)/shard_map/reduce_scatter | solution.py:744
  22.6 21.1 %collective-permute-start.9 = (bf16[512,256]{1,0:T(8,128)(2,1)S(1)}, bf16[512,256]{1,0:T(8,128)(2,1)S(1)}, u32[]{:S(2)}, u32[]{:S(2)}) collective-permute-start(bf16[512,256]{1,0:T(8,128)(2,1)S(1)} %constant_dynamic-slice_fusion.2.p0), channel_id=1, source_target_pairs={{0,1},{1,2},{2,3},{3,0},{4,5},{5,6},{6,7},{7,4},{8,9},{9,10},{10,1... | collective-permute-start | bytes 786440 | tf_op jit(solution)/shard_map/ppermute | solution.py:34
  38.4 14.9 %collective-permute-start.4 = (bf16[512,256]{1,0:T(8,128)(2,1)}, bf16[512,256]{1,0:T(8,128)(2,1)S(1)}, u32[]{:S(2)}, u32[]{:S(2)}) collective-permute-start(bf16[512,256]{1,0:T(8,128)(2,1)} %get-tuple-element.101.m0.refs_4_), channel_id=1, source_target_pairs={{0,3},{1,0},{2,1},{3,2},{4,7},{5,4},{6,5},{7,6},{8,11},{9,8},{10,9... | collective-permute-start | bytes 786440 | tf_op jit(solution)/shard_map/ppermute | solution.py:34
  40.9 12.4 %collective-permute-start.5 = (bf16[512,256]{1,0:T(8,128)(2,1)}, bf16[512,256]{1,0:T(8,128)(2,1)S(1)}, u32[]{:S(2)}, u32[]{:S(2)}) collective-permute-start(bf16[512,256]{1,0:T(8,128)(2,1)} %get-tuple-element.101.m0.refs_4_), channel_id=1, source_target_pairs={{0,2},{1,3},{2,0},{3,1},{4,6},{5,7},{6,4},{7,5},{8,10},{9,11},{10,... | collective-permute-start | bytes 786440 | tf_op jit(solution)/shard_map/ppermute | solution.py:33
  42.4 15.8 %collective-permute-start.6 = (bf16[512,256]{1,0:T(8,128)(2,1)}, bf16[512,256]{1,0:T(8,128)(2,1)S(1)}, u32[]{:S(2)}, u32[]{:S(2)}) collective-permute-start(bf16[512,256]{1,0:T(8,128)(2,1)} %get-tuple-element.101.m0.refs_4_), channel_id=1, source_target_pairs={{0,1},{1,2},{2,3},{3,0},{4,5},{5,6},{6,7},{7,4},{8,9},{9,10},{10,1... | collective-permute-start | bytes 786440 | tf_op jit(solution)/shard_map/ppermute | solution.py:34
  47.5 10.7 %collective-permute-start.10 = (bf16[512,1024]{1,0:T(8,128)(2,1)}, bf16[512,1024]{1,0:T(8,128)(2,1)S(1)}, u32[]{:S(2)}, u32[]{:S(2)}) collective-permute-start(bf16[512,1024]{1,0:T(8,128)(2,1)} %shard_map.172.half), channel_id=1, source_target_pairs={{0,4},{4,0},{8,12},{12,8},{16,20},{20,16},{24,28},{28,24},{32,36},... | collective-permute-start | bytes 3145736 | tf_op jit(solution)/shard_map/ppermute | solution.py:796
  78.8 16.0 %collective-permute-start.13 = (bf16[512,256]{1,0:T(8,128)(2,1)}, bf16[512,256]{1,0:T(8,128)(2,1)S(1)}, u32[]{:S(2)}, u32[]{:S(2)}) collective-permute-start(bf16[512,256]{1,0:T(8,128)(2,1)} %get-tuple-element.123), channel_id=1, source_target_pairs={{0,2},{1,3},{2,0},{3,1},{4,6},{5,7},{6,4},{7,5},{8,10},{9,11},{10,... | collective-permute-start | bytes 786440 | tf_op jit(solution)/shard_map/ppermute | solution.py:821
  81.3 13.5 %collective-permute-start.14 = (bf16[512,256]{1,0:T(8,128)(2,1)}, bf16[512,256]{1,0:T(8,128)(2,1)S(1)}, u32[]{:S(2)}, u32[]{:S(2)}) collective-permute-start(bf16[512,256]{1,0:T(8,128)(2,1)} %get-tuple-element.124), channel_id=1, source_target_pairs={{0,1},{1,2},{2,3},{3,0},{4,5},{5,6},{6,7},{7,4},{8,9},{9,10},{10,1... | collective-permute-start | bytes 786440 | tf_op jit(solution)/shard_map/ppermute | solution.py:821
  81.3 13.5 %collective-permute-start.15 = (bf16[512,256]{1,0:T(8,128)(2,1)}, bf16[512,256]{1,0:T(8,128)(2,1)S(1)}, u32[]{:S(2)}, u32[]{:S(2)}) collective-permute-start(bf16[512,256]{1,0:T(8,128)(2,1)} %get-tuple-element.125), channel_id=1, source_target_pairs={{0,3},{1,0},{2,1},{3,2},{4,7},{5,4},{6,5},{7,6},{8,11},{9,8},{10,9... | collective-permute-start | bytes 786440 | tf_op jit(solution)/shard_map/ppermute | solution.py:821
  94.3 6.9 %collective-permute-start.12 = (bf16[2,4,32,3456]{3,2,1,0:T(8,128)(2,1)}, bf16[2,4,32,3456]{3,2,1,0:T(8,128)(2,1)S(1)}, u32[]{:S(2)}, u32[]{:S(2)}) collective-permute-start(bf16[2,4,32,3456]{3,2,1,0:T(8,128)(2,1)} %get-tuple-element.121), channel_id=1, source_target_pairs={{0,4},{4,0},{8,12},{12,8},{16,20},{20,16},{24,28},{28,24},{32,36},... | collective-permute-start | bytes 5308424 | tf_op jit(solution)/shard_map/ppermute | solution.py:420
  98.4 10.0 %collective-permute-start.16 = (bf16[512,256]{1,0:T(8,128)(2,1)}, bf16[512,256]{1,0:T(8,128)(2,1)S(1)}, u32[]{:S(2)}, u32[]{:S(2)}) collective-permute-start(bf16[512,256]{1,0:T(8,128)(2,1)} %get-tuple-element.128), channel_id=1, source_target_pairs={{0,3},{1,0},{2,1},{3,2},{4,7},{5,4},{6,5},{7,6},{8,11},{9,8},{10,9... | collective-permute-start | bytes 786440 | tf_op jit(solution)/shard_map/ppermute | solution.py:34
  99.6 11.0 %collective-permute-start.17 = (bf16[512,256]{1,0:T(8,128)(2,1)}, bf16[512,256]{1,0:T(8,128)(2,1)S(1)}, u32[]{:S(2)}, u32[]{:S(2)}) collective-permute-start(bf16[512,256]{1,0:T(8,128)(2,1)} %get-tuple-element.128), channel_id=1, source_target_pairs={{0,2},{1,3},{2,0},{3,1},{4,6},{5,7},{6,4},{7,5},{8,10},{9,11},{10,... | collective-permute-start | bytes 786440 | tf_op jit(solution)/shard_map/ppermute | solution.py:33
  101.2 13.7 %collective-permute-start.18 = (bf16[512,256]{1,0:T(8,128)(2,1)}, bf16[512,256]{1,0:T(8,128)(2,1)S(1)}, u32[]{:S(2)}, u32[]{:S(2)}) collective-permute-start(bf16[512,256]{1,0:T(8,128)(2,1)} %get-tuple-element.128), channel_id=1, source_target_pairs={{0,1},{1,2},{2,3},{3,0},{4,5},{5,6},{6,7},{7,4},{8,9},{9,10},{10,1... | collective-permute-start | bytes 786440 | tf_op jit(solution)/shard_map/ppermute | solution.py:34
  114.9 82.8 %reduce-scatter.5.cloned.1.call-start = ((), (), s32[]{:S(2)}) async-start(), calls=%async_computation.4 | async-start | bytes 1105920 | tf_op jit(solution)/shard_map/reduce_scatter | solution.py:744
  131.7 12.4 %collective-permute-start.20 = (bf16[576,256]{1,0:T(8,128)(2,1)}, bf16[576,256]{1,0:T(8,128)(2,1)S(1)}, u32[]{:S(2)}, u32[]{:S(2)}) collective-permute-start(bf16[576,256]{1,0:T(8,128)(2,1)} %get-tuple-element.146), channel_id=1, source_target_pairs={{0,2},{1,3},{2,0},{3,1},{4,6},{5,7},{6,4},{7,5},{8,10},{9,11},{10,... | collective-permute-start | bytes 884744 | tf_op jit(solution)/shard_map/ppermute | solution.py:843
  133.0 16.6 %collective-permute-start.21 = (bf16[576,256]{1,0:T(8,128)(2,1)}, bf16[576,256]{1,0:T(8,128)(2,1)S(1)}, u32[]{:S(2)}, u32[]{:S(2)}) collective-permute-start(bf16[576,256]{1,0:T(8,128)(2,1)} %get-tuple-element.147), channel_id=1, source_target_pairs={{0,1},{1,2},{2,3},{3,0},{4,5},{5,6},{6,7},{7,4},{8,9},{9,10},{10,1... | collective-permute-start | bytes 884744 | tf_op jit(solution)/shard_map/ppermute | solution.py:843
  133.0 16.6 %collective-permute-start.22 = (bf16[576,256]{1,0:T(8,128)(2,1)}, bf16[576,256]{1,0:T(8,128)(2,1)S(1)}, u32[]{:S(2)}, u32[]{:S(2)}) collective-permute-start(bf16[576,256]{1,0:T(8,128)(2,1)} %get-tuple-element.148), channel_id=1, source_target_pairs={{0,3},{1,0},{2,1},{3,2},{4,7},{5,4},{6,5},{7,6},{8,11},{9,8},{10,9... | collective-permute-start | bytes 884744 | tf_op jit(solution)/shard_map/ppermute | solution.py:843
  142.1 14.0 %collective-permute-start.24 = (bf16[2,4,32,1024]{3,2,1,0:T(8,128)(2,1)}, bf16[2,4,32,1024]{3,2,1,0:T(8,128)(2,1)S(1)}, u32[]{:S(2)}, u32[]{:S(2)}) collective-permute-start(bf16[2,4,32,1024]{3,2,1,0:T(8,128)(2,1)} %get-tuple-element.155), channel_id=1, source_target_pairs={{0,4},{4,0},{8,12},{12,8},{16,20},{20,16},{24,28},{28,24},{32,36},... | collective-permute-start | bytes 1572872 | tf_op jit(solution)/shard_map/ppermute | solution.py:420
  144.1 12.0 %collective-permute-start.25 = (bf16[2,4,32,1024]{3,2,1,0:T(8,128)(2,1)}, bf16[2,4,32,1024]{3,2,1,0:T(8,128)(2,1)S(1)}, u32[]{:S(2)}, u32[]{:S(2)}) collective-permute-start(bf16[2,4,32,1024]{3,2,1,0:T(8,128)(2,1)} %get-tuple-element.156), channel_id=1, source_target_pairs={{0,4},{4,0},{8,12},{12,8},{16,20},{20,16},{24,28},{28,24},{32,36},... | collective-permute-start | bytes 1572872 | tf_op jit(solution)/shard_map/ppermute | solution.py:420
  161.0 9.6 %collective-permute-start.26 = (bf16[512,256]{1,0:T(8,128)(2,1)S(1)}, bf16[512,256]{1,0:T(8,128)(2,1)S(1)}, u32[]{:S(2)}, u32[]{:S(2)}) collective-permute-start(bf16[512,256]{1,0:T(8,128)(2,1)S(1)} %copy-done.36), channel_id=1, source_target_pairs={{0,2},{1,3},{2,0},{3,1},{4,6},{5,7},{6,4},{7,5},{8,10},{9,11},{10,... | collective-permute-start | bytes 786440 | tf_op jit(solution)/shard_map/ppermute | solution.py:865
  164.0 14.0 %collective-permute-start.29 = (bf16[144,1024]{1,0:T(8,128)(2,1)}, bf16[144,1024]{1,0:T(8,128)(2,1)S(1)}, u32[]{:S(2)}, u32[]{:S(2)}) collective-permute-start(bf16[144,1024]{1,0:T(8,128)(2,1)} %get-tuple-element.167), channel_id=1, source_target_pairs={{0,16},{4,20},{8,24},{12,28},{16,0},{20,4},{24,8},{28,12},{32,48},... | collective-permute-start | bytes 884744 | tf_op jit(solution)/shard_map/ppermute | solution.py:867
  165.9 14.7 %collective-permute-start.30 = (bf16[144,1024]{1,0:T(8,128)(2,1)}, bf16[144,1024]{1,0:T(8,128)(2,1)S(1)}, u32[]{:S(2)}, u32[]{:S(2)}) collective-permute-start(bf16[144,1024]{1,0:T(8,128)(2,1)} %get-tuple-element.168), channel_id=1, source_target_pairs={{0,8},{4,12},{8,16},{12,20},{16,24},{20,28},{24,0},{28,4},{32,40},... | collective-permute-start | bytes 884744 | tf_op jit(solution)/shard_map/ppermute | solution.py:867
  166.9 13.6 %collective-permute-start.31 = (bf16[144,1024]{1,0:T(8,128)(2,1)}, bf16[144,1024]{1,0:T(8,128)(2,1)S(1)}, u32[]{:S(2)}, u32[]{:S(2)}) collective-permute-start(bf16[144,1024]{1,0:T(8,128)(2,1)} %get-tuple-element.169), channel_id=1, source_target_pairs={{0,24},{4,28},{8,0},{12,4},{16,8},{20,12},{24,16},{28,20},{32,56},... | collective-permute-start | bytes 884744 | tf_op jit(solution)/shard_map/ppermute | solution.py:867
  169.2 8.6 %collective-permute-start.27 = (bf16[512,256]{1,0:T(8,128)(2,1)S(1)}, bf16[512,256]{1,0:T(8,128)(2,1)S(1)}, u32[]{:S(2)}, u32[]{:S(2)}) collective-permute-start(bf16[512,256]{1,0:T(8,128)(2,1)S(1)} %copy-done.35), channel_id=1, source_target_pairs={{0,1},{1,2},{2,3},{3,0},{4,5},{5,6},{6,7},{7,4},{8,9},{9,10},{10,1... | collective-permute-start | bytes 786440 | tf_op jit(solution)/shard_map/ppermute | solution.py:865
  170.7 7.4 %collective-permute-start.28 = (bf16[512,256]{1,0:T(8,128)(2,1)S(1)}, bf16[512,256]{1,0:T(8,128)(2,1)S(1)}, u32[]{:S(2)}, u32[]{:S(2)}) collective-permute-start(bf16[512,256]{1,0:T(8,128)(2,1)S(1)} %copy-done.34), channel_id=1, source_target_pairs={{0,3},{1,0},{2,1},{3,2},{4,7},{5,4},{6,5},{7,6},{8,11},{9,8},{10,9... | collective-permute-start | bytes 786440 | tf_op jit(solution)/shard_map/ppermute | solution.py:865
  183.6 7.1 %collective-permute-start.32 = (bf16[48,1024]{1,0:T(8,128)(2,1)}, bf16[48,1024]{1,0:T(8,128)(2,1)S(1)}, u32[]{:S(2)}, u32[]{:S(2)}) collective-permute-start(bf16[48,1024]{1,0:T(8,128)(2,1)} %get-tuple-element.179), channel_id=1, source_target_pairs={{0,64},{4,68},{8,72},{12,76},{16,80},{20,84},{24,88},{28,92},{32,9... | collective-permute-start | bytes 294920 | tf_op jit(solution)/shard_map/ppermute | solution.py:876
  (51 other events, 300.4 us)
Sparse Core Ops, SparseCore 0:
  16.9 35.9 all-gather.1
  115.0 43.0 reduce-scatter.2
  160.5 22.3 reduce-scatter.4

commit v5 on v4

--- a/solution.py
+++ b/solution.py
@@ -252,10 +252,17 @@
     planes,
     down,
     cotangent,
-    h, h_own, rms, normed, act, d_gate_up, d_own, d1, d2, d3, f0, f1, f2, f3,
-    w_out, w_in, w_down, g_rows, mixed, acc, down_acc, sem,
+    h_out, h_own, rms, normed_out, act_out, d_out, d_own, d1, d2, d3, f0, f1, f2, f3,
+    w_out, w_in, w_down, g_rows, mixed, acc, down_acc, h, normed, act, d_gate_up, sem, out_sem,
 ):
     x, core = at[0], at[1]
+    leaving = []
+
+    def leave(source, target):
+        copy = pltpu.make_async_copy(source, target, out_sem.at[len(leaving)])
+        copy.start()
+        leaving.append(copy)
+
     width = x0.shape[1]
     units = down.shape[1]
     step = units // 3
@@ -296,12 +303,14 @@
         columns = slice(j * width, (j + 1) * width)
         scale = gain[:, rel_rows(x, j, width)]
         normed[:, columns] = (h[:, columns] * r * scale).astype(BF16)
+    leave(h, h_out)
+    leave(normed, normed_out)
     for copy in planes_in + rest:
         copy.wait()
 
-    def part(i, carry):
-        f = pl.ds(pl.multiple_of(i * step, 128), step)
-        f_up = pl.ds(pl.multiple_of(units + i * step, 128), step)
+    for i in range(3):
+        f = slice(i * step, (i + 1) * step)
+        f_up = slice(units + i * step, units + (i + 1) * step)
         gate = dot_nn(normed[...], w_in[0, :, f])
         up = dot_nn(normed[...], w_in[1, :, f])
         d_act = dot_nn(g_rows[...], w_down[:, f])
@@ -312,24 +321,26 @@
         for j in range(CH):
             rows = slice(j * width, (j + 1) * width)
             term = dot_nt(active, w_down[rows, f])
-            down_acc[j] = jnp.where(i == 0, term, down_acc[j] + term)
+            down_acc[j] = term if i == 0 else down_acc[j] + term
         d_gate = (d_act * up * sigma * (1.0 + gate * (1.0 - sigma))).astype(BF16)
         d_up = (d_act * swish).astype(BF16)
         d_gate_up[:, f] = d_gate
         d_gate_up[:, f_up] = d_up
+        leave(act.at[:, f], act_out.at[:, f])
+        leave(d_gate_up.at[:, f], d_out.at[:, f])
+        leave(d_gate_up.at[:, f_up], d_out.at[:, f_up])
         for j in range(CH):
             rows = slice(j * width, (j + 1) * width)
             term = dot_nt(d_gate, w_in[0, rows, f]) + dot_nt(d_up, w_in[1, rows, f])
-            acc[j] = jnp.where(i == 0, term, acc[j] + term)
-        return carry
-
-    lax.fori_loop(0, 3, part, 0)
+            acc[j] = term if i == 0 else acc[j] + term
     d_own[...] = acc[0]
     d1[...] = acc[1].astype(BF16)
     d2[...] = acc[2].astype(BF16)
     d3[...] = acc[3].astype(BF16)
     for j, out in enumerate((f0, f1, f2, f3)):
         out[...] = down_acc[lax.rem(x + j, CH)].astype(BF16)
+    for copy in leaving:
+        copy.wait()
 
 
 def ffn(at, pieces, mixed_pieces, gain, half, other, planes, down, cotangent):
@@ -350,7 +361,7 @@
         )
         + (block,) * 7,
         in_specs=[smem()] + [vmem()] * 9 + [anywhere()] * 5,
-        out_specs=(vmem(),) * 14,
+        out_specs=(anywhere(), vmem(), vmem()) + (anywhere(),) * 3 + (vmem(),) * 8,
         scratch_shapes=[
             pltpu.VMEM((2, features // 2, features), BF16),
             pltpu.VMEM((2, features, units), BF16),
@@ -359,7 +370,12 @@
             pltpu.VMEM((rows, features), BF16),
             pltpu.VMEM((CH, rows, width), F32),
             pltpu.VMEM((CH, rows, width), F32),
+            pltpu.VMEM((rows, features), F32),
+            pltpu.VMEM((rows, features), BF16),
+            pltpu.VMEM((rows, units), BF16),
+            pltpu.VMEM((rows, 2 * units), BF16),
             pltpu.SemaphoreType.DMA((8,)),
+            pltpu.SemaphoreType.DMA((11,)),
         ],
         compiler_params=params(56),
         cost_estimate=cost(rows * features * (features + 6 * units), 20 * 2**20),
@@ -518,7 +534,7 @@
     )(at, own, *messages, small)
 
 
-def last_kernel(own, m1, m2, m3, small, in_out, out_out, small_out):
+def last_kernel(own, m1, m2, m3, small, in_out, out_out, conv_out, gain_one, gain_two):
     rows = own.shape[0]
     width = small.shape[1]
     total = own[...]
@@ -529,7 +545,9 @@
     for k in range(3):
         in_out[k] = total[:, k * width : (k + 1) * width]
     out_out[...] = total[:, 3 * width :]
-    small_out[...] = small_sum
+    conv_out[...] = small_sum[:3]
+    gain_one[...] = small_sum[3:4]
+    gain_two[...] = small_sum[4:5]
 
 
 def last(own, messages, small):
@@ -540,16 +558,20 @@
         out_shape=(
             shape((3, rows, width), F32),
             shape((rows, columns - 3 * width), F32),
-            shape(small.shape, F32),
+            shape((3, width), F32),
+            shape((1, width), F32),
+            shape((1, width), F32),
         ),
         in_specs=[vmem()] * 5,
-        out_specs=(vmem(),) * 3,
+        out_specs=(vmem(),) * 5,
         compiler_params=params(56),
         cost_estimate=cost(2**20, 2**20),
     )(own, *messages, small)
 
 
-def end_kernel(d_own, d1, d2, d3, inner, d_hidden, rows_in, rms, gain, grad, gain_grad):
+def end_kernel(
+    d_own, d1, d2, d3, inner, d_hidden, rows_in, rms, gain, conv_grad, gain_two, grad, small
+):
     rows, width = d_own.shape
     total = d_own[...]
     line = inner[...]
@@ -565,22 +587,25 @@
     )
     r = rms[...]
     xs = rows_in[...].astype(F32)
-    gain_grad[...] = jnp.sum(total * xs * r, axis=0, keepdims=True)
+    small[0:3] = conv_grad[...]
+    small[3:4] = jnp.sum(total * xs * r, axis=0, keepdims=True)
+    small[4:5] = gain_two[...]
+    small[5:8] = jnp.zeros((3, width), F32)
     grad[...] = (
         d_hidden[...] + r * gain[...] * total - xs * (r * r * r / (CH * width)) * column
     ).astype(BF16)
 
 
-def end(d_own, received, inner, d_hidden, rows_in, rms, gain):
+def end(d_own, received, inner, d_hidden, rows_in, rms, gain, conv_grad, gain_two):
     rows, width = d_own.shape
     return pl.pallas_call(
         end_kernel,
-        out_shape=(shape((rows, width), BF16), shape((1, width), F32)),
-        in_specs=[vmem()] * 9,
+        out_shape=(shape((rows, width), BF16), shape((8, width), F32)),
+        in_specs=[vmem()] * 11,
         out_specs=(vmem(),) * 2,
         compiler_params=params(56),
         cost_estimate=cost(2**32, 2**21),
-    )(d_own, *received, inner, d_hidden, rows_in, rms, gain[None])
+    )(d_own, *received, inner, d_hidden, rows_in, rms, gain[None], conv_grad, gain_two)
 
 
 def norm_kernel(d_own, d1, d2, d3, h, rms, gain, cotangent, u, u_low, gain_grad):
@@ -828,6 +853,8 @@
     )
     u_pieces = [u_own] + gather_ch(u_low)[1:]
     ffn_kept = add_cores(keep, got)
+    ffn_kept, *down_parts = tie(ffn_kept, *down_parts)
+    downs = [lax.ppermute(down_parts[j], "ch", ch_pairs(j)) for j in (2, 1, 3)]
     ffn_kept, *u_pieces = tie(ffn_kept, *u_pieces)
     groups = [[seq_index(i, k, c) for k in range(4)] for i in range(4) for c in range(2)]
     ffn_sum = scatter_groups(ffn_kept, groups)
@@ -836,10 +863,15 @@
         at, u_pieces, hidden, r_two, grad_full, out_weight, c_gate, conv_out
     )
     following = from_behind(edge, "seq", -1)
+    following, *downs = tie(following, *downs)
     d_proj, d_own, d_one, d_two, d_three, inner = back_project(
         at, pieces, d_conv, following, conv_weight, value_rows, b_gate, d_cgate, norm1_gain,
         in_planes,
     )
+    block_output = hidden_own + down_parts[0].astype(F32)
+    for down in downs:
+        block_output = block_output + down.astype(F32)
+    block_output = block_output.astype(BF16)
     received = [lax.ppermute(d, "ch", ch_pairs(j)) for j, d in ((2, d_two), (1, d_one), (3, d_three))]
 
     *gives, keep = pair_products(at, normed_one, d_proj, d_branch, mixed_rows, True, True)
@@ -852,43 +884,33 @@
         ],
         axis=0,
     )
-    input_grad, grad_gain_one = end(
-        d_own, received, inner, d_hidden, block_input, r_one, own_one
-    )
-    small = jnp.concatenate(
-        [grad_conv, grad_gain_one, grad_gain_two, jnp.zeros((3, width), F32)], axis=0
+    input_grad, small = end(
+        d_own, received, inner, d_hidden, block_input, r_one, own_one, grad_conv, grad_gain_two
     )
     small = small + lax.ppermute(small, "seq", seq_pairs(0, 0, 1))
     small, ffn_sum, *got = tie(small, ffn_sum, *got)
     own, *messages = send_z(at, keep, got, small)
-    down_parts, messages = lax.optimization_barrier((down_parts, messages))
-    downs = [lax.ppermute(down_parts[j], "ch", ch_pairs(j)) for j in (2, 1, 3)]
     messages = [
         lax.ppermute(m, "seq", seq_pairs(0, j, 0)) for j, m in ((2, messages[1]), (1, messages[0]), (3, messages[2]))
     ]
-    downs, messages = lax.optimization_barrier((downs, messages))
-    block_output = hidden_own + down_parts[0].astype(F32)
-    for down in downs:
-        block_output = block_output + down.astype(F32)
-    block_output = block_output.astype(BF16)
     own, *messages, small = turn(at, own, messages, small)
     messages = [
         lax.ppermute(m, "seq", seq_pairs(j, 0, 0)) for j, m in ((2, messages[1]), (1, messages[0]), (3, messages[2]))
     ]
-    grad_in, grad_out, small = last(own, messages, small)
-
     groups = [[seq_index(k, i, c) for k in range(4)] for i in range(4) for c in range(2)]
     ffn_sum = scatter_groups(ffn_sum, groups).astype(F32)
     grad_ffn_in = ffn_sum[:, : 2 * hidden_units].reshape(-1, 2, hidden_units)
     grad_ffn_out = ffn_sum[:, 2 * hidden_units :]
+    grad_ffn_in, grad_ffn_out, *messages = tie(grad_ffn_in, grad_ffn_out, *messages)
+    grad_in, grad_out, grad_conv, grad_gain_one, grad_gain_two = last(own, messages, small)
     return (
         block_output,
         input_grad,
-        small[3],
+        grad_gain_one.reshape(-1),
         jnp.transpose(grad_in, (1, 0, 2)),
-        small[:3],
+        grad_conv,
         grad_out,
-        small[4],
+        grad_gain_two.reshape(-1),
         grad_ffn_in,
         grad_ffn_out,
     )

time: 208 us -> 204 us (0.981)
  local copies, waits for them, and re-layouts: 22.8 us -> 19 us
    ppermute x3, waiting for transfers between devices: 2.5 us -> 10.2 us  [shards(): lax.ppermute(m, 'seq', seq_pairs(0, j, 0))]
    ppermute x3, waiting for transfers between devices: 6.1 us -> 2.23 us  [shards(): downs = [lax.ppermute(down_parts[j], 'ch', ch_pairs(j)) for j in (2, 1, 3)]]
    slice x2 -> x0, local copies, waits for them, and re-layouts: 2.63 us -> none  [the longest x1 1.34 us: shards(): small[4]]
    unnamed x90 -> x88, local copies, waits for them, and re-layouts: 9.8 us -> 9.43 us
  transfers between devices with their start and end apart: 38 -> 38, of which waited for: 15 -> 14; matrix products, arithmetic and copies ran while one was open for 7% -> 8% of each run, Pallas kernels for 27% -> 27%
where the time goes in v5:
time: 204 us; the launch traced here: 203 us
  Pallas kernels  74.1 us (36%)
  starting transfers between devices  51.5 us (25%)
  waiting for transfers between devices  38.5 us (19%)
  local copies, waits for them, and re-layouts  19 us (9%)
  between operations  14.1 us (7%)
  other arithmetic  5.85 us (3%)
    pallas_call x1, Pallas kernels, ffn(): pl.pallas_call(ffn_kernel, out_shape=(shape((rows, features), F32), shape...  18.3 us
    pallas_call x2, Pallas kernels, pair_products(): pl.pallas_call(body, grid=(4,), out_shape=(half, half, out), in_specs=[sm...  14.9 us
    ppermute x8, waiting for transfers between devices, gather_ch(): near = [lax.ppermute(block, 'ch', ch_pairs(-j)) for j in (1, 3)]  13.9 us
    ppermute x8, starting transfers between devices, gather_ch(): near = [lax.ppermute(block, 'ch', ch_pairs(-j)) for j in (1, 3)]  11.3 us
    ppermute x6, starting transfers between devices, shards(): lax.ppermute(d, 'ch', ch_pairs(j))  10.7 us
    ppermute x3, waiting for transfers between devices, shards(): lax.ppermute(m, 'seq', seq_pairs(0, j, 0))  10.2 us
    unnamed x88, local copies, waits for them, and re-layouts  9.43 us
    ppermute x3, starting transfers between devices, shards(): lax.ppermute(m, 'seq', seq_pairs(0, j, 0))  6.75 us
  transfers between devices with their start and end apart: 38, of which 14 were waited for; matrix products, arithmetic and copies ran while one was open for 8% of the time, Pallas kernels for 27%

profile of v5, /device:TPU:0, one launch (start us, length us, event | category | flops | bytes accessed | tf_op | source)
XLA Modules:
  0.0 203.1 jit_solution(9833677252837834378)
XLA Ops:
  7.2 2.9 %collective-permute-start = (bf16[512,256]{1,0:T(8,128)(2,1)}, bf16[512,256]{1,0:T(8,128)(2,1)S(1)}, u32[]{:S(2)}, u32[]{:S(2)}) collective-permute-start(bf16[512,256]{1,0:T(8,128)(2,1)} %rows_in.1), channel_id=1, source_target_pairs={{0,3},{1,0},{2,1},{3,2},{4,7},{5,4},{6,5},{7,6},{8,11},{9,8},{10,9... | collective-permute-start | bytes 786440 | tf_op jit(solution)/shard_map/ppermute | solution.py:34
  12.8 2.4 %collective-permute-start.7 = (bf16[512,256]{1,0:T(8,128)(2,1)S(1)}, bf16[512,256]{1,0:T(8,128)(2,1)S(1)}, u32[]{:S(2)}, u32[]{:S(2)}) collective-permute-start(bf16[512,256]{1,0:T(8,128)(2,1)S(1)} %constant_dynamic-slice_fusion.2.p0), channel_id=1, source_target_pairs={{0,3},{1,0},{2,1},{3,2},{4,7},{5,4},{6,5},{7,6},{8,11},{9,8},{10,9... | collective-permute-start | bytes 786440 | tf_op jit(solution)/shard_map/ppermute | solution.py:34
  18.7 3.9 %collective-permute-done.p1.x1 = bf16[512,256]{1,0:T(8,128)(2,1)S(1)} collective-permute-done((bf16[512,256]{1,0:T(8,128)(2,1)}, bf16[512,256]{1,0:T(8,128)(2,1)S(1)}, u32[]{:S(2)}, u32[]{:S(2)}) %collective-permute-start) | collective-permute-done | bytes 262176 | tf_op jit(solution)/shard_map/ppermute | solution.py:34
  27.5 5.1 %shard_map.169 = (bf16[512,1024]{1,0:T(8,128)(2,1)}, f32[512,1]{1,0:T(8,128)}, f32[512,256]{1,0:T(8,128)}, f32[512,256]{1,0:T(8,128)}, f32[512,256]{1,0:T(8,128)...) custom-call(s32[5]{0:T(128)} %stack.35.at.refs_0_, bf16[512,256]{1,0:T(8,128)(2,1)} %rows_in.1, ...), custom_call_target="tpu_custom_call" | custom-call | flops 805306368 | bytes 6291456 | tf_op jit(solution)/shard_map/pallas_call | solution.py:157
  36.0 2.5 %shard_map.170 = (bf16[512,256]{1,0:T(8,128)(2,1)}, f32[512,256]{1,0:T(8,128)}, bf16[512,256]{1,0:T(8,128)(2,1)}, bf16[512,256]{1,0:T(8,128)(2,1)}) custom-call(s32[5]{0:T(128)} %stack.35.at.refs_0_, bf16[512,256]{1,0:T(8,128)(2,1)} %get-tuple-element.101.gated, bf16[16,256]{1,0:T(8,128)(2,1)} %copy-done.28, f32[512,256]{1,0:T(8,128)} %get-tuple-element.103.c_gate, ...), custom_call_target="tpu_custom_call" | custom-call | flops 8388608 | bytes 2097152 | tf_op jit(solution)/shard_map/pallas_call | solution.py:219
  38.5 2.5 %collective-permute-start.4 = (bf16[512,256]{1,0:T(8,128)(2,1)}, bf16[512,256]{1,0:T(8,128)(2,1)S(1)}, u32[]{:S(2)}, u32[]{:S(2)}) collective-permute-start(bf16[512,256]{1,0:T(8,128)(2,1)} %get-tuple-element.104.m0.refs_4_), channel_id=1, source_target_pairs={{0,3},{1,0},{2,1},{3,2},{4,7},{5,4},{6,5},{7,6},{8,11},{9,8},{10,9... | collective-permute-start | bytes 786440 | tf_op jit(solution)/shard_map/ppermute | solution.py:34
  45.2 2.3 %shard_map.172.half = bf16[512,1024]{1,0:T(8,128)(2,1)} custom-call(bf16[512,256]{1,0:T(8,128)(2,1)} %copy-done.4, bf16[512,256]{1,0:T(8,128)(2,1)} %copy-done.20, bf16[512,256]{1,0:T(8,128)(2,1)} %copy-done.21, bf16[512,256]{1,0:T(8,128)(2,1)} %copy-done.22), custom_call_target="tpu_custom_call" | custom-call | flops 2097152 | bytes 2097152 | tf_op jit(solution)/shard_map/pallas_call | solution.py:187
  50.6 2.8 %copy.21 = bf16[1024,2,1152]{2,0,1:T(8,128)(2,1)} copy(bf16[1024,2,1152]{2,1,0:T(2,128)(2,1)S(1)} %bitcast.23) | data formatting | bytes 9437184 | tf_op jit(solution)/shard_map/optimization_barrier | solution.py:67
  53.4 4.8 %collective-permute-done.6.m3 = bf16[512,256]{1,0:T(8,128)(2,1)S(1)} collective-permute-done((bf16[512,256]{1,0:T(8,128)(2,1)}, bf16[512,256]{1,0:T(8,128)(2,1)S(1)}, u32[]{:S(2)}, u32[]{:S(2)}) %collective-permute-start.6) | collective-permute-done | bytes 262176 | tf_op jit(solution)/shard_map/ppermute | solution.py:34
  59.2 18.3 %shard_map.173 = (f32[512,1024]{1,0:T(8,128)}, f32[512,256]{1,0:T(8,128)}, f32[512,1]{1,0:T(8,128)}, bf16[512,1024]{1,0:T(8,128)(2,1)}, bf16[512,1152]{1,0:T(8,1...) custom-call(s32[5]{0:T(128)} %stack.35.at.refs_0_, ...), custom_call_target="tpu_custom_call" | custom-call | flops 8321499136 | bytes 20971520 | tf_op jit(solution)/shard_map/pallas_call | solution.py:351
  77.5 2.5 %collective-permute-start.13 = (bf16[512,256]{1,0:T(8,128)(2,1)}, bf16[512,256]{1,0:T(8,128)(2,1)S(1)}, u32[]{:S(2)}, u32[]{:S(2)}) collective-permute-start(bf16[512,256]{1,0:T(8,128)(2,1)} %get-tuple-element.127), channel_id=1, source_target_pairs={{0,2},{1,3},{2,0},{3,1},{4,6},{5,7},{6,4},{7,5},{8,10},{9,11},{10,... | collective-permute-start | bytes 786440 | tf_op jit(solution)/shard_map/ppermute | solution.py:846
  80.0 3.2 %collective-permute-start.15 = (bf16[512,256]{1,0:T(8,128)(2,1)}, bf16[512,256]{1,0:T(8,128)(2,1)S(1)}, u32[]{:S(2)}, u32[]{:S(2)}) collective-permute-start(bf16[512,256]{1,0:T(8,128)(2,1)} %get-tuple-element.129), channel_id=1, source_target_pairs={{0,3},{1,0},{2,1},{3,2},{4,7},{5,4},{6,5},{7,6},{8,11},{9,8},{10,9... | collective-permute-start | bytes 786440 | tf_op jit(solution)/shard_map/ppermute | solution.py:846
  83.2 9.8 %shard_map.174 = (bf16[2,4,32,3456]{3,2,1,0:T(8,128)(2,1)}, bf16[2,4,32,3456]{3,2,1,0:T(8,128)(2,1)}, bf16[4,4,32,3456]{3,2,1,0:T(8,128)(2,1)}) custom-call(s32[5]{0:T(128)} %stack.35.at.refs_0_, bf16[512,1024]{1,0:T(8,128)(2,1)} %get-tuple-element.114.refs_1_, bf16[512,2304]{1,0:T(8,128)(2,1)} %get-tuple-element.115.refs_2_, ...), custom_call_target="tpu_custom_call" | custom-call | flops 3623878656 | bytes 14155776 | tf_op jit(solution)/shard_map/pallas_call | solution.py:423
  94.4 2.7 %shard_map.176 = (f32[512,256]{1,0:T(8,128)}, bf16[512,256]{1,0:T(8,128)(2,1)}, f32[1,256]{1,0:T(1,128)}) custom-call(f32[512,256]{1,0:T(8,128)} %get-tuple-element.126.d_own, bf16[512,256]{1,0:T(8,128)(2,1)} %copy-done.39, bf16[512,256]{1,0:T(8,128)(2,1)} %copy-done.40, bf16[512,256]{1,0:T(8,128)(2,1)} %copy-done.41, f32[512,256]{1,0:T(8,128)} %get-tuple-element.113.h, ...), custom_call_target="tpu_custom_call" | custom-call | flops 137438953472 | bytes 2097152 | tf_op jit(solution)/shard_map/pallas_call | solution.py:624
  101.7 5.4 %shard_map.175 = bf16[4,4,32,3456]{3,2,1,0:T(8,128)(2,1)} custom-call(bf16[4,4,32,3456]{3,2,1,0:T(8,128)(2,1)} %get-tuple-element.117.keep, bf16[2,4,32,3456]{3,2,1,0:T(8,128)(2,1)} %copy-done.1, bf16[2,4,32,3456]{3,2,1,0:T(8,128)(2,1)} %copy-done.2), custom_call_target="tpu_custom_call" | custom-call | flops 2097152 | bytes 10616832 | tf_op jit(solution)/shard_map/pallas_call | solution.py:447
  109.3 4.3 %collective-permute-done.18.u3 = bf16[512,256]{1,0:T(8,128)(2,1)S(1)} collective-permute-done((bf16[512,256]{1,0:T(8,128)(2,1)}, bf16[512,256]{1,0:T(8,128)(2,1)S(1)}, u32[]{:S(2)}, u32[]{:S(2)}) %collective-permute-start.18) | collective-permute-done | bytes 262176 | tf_op jit(solution)/shard_map/ppermute | solution.py:34
  115.4 3.2 %collective-permute-start.22 = (bf16[512,256]{1,0:T(8,128)(2,1)S(1)}, bf16[512,256]{1,0:T(8,128)(2,1)S(1)}, u32[]{:S(2)}, u32[]{:S(2)}) collective-permute-start(bf16[512,256]{1,0:T(8,128)(2,1)S(1)} %copy-done.33), channel_id=1, source_target_pairs={{0,3},{1,0},{2,1},{3,2},{4,7},{5,4},{6,5},{7,6},{8,11},{9,8},{10,9... | collective-permute-start | bytes 786440 | tf_op jit(solution)/shard_map/ppermute | solution.py:857
  118.6 5.0 %shard_map.177 = (bf16[512,1024]{1,0:T(8,128)(2,1)}, f32[512,256]{1,0:T(8,128)}, f32[512,256]{1,0:T(8,128)}, bf16[512,256]{1,0:T(8,128)(2,1)}, f32[8,256]{1,0:T(8,128)}) custom-call(s32[5]{0:T(128)} %stack.35.at.refs_0_, f32[512,256]{1,0:T(8,128)} %get-tuple-element.133.u_own, bf16[512,256]{1,0:T(8,128)(2,1)} %copy-done.15, bf16[512,256]{1,0:T(8,128)(2,1)} %copy-done.16, ...), custom_call_target="tpu_custom_call" | custom-call | flops 268435456 | bytes 6291456 | tf_op jit(solution)/shard_map/pallas_call | solution.py:670
  126.9 2.2 %collective-permute-done.21 = bf16[512,256]{1,0:T(8,128)(2,1)S(1)} collective-permute-done((bf16[512,256]{1,0:T(8,128)(2,1)S(1)}, bf16[512,256]{1,0:T(8,128)(2,1)S(1)}, u32[]{:S(2)}, u32[]{:S(2)}) %collective-permute-start.21) | collective-permute-done | bytes 262176 | tf_op jit(solution)/shard_map/ppermute | solution.py:857
  129.2 6.7 %shard_map.178 = (bf16[512,768]{1,0:T(8,128)(2,1)}, f32[512,256]{1,0:T(8,128)}, bf16[576,256]{1,0:T(8,128)(2,1)}, bf16[576,256]{1,0:T(8,128)(2,1)}, bf16[576,256]{1,0:T(8,128)(2,1)}, /*index=5*/f32[16,512]{1,0:T(8,128)}) custom-call(s32[5]{0:T(128)} %stack.35.at.refs_0_, bf16[512,256]{1,0:T(8,128)(2,1)} %rows_in.1, bf16[512,256]{1,0:T(8,128)(2,1)} %copy-done.11, ...), custom_call_target="tpu_custom_call" | custom-call | flops 805306368 | bytes 6291456 | tf_op jit(solution)/shard_map/pallas_call | solution.py:747
  137.5 3.3 %collective-permute-start.25 = (bf16[576,256]{1,0:T(8,128)(2,1)}, bf16[576,256]{1,0:T(8,128)(2,1)S(1)}, u32[]{:S(2)}, u32[]{:S(2)}) collective-permute-start(bf16[576,256]{1,0:T(8,128)(2,1)} %get-tuple-element.154), channel_id=1, source_target_pairs={{0,3},{1,0},{2,1},{3,2},{4,7},{5,4},{6,5},{7,6},{8,11},{9,8},{10,9... | collective-permute-start | bytes 884744 | tf_op jit(solution)/shard_map/ppermute | solution.py:875
  141.6 5.2 %shard_map.180 = (bf16[2,4,32,1024]{3,2,1,0:T(8,128)(2,1)}, bf16[2,4,32,1024]{3,2,1,0:T(8,128)(2,1)}, bf16[4,4,32,1024]{3,2,1,0:T(8,128)(2,1)}) custom-call(s32[5]{0:T(128)} %stack.35.at.refs_0_, bf16[512,1024]{1,0:T(8,128)(2,1)} %get-tuple-element.162.refs_1_, bf16[512,768]{1,0:T(8,128)(2,1)} %get-tuple-element.163.refs_2_, ...), custom_call_target="tpu_custom_call" | custom-call | flops 1073741824 | bytes 4194304 | tf_op jit(solution)/shard_map/pallas_call | solution.py:423
  147.3 6.6 %collective-permute-done.24.d2 = bf16[576,256]{1,0:T(8,128)(2,1)S(1)} collective-permute-done((bf16[576,256]{1,0:T(8,128)(2,1)}, bf16[576,256]{1,0:T(8,128)(2,1)S(1)}, u32[]{:S(2)}, u32[]{:S(2)}) %collective-permute-start.24) | collective-permute-done | bytes 294944 | tf_op jit(solution)/shard_map/ppermute | solution.py:875
  154.7 3.0 %shard_map.179 = (bf16[512,256]{1,0:T(8,128)(2,1)}, f32[8,256]{1,0:T(8,128)}) custom-call(f32[512,256]{1,0:T(8,128)} %get-tuple-element.151.d_own, bf16[576,256]{1,0:T(8,128)(2,1)} %copy-done.30, bf16[576,256]{1,0:T(8,128)(2,1)} %copy-done.31, bf16[576,256]{1,0:T(8,128)(2,1)} %copy-done.32, f32[16,512]{1,0:T(8,128)} %get-tuple-element.155.inner, ...), custom_call_target="tpu_custom_call" | custom-call | flops 8589934592 | bytes 2097152 | tf_op jit(solution)/shard_map/pallas_call | solution.py:601
  161.4 2.8 %shard_map.181 = (f32[128,1024]{1,0:T(8,128)}, bf16[144,1024]{1,0:T(8,128)(2,1)}, bf16[144,1024]{1,0:T(8,128)(2,1)}, bf16[144,1024]{1,0:T(8,128)(2,1)}) custom-call(s32[5]{0:T(128)} %stack.35.at.refs_0_, bf16[4,4,32,1024]{3,2,1,0:T(8,128)(2,1)} %get-tuple-element.165.keep, bf16[2,4,32,1024]{3,2,1,0:T(8,128)(2,1)} %copy-done.6, ...), custom_call_target="tpu_custom_call" | custom-call | flops 2097152 | bytes 4194304 | tf_op jit(solution)/shard_map/pallas_call | solution.py:487
  164.2 3.5 %collective-permute-start.29 = (bf16[144,1024]{1,0:T(8,128)(2,1)}, bf16[144,1024]{1,0:T(8,128)(2,1)S(1)}, u32[]{:S(2)}, u32[]{:S(2)}) collective-permute-start(bf16[144,1024]{1,0:T(8,128)(2,1)} %get-tuple-element.174), channel_id=1, source_target_pairs={{0,16},{4,20},{8,24},{12,28},{16,0},{20,4},{24,8},{28,12},{32,48},... | collective-permute-start | bytes 884744 | tf_op jit(solution)/shard_map/ppermute | solution.py:894
  168.4 2.6 %collective-permute-start.31 = (bf16[144,1024]{1,0:T(8,128)(2,1)}, bf16[144,1024]{1,0:T(8,128)(2,1)S(1)}, u32[]{:S(2)}, u32[]{:S(2)}) collective-permute-start(bf16[144,1024]{1,0:T(8,128)(2,1)} %get-tuple-element.176), channel_id=1, source_target_pairs={{0,24},{4,28},{8,0},{12,4},{16,8},{20,12},{24,16},{28,20},{32,56},... | collective-permute-start | bytes 884744 | tf_op jit(solution)/shard_map/ppermute | solution.py:894
  171.8 4.0 %collective-permute-done.29.m1 = bf16[144,1024]{1,0:T(8,128)(2,1)S(1)} collective-permute-done((bf16[144,1024]{1,0:T(8,128)(2,1)}, bf16[144,1024]{1,0:T(8,128)(2,1)S(1)}, u32[]{:S(2)}, u32[]{:S(2)}) %collective-permute-start.29) | collective-permute-done | bytes 294944 | tf_op jit(solution)/shard_map/ppermute | solution.py:894
  175.8 5.8 %collective-permute-done.30.m2 = bf16[144,1024]{1,0:T(8,128)(2,1)S(1)} collective-permute-done((bf16[144,1024]{1,0:T(8,128)(2,1)}, bf16[144,1024]{1,0:T(8,128)(2,1)S(1)}, u32[]{:S(2)}, u32[]{:S(2)}) %collective-permute-start.30) | collective-permute-done | bytes 294944 | tf_op jit(solution)/shard_map/ppermute | solution.py:894
  182.7 2.2 %shard_map.182 = (f32[32,1024]{1,0:T(8,128)}, bf16[48,1024]{1,0:T(8,128)(2,1)}, bf16[48,1024]{1,0:T(8,128)(2,1)}, bf16[48,1024]{1,0:T(8,128)(2,1)}, f32[8,256]{1,0:T(8,128)}) custom-call(s32[5]{0:T(128)} %stack.35.at.refs_0_, f32[128,1024]{1,0:T(8,128)} %get-tuple-element.173.own, bf16[144,1024]{1,0:T(8,128)(2,1)} %copy-done.8, bf16[144,1024]{1,0:T(8,128)(2,1)} %copy-done.9, ...), custom_call_target="tpu_custom_call" | custom-call | flops 2097152 | bytes 2097152 | tf_op jit(solution)/shard_map/pallas_call | solution.py:520
  184.9 3.2 %collective-permute-start.32 = (bf16[48,1024]{1,0:T(8,128)(2,1)}, bf16[48,1024]{1,0:T(8,128)(2,1)S(1)}, u32[]{:S(2)}, u32[]{:S(2)}) collective-permute-start(bf16[48,1024]{1,0:T(8,128)(2,1)} %get-tuple-element.179), channel_id=1, source_target_pairs={{0,64},{4,68},{8,72},{12,76},{16,80},{20,84},{24,88},{28,92},{32,9... | collective-permute-start | bytes 294920 | tf_op jit(solution)/shard_map/ppermute | solution.py:898
  188.7 2.6 %collective-permute-start.34 = (bf16[48,1024]{1,0:T(8,128)(2,1)}, bf16[48,1024]{1,0:T(8,128)(2,1)S(1)}, u32[]{:S(2)}, u32[]{:S(2)}) collective-permute-start(bf16[48,1024]{1,0:T(8,128)(2,1)} %get-tuple-element.181), channel_id=1, source_target_pairs={{0,96},{4,100},{8,104},{12,108},{16,112},{20,116},{24,120},{28,124... | collective-permute-start | bytes 294920 | tf_op jit(solution)/shard_map/ppermute | solution.py:898
  (168 shorter events, 51.7 us)
Async XLA Ops:
  7.2 51.0 %all-gather.2.cloned.1.call-start = ((), (), s32[]{:S(2)}) async-start(), calls=%async_computation.2 | async-start | bytes 1310720 | tf_op jit(solution)/shard_map/all_gather | solution.py:805
  7.2 15.4 %collective-permute-start = (bf16[512,256]{1,0:T(8,128)(2,1)}, bf16[512,256]{1,0:T(8,128)(2,1)S(1)}, u32[]{:S(2)}, u32[]{:S(2)}) collective-permute-start(bf16[512,256]{1,0:T(8,128)(2,1)} %rows_in.1), channel_id=1, source_target_pairs={{0,3},{1,0},{2,1},{3,2},{4,7},{5,4},{6,5},{7,6},{8,11},{9,8},{10,9... | collective-permute-start | bytes 786440 | tf_op jit(solution)/shard_map/ppermute | solution.py:34
  10.1 15.7 %collective-permute-start.1 = (bf16[512,256]{1,0:T(8,128)(2,1)}, bf16[512,256]{1,0:T(8,128)(2,1)S(1)}, u32[]{:S(2)}, u32[]{:S(2)}) collective-permute-start(bf16[512,256]{1,0:T(8,128)(2,1)} %rows_in.1), channel_id=1, source_target_pairs={{0,2},{1,3},{2,0},{3,1},{4,6},{5,7},{6,4},{7,5},{8,10},{9,11},{10,... | collective-permute-start | bytes 786440 | tf_op jit(solution)/shard_map/ppermute | solution.py:33
  10.9 15.9 %collective-permute-start.2 = (bf16[512,256]{1,0:T(8,128)(2,1)}, bf16[512,256]{1,0:T(8,128)(2,1)S(1)}, u32[]{:S(2)}, u32[]{:S(2)}) collective-permute-start(bf16[512,256]{1,0:T(8,128)(2,1)} %rows_in.1), channel_id=1, source_target_pairs={{0,1},{1,2},{2,3},{3,0},{4,5},{5,6},{6,7},{7,4},{8,9},{9,10},{10,1... | collective-permute-start | bytes 786440 | tf_op jit(solution)/shard_map/ppermute | solution.py:34
  12.8 29.6 %collective-permute-start.7 = (bf16[512,256]{1,0:T(8,128)(2,1)S(1)}, bf16[512,256]{1,0:T(8,128)(2,1)S(1)}, u32[]{:S(2)}, u32[]{:S(2)}) collective-permute-start(bf16[512,256]{1,0:T(8,128)(2,1)S(1)} %constant_dynamic-slice_fusion.2.p0), channel_id=1, source_target_pairs={{0,3},{1,0},{2,1},{3,2},{4,7},{5,4},{6,5},{7,6},{8,11},{9,8},{10,9... | collective-permute-start | bytes 786440 | tf_op jit(solution)/shard_map/ppermute | solution.py:34
  15.2 28.6 %collective-permute-start.8 = (bf16[512,256]{1,0:T(8,128)(2,1)S(1)}, bf16[512,256]{1,0:T(8,128)(2,1)S(1)}, u32[]{:S(2)}, u32[]{:S(2)}) collective-permute-start(bf16[512,256]{1,0:T(8,128)(2,1)S(1)} %constant_dynamic-slice_fusion.2.p0), channel_id=1, source_target_pairs={{0,2},{1,3},{2,0},{3,1},{4,6},{5,7},{6,4},{7,5},{8,10},{9,11},{10,... | collective-permute-start | bytes 786440 | tf_op jit(solution)/shard_map/ppermute | solution.py:33
  16.8 143.7 %reduce-scatter.3.cloned.1.call-start = ((), (), s32[]{:S(2)}) async-start(), calls=%async_computation.3 | async-start | bytes 4423680 | tf_op jit(solution)/shard_map/reduce_scatter | solution.py:769
  22.6 21.2 %collective-permute-start.9 = (bf16[512,256]{1,0:T(8,128)(2,1)S(1)}, bf16[512,256]{1,0:T(8,128)(2,1)S(1)}, u32[]{:S(2)}, u32[]{:S(2)}) collective-permute-start(bf16[512,256]{1,0:T(8,128)(2,1)S(1)} %constant_dynamic-slice_fusion.2.p0), channel_id=1, source_target_pairs={{0,1},{1,2},{2,3},{3,0},{4,5},{5,6},{6,7},{7,4},{8,9},{9,10},{10,1... | collective-permute-start | bytes 786440 | tf_op jit(solution)/shard_map/ppermute | solution.py:34
  38.5 14.9 %collective-permute-start.4 = (bf16[512,256]{1,0:T(8,128)(2,1)}, bf16[512,256]{1,0:T(8,128)(2,1)S(1)}, u32[]{:S(2)}, u32[]{:S(2)}) collective-permute-start(bf16[512,256]{1,0:T(8,128)(2,1)} %get-tuple-element.104.m0.refs_4_), channel_id=1, source_target_pairs={{0,3},{1,0},{2,1},{3,2},{4,7},{5,4},{6,5},{7,6},{8,11},{9,8},{10,9... | collective-permute-start | bytes 786440 | tf_op jit(solution)/shard_map/ppermute | solution.py:34
  40.9 12.4 %collective-permute-start.5 = (bf16[512,256]{1,0:T(8,128)(2,1)}, bf16[512,256]{1,0:T(8,128)(2,1)S(1)}, u32[]{:S(2)}, u32[]{:S(2)}) collective-permute-start(bf16[512,256]{1,0:T(8,128)(2,1)} %get-tuple-element.104.m0.refs_4_), channel_id=1, source_target_pairs={{0,2},{1,3},{2,0},{3,1},{4,6},{5,7},{6,4},{7,5},{8,10},{9,11},{10,... | collective-permute-start | bytes 786440 | tf_op jit(solution)/shard_map/ppermute | solution.py:33
  42.4 15.8 %collective-permute-start.6 = (bf16[512,256]{1,0:T(8,128)(2,1)}, bf16[512,256]{1,0:T(8,128)(2,1)S(1)}, u32[]{:S(2)}, u32[]{:S(2)}) collective-permute-start(bf16[512,256]{1,0:T(8,128)(2,1)} %get-tuple-element.104.m0.refs_4_), channel_id=1, source_target_pairs={{0,1},{1,2},{2,3},{3,0},{4,5},{5,6},{6,7},{7,4},{8,9},{9,10},{10,1... | collective-permute-start | bytes 786440 | tf_op jit(solution)/shard_map/ppermute | solution.py:34
  47.5 10.7 %collective-permute-start.10 = (bf16[512,1024]{1,0:T(8,128)(2,1)}, bf16[512,1024]{1,0:T(8,128)(2,1)S(1)}, u32[]{:S(2)}, u32[]{:S(2)}) collective-permute-start(bf16[512,1024]{1,0:T(8,128)(2,1)} %shard_map.172.half), channel_id=1, source_target_pairs={{0,4},{4,0},{8,12},{12,8},{16,20},{20,16},{24,28},{28,24},{32,36},... | collective-permute-start | bytes 3145736 | tf_op jit(solution)/shard_map/ppermute | solution.py:821
  77.5 16.0 %collective-permute-start.13 = (bf16[512,256]{1,0:T(8,128)(2,1)}, bf16[512,256]{1,0:T(8,128)(2,1)S(1)}, u32[]{:S(2)}, u32[]{:S(2)}) collective-permute-start(bf16[512,256]{1,0:T(8,128)(2,1)} %get-tuple-element.127), channel_id=1, source_target_pairs={{0,2},{1,3},{2,0},{3,1},{4,6},{5,7},{6,4},{7,5},{8,10},{9,11},{10,... | collective-permute-start | bytes 786440 | tf_op jit(solution)/shard_map/ppermute | solution.py:846
  80.0 13.5 %collective-permute-start.14 = (bf16[512,256]{1,0:T(8,128)(2,1)}, bf16[512,256]{1,0:T(8,128)(2,1)S(1)}, u32[]{:S(2)}, u32[]{:S(2)}) collective-permute-start(bf16[512,256]{1,0:T(8,128)(2,1)} %get-tuple-element.128), channel_id=1, source_target_pairs={{0,1},{1,2},{2,3},{3,0},{4,5},{5,6},{6,7},{7,4},{8,9},{9,10},{10,1... | collective-permute-start | bytes 786440 | tf_op jit(solution)/shard_map/ppermute | solution.py:846
  80.0 13.5 %collective-permute-start.15 = (bf16[512,256]{1,0:T(8,128)(2,1)}, bf16[512,256]{1,0:T(8,128)(2,1)S(1)}, u32[]{:S(2)}, u32[]{:S(2)}) collective-permute-start(bf16[512,256]{1,0:T(8,128)(2,1)} %get-tuple-element.129), channel_id=1, source_target_pairs={{0,3},{1,0},{2,1},{3,2},{4,7},{5,4},{6,5},{7,6},{8,11},{9,8},{10,9... | collective-permute-start | bytes 786440 | tf_op jit(solution)/shard_map/ppermute | solution.py:846
  93.0 6.9 %collective-permute-start.12 = (bf16[2,4,32,3456]{3,2,1,0:T(8,128)(2,1)}, bf16[2,4,32,3456]{3,2,1,0:T(8,128)(2,1)S(1)}, u32[]{:S(2)}, u32[]{:S(2)}) collective-permute-start(bf16[2,4,32,3456]{3,2,1,0:T(8,128)(2,1)} %get-tuple-element.119), channel_id=1, source_target_pairs={{0,4},{4,0},{8,12},{12,8},{16,20},{20,16},{24,28},{28,24},{32,36},... | collective-permute-start | bytes 5308424 | tf_op jit(solution)/shard_map/ppermute | solution.py:436
  97.1 10.0 %collective-permute-start.16 = (bf16[512,256]{1,0:T(8,128)(2,1)}, bf16[512,256]{1,0:T(8,128)(2,1)S(1)}, u32[]{:S(2)}, u32[]{:S(2)}) collective-permute-start(bf16[512,256]{1,0:T(8,128)(2,1)} %get-tuple-element.132), channel_id=1, source_target_pairs={{0,3},{1,0},{2,1},{3,2},{4,7},{5,4},{6,5},{7,6},{8,11},{9,8},{10,9... | collective-permute-start | bytes 786440 | tf_op jit(solution)/shard_map/ppermute | solution.py:34
  98.3 11.0 %collective-permute-start.17 = (bf16[512,256]{1,0:T(8,128)(2,1)}, bf16[512,256]{1,0:T(8,128)(2,1)S(1)}, u32[]{:S(2)}, u32[]{:S(2)}) collective-permute-start(bf16[512,256]{1,0:T(8,128)(2,1)} %get-tuple-element.132), channel_id=1, source_target_pairs={{0,2},{1,3},{2,0},{3,1},{4,6},{5,7},{6,4},{7,5},{8,10},{9,11},{10,... | collective-permute-start | bytes 786440 | tf_op jit(solution)/shard_map/ppermute | solution.py:33
  99.9 13.7 %collective-permute-start.18 = (bf16[512,256]{1,0:T(8,128)(2,1)}, bf16[512,256]{1,0:T(8,128)(2,1)S(1)}, u32[]{:S(2)}, u32[]{:S(2)}) collective-permute-start(bf16[512,256]{1,0:T(8,128)(2,1)} %get-tuple-element.132), channel_id=1, source_target_pairs={{0,1},{1,2},{2,3},{3,0},{4,5},{5,6},{6,7},{7,4},{8,9},{9,10},{10,1... | collective-permute-start | bytes 786440 | tf_op jit(solution)/shard_map/ppermute | solution.py:34
  113.6 77.7 %reduce-scatter.5.cloned.1.call-start = ((), (), s32[]{:S(2)}) async-start(), calls=%async_computation.4 | async-start | bytes 1105920 | tf_op jit(solution)/shard_map/reduce_scatter | solution.py:769
  113.7 13.2 %collective-permute-start.20 = (bf16[512,256]{1,0:T(8,128)(2,1)S(1)}, bf16[512,256]{1,0:T(8,128)(2,1)S(1)}, u32[]{:S(2)}, u32[]{:S(2)}) collective-permute-start(bf16[512,256]{1,0:T(8,128)(2,1)S(1)} %copy-done.35), channel_id=1, source_target_pairs={{0,2},{1,3},{2,0},{3,1},{4,6},{5,7},{6,4},{7,5},{8,10},{9,11},{10,... | collective-permute-start | bytes 786440 | tf_op jit(solution)/shard_map/ppermute | solution.py:857
  115.4 13.8 %collective-permute-start.21 = (bf16[512,256]{1,0:T(8,128)(2,1)S(1)}, bf16[512,256]{1,0:T(8,128)(2,1)S(1)}, u32[]{:S(2)}, u32[]{:S(2)}) collective-permute-start(bf16[512,256]{1,0:T(8,128)(2,1)S(1)} %copy-done.34), channel_id=1, source_target_pairs={{0,1},{1,2},{2,3},{3,0},{4,5},{5,6},{6,7},{7,4},{8,9},{9,10},{10,1... | collective-permute-start | bytes 786440 | tf_op jit(solution)/shard_map/ppermute | solution.py:857
  115.4 13.8 %collective-permute-start.22 = (bf16[512,256]{1,0:T(8,128)(2,1)S(1)}, bf16[512,256]{1,0:T(8,128)(2,1)S(1)}, u32[]{:S(2)}, u32[]{:S(2)}) collective-permute-start(bf16[512,256]{1,0:T(8,128)(2,1)S(1)} %copy-done.33), channel_id=1, source_target_pairs={{0,3},{1,0},{2,1},{3,2},{4,7},{5,4},{6,5},{7,6},{8,11},{9,8},{10,9... | collective-permute-start | bytes 786440 | tf_op jit(solution)/shard_map/ppermute | solution.py:857
  135.9 11.4 %collective-permute-start.23 = (bf16[576,256]{1,0:T(8,128)(2,1)}, bf16[576,256]{1,0:T(8,128)(2,1)S(1)}, u32[]{:S(2)}, u32[]{:S(2)}) collective-permute-start(bf16[576,256]{1,0:T(8,128)(2,1)} %get-tuple-element.152), channel_id=1, source_target_pairs={{0,2},{1,3},{2,0},{3,1},{4,6},{5,7},{6,4},{7,5},{8,10},{9,11},{10,... | collective-permute-start | bytes 884744 | tf_op jit(solution)/shard_map/ppermute | solution.py:875
  137.5 16.3 %collective-permute-start.24 = (bf16[576,256]{1,0:T(8,128)(2,1)}, bf16[576,256]{1,0:T(8,128)(2,1)S(1)}, u32[]{:S(2)}, u32[]{:S(2)}) collective-permute-start(bf16[576,256]{1,0:T(8,128)(2,1)} %get-tuple-element.153), channel_id=1, source_target_pairs={{0,1},{1,2},{2,3},{3,0},{4,5},{5,6},{6,7},{7,4},{8,9},{9,10},{10,1... | collective-permute-start | bytes 884744 | tf_op jit(solution)/shard_map/ppermute | solution.py:875
  137.5 16.3 %collective-permute-start.25 = (bf16[576,256]{1,0:T(8,128)(2,1)}, bf16[576,256]{1,0:T(8,128)(2,1)S(1)}, u32[]{:S(2)}, u32[]{:S(2)}) collective-permute-start(bf16[576,256]{1,0:T(8,128)(2,1)} %get-tuple-element.154), channel_id=1, source_target_pairs={{0,3},{1,0},{2,1},{3,2},{4,7},{5,4},{6,5},{7,6},{8,11},{9,8},{10,9... | collective-permute-start | bytes 884744 | tf_op jit(solution)/shard_map/ppermute | solution.py:875
  146.8 13.7 %collective-permute-start.27 = (bf16[2,4,32,1024]{3,2,1,0:T(8,128)(2,1)}, bf16[2,4,32,1024]{3,2,1,0:T(8,128)(2,1)S(1)}, u32[]{:S(2)}, u32[]{:S(2)}) collective-permute-start(bf16[2,4,32,1024]{3,2,1,0:T(8,128)(2,1)} %get-tuple-element.168), channel_id=1, source_target_pairs={{0,4},{4,0},{8,12},{12,8},{16,20},{20,16},{24,28},{28,24},{32,36},... | collective-permute-start | bytes 1572872 | tf_op jit(solution)/shard_map/ppermute | solution.py:436
  146.8 13.7 %collective-permute-start.28 = (bf16[2,4,32,1024]{3,2,1,0:T(8,128)(2,1)}, bf16[2,4,32,1024]{3,2,1,0:T(8,128)(2,1)S(1)}, u32[]{:S(2)}, u32[]{:S(2)}) collective-permute-start(bf16[2,4,32,1024]{3,2,1,0:T(8,128)(2,1)} %get-tuple-element.169), channel_id=1, source_target_pairs={{0,4},{4,0},{8,12},{12,8},{16,20},{20,16},{24,28},{28,24},{32,36},... | collective-permute-start | bytes 1572872 | tf_op jit(solution)/shard_map/ppermute | solution.py:436
  164.2 11.6 %collective-permute-start.29 = (bf16[144,1024]{1,0:T(8,128)(2,1)}, bf16[144,1024]{1,0:T(8,128)(2,1)S(1)}, u32[]{:S(2)}, u32[]{:S(2)}) collective-permute-start(bf16[144,1024]{1,0:T(8,128)(2,1)} %get-tuple-element.174), channel_id=1, source_target_pairs={{0,16},{4,20},{8,24},{12,28},{16,0},{20,4},{24,8},{28,12},{32,48},... | collective-permute-start | bytes 884744 | tf_op jit(solution)/shard_map/ppermute | solution.py:894
  167.7 13.9 %collective-permute-start.30 = (bf16[144,1024]{1,0:T(8,128)(2,1)}, bf16[144,1024]{1,0:T(8,128)(2,1)S(1)}, u32[]{:S(2)}, u32[]{:S(2)}) collective-permute-start(bf16[144,1024]{1,0:T(8,128)(2,1)} %get-tuple-element.175), channel_id=1, source_target_pairs={{0,8},{4,12},{8,16},{12,20},{16,24},{20,28},{24,0},{28,4},{32,40},... | collective-permute-start | bytes 884744 | tf_op jit(solution)/shard_map/ppermute | solution.py:894
  168.4 13.6 %collective-permute-start.31 = (bf16[144,1024]{1,0:T(8,128)(2,1)}, bf16[144,1024]{1,0:T(8,128)(2,1)S(1)}, u32[]{:S(2)}, u32[]{:S(2)}) collective-permute-start(bf16[144,1024]{1,0:T(8,128)(2,1)} %get-tuple-element.176), channel_id=1, source_target_pairs={{0,24},{4,28},{8,0},{12,4},{16,8},{20,12},{24,16},{28,20},{32,56},... | collective-permute-start | bytes 884744 | tf_op jit(solution)/shard_map/ppermute | solution.py:894
  184.9 9.0 %collective-permute-start.32 = (bf16[48,1024]{1,0:T(8,128)(2,1)}, bf16[48,1024]{1,0:T(8,128)(2,1)S(1)}, u32[]{:S(2)}, u32[]{:S(2)}) collective-permute-start(bf16[48,1024]{1,0:T(8,128)(2,1)} %get-tuple-element.179), channel_id=1, source_target_pairs={{0,64},{4,68},{8,72},{12,76},{16,80},{20,84},{24,88},{28,92},{32,9... | collective-permute-start | bytes 294920 | tf_op jit(solution)/shard_map/ppermute | solution.py:898
  (50 other events, 262.5 us)
Sparse Core Ops, SparseCore 0:
  16.9 35.9 all-gather.1
  113.8 43.0 reduce-scatter.2
  160.6 23.3 reduce-scatter.4

commit v6 on v5

--- a/solution.py
+++ b/solution.py
@@ -465,7 +465,7 @@
     return message[:8, :width].astype(F32) + message[:8, width : 2 * width].astype(F32)
 
 
-def send_kernel(at, keep, got_a, got_b, small, own, m1, m2, m3):
+def send_kernel(at, keep, got_a, got_b, small_own, small_got, own, m1, m2, m3, small):
     z = at[3]
     rows = own.shape[0]
     width = small.shape[1]
@@ -475,23 +475,31 @@
         got = jnp.where(block < 2, got_a[inside].astype(F32), got_b[inside].astype(F32))
         total = keep[block].astype(F32) + got
         out[:rows] = total.reshape(own.shape).astype(out.dtype)
-    high, low = spread(jnp.concatenate([small[...], jnp.zeros_like(small[...])], axis=0))
+    sums = small_own[...] + small_got[...]
+    small[...] = sums
+    high, low = spread(jnp.concatenate([sums, jnp.zeros_like(sums)], axis=0))
     for out in (m1, m2, m3):
         out[rows:, :width] = high
         out[rows:, width : 2 * width] = low
 
 
-def send_z(at, keep, got, small):
+def send_z(at, keep, got, small, small_got):
     rows, columns = keep.shape[1] * keep.shape[2], keep.shape[3]
     message = shape((rows + 16, columns), BF16)
     return pl.pallas_call(
         send_kernel,
-        out_shape=(shape((rows, columns), F32), message, message, message),
-        in_specs=[smem()] + [vmem()] * 4,
-        out_specs=(vmem(),) * 4,
+        out_shape=(
+            shape((rows, columns), F32),
+            message,
+            message,
+            message,
+            shape(small.shape, F32),
+        ),
+        in_specs=[smem()] + [vmem()] * 5,
+        out_specs=(vmem(),) * 5,
         compiler_params=params(56),
         cost_estimate=cost(2**20, 2**22),
-    )(at, keep, *got, small)
+    )(at, keep, *got, small, small_got)
 
 
 def turn_kernel(at, own, m1, m2, m3, small, left, n1, n2, n3, small_out, total):
@@ -853,8 +861,6 @@
     )
     u_pieces = [u_own] + gather_ch(u_low)[1:]
     ffn_kept = add_cores(keep, got)
-    ffn_kept, *down_parts = tie(ffn_kept, *down_parts)
-    downs = [lax.ppermute(down_parts[j], "ch", ch_pairs(j)) for j in (2, 1, 3)]
     ffn_kept, *u_pieces = tie(ffn_kept, *u_pieces)
     groups = [[seq_index(i, k, c) for k in range(4)] for i in range(4) for c in range(2)]
     ffn_sum = scatter_groups(ffn_kept, groups)
@@ -863,15 +869,10 @@
         at, u_pieces, hidden, r_two, grad_full, out_weight, c_gate, conv_out
     )
     following = from_behind(edge, "seq", -1)
-    following, *downs = tie(following, *downs)
     d_proj, d_own, d_one, d_two, d_three, inner = back_project(
         at, pieces, d_conv, following, conv_weight, value_rows, b_gate, d_cgate, norm1_gain,
         in_planes,
     )
-    block_output = hidden_own + down_parts[0].astype(F32)
-    for down in downs:
-        block_output = block_output + down.astype(F32)
-    block_output = block_output.astype(BF16)
     received = [lax.ppermute(d, "ch", ch_pairs(j)) for j, d in ((2, d_two), (1, d_one), (3, d_three))]
 
     *gives, keep = pair_products(at, normed_one, d_proj, d_branch, mixed_rows, True, True)
@@ -887,13 +888,19 @@
     input_grad, small = end(
         d_own, received, inner, d_hidden, block_input, r_one, own_one, grad_conv, grad_gain_two
     )
-    small = small + lax.ppermute(small, "seq", seq_pairs(0, 0, 1))
-    small, ffn_sum, *got = tie(small, ffn_sum, *got)
-    own, *messages = send_z(at, keep, got, small)
+    small_got = lax.ppermute(small, "seq", seq_pairs(0, 0, 1))
+    own, *messages, small = send_z(at, keep, got, small, small_got)
+    own, ffn_sum, *down_parts = tie(own, ffn_sum, *down_parts)
     messages = [
         lax.ppermute(m, "seq", seq_pairs(0, j, 0)) for j, m in ((2, messages[1]), (1, messages[0]), (3, messages[2]))
     ]
+    downs = [lax.ppermute(down_parts[j], "ch", ch_pairs(j)) for j in (2, 1, 3)]
     own, *messages, small = turn(at, own, messages, small)
+    downs, messages = lax.optimization_barrier((downs, messages))
+    block_output = hidden_own + down_parts[0].astype(F32)
+    for down in downs:
+        block_output = block_output + down.astype(F32)
+    block_output = block_output.astype(BF16)
     messages = [
         lax.ppermute(m, "seq", seq_pairs(j, 0, 0)) for j, m in ((2, messages[1]), (1, messages[0]), (3, messages[2]))
     ]

time: 204 us -> 199 us (0.975)
  waiting for transfers between devices: 38.5 us -> 32.8 us
    ppermute x3, waiting for transfers between devices: 10.2 us -> 7.97 us  [shards(): lax.ppermute(m, 'seq', seq_pairs(0, j, 0))]
    unnamed x88 -> x90, local copies, waits for them, and re-layouts: 9.43 us -> 10.7 us
  transfers between devices with their start and end apart: 38 -> 38, of which waited for: 14 -> 13; matrix products, arithmetic and copies ran while one was open for 8% -> 7% of each run, Pallas kernels for 27% -> 28%
where the time goes in v6:
time: 199 us; the launch traced here: 198 us
  Pallas kernels  74.8 us (38%)
  starting transfers between devices  51.8 us (26%)
  waiting for transfers between devices  32.8 us (16%)
  local copies, waits for them, and re-layouts  20.3 us (10%)
  between operations  14.1 us (7%)
  other arithmetic  4.55 us (2%)
    pallas_call x1, Pallas kernels, ffn(): pl.pallas_call(ffn_kernel, out_shape=(shape((rows, features), F32), shape...  18.3 us
    pallas_call x2, Pallas kernels, pair_products(): pl.pallas_call(body, grid=(4,), out_shape=(half, half, out), in_specs=[sm...  14.9 us
    ppermute x8, waiting for transfers between devices, gather_ch(): near = [lax.ppermute(block, 'ch', ch_pairs(-j)) for j in (1, 3)]  13.9 us
    ppermute x8, starting transfers between devices, gather_ch(): near = [lax.ppermute(block, 'ch', ch_pairs(-j)) for j in (1, 3)]  11.4 us
    unnamed x90, local copies, waits for them, and re-layouts  10.7 us
    ppermute x6, starting transfers between devices, shards(): lax.ppermute(d, 'ch', ch_pairs(j))  10.3 us
    ppermute x3, waiting for transfers between devices, shards(): lax.ppermute(m, 'seq', seq_pairs(0, j, 0))  7.97 us
    ppermute x3, starting transfers between devices, shards(): lax.ppermute(m, 'seq', seq_pairs(0, j, 0))  7.38 us
  transfers between devices with their start and end apart: 38, of which 13 were waited for; matrix products, arithmetic and copies ran while one was open for 7% of the time, Pallas kernels for 28%

profile of v6, /device:TPU:0, one launch (start us, length us, event | category | flops | bytes accessed | tf_op | source)
XLA Modules:
  0.0 198.5 jit_solution(7426801141133755615)
XLA Ops:
  7.2 2.9 %collective-permute-start = (bf16[512,256]{1,0:T(8,128)(2,1)}, bf16[512,256]{1,0:T(8,128)(2,1)S(1)}, u32[]{:S(2)}, u32[]{:S(2)}) collective-permute-start(bf16[512,256]{1,0:T(8,128)(2,1)} %rows_in.1), channel_id=1, source_target_pairs={{0,3},{1,0},{2,1},{3,2},{4,7},{5,4},{6,5},{7,6},{8,11},{9,8},{10,9... | collective-permute-start | bytes 786440 | tf_op jit(solution)/shard_map/ppermute | solution.py:34
  12.8 2.4 %collective-permute-start.7 = (bf16[512,256]{1,0:T(8,128)(2,1)S(1)}, bf16[512,256]{1,0:T(8,128)(2,1)S(1)}, u32[]{:S(2)}, u32[]{:S(2)}) collective-permute-start(bf16[512,256]{1,0:T(8,128)(2,1)S(1)} %constant_dynamic-slice_fusion.2.p0), channel_id=1, source_target_pairs={{0,3},{1,0},{2,1},{3,2},{4,7},{5,4},{6,5},{7,6},{8,11},{9,8},{10,9... | collective-permute-start | bytes 786440 | tf_op jit(solution)/shard_map/ppermute | solution.py:34
  18.7 3.9 %collective-permute-done.p1.x1 = bf16[512,256]{1,0:T(8,128)(2,1)S(1)} collective-permute-done((bf16[512,256]{1,0:T(8,128)(2,1)}, bf16[512,256]{1,0:T(8,128)(2,1)S(1)}, u32[]{:S(2)}, u32[]{:S(2)}) %collective-permute-start) | collective-permute-done | bytes 262176 | tf_op jit(solution)/shard_map/ppermute | solution.py:34
  27.5 5.2 %shard_map.169 = (bf16[512,1024]{1,0:T(8,128)(2,1)}, f32[512,1]{1,0:T(8,128)}, f32[512,256]{1,0:T(8,128)}, f32[512,256]{1,0:T(8,128)}, f32[512,256]{1,0:T(8,128)...) custom-call(s32[5]{0:T(128)} %stack.35.at.refs_0_, bf16[512,256]{1,0:T(8,128)(2,1)} %rows_in.1, ...), custom_call_target="tpu_custom_call" | custom-call | flops 805306368 | bytes 6291456 | tf_op jit(solution)/shard_map/pallas_call | solution.py:157
  36.0 2.4 %shard_map.170 = (bf16[512,256]{1,0:T(8,128)(2,1)}, f32[512,256]{1,0:T(8,128)}, bf16[512,256]{1,0:T(8,128)(2,1)}, bf16[512,256]{1,0:T(8,128)(2,1)}) custom-call(s32[5]{0:T(128)} %stack.35.at.refs_0_, bf16[512,256]{1,0:T(8,128)(2,1)} %get-tuple-element.101.gated, bf16[16,256]{1,0:T(8,128)(2,1)} %copy-done.29, f32[512,256]{1,0:T(8,128)} %get-tuple-element.103.c_gate, ...), custom_call_target="tpu_custom_call" | custom-call | flops 8388608 | bytes 2097152 | tf_op jit(solution)/shard_map/pallas_call | solution.py:219
  38.5 2.5 %collective-permute-start.4 = (bf16[512,256]{1,0:T(8,128)(2,1)}, bf16[512,256]{1,0:T(8,128)(2,1)S(1)}, u32[]{:S(2)}, u32[]{:S(2)}) collective-permute-start(bf16[512,256]{1,0:T(8,128)(2,1)} %get-tuple-element.104.m0.refs_4_), channel_id=1, source_target_pairs={{0,3},{1,0},{2,1},{3,2},{4,7},{5,4},{6,5},{7,6},{8,11},{9,8},{10,9... | collective-permute-start | bytes 786440 | tf_op jit(solution)/shard_map/ppermute | solution.py:34
  45.2 2.3 %shard_map.172.half = bf16[512,1024]{1,0:T(8,128)(2,1)} custom-call(bf16[512,256]{1,0:T(8,128)(2,1)} %copy-done.4, bf16[512,256]{1,0:T(8,128)(2,1)} %copy-done.20, bf16[512,256]{1,0:T(8,128)(2,1)} %copy-done.21, bf16[512,256]{1,0:T(8,128)(2,1)} %copy-done.22), custom_call_target="tpu_custom_call" | custom-call | flops 2097152 | bytes 2097152 | tf_op jit(solution)/shard_map/pallas_call | solution.py:187
  50.7 2.8 %copy.21 = bf16[1024,2,1152]{2,0,1:T(8,128)(2,1)} copy(bf16[1024,2,1152]{2,1,0:T(2,128)(2,1)S(1)} %bitcast.23) | data formatting | bytes 9437184 | tf_op jit(solution)/shard_map/optimization_barrier | solution.py:67
  53.4 4.7 %collective-permute-done.6.m3 = bf16[512,256]{1,0:T(8,128)(2,1)S(1)} collective-permute-done((bf16[512,256]{1,0:T(8,128)(2,1)}, bf16[512,256]{1,0:T(8,128)(2,1)S(1)}, u32[]{:S(2)}, u32[]{:S(2)}) %collective-permute-start.6) | collective-permute-done | bytes 262176 | tf_op jit(solution)/shard_map/ppermute | solution.py:34
  59.2 18.3 %shard_map.173 = (f32[512,1024]{1,0:T(8,128)}, f32[512,256]{1,0:T(8,128)}, f32[512,1]{1,0:T(8,128)}, bf16[512,1024]{1,0:T(8,128)(2,1)}, bf16[512,1152]{1,0:T(8,1...) custom-call(s32[5]{0:T(128)} %stack.35.at.refs_0_, ...), custom_call_target="tpu_custom_call" | custom-call | flops 8321499136 | bytes 20971520 | tf_op jit(solution)/shard_map/pallas_call | solution.py:351
  77.5 2.5 %collective-permute-start.13 = (bf16[512,256]{1,0:T(8,128)(2,1)}, bf16[512,256]{1,0:T(8,128)(2,1)S(1)}, u32[]{:S(2)}, u32[]{:S(2)}) collective-permute-start(bf16[512,256]{1,0:T(8,128)(2,1)} %get-tuple-element.122), channel_id=1, source_target_pairs={{0,2},{1,3},{2,0},{3,1},{4,6},{5,7},{6,4},{7,5},{8,10},{9,11},{10,... | collective-permute-start | bytes 786440 | tf_op jit(solution)/shard_map/ppermute | solution.py:854
  80.0 3.2 %collective-permute-start.15 = (bf16[512,256]{1,0:T(8,128)(2,1)}, bf16[512,256]{1,0:T(8,128)(2,1)S(1)}, u32[]{:S(2)}, u32[]{:S(2)}) collective-permute-start(bf16[512,256]{1,0:T(8,128)(2,1)} %get-tuple-element.124), channel_id=1, source_target_pairs={{0,3},{1,0},{2,1},{3,2},{4,7},{5,4},{6,5},{7,6},{8,11},{9,8},{10,9... | collective-permute-start | bytes 786440 | tf_op jit(solution)/shard_map/ppermute | solution.py:854
  83.2 9.8 %shard_map.174 = (bf16[2,4,32,3456]{3,2,1,0:T(8,128)(2,1)}, bf16[2,4,32,3456]{3,2,1,0:T(8,128)(2,1)}, bf16[4,4,32,3456]{3,2,1,0:T(8,128)(2,1)}) custom-call(s32[5]{0:T(128)} %stack.35.at.refs_0_, bf16[512,1024]{1,0:T(8,128)(2,1)} %get-tuple-element.115.refs_1_, bf16[512,2304]{1,0:T(8,128)(2,1)} %get-tuple-element.116.refs_2_, ...), custom_call_target="tpu_custom_call" | custom-call | flops 3623878656 | bytes 14155776 | tf_op jit(solution)/shard_map/pallas_call | solution.py:423
  94.4 2.8 %shard_map.176 = (f32[512,256]{1,0:T(8,128)}, bf16[512,256]{1,0:T(8,128)(2,1)}, f32[1,256]{1,0:T(1,128)}) custom-call(f32[512,256]{1,0:T(8,128)} %get-tuple-element.121.d_own, bf16[512,256]{1,0:T(8,128)(2,1)} %copy-done.40, bf16[512,256]{1,0:T(8,128)(2,1)} %copy-done.41, bf16[512,256]{1,0:T(8,128)(2,1)} %copy-done.42, f32[512,256]{1,0:T(8,128)} %get-tuple-element.113.h, ...), custom_call_target="tpu_custom_call" | custom-call | flops 137438953472 | bytes 2097152 | tf_op jit(solution)/shard_map/pallas_call | solution.py:632
  101.8 5.4 %shard_map.175 = bf16[4,4,32,3456]{3,2,1,0:T(8,128)(2,1)} custom-call(bf16[4,4,32,3456]{3,2,1,0:T(8,128)(2,1)} %get-tuple-element.118.keep, bf16[2,4,32,3456]{3,2,1,0:T(8,128)(2,1)} %copy-done.1, bf16[2,4,32,3456]{3,2,1,0:T(8,128)(2,1)} %copy-done.2), custom_call_target="tpu_custom_call" | custom-call | flops 2097152 | bytes 10616832 | tf_op jit(solution)/shard_map/pallas_call | solution.py:447
  107.2 2.1 %collective-permute-done.17.u2 = bf16[512,256]{1,0:T(8,128)(2,1)S(1)} collective-permute-done((bf16[512,256]{1,0:T(8,128)(2,1)}, bf16[512,256]{1,0:T(8,128)(2,1)S(1)}, u32[]{:S(2)}, u32[]{:S(2)}) %collective-permute-start.17) | collective-permute-done | bytes 262176 | tf_op jit(solution)/shard_map/ppermute | solution.py:33
  109.4 4.3 %collective-permute-done.18.u3 = bf16[512,256]{1,0:T(8,128)(2,1)S(1)} collective-permute-done((bf16[512,256]{1,0:T(8,128)(2,1)}, bf16[512,256]{1,0:T(8,128)(2,1)S(1)}, u32[]{:S(2)}, u32[]{:S(2)}) %collective-permute-start.18) | collective-permute-done | bytes 262176 | tf_op jit(solution)/shard_map/ppermute | solution.py:34
  114.4 5.0 %shard_map.177 = (bf16[512,1024]{1,0:T(8,128)(2,1)}, f32[512,256]{1,0:T(8,128)}, f32[512,256]{1,0:T(8,128)}, bf16[512,256]{1,0:T(8,128)(2,1)}, f32[8,256]{1,0:T(8,128)}) custom-call(s32[5]{0:T(128)} %stack.35.at.refs_0_, f32[512,256]{1,0:T(8,128)} %get-tuple-element.128.u_own, bf16[512,256]{1,0:T(8,128)(2,1)} %copy-done.15, bf16[512,256]{1,0:T(8,128)(2,1)} %copy-done.16, ...), custom_call_target="tpu_custom_call" | custom-call | flops 268435456 | bytes 6291456 | tf_op jit(solution)/shard_map/pallas_call | solution.py:678
  123.3 7.1 %shard_map.178 = (bf16[512,768]{1,0:T(8,128)(2,1)}, f32[512,256]{1,0:T(8,128)}, bf16[576,256]{1,0:T(8,128)(2,1)}, bf16[576,256]{1,0:T(8,128)(2,1)}, bf16[576,256]{1,0:T(8,128)(2,1)}, /*index=5*/f32[16,512]{1,0:T(8,128)}) custom-call(s32[5]{0:T(128)} %stack.35.at.refs_0_, bf16[512,256]{1,0:T(8,128)(2,1)} %rows_in.1, bf16[512,256]{1,0:T(8,128)(2,1)} %copy-done.11, ...), custom_call_target="tpu_custom_call" | custom-call | flops 805306368 | bytes 6291456 | tf_op jit(solution)/shard_map/pallas_call | solution.py:755
  131.8 3.2 %collective-permute-start.24 = (bf16[576,256]{1,0:T(8,128)(2,1)}, bf16[576,256]{1,0:T(8,128)(2,1)S(1)}, u32[]{:S(2)}, u32[]{:S(2)}) collective-permute-start(bf16[576,256]{1,0:T(8,128)(2,1)} %get-tuple-element.147), channel_id=1, source_target_pairs={{0,3},{1,0},{2,1},{3,2},{4,7},{5,4},{6,5},{7,6},{8,11},{9,8},{10,9... | collective-permute-start | bytes 884744 | tf_op jit(solution)/shard_map/ppermute | solution.py:876
  135.8 5.2 %shard_map.179 = (bf16[2,4,32,1024]{3,2,1,0:T(8,128)(2,1)}, bf16[2,4,32,1024]{3,2,1,0:T(8,128)(2,1)}, bf16[4,4,32,1024]{3,2,1,0:T(8,128)(2,1)}) custom-call(s32[5]{0:T(128)} %stack.35.at.refs_0_, bf16[512,1024]{1,0:T(8,128)(2,1)} %get-tuple-element.114.refs_1_, bf16[512,768]{1,0:T(8,128)(2,1)} %get-tuple-element.139.refs_2_, ...), custom_call_target="tpu_custom_call" | custom-call | flops 1073741824 | bytes 4194304 | tf_op jit(solution)/shard_map/pallas_call | solution.py:423
  142.9 5.4 %collective-permute-done.23.d2 = bf16[576,256]{1,0:T(8,128)(2,1)S(1)} collective-permute-done((bf16[576,256]{1,0:T(8,128)(2,1)}, bf16[576,256]{1,0:T(8,128)(2,1)S(1)}, u32[]{:S(2)}, u32[]{:S(2)}) %collective-permute-start.23) | collective-permute-done | bytes 294944 | tf_op jit(solution)/shard_map/ppermute | solution.py:876
  149.1 3.1 %shard_map.180 = (bf16[512,256]{1,0:T(8,128)(2,1)}, f32[8,256]{1,0:T(8,128)}) custom-call(f32[512,256]{1,0:T(8,128)} %get-tuple-element.144.d_own, bf16[576,256]{1,0:T(8,128)(2,1)} %copy-done.31, bf16[576,256]{1,0:T(8,128)(2,1)} %copy-done.32, bf16[576,256]{1,0:T(8,128)(2,1)} %copy-done.33, f32[16,512]{1,0:T(8,128)} %get-tuple-element.148.inner, ...), custom_call_target="tpu_custom_call" | custom-call | flops 8589934592 | bytes 2097152 | tf_op jit(solution)/shard_map/pallas_call | solution.py:609
  154.6 3.0 %shard_map.181 = (f32[128,1024]{1,0:T(8,128)}, bf16[144,1024]{1,0:T(8,128)(2,1)}, bf16[144,1024]{1,0:T(8,128)(2,1)}, bf16[144,1024]{1,0:T(8,128)(2,1)}, f32[8,256]{1,0:T(8,128)}) custom-call(s32[5]{0:T(128)} %stack.35.at.refs_0_, bf16[4,4,32,1024]{3,2,1,0:T(8,128)(2,1)} %get-tuple-element.141.keep, bf16[2,4,32,1024]{3,2,1,0:T(8,128)(2,1)} %copy-done.6, ...), custom_call_target="tpu_custom_call" | custom-call | flops 2097152 | bytes 4194304 | tf_op jit(solution)/shard_map/pallas_call | solution.py:489
  157.6 4.1 %collective-permute-start.29 = (bf16[144,1024]{1,0:T(8,128)(2,1)}, bf16[144,1024]{1,0:T(8,128)(2,1)S(1)}, u32[]{:S(2)}, u32[]{:S(2)}) collective-permute-start(bf16[144,1024]{1,0:T(8,128)(2,1)} %get-tuple-element.166), channel_id=1, source_target_pairs={{0,16},{4,20},{8,24},{12,28},{16,0},{20,4},{24,8},{28,12},{32,48},... | collective-permute-start | bytes 884744 | tf_op jit(solution)/shard_map/ppermute | solution.py:895
  162.7 2.4 %collective-permute-start.31 = (bf16[144,1024]{1,0:T(8,128)(2,1)}, bf16[144,1024]{1,0:T(8,128)(2,1)S(1)}, u32[]{:S(2)}, u32[]{:S(2)}) collective-permute-start(bf16[144,1024]{1,0:T(8,128)(2,1)} %get-tuple-element.168), channel_id=1, source_target_pairs={{0,24},{4,28},{8,0},{12,4},{16,8},{20,12},{24,16},{28,20},{32,56},... | collective-permute-start | bytes 884744 | tf_op jit(solution)/shard_map/ppermute | solution.py:895
  165.0 2.0 collective-permute-start.26
  167.0 2.8 %collective-permute-done.29.m1 = bf16[144,1024]{1,0:T(8,128)(2,1)S(1)} collective-permute-done((bf16[144,1024]{1,0:T(8,128)(2,1)}, bf16[144,1024]{1,0:T(8,128)(2,1)S(1)}, u32[]{:S(2)}, u32[]{:S(2)}) %collective-permute-start.29) | collective-permute-done | bytes 294944 | tf_op jit(solution)/shard_map/ppermute | solution.py:895
  171.3 4.4 %collective-permute-done.30.m2 = bf16[144,1024]{1,0:T(8,128)(2,1)S(1)} collective-permute-done((bf16[144,1024]{1,0:T(8,128)(2,1)}, bf16[144,1024]{1,0:T(8,128)(2,1)S(1)}, u32[]{:S(2)}, u32[]{:S(2)}) %collective-permute-start.30) | collective-permute-done | bytes 294944 | tf_op jit(solution)/shard_map/ppermute | solution.py:895
  177.2 2.2 %shard_map.182 = (f32[32,1024]{1,0:T(8,128)}, bf16[48,1024]{1,0:T(8,128)(2,1)}, bf16[48,1024]{1,0:T(8,128)(2,1)}, bf16[48,1024]{1,0:T(8,128)(2,1)}, f32[8,256]{1,0:T(8,128)}) custom-call(s32[5]{0:T(128)} %stack.35.at.refs_0_, f32[128,1024]{1,0:T(8,128)} %get-tuple-element.165.own, bf16[144,1024]{1,0:T(8,128)(2,1)} %copy-done.8, bf16[144,1024]{1,0:T(8,128)(2,1)} %copy-done.9, ...), custom_call_target="tpu_custom_call" | custom-call | flops 2097152 | bytes 2097152 | tf_op jit(solution)/shard_map/pallas_call | solution.py:528
  179.7 3.2 %collective-permute-start.32 = (bf16[48,1024]{1,0:T(8,128)(2,1)}, bf16[48,1024]{1,0:T(8,128)(2,1)S(1)}, u32[]{:S(2)}, u32[]{:S(2)}) collective-permute-start(bf16[48,1024]{1,0:T(8,128)(2,1)} %get-tuple-element.179), channel_id=1, source_target_pairs={{0,64},{4,68},{8,72},{12,76},{16,80},{20,84},{24,88},{28,92},{32,9... | collective-permute-start | bytes 294920 | tf_op jit(solution)/shard_map/ppermute | solution.py:905
  183.5 2.6 %collective-permute-start.34 = (bf16[48,1024]{1,0:T(8,128)(2,1)}, bf16[48,1024]{1,0:T(8,128)(2,1)S(1)}, u32[]{:S(2)}, u32[]{:S(2)}) collective-permute-start(bf16[48,1024]{1,0:T(8,128)(2,1)} %get-tuple-element.181), channel_id=1, source_target_pairs={{0,96},{4,100},{8,104},{12,108},{16,112},{20,116},{24,120},{28,124... | collective-permute-start | bytes 294920 | tf_op jit(solution)/shard_map/ppermute | solution.py:905
  (169 shorter events, 51.1 us)
Async XLA Ops:
  7.2 51.0 %all-gather.2.cloned.1.call-start = ((), (), s32[]{:S(2)}) async-start(), calls=%async_computation.2 | async-start | bytes 1310720 | tf_op jit(solution)/shard_map/all_gather | solution.py:813
  7.2 15.4 %collective-permute-start = (bf16[512,256]{1,0:T(8,128)(2,1)}, bf16[512,256]{1,0:T(8,128)(2,1)S(1)}, u32[]{:S(2)}, u32[]{:S(2)}) collective-permute-start(bf16[512,256]{1,0:T(8,128)(2,1)} %rows_in.1), channel_id=1, source_target_pairs={{0,3},{1,0},{2,1},{3,2},{4,7},{5,4},{6,5},{7,6},{8,11},{9,8},{10,9... | collective-permute-start | bytes 786440 | tf_op jit(solution)/shard_map/ppermute | solution.py:34
  10.1 15.7 %collective-permute-start.1 = (bf16[512,256]{1,0:T(8,128)(2,1)}, bf16[512,256]{1,0:T(8,128)(2,1)S(1)}, u32[]{:S(2)}, u32[]{:S(2)}) collective-permute-start(bf16[512,256]{1,0:T(8,128)(2,1)} %rows_in.1), channel_id=1, source_target_pairs={{0,2},{1,3},{2,0},{3,1},{4,6},{5,7},{6,4},{7,5},{8,10},{9,11},{10,... | collective-permute-start | bytes 786440 | tf_op jit(solution)/shard_map/ppermute | solution.py:33
  10.9 15.9 %collective-permute-start.2 = (bf16[512,256]{1,0:T(8,128)(2,1)}, bf16[512,256]{1,0:T(8,128)(2,1)S(1)}, u32[]{:S(2)}, u32[]{:S(2)}) collective-permute-start(bf16[512,256]{1,0:T(8,128)(2,1)} %rows_in.1), channel_id=1, source_target_pairs={{0,1},{1,2},{2,3},{3,0},{4,5},{5,6},{6,7},{7,4},{8,9},{9,10},{10,1... | collective-permute-start | bytes 786440 | tf_op jit(solution)/shard_map/ppermute | solution.py:34
  12.8 29.6 %collective-permute-start.7 = (bf16[512,256]{1,0:T(8,128)(2,1)S(1)}, bf16[512,256]{1,0:T(8,128)(2,1)S(1)}, u32[]{:S(2)}, u32[]{:S(2)}) collective-permute-start(bf16[512,256]{1,0:T(8,128)(2,1)S(1)} %constant_dynamic-slice_fusion.2.p0), channel_id=1, source_target_pairs={{0,3},{1,0},{2,1},{3,2},{4,7},{5,4},{6,5},{7,6},{8,11},{9,8},{10,9... | collective-permute-start | bytes 786440 | tf_op jit(solution)/shard_map/ppermute | solution.py:34
  15.2 28.6 %collective-permute-start.8 = (bf16[512,256]{1,0:T(8,128)(2,1)S(1)}, bf16[512,256]{1,0:T(8,128)(2,1)S(1)}, u32[]{:S(2)}, u32[]{:S(2)}) collective-permute-start(bf16[512,256]{1,0:T(8,128)(2,1)S(1)} %constant_dynamic-slice_fusion.2.p0), channel_id=1, source_target_pairs={{0,2},{1,3},{2,0},{3,1},{4,6},{5,7},{6,4},{7,5},{8,10},{9,11},{10,... | collective-permute-start | bytes 786440 | tf_op jit(solution)/shard_map/ppermute | solution.py:33
  16.8 140.8 %reduce-scatter.3.cloned.1.call-start = ((), (), s32[]{:S(2)}) async-start(), calls=%async_computation.3 | async-start | bytes 4423680 | tf_op jit(solution)/shard_map/reduce_scatter | solution.py:777
  22.6 21.2 %collective-permute-start.9 = (bf16[512,256]{1,0:T(8,128)(2,1)S(1)}, bf16[512,256]{1,0:T(8,128)(2,1)S(1)}, u32[]{:S(2)}, u32[]{:S(2)}) collective-permute-start(bf16[512,256]{1,0:T(8,128)(2,1)S(1)} %constant_dynamic-slice_fusion.2.p0), channel_id=1, source_target_pairs={{0,1},{1,2},{2,3},{3,0},{4,5},{5,6},{6,7},{7,4},{8,9},{9,10},{10,1... | collective-permute-start | bytes 786440 | tf_op jit(solution)/shard_map/ppermute | solution.py:34
  38.5 14.9 %collective-permute-start.4 = (bf16[512,256]{1,0:T(8,128)(2,1)}, bf16[512,256]{1,0:T(8,128)(2,1)S(1)}, u32[]{:S(2)}, u32[]{:S(2)}) collective-permute-start(bf16[512,256]{1,0:T(8,128)(2,1)} %get-tuple-element.104.m0.refs_4_), channel_id=1, source_target_pairs={{0,3},{1,0},{2,1},{3,2},{4,7},{5,4},{6,5},{7,6},{8,11},{9,8},{10,9... | collective-permute-start | bytes 786440 | tf_op jit(solution)/shard_map/ppermute | solution.py:34
  41.0 12.4 %collective-permute-start.5 = (bf16[512,256]{1,0:T(8,128)(2,1)}, bf16[512,256]{1,0:T(8,128)(2,1)S(1)}, u32[]{:S(2)}, u32[]{:S(2)}) collective-permute-start(bf16[512,256]{1,0:T(8,128)(2,1)} %get-tuple-element.104.m0.refs_4_), channel_id=1, source_target_pairs={{0,2},{1,3},{2,0},{3,1},{4,6},{5,7},{6,4},{7,5},{8,10},{9,11},{10,... | collective-permute-start | bytes 786440 | tf_op jit(solution)/shard_map/ppermute | solution.py:33
  42.4 15.8 %collective-permute-start.6 = (bf16[512,256]{1,0:T(8,128)(2,1)}, bf16[512,256]{1,0:T(8,128)(2,1)S(1)}, u32[]{:S(2)}, u32[]{:S(2)}) collective-permute-start(bf16[512,256]{1,0:T(8,128)(2,1)} %get-tuple-element.104.m0.refs_4_), channel_id=1, source_target_pairs={{0,1},{1,2},{2,3},{3,0},{4,5},{5,6},{6,7},{7,4},{8,9},{9,10},{10,1... | collective-permute-start | bytes 786440 | tf_op jit(solution)/shard_map/ppermute | solution.py:34
  47.6 10.6 %collective-permute-start.10 = (bf16[512,1024]{1,0:T(8,128)(2,1)}, bf16[512,1024]{1,0:T(8,128)(2,1)S(1)}, u32[]{:S(2)}, u32[]{:S(2)}) collective-permute-start(bf16[512,1024]{1,0:T(8,128)(2,1)} %shard_map.172.half), channel_id=1, source_target_pairs={{0,4},{4,0},{8,12},{12,8},{16,20},{20,16},{24,28},{28,24},{32,36},... | collective-permute-start | bytes 3145736 | tf_op jit(solution)/shard_map/ppermute | solution.py:829
  77.5 16.0 %collective-permute-start.13 = (bf16[512,256]{1,0:T(8,128)(2,1)}, bf16[512,256]{1,0:T(8,128)(2,1)S(1)}, u32[]{:S(2)}, u32[]{:S(2)}) collective-permute-start(bf16[512,256]{1,0:T(8,128)(2,1)} %get-tuple-element.122), channel_id=1, source_target_pairs={{0,2},{1,3},{2,0},{3,1},{4,6},{5,7},{6,4},{7,5},{8,10},{9,11},{10,... | collective-permute-start | bytes 786440 | tf_op jit(solution)/shard_map/ppermute | solution.py:854
  80.0 13.5 %collective-permute-start.14 = (bf16[512,256]{1,0:T(8,128)(2,1)}, bf16[512,256]{1,0:T(8,128)(2,1)S(1)}, u32[]{:S(2)}, u32[]{:S(2)}) collective-permute-start(bf16[512,256]{1,0:T(8,128)(2,1)} %get-tuple-element.123), channel_id=1, source_target_pairs={{0,1},{1,2},{2,3},{3,0},{4,5},{5,6},{6,7},{7,4},{8,9},{9,10},{10,1... | collective-permute-start | bytes 786440 | tf_op jit(solution)/shard_map/ppermute | solution.py:854
  80.0 13.5 %collective-permute-start.15 = (bf16[512,256]{1,0:T(8,128)(2,1)}, bf16[512,256]{1,0:T(8,128)(2,1)S(1)}, u32[]{:S(2)}, u32[]{:S(2)}) collective-permute-start(bf16[512,256]{1,0:T(8,128)(2,1)} %get-tuple-element.124), channel_id=1, source_target_pairs={{0,3},{1,0},{2,1},{3,2},{4,7},{5,4},{6,5},{7,6},{8,11},{9,8},{10,9... | collective-permute-start | bytes 786440 | tf_op jit(solution)/shard_map/ppermute | solution.py:854
  93.0 7.0 %collective-permute-start.12 = (bf16[2,4,32,3456]{3,2,1,0:T(8,128)(2,1)}, bf16[2,4,32,3456]{3,2,1,0:T(8,128)(2,1)S(1)}, u32[]{:S(2)}, u32[]{:S(2)}) collective-permute-start(bf16[2,4,32,3456]{3,2,1,0:T(8,128)(2,1)} %get-tuple-element.120), channel_id=1, source_target_pairs={{0,4},{4,0},{8,12},{12,8},{16,20},{20,16},{24,28},{28,24},{32,36},... | collective-permute-start | bytes 5308424 | tf_op jit(solution)/shard_map/ppermute | solution.py:436
  97.1 10.1 %collective-permute-start.16 = (bf16[512,256]{1,0:T(8,128)(2,1)}, bf16[512,256]{1,0:T(8,128)(2,1)S(1)}, u32[]{:S(2)}, u32[]{:S(2)}) collective-permute-start(bf16[512,256]{1,0:T(8,128)(2,1)} %get-tuple-element.127), channel_id=1, source_target_pairs={{0,3},{1,0},{2,1},{3,2},{4,7},{5,4},{6,5},{7,6},{8,11},{9,8},{10,9... | collective-permute-start | bytes 786440 | tf_op jit(solution)/shard_map/ppermute | solution.py:34
  98.4 11.0 %collective-permute-start.17 = (bf16[512,256]{1,0:T(8,128)(2,1)}, bf16[512,256]{1,0:T(8,128)(2,1)S(1)}, u32[]{:S(2)}, u32[]{:S(2)}) collective-permute-start(bf16[512,256]{1,0:T(8,128)(2,1)} %get-tuple-element.127), channel_id=1, source_target_pairs={{0,2},{1,3},{2,0},{3,1},{4,6},{5,7},{6,4},{7,5},{8,10},{9,11},{10,... | collective-permute-start | bytes 786440 | tf_op jit(solution)/shard_map/ppermute | solution.py:33
  100.0 13.7 %collective-permute-start.18 = (bf16[512,256]{1,0:T(8,128)(2,1)}, bf16[512,256]{1,0:T(8,128)(2,1)S(1)}, u32[]{:S(2)}, u32[]{:S(2)}) collective-permute-start(bf16[512,256]{1,0:T(8,128)(2,1)} %get-tuple-element.127), channel_id=1, source_target_pairs={{0,1},{1,2},{2,3},{3,0},{4,5},{5,6},{6,7},{7,4},{8,9},{9,10},{10,1... | collective-permute-start | bytes 786440 | tf_op jit(solution)/shard_map/ppermute | solution.py:34
  113.7 73.2 %reduce-scatter.5.cloned.1.call-start = ((), (), s32[]{:S(2)}) async-start(), calls=%async_computation.4 | async-start | bytes 1105920 | tf_op jit(solution)/shard_map/reduce_scatter | solution.py:777
  130.4 12.4 %collective-permute-start.22 = (bf16[576,256]{1,0:T(8,128)(2,1)}, bf16[576,256]{1,0:T(8,128)(2,1)S(1)}, u32[]{:S(2)}, u32[]{:S(2)}) collective-permute-start(bf16[576,256]{1,0:T(8,128)(2,1)} %get-tuple-element.145), channel_id=1, source_target_pairs={{0,2},{1,3},{2,0},{3,1},{4,6},{5,7},{6,4},{7,5},{8,10},{9,11},{10,... | collective-permute-start | bytes 884744 | tf_op jit(solution)/shard_map/ppermute | solution.py:876
  131.8 16.6 %collective-permute-start.23 = (bf16[576,256]{1,0:T(8,128)(2,1)}, bf16[576,256]{1,0:T(8,128)(2,1)S(1)}, u32[]{:S(2)}, u32[]{:S(2)}) collective-permute-start(bf16[576,256]{1,0:T(8,128)(2,1)} %get-tuple-element.146), channel_id=1, source_target_pairs={{0,1},{1,2},{2,3},{3,0},{4,5},{5,6},{6,7},{7,4},{8,9},{9,10},{10,1... | collective-permute-start | bytes 884744 | tf_op jit(solution)/shard_map/ppermute | solution.py:876
  131.8 16.6 %collective-permute-start.24 = (bf16[576,256]{1,0:T(8,128)(2,1)}, bf16[576,256]{1,0:T(8,128)(2,1)S(1)}, u32[]{:S(2)}, u32[]{:S(2)}) collective-permute-start(bf16[576,256]{1,0:T(8,128)(2,1)} %get-tuple-element.147), channel_id=1, source_target_pairs={{0,3},{1,0},{2,1},{3,2},{4,7},{5,4},{6,5},{7,6},{8,11},{9,8},{10,9... | collective-permute-start | bytes 884744 | tf_op jit(solution)/shard_map/ppermute | solution.py:876
  140.9 12.7 %collective-permute-start.20 = (bf16[2,4,32,1024]{3,2,1,0:T(8,128)(2,1)}, bf16[2,4,32,1024]{3,2,1,0:T(8,128)(2,1)S(1)}, u32[]{:S(2)}, u32[]{:S(2)}) collective-permute-start(bf16[2,4,32,1024]{3,2,1,0:T(8,128)(2,1)} %get-tuple-element.142), channel_id=1, source_target_pairs={{0,4},{4,0},{8,12},{12,8},{16,20},{20,16},{24,28},{28,24},{32,36},... | collective-permute-start | bytes 1572872 | tf_op jit(solution)/shard_map/ppermute | solution.py:436
  142.8 10.8 %collective-permute-start.21 = (bf16[2,4,32,1024]{3,2,1,0:T(8,128)(2,1)}, bf16[2,4,32,1024]{3,2,1,0:T(8,128)(2,1)S(1)}, u32[]{:S(2)}, u32[]{:S(2)}) collective-permute-start(bf16[2,4,32,1024]{3,2,1,0:T(8,128)(2,1)} %get-tuple-element.143), channel_id=1, source_target_pairs={{0,4},{4,0},{8,12},{12,8},{16,20},{20,16},{24,28},{28,24},{32,36},... | collective-permute-start | bytes 1572872 | tf_op jit(solution)/shard_map/ppermute | solution.py:436
  157.6 12.2 %collective-permute-start.29 = (bf16[144,1024]{1,0:T(8,128)(2,1)}, bf16[144,1024]{1,0:T(8,128)(2,1)S(1)}, u32[]{:S(2)}, u32[]{:S(2)}) collective-permute-start(bf16[144,1024]{1,0:T(8,128)(2,1)} %get-tuple-element.166), channel_id=1, source_target_pairs={{0,16},{4,20},{8,24},{12,28},{16,0},{20,4},{24,8},{28,12},{32,48},... | collective-permute-start | bytes 884744 | tf_op jit(solution)/shard_map/ppermute | solution.py:895
  161.8 13.9 %collective-permute-start.30 = (bf16[144,1024]{1,0:T(8,128)(2,1)}, bf16[144,1024]{1,0:T(8,128)(2,1)S(1)}, u32[]{:S(2)}, u32[]{:S(2)}) collective-permute-start(bf16[144,1024]{1,0:T(8,128)(2,1)} %get-tuple-element.167), channel_id=1, source_target_pairs={{0,8},{4,12},{8,16},{12,20},{16,24},{20,28},{24,0},{28,4},{32,40},... | collective-permute-start | bytes 884744 | tf_op jit(solution)/shard_map/ppermute | solution.py:895
  162.7 13.8 %collective-permute-start.31 = (bf16[144,1024]{1,0:T(8,128)(2,1)}, bf16[144,1024]{1,0:T(8,128)(2,1)S(1)}, u32[]{:S(2)}, u32[]{:S(2)}) collective-permute-start(bf16[144,1024]{1,0:T(8,128)(2,1)} %get-tuple-element.168), channel_id=1, source_target_pairs={{0,24},{4,28},{8,0},{12,4},{16,8},{20,12},{24,16},{28,20},{32,56},... | collective-permute-start | bytes 884744 | tf_op jit(solution)/shard_map/ppermute | solution.py:895
  165.0 14.4 %collective-permute-start.26 = (bf16[512,256]{1,0:T(8,128)(2,1)S(1)}, bf16[512,256]{1,0:T(8,128)(2,1)S(1)}, u32[]{:S(2)}, u32[]{:S(2)}) collective-permute-start(bf16[512,256]{1,0:T(8,128)(2,1)S(1)} %copy-done.36), channel_id=1, source_target_pairs={{0,2},{1,3},{2,0},{3,1},{4,6},{5,7},{6,4},{7,5},{8,10},{9,11},{10,... | collective-permute-start | bytes 786440 | tf_op jit(solution)/shard_map/ppermute | solution.py:897
  167.0 12.7 %collective-permute-start.27 = (bf16[512,256]{1,0:T(8,128)(2,1)S(1)}, bf16[512,256]{1,0:T(8,128)(2,1)S(1)}, u32[]{:S(2)}, u32[]{:S(2)}) collective-permute-start(bf16[512,256]{1,0:T(8,128)(2,1)S(1)} %copy-done.35), channel_id=1, source_target_pairs={{0,1},{1,2},{2,3},{3,0},{4,5},{5,6},{6,7},{7,4},{8,9},{9,10},{10,1... | collective-permute-start | bytes 786440 | tf_op jit(solution)/shard_map/ppermute | solution.py:897
  169.8 9.9 %collective-permute-start.28 = (bf16[512,256]{1,0:T(8,128)(2,1)S(1)}, bf16[512,256]{1,0:T(8,128)(2,1)S(1)}, u32[]{:S(2)}, u32[]{:S(2)}) collective-permute-start(bf16[512,256]{1,0:T(8,128)(2,1)S(1)} %copy-done.34), channel_id=1, source_target_pairs={{0,3},{1,0},{2,1},{3,2},{4,7},{5,4},{6,5},{7,6},{8,11},{9,8},{10,9... | collective-permute-start | bytes 786440 | tf_op jit(solution)/shard_map/ppermute | solution.py:897
  179.7 9.8 %collective-permute-start.32 = (bf16[48,1024]{1,0:T(8,128)(2,1)}, bf16[48,1024]{1,0:T(8,128)(2,1)S(1)}, u32[]{:S(2)}, u32[]{:S(2)}) collective-permute-start(bf16[48,1024]{1,0:T(8,128)(2,1)} %get-tuple-element.179), channel_id=1, source_target_pairs={{0,64},{4,68},{8,72},{12,76},{16,80},{20,84},{24,88},{28,92},{32,9... | collective-permute-start | bytes 294920 | tf_op jit(solution)/shard_map/ppermute | solution.py:905
  (51 other events, 302.0 us)
Sparse Core Ops, SparseCore 0:
  16.9 35.7 all-gather.1
  113.8 42.9 reduce-scatter.2
  159.3 22.6 reduce-scatter.4

commit v7 on v6

--- a/solution.py
+++ b/solution.py
@@ -146,7 +146,10 @@
     v_out[...] = v
     product = (b * v).astype(BF16)
     gated[...] = product
-    edge[...] = product[-16:]
+    rows = product.shape[0]
+    token = lax.broadcasted_iota(jnp.int32, (16, width), 0)
+    crosses = (token == 14) & (at[2] == rows - 1)
+    edge[...] = jnp.where(crosses, 0.0, product[-16:].astype(F32)).astype(BF16)
     c_out[...] = dot_nn(normed[...], held[1])
 
 
@@ -714,7 +717,7 @@
     after_one = jnp.where(token == rows - 1, next_one, after_one)
     after_two = pltpu.roll(d, rows - 2, 0)
     after_two = jnp.where((token + 2 == count) | (token + 1 == count), 0.0, after_two)
-    after_two = jnp.where(token == rows - 2, next_one, after_two)
+    after_two = jnp.where(token == rows - 2, jnp.where(count == rows - 1, 0.0, next_one), after_two)
     after_two = jnp.where(token == rows - 1, next_two, after_two)
     d_gated = taps[0:1, :] * d + taps[1:2, :] * after_one + taps[2:3, :] * after_two
     grads[:, :width] = (d_gated * value[...]).astype(BF16)

time: 199 us -> 199 us (level)
  no operation moved by 1% of the time
where the time goes in v7:
time: 199 us; the launch traced here: 198 us
  Pallas kernels  74.8 us (38%)
  starting transfers between devices  51.8 us (26%)
  waiting for transfers between devices  32.8 us (16%)
  local copies, waits for them, and re-layouts  20.3 us (10%)
  between operations  14.1 us (7%)
  other arithmetic  4.55 us (2%)
    pallas_call x1, Pallas kernels, ffn(): pl.pallas_call(ffn_kernel, out_shape=(shape((rows, features), F32), shape...  18.3 us
    pallas_call x2, Pallas kernels, pair_products(): pl.pallas_call(body, grid=(4,), out_shape=(half, half, out), in_specs=[sm...  14.9 us
    ppermute x8, waiting for transfers between devices, gather_ch(): near = [lax.ppermute(block, 'ch', ch_pairs(-j)) for j in (1, 3)]  13.9 us
    ppermute x8, starting transfers between devices, gather_ch(): near = [lax.ppermute(block, 'ch', ch_pairs(-j)) for j in (1, 3)]  11.4 us
    unnamed x90, local copies, waits for them, and re-layouts  10.7 us
    ppermute x6, starting transfers between devices, shards(): lax.ppermute(d, 'ch', ch_pairs(j))  10.3 us
    ppermute x3, waiting for transfers between devices, shards(): lax.ppermute(m, 'seq', seq_pairs(0, j, 0))  7.97 us
    ppermute x3, starting transfers between devices, shards(): lax.ppermute(m, 'seq', seq_pairs(0, j, 0))  7.38 us
  transfers between devices with their start and end apart: 38, of which 13 were waited for; matrix products, arithmetic and copies ran while one was open for 7% of the time, Pallas kernels for 28%

profile of v7, /device:TPU:0, one launch (start us, length us, event | category | flops | bytes accessed | tf_op | source)
XLA Modules:
  0.0 198.5 jit_solution(4165475147180959646)
XLA Ops:
  7.2 2.9 %collective-permute-start = (bf16[512,256]{1,0:T(8,128)(2,1)}, bf16[512,256]{1,0:T(8,128)(2,1)S(1)}, u32[]{:S(2)}, u32[]{:S(2)}) collective-permute-start(bf16[512,256]{1,0:T(8,128)(2,1)} %rows_in.1), channel_id=1, source_target_pairs={{0,3},{1,0},{2,1},{3,2},{4,7},{5,4},{6,5},{7,6},{8,11},{9,8},{10,9... | collective-permute-start | bytes 786440 | tf_op jit(solution)/shard_map/ppermute | solution.py:34
  12.8 2.4 %collective-permute-start.7 = (bf16[512,256]{1,0:T(8,128)(2,1)S(1)}, bf16[512,256]{1,0:T(8,128)(2,1)S(1)}, u32[]{:S(2)}, u32[]{:S(2)}) collective-permute-start(bf16[512,256]{1,0:T(8,128)(2,1)S(1)} %constant_dynamic-slice_fusion.2.p0), channel_id=1, source_target_pairs={{0,3},{1,0},{2,1},{3,2},{4,7},{5,4},{6,5},{7,6},{8,11},{9,8},{10,9... | collective-permute-start | bytes 786440 | tf_op jit(solution)/shard_map/ppermute | solution.py:34
  18.7 3.9 %collective-permute-done.p1.x1 = bf16[512,256]{1,0:T(8,128)(2,1)S(1)} collective-permute-done((bf16[512,256]{1,0:T(8,128)(2,1)}, bf16[512,256]{1,0:T(8,128)(2,1)S(1)}, u32[]{:S(2)}, u32[]{:S(2)}) %collective-permute-start) | collective-permute-done | bytes 262176 | tf_op jit(solution)/shard_map/ppermute | solution.py:34
  27.5 5.2 %shard_map.169 = (bf16[512,1024]{1,0:T(8,128)(2,1)}, f32[512,1]{1,0:T(8,128)}, f32[512,256]{1,0:T(8,128)}, f32[512,256]{1,0:T(8,128)}, f32[512,256]{1,0:T(8,128)...) custom-call(s32[5]{0:T(128)} %stack.35.at.refs_0_, bf16[512,256]{1,0:T(8,128)(2,1)} %rows_in.1, ...), custom_call_target="tpu_custom_call" | custom-call | flops 805306368 | bytes 6291456 | tf_op jit(solution)/shard_map/pallas_call | solution.py:160
  36.0 2.4 %shard_map.170 = (bf16[512,256]{1,0:T(8,128)(2,1)}, f32[512,256]{1,0:T(8,128)}, bf16[512,256]{1,0:T(8,128)(2,1)}, bf16[512,256]{1,0:T(8,128)(2,1)}) custom-call(s32[5]{0:T(128)} %stack.35.at.refs_0_, bf16[512,256]{1,0:T(8,128)(2,1)} %get-tuple-element.101.gated, bf16[16,256]{1,0:T(8,128)(2,1)} %copy-done.29, f32[512,256]{1,0:T(8,128)} %get-tuple-element.103.c_gate, ...), custom_call_target="tpu_custom_call" | custom-call | flops 8388608 | bytes 2097152 | tf_op jit(solution)/shard_map/pallas_call | solution.py:222
  38.5 2.5 %collective-permute-start.4 = (bf16[512,256]{1,0:T(8,128)(2,1)}, bf16[512,256]{1,0:T(8,128)(2,1)S(1)}, u32[]{:S(2)}, u32[]{:S(2)}) collective-permute-start(bf16[512,256]{1,0:T(8,128)(2,1)} %get-tuple-element.104.m0.refs_4_), channel_id=1, source_target_pairs={{0,3},{1,0},{2,1},{3,2},{4,7},{5,4},{6,5},{7,6},{8,11},{9,8},{10,9... | collective-permute-start | bytes 786440 | tf_op jit(solution)/shard_map/ppermute | solution.py:34
  45.2 2.3 %shard_map.172.half = bf16[512,1024]{1,0:T(8,128)(2,1)} custom-call(bf16[512,256]{1,0:T(8,128)(2,1)} %copy-done.4, bf16[512,256]{1,0:T(8,128)(2,1)} %copy-done.20, bf16[512,256]{1,0:T(8,128)(2,1)} %copy-done.21, bf16[512,256]{1,0:T(8,128)(2,1)} %copy-done.22), custom_call_target="tpu_custom_call" | custom-call | flops 2097152 | bytes 2097152 | tf_op jit(solution)/shard_map/pallas_call | solution.py:190
  50.7 2.8 %copy.21 = bf16[1024,2,1152]{2,0,1:T(8,128)(2,1)} copy(bf16[1024,2,1152]{2,1,0:T(2,128)(2,1)S(1)} %bitcast.23) | data formatting | bytes 9437184 | tf_op jit(solution)/shard_map/optimization_barrier | solution.py:67
  53.4 4.7 %collective-permute-done.6.m3 = bf16[512,256]{1,0:T(8,128)(2,1)S(1)} collective-permute-done((bf16[512,256]{1,0:T(8,128)(2,1)}, bf16[512,256]{1,0:T(8,128)(2,1)S(1)}, u32[]{:S(2)}, u32[]{:S(2)}) %collective-permute-start.6) | collective-permute-done | bytes 262176 | tf_op jit(solution)/shard_map/ppermute | solution.py:34
  59.2 18.3 %shard_map.173 = (f32[512,1024]{1,0:T(8,128)}, f32[512,256]{1,0:T(8,128)}, f32[512,1]{1,0:T(8,128)}, bf16[512,1024]{1,0:T(8,128)(2,1)}, bf16[512,1152]{1,0:T(8,1...) custom-call(s32[5]{0:T(128)} %stack.35.at.refs_0_, ...), custom_call_target="tpu_custom_call" | custom-call | flops 8321499136 | bytes 20971520 | tf_op jit(solution)/shard_map/pallas_call | solution.py:354
  77.5 2.5 %collective-permute-start.13 = (bf16[512,256]{1,0:T(8,128)(2,1)}, bf16[512,256]{1,0:T(8,128)(2,1)S(1)}, u32[]{:S(2)}, u32[]{:S(2)}) collective-permute-start(bf16[512,256]{1,0:T(8,128)(2,1)} %get-tuple-element.122), channel_id=1, source_target_pairs={{0,2},{1,3},{2,0},{3,1},{4,6},{5,7},{6,4},{7,5},{8,10},{9,11},{10,... | collective-permute-start | bytes 786440 | tf_op jit(solution)/shard_map/ppermute | solution.py:857
  80.0 3.2 %collective-permute-start.15 = (bf16[512,256]{1,0:T(8,128)(2,1)}, bf16[512,256]{1,0:T(8,128)(2,1)S(1)}, u32[]{:S(2)}, u32[]{:S(2)}) collective-permute-start(bf16[512,256]{1,0:T(8,128)(2,1)} %get-tuple-element.124), channel_id=1, source_target_pairs={{0,3},{1,0},{2,1},{3,2},{4,7},{5,4},{6,5},{7,6},{8,11},{9,8},{10,9... | collective-permute-start | bytes 786440 | tf_op jit(solution)/shard_map/ppermute | solution.py:857
  83.2 9.8 %shard_map.174 = (bf16[2,4,32,3456]{3,2,1,0:T(8,128)(2,1)}, bf16[2,4,32,3456]{3,2,1,0:T(8,128)(2,1)}, bf16[4,4,32,3456]{3,2,1,0:T(8,128)(2,1)}) custom-call(s32[5]{0:T(128)} %stack.35.at.refs_0_, bf16[512,1024]{1,0:T(8,128)(2,1)} %get-tuple-element.115.refs_1_, bf16[512,2304]{1,0:T(8,128)(2,1)} %get-tuple-element.116.refs_2_, ...), custom_call_target="tpu_custom_call" | custom-call | flops 3623878656 | bytes 14155776 | tf_op jit(solution)/shard_map/pallas_call | solution.py:426
  94.4 2.8 %shard_map.176 = (f32[512,256]{1,0:T(8,128)}, bf16[512,256]{1,0:T(8,128)(2,1)}, f32[1,256]{1,0:T(1,128)}) custom-call(f32[512,256]{1,0:T(8,128)} %get-tuple-element.121.d_own, bf16[512,256]{1,0:T(8,128)(2,1)} %copy-done.40, bf16[512,256]{1,0:T(8,128)(2,1)} %copy-done.41, bf16[512,256]{1,0:T(8,128)(2,1)} %copy-done.42, f32[512,256]{1,0:T(8,128)} %get-tuple-element.113.h, ...), custom_call_target="tpu_custom_call" | custom-call | flops 137438953472 | bytes 2097152 | tf_op jit(solution)/shard_map/pallas_call | solution.py:635
  101.8 5.4 %shard_map.175 = bf16[4,4,32,3456]{3,2,1,0:T(8,128)(2,1)} custom-call(bf16[4,4,32,3456]{3,2,1,0:T(8,128)(2,1)} %get-tuple-element.118.keep, bf16[2,4,32,3456]{3,2,1,0:T(8,128)(2,1)} %copy-done.1, bf16[2,4,32,3456]{3,2,1,0:T(8,128)(2,1)} %copy-done.2), custom_call_target="tpu_custom_call" | custom-call | flops 2097152 | bytes 10616832 | tf_op jit(solution)/shard_map/pallas_call | solution.py:450
  107.2 2.1 %collective-permute-done.17.u2 = bf16[512,256]{1,0:T(8,128)(2,1)S(1)} collective-permute-done((bf16[512,256]{1,0:T(8,128)(2,1)}, bf16[512,256]{1,0:T(8,128)(2,1)S(1)}, u32[]{:S(2)}, u32[]{:S(2)}) %collective-permute-start.17) | collective-permute-done | bytes 262176 | tf_op jit(solution)/shard_map/ppermute | solution.py:33
  109.4 4.3 %collective-permute-done.18.u3 = bf16[512,256]{1,0:T(8,128)(2,1)S(1)} collective-permute-done((bf16[512,256]{1,0:T(8,128)(2,1)}, bf16[512,256]{1,0:T(8,128)(2,1)S(1)}, u32[]{:S(2)}, u32[]{:S(2)}) %collective-permute-start.18) | collective-permute-done | bytes 262176 | tf_op jit(solution)/shard_map/ppermute | solution.py:34
  114.4 5.0 %shard_map.177 = (bf16[512,1024]{1,0:T(8,128)(2,1)}, f32[512,256]{1,0:T(8,128)}, f32[512,256]{1,0:T(8,128)}, bf16[512,256]{1,0:T(8,128)(2,1)}, f32[8,256]{1,0:T(8,128)}) custom-call(s32[5]{0:T(128)} %stack.35.at.refs_0_, f32[512,256]{1,0:T(8,128)} %get-tuple-element.128.u_own, bf16[512,256]{1,0:T(8,128)(2,1)} %copy-done.15, bf16[512,256]{1,0:T(8,128)(2,1)} %copy-done.16, ...), custom_call_target="tpu_custom_call" | custom-call | flops 268435456 | bytes 6291456 | tf_op jit(solution)/shard_map/pallas_call | solution.py:681
  123.3 7.1 %shard_map.178 = (bf16[512,768]{1,0:T(8,128)(2,1)}, f32[512,256]{1,0:T(8,128)}, bf16[576,256]{1,0:T(8,128)(2,1)}, bf16[576,256]{1,0:T(8,128)(2,1)}, bf16[576,256]{1,0:T(8,128)(2,1)}, /*index=5*/f32[16,512]{1,0:T(8,128)}) custom-call(s32[5]{0:T(128)} %stack.35.at.refs_0_, bf16[512,256]{1,0:T(8,128)(2,1)} %rows_in.1, bf16[512,256]{1,0:T(8,128)(2,1)} %copy-done.11, ...), custom_call_target="tpu_custom_call" | custom-call | flops 805306368 | bytes 6291456 | tf_op jit(solution)/shard_map/pallas_call | solution.py:758
  131.8 3.2 %collective-permute-start.24 = (bf16[576,256]{1,0:T(8,128)(2,1)}, bf16[576,256]{1,0:T(8,128)(2,1)S(1)}, u32[]{:S(2)}, u32[]{:S(2)}) collective-permute-start(bf16[576,256]{1,0:T(8,128)(2,1)} %get-tuple-element.147), channel_id=1, source_target_pairs={{0,3},{1,0},{2,1},{3,2},{4,7},{5,4},{6,5},{7,6},{8,11},{9,8},{10,9... | collective-permute-start | bytes 884744 | tf_op jit(solution)/shard_map/ppermute | solution.py:879
  135.8 5.2 %shard_map.179 = (bf16[2,4,32,1024]{3,2,1,0:T(8,128)(2,1)}, bf16[2,4,32,1024]{3,2,1,0:T(8,128)(2,1)}, bf16[4,4,32,1024]{3,2,1,0:T(8,128)(2,1)}) custom-call(s32[5]{0:T(128)} %stack.35.at.refs_0_, bf16[512,1024]{1,0:T(8,128)(2,1)} %get-tuple-element.114.refs_1_, bf16[512,768]{1,0:T(8,128)(2,1)} %get-tuple-element.139.refs_2_, ...), custom_call_target="tpu_custom_call" | custom-call | flops 1073741824 | bytes 4194304 | tf_op jit(solution)/shard_map/pallas_call | solution.py:426
  142.9 5.4 %collective-permute-done.23.d2 = bf16[576,256]{1,0:T(8,128)(2,1)S(1)} collective-permute-done((bf16[576,256]{1,0:T(8,128)(2,1)}, bf16[576,256]{1,0:T(8,128)(2,1)S(1)}, u32[]{:S(2)}, u32[]{:S(2)}) %collective-permute-start.23) | collective-permute-done | bytes 294944 | tf_op jit(solution)/shard_map/ppermute | solution.py:879
  149.1 3.1 %shard_map.180 = (bf16[512,256]{1,0:T(8,128)(2,1)}, f32[8,256]{1,0:T(8,128)}) custom-call(f32[512,256]{1,0:T(8,128)} %get-tuple-element.144.d_own, bf16[576,256]{1,0:T(8,128)(2,1)} %copy-done.31, bf16[576,256]{1,0:T(8,128)(2,1)} %copy-done.32, bf16[576,256]{1,0:T(8,128)(2,1)} %copy-done.33, f32[16,512]{1,0:T(8,128)} %get-tuple-element.148.inner, ...), custom_call_target="tpu_custom_call" | custom-call | flops 8589934592 | bytes 2097152 | tf_op jit(solution)/shard_map/pallas_call | solution.py:612
  154.6 3.0 %shard_map.181 = (f32[128,1024]{1,0:T(8,128)}, bf16[144,1024]{1,0:T(8,128)(2,1)}, bf16[144,1024]{1,0:T(8,128)(2,1)}, bf16[144,1024]{1,0:T(8,128)(2,1)}, f32[8,256]{1,0:T(8,128)}) custom-call(s32[5]{0:T(128)} %stack.35.at.refs_0_, bf16[4,4,32,1024]{3,2,1,0:T(8,128)(2,1)} %get-tuple-element.141.keep, bf16[2,4,32,1024]{3,2,1,0:T(8,128)(2,1)} %copy-done.6, ...), custom_call_target="tpu_custom_call" | custom-call | flops 2097152 | bytes 4194304 | tf_op jit(solution)/shard_map/pallas_call | solution.py:492
  157.6 4.1 %collective-permute-start.29 = (bf16[144,1024]{1,0:T(8,128)(2,1)}, bf16[144,1024]{1,0:T(8,128)(2,1)S(1)}, u32[]{:S(2)}, u32[]{:S(2)}) collective-permute-start(bf16[144,1024]{1,0:T(8,128)(2,1)} %get-tuple-element.166), channel_id=1, source_target_pairs={{0,16},{4,20},{8,24},{12,28},{16,0},{20,4},{24,8},{28,12},{32,48},... | collective-permute-start | bytes 884744 | tf_op jit(solution)/shard_map/ppermute | solution.py:898
  162.7 2.4 %collective-permute-start.31 = (bf16[144,1024]{1,0:T(8,128)(2,1)}, bf16[144,1024]{1,0:T(8,128)(2,1)S(1)}, u32[]{:S(2)}, u32[]{:S(2)}) collective-permute-start(bf16[144,1024]{1,0:T(8,128)(2,1)} %get-tuple-element.168), channel_id=1, source_target_pairs={{0,24},{4,28},{8,0},{12,4},{16,8},{20,12},{24,16},{28,20},{32,56},... | collective-permute-start | bytes 884744 | tf_op jit(solution)/shard_map/ppermute | solution.py:898
  165.0 2.0 collective-permute-start.26
  167.0 2.8 %collective-permute-done.29.m1 = bf16[144,1024]{1,0:T(8,128)(2,1)S(1)} collective-permute-done((bf16[144,1024]{1,0:T(8,128)(2,1)}, bf16[144,1024]{1,0:T(8,128)(2,1)S(1)}, u32[]{:S(2)}, u32[]{:S(2)}) %collective-permute-start.29) | collective-permute-done | bytes 294944 | tf_op jit(solution)/shard_map/ppermute | solution.py:898
  171.3 4.4 %collective-permute-done.30.m2 = bf16[144,1024]{1,0:T(8,128)(2,1)S(1)} collective-permute-done((bf16[144,1024]{1,0:T(8,128)(2,1)}, bf16[144,1024]{1,0:T(8,128)(2,1)S(1)}, u32[]{:S(2)}, u32[]{:S(2)}) %collective-permute-start.30) | collective-permute-done | bytes 294944 | tf_op jit(solution)/shard_map/ppermute | solution.py:898
  177.2 2.2 %shard_map.182 = (f32[32,1024]{1,0:T(8,128)}, bf16[48,1024]{1,0:T(8,128)(2,1)}, bf16[48,1024]{1,0:T(8,128)(2,1)}, bf16[48,1024]{1,0:T(8,128)(2,1)}, f32[8,256]{1,0:T(8,128)}) custom-call(s32[5]{0:T(128)} %stack.35.at.refs_0_, f32[128,1024]{1,0:T(8,128)} %get-tuple-element.165.own, bf16[144,1024]{1,0:T(8,128)(2,1)} %copy-done.8, bf16[144,1024]{1,0:T(8,128)(2,1)} %copy-done.9, ...), custom_call_target="tpu_custom_call" | custom-call | flops 2097152 | bytes 2097152 | tf_op jit(solution)/shard_map/pallas_call | solution.py:531
  179.7 3.2 %collective-permute-start.32 = (bf16[48,1024]{1,0:T(8,128)(2,1)}, bf16[48,1024]{1,0:T(8,128)(2,1)S(1)}, u32[]{:S(2)}, u32[]{:S(2)}) collective-permute-start(bf16[48,1024]{1,0:T(8,128)(2,1)} %get-tuple-element.179), channel_id=1, source_target_pairs={{0,64},{4,68},{8,72},{12,76},{16,80},{20,84},{24,88},{28,92},{32,9... | collective-permute-start | bytes 294920 | tf_op jit(solution)/shard_map/ppermute | solution.py:908
  183.5 2.6 %collective-permute-start.34 = (bf16[48,1024]{1,0:T(8,128)(2,1)}, bf16[48,1024]{1,0:T(8,128)(2,1)S(1)}, u32[]{:S(2)}, u32[]{:S(2)}) collective-permute-start(bf16[48,1024]{1,0:T(8,128)(2,1)} %get-tuple-element.181), channel_id=1, source_target_pairs={{0,96},{4,100},{8,104},{12,108},{16,112},{20,116},{24,120},{28,124... | collective-permute-start | bytes 294920 | tf_op jit(solution)/shard_map/ppermute | solution.py:908
  (169 shorter events, 51.1 us)
Async XLA Ops:
  7.2 51.0 %all-gather.2.cloned.1.call-start = ((), (), s32[]{:S(2)}) async-start(), calls=%async_computation.2 | async-start | bytes 1310720 | tf_op jit(solution)/shard_map/all_gather | solution.py:816
  7.2 15.4 %collective-permute-start = (bf16[512,256]{1,0:T(8,128)(2,1)}, bf16[512,256]{1,0:T(8,128)(2,1)S(1)}, u32[]{:S(2)}, u32[]{:S(2)}) collective-permute-start(bf16[512,256]{1,0:T(8,128)(2,1)} %rows_in.1), channel_id=1, source_target_pairs={{0,3},{1,0},{2,1},{3,2},{4,7},{5,4},{6,5},{7,6},{8,11},{9,8},{10,9... | collective-permute-start | bytes 786440 | tf_op jit(solution)/shard_map/ppermute | solution.py:34
  10.1 15.7 %collective-permute-start.1 = (bf16[512,256]{1,0:T(8,128)(2,1)}, bf16[512,256]{1,0:T(8,128)(2,1)S(1)}, u32[]{:S(2)}, u32[]{:S(2)}) collective-permute-start(bf16[512,256]{1,0:T(8,128)(2,1)} %rows_in.1), channel_id=1, source_target_pairs={{0,2},{1,3},{2,0},{3,1},{4,6},{5,7},{6,4},{7,5},{8,10},{9,11},{10,... | collective-permute-start | bytes 786440 | tf_op jit(solution)/shard_map/ppermute | solution.py:33
  10.9 15.9 %collective-permute-start.2 = (bf16[512,256]{1,0:T(8,128)(2,1)}, bf16[512,256]{1,0:T(8,128)(2,1)S(1)}, u32[]{:S(2)}, u32[]{:S(2)}) collective-permute-start(bf16[512,256]{1,0:T(8,128)(2,1)} %rows_in.1), channel_id=1, source_target_pairs={{0,1},{1,2},{2,3},{3,0},{4,5},{5,6},{6,7},{7,4},{8,9},{9,10},{10,1... | collective-permute-start | bytes 786440 | tf_op jit(solution)/shard_map/ppermute | solution.py:34
  12.8 29.6 %collective-permute-start.7 = (bf16[512,256]{1,0:T(8,128)(2,1)S(1)}, bf16[512,256]{1,0:T(8,128)(2,1)S(1)}, u32[]{:S(2)}, u32[]{:S(2)}) collective-permute-start(bf16[512,256]{1,0:T(8,128)(2,1)S(1)} %constant_dynamic-slice_fusion.2.p0), channel_id=1, source_target_pairs={{0,3},{1,0},{2,1},{3,2},{4,7},{5,4},{6,5},{7,6},{8,11},{9,8},{10,9... | collective-permute-start | bytes 786440 | tf_op jit(solution)/shard_map/ppermute | solution.py:34
  15.2 28.6 %collective-permute-start.8 = (bf16[512,256]{1,0:T(8,128)(2,1)S(1)}, bf16[512,256]{1,0:T(8,128)(2,1)S(1)}, u32[]{:S(2)}, u32[]{:S(2)}) collective-permute-start(bf16[512,256]{1,0:T(8,128)(2,1)S(1)} %constant_dynamic-slice_fusion.2.p0), channel_id=1, source_target_pairs={{0,2},{1,3},{2,0},{3,1},{4,6},{5,7},{6,4},{7,5},{8,10},{9,11},{10,... | collective-permute-start | bytes 786440 | tf_op jit(solution)/shard_map/ppermute | solution.py:33
  16.8 140.8 %reduce-scatter.3.cloned.1.call-start = ((), (), s32[]{:S(2)}) async-start(), calls=%async_computation.3 | async-start | bytes 4423680 | tf_op jit(solution)/shard_map/reduce_scatter | solution.py:780
  22.6 21.2 %collective-permute-start.9 = (bf16[512,256]{1,0:T(8,128)(2,1)S(1)}, bf16[512,256]{1,0:T(8,128)(2,1)S(1)}, u32[]{:S(2)}, u32[]{:S(2)}) collective-permute-start(bf16[512,256]{1,0:T(8,128)(2,1)S(1)} %constant_dynamic-slice_fusion.2.p0), channel_id=1, source_target_pairs={{0,1},{1,2},{2,3},{3,0},{4,5},{5,6},{6,7},{7,4},{8,9},{9,10},{10,1... | collective-permute-start | bytes 786440 | tf_op jit(solution)/shard_map/ppermute | solution.py:34
  38.5 14.9 %collective-permute-start.4 = (bf16[512,256]{1,0:T(8,128)(2,1)}, bf16[512,256]{1,0:T(8,128)(2,1)S(1)}, u32[]{:S(2)}, u32[]{:S(2)}) collective-permute-start(bf16[512,256]{1,0:T(8,128)(2,1)} %get-tuple-element.104.m0.refs_4_), channel_id=1, source_target_pairs={{0,3},{1,0},{2,1},{3,2},{4,7},{5,4},{6,5},{7,6},{8,11},{9,8},{10,9... | collective-permute-start | bytes 786440 | tf_op jit(solution)/shard_map/ppermute | solution.py:34
  41.0 12.4 %collective-permute-start.5 = (bf16[512,256]{1,0:T(8,128)(2,1)}, bf16[512,256]{1,0:T(8,128)(2,1)S(1)}, u32[]{:S(2)}, u32[]{:S(2)}) collective-permute-start(bf16[512,256]{1,0:T(8,128)(2,1)} %get-tuple-element.104.m0.refs_4_), channel_id=1, source_target_pairs={{0,2},{1,3},{2,0},{3,1},{4,6},{5,7},{6,4},{7,5},{8,10},{9,11},{10,... | collective-permute-start | bytes 786440 | tf_op jit(solution)/shard_map/ppermute | solution.py:33
  42.4 15.8 %collective-permute-start.6 = (bf16[512,256]{1,0:T(8,128)(2,1)}, bf16[512,256]{1,0:T(8,128)(2,1)S(1)}, u32[]{:S(2)}, u32[]{:S(2)}) collective-permute-start(bf16[512,256]{1,0:T(8,128)(2,1)} %get-tuple-element.104.m0.refs_4_), channel_id=1, source_target_pairs={{0,1},{1,2},{2,3},{3,0},{4,5},{5,6},{6,7},{7,4},{8,9},{9,10},{10,1... | collective-permute-start | bytes 786440 | tf_op jit(solution)/shard_map/ppermute | solution.py:34
  47.6 10.6 %collective-permute-start.10 = (bf16[512,1024]{1,0:T(8,128)(2,1)}, bf16[512,1024]{1,0:T(8,128)(2,1)S(1)}, u32[]{:S(2)}, u32[]{:S(2)}) collective-permute-start(bf16[512,1024]{1,0:T(8,128)(2,1)} %shard_map.172.half), channel_id=1, source_target_pairs={{0,4},{4,0},{8,12},{12,8},{16,20},{20,16},{24,28},{28,24},{32,36},... | collective-permute-start | bytes 3145736 | tf_op jit(solution)/shard_map/ppermute | solution.py:832
  77.5 16.0 %collective-permute-start.13 = (bf16[512,256]{1,0:T(8,128)(2,1)}, bf16[512,256]{1,0:T(8,128)(2,1)S(1)}, u32[]{:S(2)}, u32[]{:S(2)}) collective-permute-start(bf16[512,256]{1,0:T(8,128)(2,1)} %get-tuple-element.122), channel_id=1, source_target_pairs={{0,2},{1,3},{2,0},{3,1},{4,6},{5,7},{6,4},{7,5},{8,10},{9,11},{10,... | collective-permute-start | bytes 786440 | tf_op jit(solution)/shard_map/ppermute | solution.py:857
  80.0 13.5 %collective-permute-start.14 = (bf16[512,256]{1,0:T(8,128)(2,1)}, bf16[512,256]{1,0:T(8,128)(2,1)S(1)}, u32[]{:S(2)}, u32[]{:S(2)}) collective-permute-start(bf16[512,256]{1,0:T(8,128)(2,1)} %get-tuple-element.123), channel_id=1, source_target_pairs={{0,1},{1,2},{2,3},{3,0},{4,5},{5,6},{6,7},{7,4},{8,9},{9,10},{10,1... | collective-permute-start | bytes 786440 | tf_op jit(solution)/shard_map/ppermute | solution.py:857
  80.0 13.5 %collective-permute-start.15 = (bf16[512,256]{1,0:T(8,128)(2,1)}, bf16[512,256]{1,0:T(8,128)(2,1)S(1)}, u32[]{:S(2)}, u32[]{:S(2)}) collective-permute-start(bf16[512,256]{1,0:T(8,128)(2,1)} %get-tuple-element.124), channel_id=1, source_target_pairs={{0,3},{1,0},{2,1},{3,2},{4,7},{5,4},{6,5},{7,6},{8,11},{9,8},{10,9... | collective-permute-start | bytes 786440 | tf_op jit(solution)/shard_map/ppermute | solution.py:857
  93.0 7.0 %collective-permute-start.12 = (bf16[2,4,32,3456]{3,2,1,0:T(8,128)(2,1)}, bf16[2,4,32,3456]{3,2,1,0:T(8,128)(2,1)S(1)}, u32[]{:S(2)}, u32[]{:S(2)}) collective-permute-start(bf16[2,4,32,3456]{3,2,1,0:T(8,128)(2,1)} %get-tuple-element.120), channel_id=1, source_target_pairs={{0,4},{4,0},{8,12},{12,8},{16,20},{20,16},{24,28},{28,24},{32,36},... | collective-permute-start | bytes 5308424 | tf_op jit(solution)/shard_map/ppermute | solution.py:439
  97.1 10.1 %collective-permute-start.16 = (bf16[512,256]{1,0:T(8,128)(2,1)}, bf16[512,256]{1,0:T(8,128)(2,1)S(1)}, u32[]{:S(2)}, u32[]{:S(2)}) collective-permute-start(bf16[512,256]{1,0:T(8,128)(2,1)} %get-tuple-element.127), channel_id=1, source_target_pairs={{0,3},{1,0},{2,1},{3,2},{4,7},{5,4},{6,5},{7,6},{8,11},{9,8},{10,9... | collective-permute-start | bytes 786440 | tf_op jit(solution)/shard_map/ppermute | solution.py:34
  98.4 11.0 %collective-permute-start.17 = (bf16[512,256]{1,0:T(8,128)(2,1)}, bf16[512,256]{1,0:T(8,128)(2,1)S(1)}, u32[]{:S(2)}, u32[]{:S(2)}) collective-permute-start(bf16[512,256]{1,0:T(8,128)(2,1)} %get-tuple-element.127), channel_id=1, source_target_pairs={{0,2},{1,3},{2,0},{3,1},{4,6},{5,7},{6,4},{7,5},{8,10},{9,11},{10,... | collective-permute-start | bytes 786440 | tf_op jit(solution)/shard_map/ppermute | solution.py:33
  100.0 13.7 %collective-permute-start.18 = (bf16[512,256]{1,0:T(8,128)(2,1)}, bf16[512,256]{1,0:T(8,128)(2,1)S(1)}, u32[]{:S(2)}, u32[]{:S(2)}) collective-permute-start(bf16[512,256]{1,0:T(8,128)(2,1)} %get-tuple-element.127), channel_id=1, source_target_pairs={{0,1},{1,2},{2,3},{3,0},{4,5},{5,6},{6,7},{7,4},{8,9},{9,10},{10,1... | collective-permute-start | bytes 786440 | tf_op jit(solution)/shard_map/ppermute | solution.py:34
  113.7 73.2 %reduce-scatter.5.cloned.1.call-start = ((), (), s32[]{:S(2)}) async-start(), calls=%async_computation.4 | async-start | bytes 1105920 | tf_op jit(solution)/shard_map/reduce_scatter | solution.py:780
  130.4 12.4 %collective-permute-start.22 = (bf16[576,256]{1,0:T(8,128)(2,1)}, bf16[576,256]{1,0:T(8,128)(2,1)S(1)}, u32[]{:S(2)}, u32[]{:S(2)}) collective-permute-start(bf16[576,256]{1,0:T(8,128)(2,1)} %get-tuple-element.145), channel_id=1, source_target_pairs={{0,2},{1,3},{2,0},{3,1},{4,6},{5,7},{6,4},{7,5},{8,10},{9,11},{10,... | collective-permute-start | bytes 884744 | tf_op jit(solution)/shard_map/ppermute | solution.py:879
  131.8 16.6 %collective-permute-start.23 = (bf16[576,256]{1,0:T(8,128)(2,1)}, bf16[576,256]{1,0:T(8,128)(2,1)S(1)}, u32[]{:S(2)}, u32[]{:S(2)}) collective-permute-start(bf16[576,256]{1,0:T(8,128)(2,1)} %get-tuple-element.146), channel_id=1, source_target_pairs={{0,1},{1,2},{2,3},{3,0},{4,5},{5,6},{6,7},{7,4},{8,9},{9,10},{10,1... | collective-permute-start | bytes 884744 | tf_op jit(solution)/shard_map/ppermute | solution.py:879
  131.8 16.6 %collective-permute-start.24 = (bf16[576,256]{1,0:T(8,128)(2,1)}, bf16[576,256]{1,0:T(8,128)(2,1)S(1)}, u32[]{:S(2)}, u32[]{:S(2)}) collective-permute-start(bf16[576,256]{1,0:T(8,128)(2,1)} %get-tuple-element.147), channel_id=1, source_target_pairs={{0,3},{1,0},{2,1},{3,2},{4,7},{5,4},{6,5},{7,6},{8,11},{9,8},{10,9... | collective-permute-start | bytes 884744 | tf_op jit(solution)/shard_map/ppermute | solution.py:879
  140.9 12.7 %collective-permute-start.20 = (bf16[2,4,32,1024]{3,2,1,0:T(8,128)(2,1)}, bf16[2,4,32,1024]{3,2,1,0:T(8,128)(2,1)S(1)}, u32[]{:S(2)}, u32[]{:S(2)}) collective-permute-start(bf16[2,4,32,1024]{3,2,1,0:T(8,128)(2,1)} %get-tuple-element.142), channel_id=1, source_target_pairs={{0,4},{4,0},{8,12},{12,8},{16,20},{20,16},{24,28},{28,24},{32,36},... | collective-permute-start | bytes 1572872 | tf_op jit(solution)/shard_map/ppermute | solution.py:439
  142.8 10.8 %collective-permute-start.21 = (bf16[2,4,32,1024]{3,2,1,0:T(8,128)(2,1)}, bf16[2,4,32,1024]{3,2,1,0:T(8,128)(2,1)S(1)}, u32[]{:S(2)}, u32[]{:S(2)}) collective-permute-start(bf16[2,4,32,1024]{3,2,1,0:T(8,128)(2,1)} %get-tuple-element.143), channel_id=1, source_target_pairs={{0,4},{4,0},{8,12},{12,8},{16,20},{20,16},{24,28},{28,24},{32,36},... | collective-permute-start | bytes 1572872 | tf_op jit(solution)/shard_map/ppermute | solution.py:439
  157.6 12.2 %collective-permute-start.29 = (bf16[144,1024]{1,0:T(8,128)(2,1)}, bf16[144,1024]{1,0:T(8,128)(2,1)S(1)}, u32[]{:S(2)}, u32[]{:S(2)}) collective-permute-start(bf16[144,1024]{1,0:T(8,128)(2,1)} %get-tuple-element.166), channel_id=1, source_target_pairs={{0,16},{4,20},{8,24},{12,28},{16,0},{20,4},{24,8},{28,12},{32,48},... | collective-permute-start | bytes 884744 | tf_op jit(solution)/shard_map/ppermute | solution.py:898
  161.8 13.9 %collective-permute-start.30 = (bf16[144,1024]{1,0:T(8,128)(2,1)}, bf16[144,1024]{1,0:T(8,128)(2,1)S(1)}, u32[]{:S(2)}, u32[]{:S(2)}) collective-permute-start(bf16[144,1024]{1,0:T(8,128)(2,1)} %get-tuple-element.167), channel_id=1, source_target_pairs={{0,8},{4,12},{8,16},{12,20},{16,24},{20,28},{24,0},{28,4},{32,40},... | collective-permute-start | bytes 884744 | tf_op jit(solution)/shard_map/ppermute | solution.py:898
  162.7 13.8 %collective-permute-start.31 = (bf16[144,1024]{1,0:T(8,128)(2,1)}, bf16[144,1024]{1,0:T(8,128)(2,1)S(1)}, u32[]{:S(2)}, u32[]{:S(2)}) collective-permute-start(bf16[144,1024]{1,0:T(8,128)(2,1)} %get-tuple-element.168), channel_id=1, source_target_pairs={{0,24},{4,28},{8,0},{12,4},{16,8},{20,12},{24,16},{28,20},{32,56},... | collective-permute-start | bytes 884744 | tf_op jit(solution)/shard_map/ppermute | solution.py:898
  165.0 14.4 %collective-permute-start.26 = (bf16[512,256]{1,0:T(8,128)(2,1)S(1)}, bf16[512,256]{1,0:T(8,128)(2,1)S(1)}, u32[]{:S(2)}, u32[]{:S(2)}) collective-permute-start(bf16[512,256]{1,0:T(8,128)(2,1)S(1)} %copy-done.36), channel_id=1, source_target_pairs={{0,2},{1,3},{2,0},{3,1},{4,6},{5,7},{6,4},{7,5},{8,10},{9,11},{10,... | collective-permute-start | bytes 786440 | tf_op jit(solution)/shard_map/ppermute | solution.py:900
  167.0 12.7 %collective-permute-start.27 = (bf16[512,256]{1,0:T(8,128)(2,1)S(1)}, bf16[512,256]{1,0:T(8,128)(2,1)S(1)}, u32[]{:S(2)}, u32[]{:S(2)}) collective-permute-start(bf16[512,256]{1,0:T(8,128)(2,1)S(1)} %copy-done.35), channel_id=1, source_target_pairs={{0,1},{1,2},{2,3},{3,0},{4,5},{5,6},{6,7},{7,4},{8,9},{9,10},{10,1... | collective-permute-start | bytes 786440 | tf_op jit(solution)/shard_map/ppermute | solution.py:900
  169.8 9.9 %collective-permute-start.28 = (bf16[512,256]{1,0:T(8,128)(2,1)S(1)}, bf16[512,256]{1,0:T(8,128)(2,1)S(1)}, u32[]{:S(2)}, u32[]{:S(2)}) collective-permute-start(bf16[512,256]{1,0:T(8,128)(2,1)S(1)} %copy-done.34), channel_id=1, source_target_pairs={{0,3},{1,0},{2,1},{3,2},{4,7},{5,4},{6,5},{7,6},{8,11},{9,8},{10,9... | collective-permute-start | bytes 786440 | tf_op jit(solution)/shard_map/ppermute | solution.py:900
  179.7 9.8 %collective-permute-start.32 = (bf16[48,1024]{1,0:T(8,128)(2,1)}, bf16[48,1024]{1,0:T(8,128)(2,1)S(1)}, u32[]{:S(2)}, u32[]{:S(2)}) collective-permute-start(bf16[48,1024]{1,0:T(8,128)(2,1)} %get-tuple-element.179), channel_id=1, source_target_pairs={{0,64},{4,68},{8,72},{12,76},{16,80},{20,84},{24,88},{28,92},{32,9... | collective-permute-start | bytes 294920 | tf_op jit(solution)/shard_map/ppermute | solution.py:908
  (51 other events, 302.0 us)
Sparse Core Ops, SparseCore 0:
  16.9 35.7 all-gather.1
  113.8 42.9 reduce-scatter.2
  159.3 22.6 reduce-scatter.4
